TPU v7x, 32 devices: a whole 2x2x4 slice. The times are simulated.
32 devices in a mesh: dp: 4 (over z), dom: 8 (over y, x, core).
Axes of the slice: x: 2, y: 2, z: 4, core: 2. Of those that a mesh axis runs over, the one named last changes fastest.
Arguments:
- grad_out: bfloat16 [4, 24, 512, 256], P('dp', 'dom'), may hold values from -6 to 6
- pre_act: bfloat16 [4, 24, 512, 256], P('dp', 'dom'), may hold values from -6 to 6
- conv_weight: bfloat16 [27, 256, 256], replicated, may hold values from -0.078125 to 0.078125
- down_weight: bfloat16 [8, 128, 256], replicated, may hold values from -0.1875 to 0.1875
- fine_act: bfloat16 [4, 192, 512, 128], P('dp', 'dom'), may hold values from -6 to 6
- neighbours: int32 [4, 24, 27], P('dp', 'dom'), may hold values from -1 to 2, as said below
- octant_routes: int32 [4, 8, 3, 8], P('dp', 'dom'), may hold values from -1 to 23, as said below
Outputs:
- fine_grad: bfloat16 [4, 192, 512, 128], P('dp', 'dom')
- conv_weight_grad: float32 [6912, 256], P('dp')
- down_weight_grad: float32 [1024, 256], P('dp')
Inputs may be any that keep to these rules, and one draw needn't show every extreme that they name: `neighbours`: each device of a scene group has between half of 3 (rounded up) and 3 live slots, always the first ones, and some device of each scene group has all 3 live. A live slot's entry 13 is itself; entry 9(a+1)+3(b+1)+(c+1) is the slot, on the device a steps along dom, of the block displaced by (a, b, c) block edges within a slab of 3 x 3 positions, or -1 where that block is empty or outside the scene group; dead slots hold -1 in all 27 entries; the relation is symmetric. `octant_routes`: row (d, k) lists what device d sends to the device d + k - 1 along dom, taken cyclically: entries 8 s + o name octant o of slot s; each live slot's 8 octants stand together, in order, in exactly one row; live entries come first, then -1. A row holds at most 8 entries, and some row of the fullest device holds exactly 8. Dead slots are never named.
All inputs are finite; a program needn't handle non-finite values.
Results may differ from a plain program's by a relative error of at most 0.0065.
Values may be sent and summed in bfloat16 or wider, within the bound.
No kernel may reach another device: no remote copies, remote signals or barrier semaphores. Data moves between devices by JAX's collectives and lax.ppermute only.
A program may use at most 128 MiB of HBM per device.

v0:
```python
import functools
import math

import jax
import jax.numpy as jnp
from jax import lax
from jax.experimental import pallas as pl
from jax.experimental.pallas import tpu as pltpu
from jax.sharding import PartitionSpec as P

BE = 8
PLANE = BE * BE
HALF = BE // 2
F32 = jnp.float32
BF16 = jnp.bfloat16
MIB = 1 << 20

VMEM = pl.BlockSpec(memory_space=pltpu.VMEM)
SMEM = pl.BlockSpec(memory_space=pltpu.SMEM)
ANY = pl.BlockSpec(memory_space=pl.ANY)


def params(mib):
    return pltpu.CompilerParams(vmem_limit_bytes=mib * MIB)


def relative(index, step, count):
    if count & (count - 1) == 0:
        return index ^ step
    return lax.rem(index + step, count)


def source_of(index, step, count):
    if count & (count - 1) == 0:
        return index ^ step
    return (index - step) % count if isinstance(index, int) else lax.rem(index + count - step, count)


def exchange(value, axis, step, stride):
    count = lax.axis_size(axis) // stride
    pairs = []
    for index in range(lax.axis_size(axis)):
        high, low = divmod(index, stride)
        other = high ^ step if count & (count - 1) == 0 else (high + step) % count
        pairs.append((index, other * stride + low))
    return lax.ppermute(value, axis, pairs)


def fetch(ref, slot, start, rows):
    value = ref[jnp.maximum(slot, 0), pl.ds(start, rows), :].astype(F32)
    return jnp.where(slot >= 0, value, 0.0)


def spread(links_ref, ref, start, step_x, slot, row, win_ref):
    channels = ref.shape[-1]

    def link(step_y, step_z):
        return links_ref[slot, 9 * (step_x + 1) + 3 * (step_y + 1) + step_z + 1]

    columns = {}
    for step_z in (-1, 0, 1):
        below = fetch(ref, link(-1, step_z), start + PLANE - 16, 16).reshape(2, BE, channels)[1:]
        middle = fetch(ref, link(0, step_z), start, PLANE).reshape(BE, BE, channels)
        above = fetch(ref, link(1, step_z), start, 16).reshape(2, BE, channels)[:1]
        columns[step_z] = jnp.concatenate([below, middle, above], axis=0)
    place_z = lax.broadcasted_iota(jnp.int32, columns[0].shape, 1)
    shifted = {
        0: columns[0],
        -1: jnp.where(
            place_z == 0, pltpu.roll(columns[-1], 1, axis=1), pltpu.roll(columns[0], 1, axis=1)
        ),
        1: jnp.where(
            place_z == BE - 1,
            pltpu.roll(columns[1], BE - 1, axis=1),
            pltpu.roll(columns[0], BE - 1, axis=1),
        ),
    }
    for tap_y in (-1, 0, 1):
        for tap_z in (-1, 0, 1):
            tap = 3 * (tap_y + 1) + tap_z + 1
            value = shifted[-tap_z][1 - tap_y : 1 - tap_y + BE].reshape(PLANE, channels)
            win_ref[pl.ds(row, PLANE), tap * channels : (tap + 1) * channels] = value.astype(BF16)


def build_windows(links_ref, own_ref, low_ref, high_ref, win_ref):
    slots = own_ref.shape[0]

    def edge(slot, carry):
        spread(links_ref, low_ref, 0, -1, slot, pl.multiple_of(slot * PLANE, PLANE), win_ref)
        row = ((BE + 1) * slots + slot) * PLANE
        spread(links_ref, high_ref, 0, 1, slot, pl.multiple_of(row, PLANE), win_ref)
        return carry

    def inner(step, carry):
        x = step // slots
        slot = step - x * slots
        row = (x + 1) * slots * PLANE + slot * PLANE
        start = pl.multiple_of(x * PLANE, PLANE)
        spread(links_ref, own_ref, start, 0, slot, pl.multiple_of(row, PLANE), win_ref)
        return carry

    lax.fori_loop(0, slots, edge, 0)
    lax.fori_loop(0, BE * slots, inner, 0)


def input_kernel(
    links_ref, routes_ref, own_ref, low_ref, high_ref, pre_ref, weight_ref,
    windows_ref, to_lower_ref, stay_ref, to_upper_ref,
    win_ref, taps_ref, acc_ref, octants_ref, tap_sems, out_sems,
):
    slots, voxels, channels = own_ref.shape
    places = routes_ref.shape[1]
    groups = places // 8
    copies = []
    for tap in range(27):
        index_x, rest = divmod(tap, 9)
        copy = pltpu.make_async_copy(
            weight_ref.at[tap],
            taps_ref.at[index_x, :, rest * channels : (rest + 1) * channels],
            tap_sems.at[tap],
        )
        copy.start()
        copies.append(copy)
    build_windows(links_ref, own_ref, low_ref, high_ref, win_ref)
    for copy in copies:
        copy.wait()
    outs = [pltpu.make_async_copy(win_ref, windows_ref, out_sems.at[3])]
    outs[0].start()
    slab = slots * PLANE
    rows = BE * slab
    half = rows // 2

    def multiply(part, carry):
        start = part * half
        total = None
        for index_x in range(3):
            offset = pl.multiple_of(start + (2 - index_x) * slab, PLANE)
            term = lax.dot_general(
                win_ref[pl.ds(offset, half), :],
                taps_ref[index_x],
                (((1,), (1,)), ((), ())),
                preferred_element_type=F32,
            )
            total = term if total is None else total + term
        acc_ref[pl.ds(pl.multiple_of(start, PLANE), half), :] = total
        return carry

    lax.fori_loop(0, 2, multiply, 0)
    octants_ref[...] = jnp.zeros_like(octants_ref)
    place_z = lax.broadcasted_iota(jnp.int32, (BE // 2, BE, channels), 1)
    for slot in range(slots):
        group = jnp.int32(3 * groups)
        for row in range(3):
            for part in range(groups):
                group = jnp.where(
                    routes_ref[row, 8 * part] == 8 * slot, row * groups + part, group
                )

        def finish(x, carry):
            value = acc_ref[pl.ds(pl.multiple_of(x * slab + slot * PLANE, PLANE), PLANE), :]
            pre = pre_ref[slot, pl.ds(pl.multiple_of(x * PLANE, PLANE), PLANE), :].astype(F32)
            value = jnp.where(pre > 0, value, 0.0).reshape(BE // 2, 2, BE, channels)
            even, odd = value[:, 0], value[:, 1]
            near = jnp.where(place_z < HALF, even, pltpu.roll(odd, HALF, axis=1))
            far = jnp.where(place_z < HALF, pltpu.roll(even, HALF, axis=1), odd)
            side = x // HALF
            row = (x - side * HALF) * 16
            for side_y in range(2):
                for side_z, piece in enumerate((near, far)):
                    block = piece[2 * side_y : 2 * side_y + 2].reshape(16, channels).astype(BF16)
                    start = (4 * side + 2 * side_y + side_z) * PLANE + row
                    octants_ref[group, pl.ds(pl.multiple_of(start, 16), 16), :] = block
            return carry

        lax.fori_loop(0, BE, finish, 0)
    for row, ref in enumerate((to_lower_ref, stay_ref, to_upper_ref)):
        copy = pltpu.make_async_copy(
            octants_ref.at[pl.ds(row * groups, groups)], ref, out_sems.at[row]
        )
        copy.start()
        outs.append(copy)
    for copy in outs:
        copy.wait()


def input_gradient(links, routes, own, low, high, pre, weight):
    slots, voxels, channels = own.shape
    groups = routes.shape[1] // 8
    rows = slots * voxels
    out = jax.ShapeDtypeStruct((groups, voxels, channels), BF16)
    windows = jax.ShapeDtypeStruct((slots * PLANE * (BE + 2), 9 * channels), BF16)
    return pl.pallas_call(
        input_kernel,
        out_shape=(windows, out, out, out),
        in_specs=[SMEM, SMEM, VMEM, VMEM, VMEM, VMEM, ANY],
        out_specs=(ANY, ANY, ANY, ANY),
        scratch_shapes=[
            pltpu.VMEM(windows.shape, BF16),
            pltpu.VMEM((3, channels, 9 * channels), BF16),
            pltpu.VMEM((rows, channels), F32),
            pltpu.VMEM((3 * groups + 1, voxels, channels), BF16),
            pltpu.SemaphoreType.DMA((27,)),
            pltpu.SemaphoreType.DMA((4,)),
        ],
        compiler_params=params(48),
        cost_estimate=pl.CostEstimate(
            flops=2 * rows * 27 * channels * channels, bytes_accessed=8 * MIB, transcendentals=0
        ),
        name="input_gradient",
    )(links, routes, own, low, high, pre, weight)


def filter_kernel(shard_rows, win_ref, pre_ref, keep_ref, send_ref, act_ref):
    slots, _, channels = pre_ref.shape
    slab = slots * PLANE
    rows = BE * slab
    lanes = channels // 2
    rest = pl.program_id(0)

    @pl.when(rest == 0)
    def _():
        for pair in range(BE // 2):
            parts = []
            for x in (2 * pair, 2 * pair + 1):
                for slot in range(slots):
                    parts.append(pre_ref[slot, x * PLANE : (x + 1) * PLANE, :])
            block = jnp.maximum(jnp.concatenate(parts, axis=0).astype(F32), 0.0)
            act_ref[:, pair * 2 * slab : (pair + 1) * 2 * slab] = block.T.astype(BF16)

    first = lax.rem(lax.axis_index("dom"), 2) == 0
    unit = math.gcd(channels, shard_rows)
    for index_x in range(3):
        offset = (2 - index_x) * slab
        total = jnp.dot(
            act_ref[...], win_ref[offset : offset + rows, :], preferred_element_type=F32
        )
        left, right = total[:, :lanes], total[:, lanes:]
        keep = jnp.where(first, left, right).astype(BF16)
        send = jnp.where(first, right, left).astype(BF16)
        for part in range(channels // unit):
            row = (index_x * 9 + rest) * channels + part * unit
            shard = row // shard_rows
            start = pl.multiple_of(row - shard * shard_rows, unit)
            span = slice(part * unit, (part + 1) * unit)
            keep_ref[shard, pl.ds(start, unit), :] = keep[span]
            send_ref[shard, pl.ds(start, unit), :] = send[span]


def filter_gradient(shards, windows, pre):
    slots, voxels, channels = pre.shape
    shard_rows = 27 * channels // shards
    rows = slots * voxels
    out = jax.ShapeDtypeStruct((shards, shard_rows, channels // 2), BF16)
    same = pl.BlockSpec(out.shape, lambda i: (0, 0, 0))
    return pl.pallas_call(
        functools.partial(filter_kernel, shard_rows),
        grid=(9,),
        out_shape=(out, out),
        in_specs=[
            pl.BlockSpec((windows.shape[0], channels), lambda i: (0, i)),
            pl.BlockSpec(pre.shape, lambda i: (0, 0, 0)),
        ],
        out_specs=(same, same),
        scratch_shapes=[pltpu.VMEM((channels, rows), BF16)],
        compiler_params=params(40),
        cost_estimate=pl.CostEstimate(
            flops=2 * rows * 27 * channels * channels, bytes_accessed=12 * MIB, transcendentals=0
        ),
        name="filter_gradient",
    )(windows, pre)


def fine_kernel(
    groups, upper_ref, stay_ref, lower_ref, weight_ref, act_ref,
    grad_ref, keep_ref, send_ref, acc_ref,
):
    step = pl.program_id(0)
    fine, voxels, fine_channels = act_ref.shape
    channels = upper_ref.shape[-1]
    taps = weight_ref.shape[0]
    cells = voxels // taps

    @pl.when(step == 0)
    def _():
        acc_ref[...] = jnp.zeros_like(acc_ref)

    def work(ref):
        octants = ref[0]
        product = lax.dot_general(
            octants,
            weight_ref[...].reshape(taps * fine_channels, channels),
            (((1,), (1,)), ((), ())),
            preferred_element_type=F32,
        ).astype(BF16)
        wide = []
        for place in range(fine):
            for tap in range(taps):
                grad_ref[place, tap * cells : (tap + 1) * cells, :] = product[
                    place * cells : (place + 1) * cells,
                    tap * fine_channels : (tap + 1) * fine_channels,
                ]
            wide.append(
                jnp.concatenate(
                    [act_ref[place, tap * cells : (tap + 1) * cells, :] for tap in range(taps)],
                    axis=1,
                )
            )
        acc_ref[...] += jnp.dot(
            octants.T, jnp.concatenate(wide, axis=0), preferred_element_type=F32
        )

    for row, ref in enumerate((upper_ref, stay_ref, lower_ref)):
        pl.when(step // groups == row)(functools.partial(work, ref))

    @pl.when(step == pl.num_programs(0) - 1)
    def _():
        total = acc_ref[...].T
        first = lax.rem(lax.axis_index("dom"), 2) == 0
        lanes = channels // 2
        shards = keep_ref.shape[0]
        rows = total.shape[0] // shards
        left = total[:, :lanes].reshape(shards, rows, lanes)
        right = total[:, lanes:].reshape(shards, rows, lanes)
        keep_ref[:, :rows, :] = jnp.where(first, left, right).astype(BF16)
        send_ref[:, :rows, :] = jnp.where(first, right, left).astype(BF16)


def fine_gradient(shards, count, from_upper, stay, from_lower, weight, fine_act):
    fine, voxels, fine_channels = fine_act.shape
    groups, _, channels = stay.shape
    taps = weight.shape[0]
    whole = pl.BlockSpec((1, voxels, channels), lambda i: (i % groups, 0, 0))
    rows = count * piece_rows(taps * fine_channels // shards, count)
    down = jax.ShapeDtypeStruct((shards, rows, channels // 2), BF16)
    same = pl.BlockSpec(down.shape, lambda i: (0, 0, 0))
    block = pl.BlockSpec((8, voxels, fine_channels), lambda i: (i, 0, 0))
    return pl.pallas_call(
        functools.partial(fine_kernel, groups),
        grid=(3 * groups,),
        out_shape=(jax.ShapeDtypeStruct(fine_act.shape, BF16), down, down),
        in_specs=[
            whole, whole, whole,
            pl.BlockSpec(weight.shape, lambda i: (0, 0, 0)),
            block,
        ],
        out_specs=(block, same, same),
        scratch_shapes=[pltpu.VMEM((channels, taps * fine_channels), F32)],
        compiler_params=params(40),
        cost_estimate=pl.CostEstimate(
            flops=64 * fine * voxels * fine_channels * channels, bytes_accessed=8 * MIB,
            transcendentals=0,
        ),
        name="fine_gradient",
    )(from_upper, stay, from_lower, weight, fine_act)


def piece_rows(rows, count):
    return -(-rows // (16 * count)) * 16


def cost(*arrays):
    moved = sum(math.prod(x.shape) * jnp.dtype(x.dtype).itemsize for x in arrays)
    return pl.CostEstimate(flops=moved, bytes_accessed=moved, transcendentals=0)


def shapes_of(count, shape):
    return [jax.ShapeDtypeStruct(shape, F32 if step == 0 else BF16) for step in range(count)]


def pair_kernel(count, conv_ref, conv_got_ref, down_ref, down_got_ref, plane_ref, *slabs):
    shards, rows, _ = conv_ref.shape
    down_piece = down_ref.shape[1] // count
    piece = plane_ref.shape[2] - down_piece
    for place in range(count):
        for keep_ref, got_ref, size, start in (
            (conv_ref, conv_got_ref, piece, 0),
            (down_ref, down_got_ref, down_piece, piece),
        ):
            span = slice(place * size, (place + 1) * size)
            total = keep_ref[:, span, :].astype(F32) + got_ref[:, span, :].astype(F32)
            plane_ref[place, :, start : start + size, :] = total.astype(BF16)
    cut = count * piece
    for step, ref in enumerate(slabs):
        shard = relative(lax.axis_index("dp"), step, shards)
        total = conv_ref[shard, cut:, :].astype(F32) + conv_got_ref[shard, cut:, :].astype(F32)
        ref[: rows - cut, :] = total.astype(ref.dtype)


def pair_sum(count, conv, conv_got, down, down_got):
    shards, rows, lanes = conv.shape
    down_piece = down.shape[1] // count
    unit = 16 * count
    piece = 16 * round((2 * (rows + down.shape[1]) / 3 - down.shape[1]) / unit)
    rest = count * piece_rows(rows - count * piece, count)
    outs = [jax.ShapeDtypeStruct((count, shards, piece + down_piece, lanes), BF16)]
    outs += shapes_of(shards, (rest, lanes))
    outs = pl.pallas_call(
        functools.partial(pair_kernel, count),
        out_shape=outs,
        in_specs=[VMEM] * 4,
        out_specs=[VMEM] * len(outs),
        compiler_params=params(32),
        cost_estimate=cost(conv, conv_got, *outs),
        name="pair_sum",
    )(conv, conv_got, down, down_got)
    return outs[0], outs[1:], (piece, down_piece, rest // count)


def middle_kernel(shards, plane_ref, *refs):
    slabs, to_slabs_ref, to_planes = refs[:shards], refs[shards], refs[shards + 1 :]
    count = plane_ref.shape[0]
    for shard in range(shards):
        total = plane_ref[0, shard].astype(F32)
        for place in range(1, count):
            total = total + plane_ref[place, shard].astype(F32)
        to_slabs_ref[shard] = total.astype(BF16)
    piece = to_planes[0].shape[0]
    high = lax.axis_index("dom") // 2
    for step, ref in enumerate(to_planes):
        span = pl.ds(pl.multiple_of(relative(high, step, count) * piece, 16), piece)
        total = slabs[0][span, :]
        for part in slabs[1:]:
            total = total + part[span, :].astype(F32)
        ref[...] = total.astype(ref.dtype)


def middle_sum(planes, slabs):
    count, shards, piece, lanes = planes.shape
    outs = [jax.ShapeDtypeStruct((shards, piece, lanes), BF16)]
    outs += shapes_of(count, (slabs[0].shape[0] // count, lanes))
    parts = [planes, *slabs]
    outs = pl.pallas_call(
        functools.partial(middle_kernel, shards),
        out_shape=outs,
        in_specs=[VMEM] * len(parts),
        out_specs=[VMEM] * len(outs),
        compiler_params=params(32),
        cost_estimate=cost(*parts, *outs),
        name="middle_sum",
    )(*parts)
    return outs[0], outs[1:]


def last_kernel(factor, slabs_ref, *refs):
    planes, out_ref = refs[:-1], refs[-1]
    piece = slabs_ref.shape[1]
    total = slabs_ref[0].astype(F32)
    for shard in range(1, slabs_ref.shape[0]):
        total = total + slabs_ref[shard].astype(F32)
    out_ref[:piece, :] = (total * factor).astype(BF16)
    total = planes[0][...]
    for part in planes[1:]:
        total = total + part[...].astype(F32)
    out_ref[piece:, :] = (total * factor).astype(BF16)


def last_sum(factor, slabs, planes):
    _, piece, lanes = slabs.shape
    parts = [slabs, *planes]
    return pl.pallas_call(
        functools.partial(last_kernel, factor),
        out_shape=jax.ShapeDtypeStruct((piece + planes[0].shape[0], lanes), BF16),
        in_specs=[VMEM] * len(parts),
        out_specs=VMEM,
        compiler_params=params(32),
        cost_estimate=cost(*parts),
        name="last_sum",
    )(*parts)


def gather_kernel(count, pieces, *refs):
    near, far = refs[:count], refs[count : 2 * count]
    conv_ref, down_ref, *scratches = refs[2 * count :]
    lanes = near[0].shape[1]
    high = lax.axis_index("dom") // 2
    low = lax.rem(lax.axis_index("dom"), 2)
    start = 0
    firsts = (0, 0, count * pieces[0])
    for piece, first, out_ref, whole in zip(
        pieces, firsts, (conv_ref, down_ref, conv_ref), scratches
    ):
        for side, group in ((low, near), (1 - low, far)):
            lane = pl.ds(pl.multiple_of(side * lanes, lanes), lanes)
            for step, ref in enumerate(group):
                row = pl.multiple_of(source_of(high, step, count) * piece, 16)
                whole[pl.ds(row, piece), lane] = ref[start : start + piece, :].astype(F32)
        rows = min(count * piece, out_ref.shape[0] - first)
        out_ref[first : first + rows, :] = whole[:rows, :]
        start += piece


def gather_up(conv_rows, down_rows, pieces, near, far):
    count = len(near)
    lanes = near[0].shape[1]
    outs = [jax.ShapeDtypeStruct((rows, 2 * lanes), F32) for rows in (conv_rows, down_rows)]
    return pl.pallas_call(
        functools.partial(gather_kernel, count, pieces),
        out_shape=outs,
        in_specs=[VMEM] * (2 * count),
        out_specs=[VMEM] * 2,
        scratch_shapes=[pltpu.VMEM((count * piece, 2 * lanes), F32) for piece in pieces],
        compiler_params=params(32),
        cost_estimate=cost(*near, *far, *outs),
        name="gather_up",
    )(*near, *far)


def body(grad_out, pre_act, conv_weight, down_weight, fine_act, neighbours, octant_routes):
    own = grad_out[0]
    pre = pre_act[0]
    links = neighbours[0]
    routes = octant_routes[0, 0]
    slots, voxels, channels = own.shape
    devices = lax.axis_size("dom")
    shards = lax.axis_size("dp")
    count = devices // 2
    factor = 1.0 / math.sqrt(shards * devices * slots * voxels)

    forward = [(i, i + 1) for i in range(devices - 1)]
    backward = [(i + 1, i) for i in range(devices - 1)]
    ring = [(i, (i + 1) % devices) for i in range(devices)]
    swap = [(i, i ^ 1) for i in range(devices)]

    def spread_out(parts, axis, stride):
        return [parts[0]] + [
            exchange(parts[step], axis, step, stride) for step in range(1, len(parts))
        ]

    low = lax.ppermute(own[:, voxels - PLANE :], "dom", forward)
    high = lax.ppermute(own[:, :PLANE], "dom", backward)
    windows, to_lower, stay, to_upper = input_gradient(
        links, routes, own, low, high, pre, conv_weight
    )
    from_upper = lax.ppermute(to_lower, "dom", [(b, a) for a, b in ring])
    from_lower = lax.ppermute(to_upper, "dom", ring)
    conv_keep, conv_send = filter_gradient(shards, windows, pre)
    fine_grad, down_keep, down_send = fine_gradient(
        shards, count, from_upper, stay, from_lower, down_weight, fine_act[0]
    )
    conv_got = lax.ppermute(conv_send, "dom", swap)
    down_got = lax.ppermute(down_send, "dom", swap)

    planes, slabs, pieces = pair_sum(count, conv_keep, conv_got, down_keep, down_got)
    same_core = [[2 * high + low for high in range(count)] for low in range(2)]
    slabs = spread_out(slabs, "dp", 1)
    planes = lax.all_to_all(planes, "dom", 0, 0, axis_index_groups=same_core)
    to_slabs, to_planes = middle_sum(planes, slabs)
    to_planes = spread_out(to_planes, "dom", 2)
    to_slabs = lax.all_to_all(to_slabs, "dp", 0, 0)
    mine = last_sum(factor, to_slabs, to_planes)
    near = spread_out([mine] * count, "dom", 2)
    far = [lax.ppermute(value, "dom", swap) for value in near]
    conv_rows = 27 * channels // shards
    down_rows = down_weight.shape[0] * down_weight.shape[1] // shards
    conv_grad, down_grad = gather_up(conv_rows, down_rows, pieces, near, far)
    return (fine_grad[None], conv_grad, down_grad)


def solution(mesh):
    return jax.shard_map(
        body,
        mesh=mesh,
        in_specs=(
            P("dp", "dom", None, None),
            P("dp", "dom", None, None),
            P(),
            P(),
            P("dp", "dom", None, None),
            P("dp", "dom", None),
            P("dp", "dom", None, None),
        ),
        out_specs=(P("dp", "dom", None, None), P("dp", None), P("dp", None)),
        check_vma=False,
    )
```

profile of v0, /device:TPU:0, one launch (start us, length us, event | category | flops | bytes accessed | tf_op | source)
XLA Modules:
  0.0 94.0 jit_solution(17455888628293843078)
XLA Ops:
  0.6 1.0 %fusion = (bf16[3,64,256]{2,1,0:T(8,128)(2,1)S(1)}, bf16[3,64,256]{2,1,0:T(8,128)(2,1)S(1)}) fusion(bf16[3,512,256]{2,1,0:T(8,128)(2,1)} %bitcast.10), kind=kLoop, calls=%fused_computation.2 | loop fusion | bytes 393216 | tf_op jit(solution)/shard_map/slice | solution.py:530
  1.6 1.3 %collective-permute-start.1 = (bf16[3,64,256]{2,1,0:T(8,128)(2,1)S(1)}, bf16[3,64,256]{2,1,0:T(8,128)(2,1)S(1)}, u32[]{:S(2)}, u32[]{:S(2)}) collective-permute-start(bf16[3,64,256]{2,1,0:T(8,128)(2,1)S(1)} %get-tuple-element.45), channel_id=1, source_target_pairs={{1,0},{2,1},{3,2},{4,3},{5,4},{6,5},{7,6},{9,8},{10,9},{11,10},{12... | collective-permute-start | bytes 294920 | tf_op jit(solution)/shard_map/ppermute | solution.py:530
  2.9 3.0 %collective-permute-start = (bf16[3,64,256]{2,1,0:T(8,128)(2,1)S(1)}, bf16[3,64,256]{2,1,0:T(8,128)(2,1)S(1)}, u32[]{:S(2)}, u32[]{:S(2)}) collective-permute-start(bf16[3,64,256]{2,1,0:T(8,128)(2,1)S(1)} %get-tuple-element.46), channel_id=1, source_target_pairs={{0,1},{1,2},{2,3},{3,4},{4,5},{5,6},{6,7},{8,9},{9,10},{10,11},{11... | collective-permute-start | bytes 294920 | tf_op jit(solution)/shard_map/ppermute | solution.py:529
  5.9 0.7 copy.15
  6.6 0.7 copy.14
  7.3 0.0 collective-permute-done.1.high_ref
  7.3 0.0 collective-permute-done.low_ref
  7.3 0.0 copy-start
  7.3 1.1 %copy-done = bf16[1,3,512,256]{3,2,1,0:T(8,128)(2,1)S(1)} copy-done((bf16[1,3,512,256]{3,2,1,0:T(8,128)(2,1)S(1)}, bf16[1,3,512,256]{3,2,1,0:T(8,128)(2,1)}, u32[]{:S(2)}) %copy-start) | copy-done | bytes 786456
  8.4 0.0 copy-start.1
  8.4 2.0 %copy-done.1 = bf16[27,256,256]{2,1,0:T(8,128)(2,1)S(1)} copy-done((bf16[27,256,256]{2,1,0:T(8,128)(2,1)S(1)}, bf16[27,256,256]{2,1,0:T(8,128)(2,1)}, u32[]{:S(2)}) %copy-start.1) | copy-done | bytes 3538968
  10.4 1.1 %copy-done.3 = bf16[1,3,512,256]{3,2,1,0:T(8,128)(2,1)S(1)} copy-done((bf16[1,3,512,256]{3,2,1,0:T(8,128)(2,1)S(1)}, bf16[1,3,512,256]{3,2,1,0:T(8,128)(2,1)}, u32[]{:S(2)}) %copy-start.3) | copy-done | bytes 786456
  11.6 0.0 copy-start.4
  11.6 9.5 %input_gradient.1 = (bf16[1920,2304]{1,0:T(8,128)(2,1)}, bf16[1,512,256]{2,1,0:T(8,128)(2,1)S(1)}, bf16[1,512,256]{2,1,0:T(8,128)(2,1)S(1)}, bf16[1,512,256]{2,1,0:T(8,128)(2,1)S(1)}) custom-call(s32[3,27]{1,0:T(4,128)S(1)} %bitcast.12, s32[3,8]{1,0:T(4,128)S(1)} %bitcast.13, bf16[3,512,256]{2,1,0:T(8,128)(2,1)S(1)} %bitcast.11, ...), custom_call_target="tpu_custom_call" | custom-call | flops 5435817984 | bytes 8388608 | tf_op jit(solution)/shard_map/input_gradient/pallas_call | solution.py:192
  21.1 3.5 %collective-permute-start.2 = (bf16[1,512,256]{2,1,0:T(8,128)(2,1)S(1)}, bf16[1,512,256]{2,1,0:T(8,128)(2,1)S(1)}, u32[]{:S(2)}, u32[]{:S(2)}) collective-permute-start(bf16[1,512,256]{2,1,0:T(8,128)(2,1)S(1)} %get-tuple-element.24), channel_id=1, source_target_pairs={{1,0},{2,1},{3,2},{4,3},{5,4},{6,5},{7,6},{0,7},{9,8},{10,9},{11,1... | collective-permute-start | bytes 786440 | tf_op jit(solution)/shard_map/ppermute | solution.py:534
  24.5 0.0 collective-permute-start.3
  24.5 0.0 copy-done.4
  24.5 0.0 copy-start.6
  24.5 3.5 %copy-done.6 = bf16[1920,2304]{1,0:T(8,128)(2,1)S(1)} copy-done((bf16[1920,2304]{1,0:T(8,128)(2,1)S(1)}, bf16[1920,2304]{1,0:T(8,128)(2,1)}, u32[]{:S(2)}) %copy-start.6) | copy-done | bytes 8847384
  28.0 0.0 copy-start.2
  28.0 8.1 %filter_gradient.1 = (bf16[4,1728,128]{2,1,0:T(8,128)(2,1)S(1)}, bf16[4,1728,128]{2,1,0:T(8,128)(2,1)S(1)}) custom-call(bf16[1920,2304]{1,0:T(8,128)(2,1)S(1)} %copy-done.6, bf16[3,512,256]{2,1,0:T(8,128)(2,1)S(1)} %bitcast.16), custom_call_target="tpu_custom_call" | custom-call | flops 5435817984 | bytes 12582912 | tf_op jit(solution)/shard_map/filter_gradient/pallas_call | solution.py:255
  36.1 1.9 %collective-permute-start.4 = (bf16[4,1728,128]{2,1,0:T(8,128)(2,1)S(1)}, bf16[4,1728,128]{2,1,0:T(8,128)(2,1)S(1)}, u32[]{:S(2)}, u32[]{:S(2)}) collective-permute-start(bf16[4,1728,128]{2,1,0:T(8,128)(2,1)S(1)} %get-tuple-element.30), channel_id=1, source_target_pairs={{0,1},{1,0},{2,3},{3,2},{4,5},{5,4},{6,7},{7,6},{8,9},{9,8},{10,11... | collective-permute-start | bytes 5308424 | tf_op jit(solution)/shard_map/ppermute | solution.py:540
  38.1 0.0 collective-permute-done.2.upper_ref
  38.1 0.0 collective-permute-done.3.lower_ref
  38.1 0.0 copy-done.2
  38.1 0.0 copy-done.5
  38.1 3.6 %fine_gradient.1 = (bf16[24,512,128]{2,1,0:T(8,128)(2,1)}, bf16[4,256,128]{2,1,0:T(8,128)(2,1)S(1)}, bf16[4,256,128]{2,1,0:T(8,128)(2,1)S(1)}) custom-call(bf16[1,512,256]{2,1,0:T(8,128)(2,1)S(1)} %collective-permute-done.2.upper_ref, bf16[1,512,256]{2,1,0:T(8,128)(2,1)S(1)} %get-tuple-element.25.stay_ref, ...), custom_call_target="tpu_custom_call" | custom-call | flops 25769803776 | bytes 8388608 | tf_op jit(solution)/shard_map/fine_gradient/pallas_call | solution.py:337
  41.7 0.0 collective-permute-start.5
  41.7 1.5 %collective-permute-done.5.down_got_ref = bf16[4,256,128]{2,1,0:T(8,128)(2,1)S(1)} collective-permute-done((bf16[4,256,128]{2,1,0:T(8,128)(2,1)S(1)}, bf16[4,256,128]{2,1,0:T(8,128)(2,1)S(1)}, u32[]{:S(2)}, u32[]{:S(2)}) %collective-permute-start.5) | collective-permute-done | bytes 262176 | tf_op jit(solution)/shard_map/ppermute | solution.py:541
  43.2 0.0 collective-permute-done.4.conv_got_ref
  43.2 1.5 %pair_sum.1 = (bf16[4,4,336,128]{3,2,1,0:T(8,128)(2,1)}, f32[640,128]{1,0:T(8,128)S(1)}, bf16[640,128]{1,0:T(8,128)(2,1)S(1)}, bf16[640,128]{1,0:T(8,128)(2,1)S(1)}, bf16[640,128]{1,0:T(8,128)(2,1)S(1)}) custom-call(bf16[4,1728,128]{2,1,0:T(8,128)(2,1)S(1)} %get-tuple-element.29.conv_ref, bf16[4,1728,128]{2,1,0:T(8,128)(2,1)S(1)} %collective-permute-done.4.conv_got_ref, ...), custom_call_target="tpu_custom_call" | custom-call | flops 5734400 | bytes 5734400 | tf_op jit(solution)/shard_map/pair_sum/pallas_call | solution.py:397
  44.7 4.5 %all-to-all-start = ((bf16[4,4,336,128]{3,2,1,0:T(8,128)(2,1)}), bf16[4,4,336,128]{3,2,1,0:T(8,128)(2,1)S(1)}, u32[]{:S(2)}, u32[]{:S(2)}) async-start(bf16[4,4,336,128]{3,2,1,0:T(8,128)(2,1)} %get-tuple-element.33), calls=%async_computation | async-start | bytes 2752512 | tf_op jit(solution)/shard_map/all_to_all | solution.py:546
  49.2 1.6 %collective-permute-start.6 = (bf16[640,128]{1,0:T(8,128)(2,1)S(1)}, bf16[640,128]{1,0:T(8,128)(2,1)S(1)}, u32[]{:S(2)}, u32[]{:S(2)}) collective-permute-start(bf16[640,128]{1,0:T(8,128)(2,1)S(1)} %get-tuple-element.35), channel_id=1, source_target_pairs={{0,8},{8,0},{16,24},{24,16},{1,9},{9,1},{17,25},{25,17},{2,10},{10... | collective-permute-start | bytes 491528 | tf_op jit(solution)/shard_map/ppermute | solution.py:46
  50.8 2.6 %collective-permute-start.7 = (bf16[640,128]{1,0:T(8,128)(2,1)S(1)}, bf16[640,128]{1,0:T(8,128)(2,1)S(1)}, u32[]{:S(2)}, u32[]{:S(2)}) collective-permute-start(bf16[640,128]{1,0:T(8,128)(2,1)S(1)} %get-tuple-element.36), channel_id=1, source_target_pairs={{0,16},{8,24},{16,0},{24,8},{1,17},{9,25},{17,1},{25,9},{2,18},{10... | collective-permute-start | bytes 491528 | tf_op jit(solution)/shard_map/ppermute | solution.py:46
  53.3 0.2 collective-permute-start.8
  53.6 4.1 %collective-permute-done.6.refs_1_ = bf16[640,128]{1,0:T(8,128)(2,1)S(1)} collective-permute-done((bf16[640,128]{1,0:T(8,128)(2,1)S(1)}, bf16[640,128]{1,0:T(8,128)(2,1)S(1)}, u32[]{:S(2)}, u32[]{:S(2)}) %collective-permute-start.6) | collective-permute-done | bytes 163872 | tf_op jit(solution)/shard_map/ppermute | solution.py:46
  57.7 8.1 %collective-permute-done.7.refs_2_ = bf16[640,128]{1,0:T(8,128)(2,1)S(1)} collective-permute-done((bf16[640,128]{1,0:T(8,128)(2,1)S(1)}, bf16[640,128]{1,0:T(8,128)(2,1)S(1)}, u32[]{:S(2)}, u32[]{:S(2)}) %collective-permute-start.7) | collective-permute-done | bytes 163872 | tf_op jit(solution)/shard_map/ppermute | solution.py:46
  65.8 0.0 collective-permute-done.8.refs_3_
  65.8 1.6 %all-to-all-done.plane_ref = bf16[4,4,336,128]{3,2,1,0:T(8,128)(2,1)S(1)} async-done(((bf16[4,4,336,128]{3,2,1,0:T(8,128)(2,1)}), bf16[4,4,336,128]{3,2,1,0:T(8,128)(2,1)S(1)}, u32[]{:S(2)}, u32[]{:S(2)}) %all-to-all-start) | async-done | bytes 1376288 | tf_op jit(solution)/shard_map/all_to_all | solution.py:546
  67.4 0.9 middle_sum.1
  68.3 4.9 %all-to-all-start.1 = ((bf16[4,336,128]{2,1,0:T(8,128)(2,1)}), bf16[4,336,128]{2,1,0:T(8,128)(2,1)S(1)}, u32[]{:S(2)}, u32[]{:S(2)}) async-start(bf16[4,336,128]{2,1,0:T(8,128)(2,1)} %get-tuple-element.38), calls=%async_computation.1 | async-start | bytes 688128 | tf_op jit(solution)/shard_map/all_to_all | solution.py:549
  73.2 1.1 %collective-permute-start.9 = (bf16[160,128]{1,0:T(8,128)(2,1)S(1)}, bf16[160,128]{1,0:T(8,128)(2,1)S(1)}, u32[]{:S(2)}, u32[]{:S(2)}) collective-permute-start(bf16[160,128]{1,0:T(8,128)(2,1)S(1)} %get-tuple-element.40), channel_id=1, source_target_pairs={{0,2},{1,3},{2,0},{3,1},{4,6},{5,7},{6,4},{7,5},{8,10},{9,11},{10,... | collective-permute-start | bytes 122888 | tf_op jit(solution)/shard_map/ppermute | solution.py:46
  74.3 0.9 collective-permute-start.10
  75.2 1.5 %collective-permute-start.11 = (bf16[160,128]{1,0:T(8,128)(2,1)S(1)}, bf16[160,128]{1,0:T(8,128)(2,1)S(1)}, u32[]{:S(2)}, u32[]{:S(2)}) collective-permute-start(bf16[160,128]{1,0:T(8,128)(2,1)S(1)} %get-tuple-element.42), channel_id=1, source_target_pairs={{0,6},{1,7},{2,4},{3,5},{4,2},{5,3},{6,0},{7,1},{8,14},{9,15},{10,... | collective-permute-start | bytes 122888 | tf_op jit(solution)/shard_map/ppermute | solution.py:46
  76.7 0.7 collective-permute-done.9.refs_1_
  77.4 0.9 collective-permute-done.10.refs_2_
  78.3 1.7 %collective-permute-done.11.refs_3_ = bf16[160,128]{1,0:T(8,128)(2,1)S(1)} collective-permute-done((bf16[160,128]{1,0:T(8,128)(2,1)S(1)}, bf16[160,128]{1,0:T(8,128)(2,1)S(1)}, u32[]{:S(2)}, u32[]{:S(2)}) %collective-permute-start.11) | collective-permute-done | bytes 40992 | tf_op jit(solution)/shard_map/ppermute | solution.py:46
  80.1 3.5 %all-to-all-done.1.slabs_ref = bf16[4,336,128]{2,1,0:T(8,128)(2,1)S(1)} async-done(((bf16[4,336,128]{2,1,0:T(8,128)(2,1)}), bf16[4,336,128]{2,1,0:T(8,128)(2,1)S(1)}, u32[]{:S(2)}, u32[]{:S(2)}) %all-to-all-start.1) | async-done | bytes 344096 | tf_op jit(solution)/shard_map/all_to_all | solution.py:549
  83.6 0.1 last_sum.1.refs_0_
  83.7 1.5 %collective-permute-start.14 = (bf16[496,128]{1,0:T(8,128)(2,1)S(1)}, bf16[496,128]{1,0:T(8,128)(2,1)S(1)}, u32[]{:S(2)}, u32[]{:S(2)}) collective-permute-start(bf16[496,128]{1,0:T(8,128)(2,1)S(1)} %last_sum.1.refs_0_), channel_id=1, source_target_pairs={{0,6},{1,7},{2,4},{3,5},{4,2},{5,3},{6,0},{7,1},{8,14},{9,15},{10,... | collective-permute-start | bytes 380936 | tf_op jit(solution)/shard_map/ppermute | solution.py:46
  85.2 0.5 collective-permute-start.13
  85.7 1.5 %collective-permute-start.12 = (bf16[496,128]{1,0:T(8,128)(2,1)S(1)}, bf16[496,128]{1,0:T(8,128)(2,1)S(1)}, u32[]{:S(2)}, u32[]{:S(2)}) collective-permute-start(bf16[496,128]{1,0:T(8,128)(2,1)S(1)} %last_sum.1.refs_0_), channel_id=1, source_target_pairs={{0,2},{1,3},{2,0},{3,1},{4,6},{5,7},{6,4},{7,5},{8,10},{9,11},{10,... | collective-permute-start | bytes 380936 | tf_op jit(solution)/shard_map/ppermute | solution.py:46
  87.3 0.0 collective-permute-start.15
  87.3 2.4 %collective-permute-done.14.refs_3_ = bf16[496,128]{1,0:T(8,128)(2,1)S(1)} collective-permute-done((bf16[496,128]{1,0:T(8,128)(2,1)S(1)}, bf16[496,128]{1,0:T(8,128)(2,1)S(1)}, u32[]{:S(2)}, u32[]{:S(2)}) %collective-permute-start.14) | collective-permute-done | bytes 127008 | tf_op jit(solution)/shard_map/ppermute | solution.py:46
  89.7 0.0 collective-permute-start.18
  89.7 1.3 %collective-permute-done.13.refs_2_ = bf16[496,128]{1,0:T(8,128)(2,1)S(1)} collective-permute-done((bf16[496,128]{1,0:T(8,128)(2,1)S(1)}, bf16[496,128]{1,0:T(8,128)(2,1)S(1)}, u32[]{:S(2)}, u32[]{:S(2)}) %collective-permute-start.13) | collective-permute-done | bytes 127008 | tf_op jit(solution)/shard_map/ppermute | solution.py:46
  91.0 0.0 collective-permute-start.17
  91.0 0.0 collective-permute-done.12.refs_1_
  91.0 0.5 collective-permute-start.16
  91.5 0.0 collective-permute-done.15.refs_4_
  91.5 0.0 collective-permute-done.18.refs_7_
  91.5 0.8 collective-permute-done.17.refs_6_
  92.3 0.2 collective-permute-done.16.refs_5_
  92.5 1.5 %gather_up.1 = (f32[1728,256]{1,0:T(8,128)}, f32[256,256]{1,0:T(8,128)}) custom-call(bf16[496,128]{1,0:T(8,128)(2,1)S(1)} %last_sum.1.refs_0_, bf16[496,128]{1,0:T(8,128)(2,1)S(1)} %collective-permute-done.12.refs_1_, bf16[496,128]{1,0:T(8,128)(2,1)S(1)} %collective-permute-done.13.refs_2_, bf16[496,128]{1,0:T(8,128)(2,1)S(1)} %collective-permute-done.14.refs_3_, ...), custom_call_target="tpu_custom_call" | custom-call | flops 3047424 | bytes 3047424 | tf_op jit(solution)/shard_map/gather_up/pallas_call | solution.py:496
  (2 shorter events, 0.0 us)
Async XLA Ops:
  1.6 5.7 %collective-permute-start.1 = (bf16[3,64,256]{2,1,0:T(8,128)(2,1)S(1)}, bf16[3,64,256]{2,1,0:T(8,128)(2,1)S(1)}, u32[]{:S(2)}, u32[]{:S(2)}) collective-permute-start(bf16[3,64,256]{2,1,0:T(8,128)(2,1)S(1)} %get-tuple-element.45), channel_id=1, source_target_pairs={{1,0},{2,1},{3,2},{4,3},{5,4},{6,5},{7,6},{9,8},{10,9},{11,10},{12... | collective-permute-start | bytes 294920 | tf_op jit(solution)/shard_map/ppermute | solution.py:530
  2.9 4.4 %collective-permute-start = (bf16[3,64,256]{2,1,0:T(8,128)(2,1)S(1)}, bf16[3,64,256]{2,1,0:T(8,128)(2,1)S(1)}, u32[]{:S(2)}, u32[]{:S(2)}) collective-permute-start(bf16[3,64,256]{2,1,0:T(8,128)(2,1)S(1)} %get-tuple-element.46), channel_id=1, source_target_pairs={{0,1},{1,2},{2,3},{3,4},{4,5},{5,6},{6,7},{8,9},{9,10},{10,11},{11... | collective-permute-start | bytes 294920 | tf_op jit(solution)/shard_map/ppermute | solution.py:529
  7.3 1.1 %copy-start = (bf16[1,3,512,256]{3,2,1,0:T(8,128)(2,1)S(1)}, bf16[1,3,512,256]{3,2,1,0:T(8,128)(2,1)}, u32[]{:S(2)}) copy-start(bf16[1,3,512,256]{3,2,1,0:T(8,128)(2,1)} %param.7) | copy-start | bytes 2359300
  8.4 2.0 %copy-start.1 = (bf16[27,256,256]{2,1,0:T(8,128)(2,1)S(1)}, bf16[27,256,256]{2,1,0:T(8,128)(2,1)}, u32[]{:S(2)}) copy-start(bf16[27,256,256]{2,1,0:T(8,128)(2,1)} %weight_ref.2) | copy-start | bytes 10616836
  10.4 1.1 %copy-start.3 = (bf16[1,3,512,256]{3,2,1,0:T(8,128)(2,1)S(1)}, bf16[1,3,512,256]{3,2,1,0:T(8,128)(2,1)}, u32[]{:S(2)}) copy-start(bf16[1,3,512,256]{3,2,1,0:T(8,128)(2,1)} %param.8) | copy-start | bytes 2359300
  11.6 12.9 %copy-start.4 = (bf16[1,3,512,256]{3,2,1,0:T(8,128)(2,1)S(1)}, bf16[1,3,512,256]{3,2,1,0:T(8,128)(2,1)}, u32[]{:S(2)}) copy-start(bf16[1,3,512,256]{3,2,1,0:T(8,128)(2,1)} %param.8) | copy-start | bytes 2359300
  21.1 17.0 %collective-permute-start.2 = (bf16[1,512,256]{2,1,0:T(8,128)(2,1)S(1)}, bf16[1,512,256]{2,1,0:T(8,128)(2,1)S(1)}, u32[]{:S(2)}, u32[]{:S(2)}) collective-permute-start(bf16[1,512,256]{2,1,0:T(8,128)(2,1)S(1)} %get-tuple-element.24), channel_id=1, source_target_pairs={{1,0},{2,1},{3,2},{4,3},{5,4},{6,5},{7,6},{0,7},{9,8},{10,9},{11,1... | collective-permute-start | bytes 786440 | tf_op jit(solution)/shard_map/ppermute | solution.py:534
  24.5 13.6 %collective-permute-start.3 = (bf16[1,512,256]{2,1,0:T(8,128)(2,1)S(1)}, bf16[1,512,256]{2,1,0:T(8,128)(2,1)S(1)}, u32[]{:S(2)}, u32[]{:S(2)}) collective-permute-start(bf16[1,512,256]{2,1,0:T(8,128)(2,1)S(1)} %get-tuple-element.26), channel_id=1, source_target_pairs={{0,1},{1,2},{2,3},{3,4},{4,5},{5,6},{6,7},{7,0},{8,9},{9,10},{10,1... | collective-permute-start | bytes 786440 | tf_op jit(solution)/shard_map/ppermute | solution.py:535
  24.5 3.5 %copy-start.6 = (bf16[1920,2304]{1,0:T(8,128)(2,1)S(1)}, bf16[1920,2304]{1,0:T(8,128)(2,1)}, u32[]{:S(2)}) copy-start(bf16[1920,2304]{1,0:T(8,128)(2,1)} %get-tuple-element.28.win_ref) | copy-start | bytes 26542084
  28.0 10.1 %copy-start.2 = (bf16[1,24,512,128]{3,2,1,0:T(8,128)(2,1)S(1)}, bf16[1,24,512,128]{3,2,1,0:T(8,128)(2,1)}, u32[]{:S(2)}) copy-start(bf16[1,24,512,128]{3,2,1,0:T(8,128)(2,1)} %param.11) | copy-start | bytes 9437188
  28.0 10.1 %copy-start.5 = (bf16[8,128,256]{2,1,0:T(8,128)(2,1)S(1)}, bf16[8,128,256]{2,1,0:T(8,128)(2,1)}, u32[]{:S(2)}) copy-start(bf16[8,128,256]{2,1,0:T(8,128)(2,1)} %weight_ref.3) | copy-start | bytes 1572868
  36.1 7.1 %collective-permute-start.4 = (bf16[4,1728,128]{2,1,0:T(8,128)(2,1)S(1)}, bf16[4,1728,128]{2,1,0:T(8,128)(2,1)S(1)}, u32[]{:S(2)}, u32[]{:S(2)}) collective-permute-start(bf16[4,1728,128]{2,1,0:T(8,128)(2,1)S(1)} %get-tuple-element.30), channel_id=1, source_target_pairs={{0,1},{1,0},{2,3},{3,2},{4,5},{5,4},{6,7},{7,6},{8,9},{9,8},{10,11... | collective-permute-start | bytes 5308424 | tf_op jit(solution)/shard_map/ppermute | solution.py:540
  41.7 1.5 %collective-permute-start.5 = (bf16[4,256,128]{2,1,0:T(8,128)(2,1)S(1)}, bf16[4,256,128]{2,1,0:T(8,128)(2,1)S(1)}, u32[]{:S(2)}, u32[]{:S(2)}) collective-permute-start(bf16[4,256,128]{2,1,0:T(8,128)(2,1)S(1)} %get-tuple-element.32), channel_id=1, source_target_pairs={{0,1},{1,0},{2,3},{3,2},{4,5},{5,4},{6,7},{7,6},{8,9},{9,8},{10,11... | collective-permute-start | bytes 786440 | tf_op jit(solution)/shard_map/ppermute | solution.py:541
  44.7 22.8 %all-to-all-start = ((bf16[4,4,336,128]{3,2,1,0:T(8,128)(2,1)}), bf16[4,4,336,128]{3,2,1,0:T(8,128)(2,1)S(1)}, u32[]{:S(2)}, u32[]{:S(2)}) async-start(bf16[4,4,336,128]{3,2,1,0:T(8,128)(2,1)} %get-tuple-element.33), calls=%async_computation | async-start | bytes 2752512 | tf_op jit(solution)/shard_map/all_to_all | solution.py:546
  49.2 8.5 %collective-permute-start.6 = (bf16[640,128]{1,0:T(8,128)(2,1)S(1)}, bf16[640,128]{1,0:T(8,128)(2,1)S(1)}, u32[]{:S(2)}, u32[]{:S(2)}) collective-permute-start(bf16[640,128]{1,0:T(8,128)(2,1)S(1)} %get-tuple-element.35), channel_id=1, source_target_pairs={{0,8},{8,0},{16,24},{24,16},{1,9},{9,1},{17,25},{25,17},{2,10},{10... | collective-permute-start | bytes 491528 | tf_op jit(solution)/shard_map/ppermute | solution.py:46
  50.8 15.0 %collective-permute-start.7 = (bf16[640,128]{1,0:T(8,128)(2,1)S(1)}, bf16[640,128]{1,0:T(8,128)(2,1)S(1)}, u32[]{:S(2)}, u32[]{:S(2)}) collective-permute-start(bf16[640,128]{1,0:T(8,128)(2,1)S(1)} %get-tuple-element.36), channel_id=1, source_target_pairs={{0,16},{8,24},{16,0},{24,8},{1,17},{9,25},{17,1},{25,9},{2,18},{10... | collective-permute-start | bytes 491528 | tf_op jit(solution)/shard_map/ppermute | solution.py:46
  53.3 12.5 %collective-permute-start.8 = (bf16[640,128]{1,0:T(8,128)(2,1)S(1)}, bf16[640,128]{1,0:T(8,128)(2,1)S(1)}, u32[]{:S(2)}, u32[]{:S(2)}) collective-permute-start(bf16[640,128]{1,0:T(8,128)(2,1)S(1)} %get-tuple-element.37), channel_id=1, source_target_pairs={{0,24},{8,16},{16,8},{24,0},{1,25},{9,17},{17,9},{25,1},{2,26},{10... | collective-permute-start | bytes 491528 | tf_op jit(solution)/shard_map/ppermute | solution.py:46
  68.3 15.3 %all-to-all-start.1 = ((bf16[4,336,128]{2,1,0:T(8,128)(2,1)}), bf16[4,336,128]{2,1,0:T(8,128)(2,1)S(1)}, u32[]{:S(2)}, u32[]{:S(2)}) async-start(bf16[4,336,128]{2,1,0:T(8,128)(2,1)} %get-tuple-element.38), calls=%async_computation.1 | async-start | bytes 688128 | tf_op jit(solution)/shard_map/all_to_all | solution.py:549
  73.2 4.2 %collective-permute-start.9 = (bf16[160,128]{1,0:T(8,128)(2,1)S(1)}, bf16[160,128]{1,0:T(8,128)(2,1)S(1)}, u32[]{:S(2)}, u32[]{:S(2)}) collective-permute-start(bf16[160,128]{1,0:T(8,128)(2,1)S(1)} %get-tuple-element.40), channel_id=1, source_target_pairs={{0,2},{1,3},{2,0},{3,1},{4,6},{5,7},{6,4},{7,5},{8,10},{9,11},{10,... | collective-permute-start | bytes 122888 | tf_op jit(solution)/shard_map/ppermute | solution.py:46
  74.3 4.0 %collective-permute-start.10 = (bf16[160,128]{1,0:T(8,128)(2,1)S(1)}, bf16[160,128]{1,0:T(8,128)(2,1)S(1)}, u32[]{:S(2)}, u32[]{:S(2)}) collective-permute-start(bf16[160,128]{1,0:T(8,128)(2,1)S(1)} %get-tuple-element.41), channel_id=1, source_target_pairs={{0,4},{1,5},{2,6},{3,7},{4,0},{5,1},{6,2},{7,3},{8,12},{9,13},{10,... | collective-permute-start | bytes 122888 | tf_op jit(solution)/shard_map/ppermute | solution.py:46
  75.2 4.9 %collective-permute-start.11 = (bf16[160,128]{1,0:T(8,128)(2,1)S(1)}, bf16[160,128]{1,0:T(8,128)(2,1)S(1)}, u32[]{:S(2)}, u32[]{:S(2)}) collective-permute-start(bf16[160,128]{1,0:T(8,128)(2,1)S(1)} %get-tuple-element.42), channel_id=1, source_target_pairs={{0,6},{1,7},{2,4},{3,5},{4,2},{5,3},{6,0},{7,1},{8,14},{9,15},{10,... | collective-permute-start | bytes 122888 | tf_op jit(solution)/shard_map/ppermute | solution.py:46
  83.7 6.0 %collective-permute-start.14 = (bf16[496,128]{1,0:T(8,128)(2,1)S(1)}, bf16[496,128]{1,0:T(8,128)(2,1)S(1)}, u32[]{:S(2)}, u32[]{:S(2)}) collective-permute-start(bf16[496,128]{1,0:T(8,128)(2,1)S(1)} %last_sum.1.refs_0_), channel_id=1, source_target_pairs={{0,6},{1,7},{2,4},{3,5},{4,2},{5,3},{6,0},{7,1},{8,14},{9,15},{10,... | collective-permute-start | bytes 380936 | tf_op jit(solution)/shard_map/ppermute | solution.py:46
  85.2 5.7 %collective-permute-start.13 = (bf16[496,128]{1,0:T(8,128)(2,1)S(1)}, bf16[496,128]{1,0:T(8,128)(2,1)S(1)}, u32[]{:S(2)}, u32[]{:S(2)}) collective-permute-start(bf16[496,128]{1,0:T(8,128)(2,1)S(1)} %last_sum.1.refs_0_), channel_id=1, source_target_pairs={{0,4},{1,5},{2,6},{3,7},{4,0},{5,1},{6,2},{7,3},{8,12},{9,13},{10,... | collective-permute-start | bytes 380936 | tf_op jit(solution)/shard_map/ppermute | solution.py:46
  85.7 5.2 %collective-permute-start.12 = (bf16[496,128]{1,0:T(8,128)(2,1)S(1)}, bf16[496,128]{1,0:T(8,128)(2,1)S(1)}, u32[]{:S(2)}, u32[]{:S(2)}) collective-permute-start(bf16[496,128]{1,0:T(8,128)(2,1)S(1)} %last_sum.1.refs_0_), channel_id=1, source_target_pairs={{0,2},{1,3},{2,0},{3,1},{4,6},{5,7},{6,4},{7,5},{8,10},{9,11},{10,... | collective-permute-start | bytes 380936 | tf_op jit(solution)/shard_map/ppermute | solution.py:46
  87.3 4.2 %collective-permute-start.15 = (bf16[496,128]{1,0:T(8,128)(2,1)S(1)}, bf16[496,128]{1,0:T(8,128)(2,1)S(1)}, u32[]{:S(2)}, u32[]{:S(2)}) collective-permute-start(bf16[496,128]{1,0:T(8,128)(2,1)S(1)} %last_sum.1.refs_0_), channel_id=1, source_target_pairs={{0,1},{1,0},{2,3},{3,2},{4,5},{5,4},{6,7},{7,6},{8,9},{9,8},{10,11... | collective-permute-start | bytes 380936 | tf_op jit(solution)/shard_map/ppermute | solution.py:552
  89.7 1.8 %collective-permute-start.18 = (bf16[496,128]{1,0:T(8,128)(2,1)S(1)}, bf16[496,128]{1,0:T(8,128)(2,1)S(1)}, u32[]{:S(2)}, u32[]{:S(2)}) collective-permute-start(bf16[496,128]{1,0:T(8,128)(2,1)S(1)} %collective-permute-done.14.refs_3_), channel_id=1, source_target_pairs={{0,1},{1,0},{2,3},{3,2},{4,5},{5,4},{6,7},{7,6},{8,9},{9,8},{10,11... | collective-permute-start | bytes 380936 | tf_op jit(solution)/shard_map/ppermute | solution.py:552
  91.0 1.3 %collective-permute-start.17 = (bf16[496,128]{1,0:T(8,128)(2,1)S(1)}, bf16[496,128]{1,0:T(8,128)(2,1)S(1)}, u32[]{:S(2)}, u32[]{:S(2)}) collective-permute-start(bf16[496,128]{1,0:T(8,128)(2,1)S(1)} %collective-permute-done.13.refs_2_), channel_id=1, source_target_pairs={{0,1},{1,0},{2,3},{3,2},{4,5},{5,4},{6,7},{7,6},{8,9},{9,8},{10,11... | collective-permute-start | bytes 380936 | tf_op jit(solution)/shard_map/ppermute | solution.py:552
  91.0 1.5 %collective-permute-start.16 = (bf16[496,128]{1,0:T(8,128)(2,1)S(1)}, bf16[496,128]{1,0:T(8,128)(2,1)S(1)}, u32[]{:S(2)}, u32[]{:S(2)}) collective-permute-start(bf16[496,128]{1,0:T(8,128)(2,1)S(1)} %collective-permute-done.12.refs_1_), channel_id=1, source_target_pairs={{0,1},{1,0},{2,3},{3,2},{4,5},{5,4},{6,7},{7,6},{8,9},{9,8},{10,11... | collective-permute-start | bytes 380936 | tf_op jit(solution)/shard_map/ppermute | solution.py:552
where the time goes:
time: 94.5 us; the launch traced here: 94 us
  starting transfers between devices  31.1 us (33%)
  waiting for transfers between devices  27 us (29%)
  Pallas kernels  25.1 us (27%)
  local copies, waits for them, and re-layouts  10.1 us (11%)
    ppermute x9, waiting for transfers between devices, exchange(): return lax.ppermute(value, axis, pairs)  19.3 us
    ppermute x9, starting transfers between devices, exchange(): return lax.ppermute(value, axis, pairs)  11.4 us
    pallas_call x1, Pallas kernels, input_gradient(): pl.pallas_call(input_kernel, out_shape=(windows, out, out, out), in_specs...  9.47 us
    unnamed x16, local copies, waits for them, and re-layouts  9.15 us
    pallas_call x1, Pallas kernels, filter_gradient(): pl.pallas_call(functools.partial(filter_kernel, shard_rows), grid=(9,), o...  8.1 us
    all_to_all x1, starting transfers between devices, body(): to_slabs = lax.all_to_all(to_slabs, 'dp', 0, 0)  4.87 us
    all_to_all x1, starting transfers between devices, body(): planes = lax.all_to_all(planes, 'dom', 0, 0, axis_index_groups=same_core)  4.53 us
    pallas_call x1, Pallas kernels, fine_gradient(): pl.pallas_call(functools.partial(fine_kernel, groups), grid=(3 * groups,)...  3.56 us
  transfers between devices with their start and end apart: 21, of which 12 were waited for; matrix products, arithmetic and copies ran while one was open for 1% of the time, Pallas kernels for 12%

commit v1 on v0

v1 whole, which is shorter than its diff:
```python
import functools
import math

import jax
import jax.numpy as jnp
from jax import lax
from jax.experimental import pallas as pl
from jax.experimental.pallas import tpu as pltpu
from jax.sharding import PartitionSpec as P

BE = 8
PLANE = BE * BE
HALF = BE // 2
F32 = jnp.float32
BF16 = jnp.bfloat16
MIB = 1 << 20

VMEM = pl.BlockSpec(memory_space=pltpu.VMEM)
SMEM = pl.BlockSpec(memory_space=pltpu.SMEM)
ANY = pl.BlockSpec(memory_space=pl.ANY)
HBM = pl.BlockSpec(memory_space=pltpu.HBM)


def params(mib):
    return pltpu.CompilerParams(vmem_limit_bytes=mib * MIB)


def relative(index, step, count):
    if count & (count - 1) == 0:
        return index ^ step
    return lax.rem(index + step, count)


def source_of(index, step, count):
    if count & (count - 1) == 0:
        return index ^ step
    return (index - step) % count if isinstance(index, int) else lax.rem(index + count - step, count)


def exchange(value, axis, step, stride):
    count = lax.axis_size(axis) // stride
    pairs = []
    for index in range(lax.axis_size(axis)):
        high, low = divmod(index, stride)
        other = high ^ step if count & (count - 1) == 0 else (high + step) % count
        pairs.append((index, other * stride + low))
    return lax.ppermute(value, axis, pairs)


def fetch(ref, slot, start, rows):
    value = ref[jnp.maximum(slot, 0), pl.ds(start, rows), :].astype(F32)
    return jnp.where(slot >= 0, value, 0.0)


def spread(table_ref, ref, start, step_x, slot, row, win_ref):
    channels = ref.shape[-1]

    def link(step_y, step_z):
        return table_ref[27 * slot + 9 * (step_x + 1) + 3 * (step_y + 1) + step_z + 1]

    columns = {}
    for step_z in (-1, 0, 1):
        below = fetch(ref, link(-1, step_z), start + PLANE - 16, 16).reshape(2, BE, channels)[1:]
        middle = fetch(ref, link(0, step_z), start, PLANE).reshape(BE, BE, channels)
        above = fetch(ref, link(1, step_z), start, 16).reshape(2, BE, channels)[:1]
        columns[step_z] = jnp.concatenate([below, middle, above], axis=0)
    place_z = lax.broadcasted_iota(jnp.int32, columns[0].shape, 1)
    shifted = {
        0: columns[0],
        -1: jnp.where(
            place_z == 0, pltpu.roll(columns[-1], 1, axis=1), pltpu.roll(columns[0], 1, axis=1)
        ),
        1: jnp.where(
            place_z == BE - 1,
            pltpu.roll(columns[1], BE - 1, axis=1),
            pltpu.roll(columns[0], BE - 1, axis=1),
        ),
    }
    for tap_y in (-1, 0, 1):
        for tap_z in (-1, 0, 1):
            tap = 3 * (tap_y + 1) + tap_z + 1
            value = shifted[-tap_z][1 - tap_y : 1 - tap_y + BE].reshape(PLANE, channels)
            win_ref[pl.ds(row, PLANE), tap * channels : (tap + 1) * channels] = value.astype(BF16)


def build_windows(table_ref, own_ref, low_ref, high_ref, win_ref):
    slots = own_ref.shape[0]

    def edge(slot, carry):
        spread(table_ref, low_ref, 0, -1, slot, pl.multiple_of(slot * PLANE, PLANE), win_ref)
        row = ((BE + 1) * slots + slot) * PLANE
        spread(table_ref, high_ref, 0, 1, slot, pl.multiple_of(row, PLANE), win_ref)
        return carry

    def inner(step, carry):
        x = step // slots
        slot = step - x * slots
        row = (x + 1) * slots * PLANE + slot * PLANE
        start = pl.multiple_of(x * PLANE, PLANE)
        spread(table_ref, own_ref, start, 0, slot, pl.multiple_of(row, PLANE), win_ref)
        return carry

    lax.fori_loop(0, slots, edge, 0)
    lax.fori_loop(0, BE * slots, inner, 0)


def started(source, target, sem):
    copy = pltpu.make_async_copy(source, target, sem)
    copy.start()
    return copy


def input_kernel(
    places, table_ref, own_hbm, low_ref, high_ref, pre_hbm, weight_ref,
    to_lower_ref, stay_ref, to_upper_ref,
    own_ref, pre_ref, win_ref, taps_ref, acc_ref, octants_ref,
    in_sems, tap_sems, out_sems,
):
    slots, voxels, channels = own_ref.shape
    groups = places // 8
    own_copy = started(own_hbm.at[0], own_ref, in_sems.at[1])
    copies = []
    for tap in range(27):
        index_x, rest = divmod(tap, 9)
        lanes = slice(rest * channels, (rest + 1) * channels)
        copies.append(
            started(weight_ref.at[tap], taps_ref.at[index_x, :, lanes], tap_sems.at[tap])
        )
    pre_copy = started(pre_hbm.at[0], pre_ref, in_sems.at[2])
    own_copy.wait()
    build_windows(table_ref, own_ref, low_ref, high_ref, win_ref)
    for copy in copies:
        copy.wait()
    slab = slots * PLANE
    rows = BE * slab
    half = rows // 2

    def multiply(part, carry):
        start = part * half
        total = None
        for index_x in range(3):
            offset = pl.multiple_of(start + (2 - index_x) * slab, PLANE)
            term = lax.dot_general(
                win_ref[pl.ds(offset, half), :],
                taps_ref[index_x],
                (((1,), (1,)), ((), ())),
                preferred_element_type=F32,
            )
            total = term if total is None else total + term
        acc_ref[pl.ds(pl.multiple_of(start, PLANE), half), :] = total
        return carry

    lax.fori_loop(0, 2, multiply, 0)
    pre_copy.wait()
    octants_ref[...] = jnp.zeros_like(octants_ref)
    place_z = lax.broadcasted_iota(jnp.int32, (BE // 2, BE, channels), 1)
    for slot in range(slots):
        group = jnp.int32(3 * groups)
        for row in range(3):
            for part in range(groups):
                entry = table_ref[27 * slots + row * places + 8 * part]
                group = jnp.where(entry == 8 * slot, row * groups + part, group)

        def finish(x, carry):
            value = acc_ref[pl.ds(pl.multiple_of(x * slab + slot * PLANE, PLANE), PLANE), :]
            pre = pre_ref[slot, pl.ds(pl.multiple_of(x * PLANE, PLANE), PLANE), :].astype(F32)
            value = jnp.where(pre > 0, value, 0.0).reshape(BE // 2, 2, BE, channels)
            even, odd = value[:, 0], value[:, 1]
            near = jnp.where(place_z < HALF, even, pltpu.roll(odd, HALF, axis=1))
            far = jnp.where(place_z < HALF, pltpu.roll(even, HALF, axis=1), odd)
            side = x // HALF
            row = (x - side * HALF) * 16
            for side_y in range(2):
                for side_z, piece in enumerate((near, far)):
                    block = piece[2 * side_y : 2 * side_y + 2].reshape(16, channels).astype(BF16)
                    start = (4 * side + 2 * side_y + side_z) * PLANE + row
                    octants_ref[group, pl.ds(pl.multiple_of(start, 16), 16), :] = block
            return carry

        lax.fori_loop(0, BE, finish, 0)
    outs = []
    for row, ref in enumerate((to_lower_ref, stay_ref, to_upper_ref)):
        copy = pltpu.make_async_copy(
            octants_ref.at[pl.ds(row * groups, groups)], ref, out_sems.at[row]
        )
        copy.start()
        outs.append(copy)
    for copy in outs:
        copy.wait()


def input_gradient(table, places, own, low, high, pre, weight):
    _, slots, voxels, channels = own.shape
    groups = places // 8
    rows = slots * voxels
    out = jax.ShapeDtypeStruct((groups, voxels, channels), BF16)
    return pl.pallas_call(
        functools.partial(input_kernel, places),
        out_shape=(out, out, out),
        in_specs=[SMEM, HBM, VMEM, VMEM, HBM, HBM],
        out_specs=(ANY, ANY, ANY),
        scratch_shapes=[
            pltpu.VMEM(own.shape[1:], BF16),
            pltpu.VMEM(pre.shape[1:], BF16),
            pltpu.VMEM((slots * PLANE * (BE + 2), 9 * channels), BF16),
            pltpu.VMEM((3, channels, 9 * channels), BF16),
            pltpu.VMEM((rows, channels), F32),
            pltpu.VMEM((3 * groups + 1, voxels, channels), BF16),
            pltpu.SemaphoreType.DMA((3,)),
            pltpu.SemaphoreType.DMA((27,)),
            pltpu.SemaphoreType.DMA((3,)),
        ],
        compiler_params=params(62),
        cost_estimate=pl.CostEstimate(
            flops=2 * rows * 27 * channels * channels, bytes_accessed=8 * MIB, transcendentals=0
        ),
        name="input_gradient",
    )(table, own, low, high, pre, weight)


def filter_kernel(
    shard_rows, table_ref, own_hbm, low_ref, high_ref, pre_hbm,
    keep_ref, send_ref, own_ref, pre_ref, win_ref, act_ref, in_sems,
):
    slots, voxels, channels = own_ref.shape
    slab = slots * PLANE
    rows = BE * slab
    lanes = channels // 2
    pre_copy = started(pre_hbm.at[0], pre_ref, in_sems.at[2])
    own_copy = started(own_hbm.at[0], own_ref, in_sems.at[1])
    pre_copy.wait()
    for pair in range(BE // 2):
        parts = []
        for x in (2 * pair, 2 * pair + 1):
            for slot in range(slots):
                parts.append(pre_ref[slot, x * PLANE : (x + 1) * PLANE, :])
        block = jnp.maximum(jnp.concatenate(parts, axis=0).astype(F32), 0.0)
        act_ref[:, pair * 2 * slab : (pair + 1) * 2 * slab] = block.T.astype(BF16)
    own_copy.wait()
    build_windows(table_ref, own_ref, low_ref, high_ref, win_ref)
    first = lax.rem(lax.axis_index("dom"), 2) == 0
    unit = math.gcd(channels, shard_rows)

    def step(index_x, carry):
        offset = pl.multiple_of((2 - index_x) * slab, PLANE)
        for rest in range(9):
            total = jnp.dot(
                act_ref[...],
                win_ref[pl.ds(offset, rows), rest * channels : (rest + 1) * channels],
                preferred_element_type=F32,
            )
            left, right = total[:, :lanes], total[:, lanes:]
            keep = jnp.where(first, left, right).astype(BF16)
            send = jnp.where(first, right, left).astype(BF16)
            for part in range(channels // unit):
                row = (index_x * 9 + rest) * channels + part * unit
                shard = row // shard_rows
                start = pl.multiple_of(row - shard * shard_rows, unit)
                span = slice(part * unit, (part + 1) * unit)
                keep_ref[shard, pl.ds(start, unit), :] = keep[span]
                send_ref[shard, pl.ds(start, unit), :] = send[span]
        return carry

    lax.fori_loop(0, 3, step, 0)


def filter_gradient(shards, table, own, low, high, pre):
    _, slots, voxels, channels = own.shape
    shard_rows = 27 * channels // shards
    rows = slots * voxels
    out = jax.ShapeDtypeStruct((shards, shard_rows, channels // 2), BF16)
    return pl.pallas_call(
        functools.partial(filter_kernel, shard_rows),
        out_shape=(out, out),
        in_specs=[SMEM, HBM, VMEM, VMEM, HBM],
        out_specs=(VMEM, VMEM),
        scratch_shapes=[
            pltpu.VMEM(own.shape[1:], BF16),
            pltpu.VMEM(pre.shape[1:], BF16),
            pltpu.VMEM((slots * PLANE * (BE + 2), 9 * channels), BF16),
            pltpu.VMEM((channels, rows), BF16),
            pltpu.SemaphoreType.DMA((3,)),
        ],
        compiler_params=params(62),
        cost_estimate=pl.CostEstimate(
            flops=2 * rows * 27 * channels * channels, bytes_accessed=8 * MIB, transcendentals=0
        ),
        name="filter_gradient",
    )(table, own, low, high, pre)


def fine_kernel(
    groups, upper_ref, stay_ref, lower_ref, weight_ref, act_ref,
    grad_ref, keep_ref, send_ref, acc_ref,
):
    step = pl.program_id(0)
    fine, voxels, fine_channels = act_ref.shape
    channels = upper_ref.shape[-1]
    taps = weight_ref.shape[0]
    cells = voxels // taps

    @pl.when(step == 0)
    def _():
        acc_ref[...] = jnp.zeros_like(acc_ref)

    def work(ref):
        octants = ref[0]
        product = lax.dot_general(
            octants,
            weight_ref[...].reshape(taps * fine_channels, channels),
            (((1,), (1,)), ((), ())),
            preferred_element_type=F32,
        ).astype(BF16)
        wide = []
        for place in range(fine):
            for tap in range(taps):
                grad_ref[place, tap * cells : (tap + 1) * cells, :] = product[
                    place * cells : (place + 1) * cells,
                    tap * fine_channels : (tap + 1) * fine_channels,
                ]
            wide.append(
                jnp.concatenate(
                    [act_ref[place, tap * cells : (tap + 1) * cells, :] for tap in range(taps)],
                    axis=1,
                )
            )
        acc_ref[...] += jnp.dot(
            octants.T, jnp.concatenate(wide, axis=0), preferred_element_type=F32
        )

    for row, ref in enumerate((upper_ref, stay_ref, lower_ref)):
        pl.when(step // groups == row)(functools.partial(work, ref))

    @pl.when(step == pl.num_programs(0) - 1)
    def _():
        total = acc_ref[...].T
        first = lax.rem(lax.axis_index("dom"), 2) == 0
        lanes = channels // 2
        shards = keep_ref.shape[0]
        rows = total.shape[0] // shards
        left = total[:, :lanes].reshape(shards, rows, lanes)
        right = total[:, lanes:].reshape(shards, rows, lanes)
        keep_ref[:, :rows, :] = jnp.where(first, left, right).astype(BF16)
        send_ref[:, :rows, :] = jnp.where(first, right, left).astype(BF16)


def fine_gradient(shards, count, from_upper, stay, from_lower, weight, fine_act):
    fine, voxels, fine_channels = fine_act.shape
    groups, _, channels = stay.shape
    taps = weight.shape[0]
    whole = pl.BlockSpec((1, voxels, channels), lambda i: (i % groups, 0, 0))
    rows = count * piece_rows(taps * fine_channels // shards, count)
    down = jax.ShapeDtypeStruct((shards, rows, channels // 2), BF16)
    same = pl.BlockSpec(down.shape, lambda i: (0, 0, 0))
    block = pl.BlockSpec((8, voxels, fine_channels), lambda i: (i, 0, 0))
    return pl.pallas_call(
        functools.partial(fine_kernel, groups),
        grid=(3 * groups,),
        out_shape=(jax.ShapeDtypeStruct(fine_act.shape, BF16), down, down),
        in_specs=[
            whole, whole, whole,
            pl.BlockSpec(weight.shape, lambda i: (0, 0, 0)),
            block,
        ],
        out_specs=(block, same, same),
        scratch_shapes=[pltpu.VMEM((channels, taps * fine_channels), F32)],
        compiler_params=params(61),
        cost_estimate=pl.CostEstimate(
            flops=64 * fine * voxels * fine_channels * channels, bytes_accessed=8 * MIB,
            transcendentals=0,
        ),
        name="fine_gradient",
    )(from_upper, stay, from_lower, weight, fine_act)


def piece_rows(rows, count):
    return -(-rows // (16 * count)) * 16


def tree(values):
    while len(values) > 1:
        values = [
            values[i] + values[i + 1] if i + 1 < len(values) else values[i]
            for i in range(0, len(values), 2)
        ]
    return values[0]


def cost(*arrays):
    moved = sum(math.prod(x.shape) * jnp.dtype(x.dtype).itemsize for x in arrays)
    return pl.CostEstimate(flops=moved, bytes_accessed=moved, transcendentals=0)


def shapes_of(count, shape):
    return [jax.ShapeDtypeStruct(shape, F32 if step == 0 else BF16) for step in range(count)]


def pair_kernel(count, conv_ref, conv_got_ref, down_ref, down_got_ref, *outs):
    planes, slabs = outs[:count], outs[count:]
    shards, rows, _ = conv_ref.shape
    down_piece = down_ref.shape[1] // count
    piece = planes[0].shape[1] - down_piece
    cut = count * piece
    for step, ref in enumerate(slabs):
        shard = relative(lax.axis_index("dp"), step, shards)
        total = conv_ref[shard, cut:, :].astype(F32) + conv_got_ref[shard, cut:, :].astype(F32)
        ref[...] = total.astype(ref.dtype)
    high = lax.axis_index("dom") // 2
    for step, ref in enumerate(planes):
        place = relative(high, step, count)
        for keep_ref, got_ref, size, start in (
            (conv_ref, conv_got_ref, piece, 0),
            (down_ref, down_got_ref, down_piece, piece),
        ):
            span = pl.ds(pl.multiple_of(place * size, 16), size)
            total = keep_ref[:, span, :].astype(F32) + got_ref[:, span, :].astype(F32)
            ref[:, start : start + size, :] = total.astype(ref.dtype)


def pair_sum(count, conv, conv_got, down, down_got):
    shards, rows, lanes = conv.shape
    down_piece = down.shape[1] // count
    unit = 16 * count
    piece = 16 * round((2 * (rows + down.shape[1]) / 3 - down.shape[1]) / unit)
    outs = shapes_of(count, (shards, piece + down_piece, lanes))
    outs += shapes_of(shards, (rows - count * piece, lanes))
    outs = pl.pallas_call(
        functools.partial(pair_kernel, count),
        out_shape=outs,
        in_specs=[VMEM] * 4,
        out_specs=[VMEM] * len(outs),
        compiler_params=params(32),
        cost_estimate=cost(conv, conv_got, *outs),
        name="pair_sum",
    )(conv, conv_got, down, down_got)
    return outs[:count], outs[count:], (piece, down_piece)


def middle_kernel(count, shards, *refs):
    planes, slabs = refs[:count], refs[count : count + shards]
    to_slabs, mine_ref = refs[count + shards : -1], refs[-1]
    mine_ref[...] = tree([part[...].astype(F32) for part in slabs]).astype(BF16)
    for step, ref in enumerate(to_slabs):
        shard = relative(lax.axis_index("dp"), step, shards)
        ref[...] = tree([part[shard].astype(F32) for part in planes]).astype(ref.dtype)


def middle_sum(planes, slabs):
    count, shards = len(planes), len(slabs)
    _, piece, lanes = planes[0].shape
    outs = shapes_of(shards, (piece, lanes)) + [jax.ShapeDtypeStruct(slabs[0].shape, BF16)]
    parts = [*planes, *slabs]
    outs = pl.pallas_call(
        functools.partial(middle_kernel, count, shards),
        out_shape=outs,
        in_specs=[VMEM] * len(parts),
        out_specs=[VMEM] * len(outs),
        compiler_params=params(32),
        cost_estimate=cost(*parts, *outs),
        name="middle_sum",
    )(*parts)
    return outs[:shards], outs[shards]


def last_kernel(factor, shards, *refs):
    planes_ref, slabs_ref = refs[-2:]
    total = tree([part[...].astype(F32) for part in refs[:shards]])
    planes_ref[...] = (total * factor).astype(BF16)
    total = tree([part[...].astype(F32) for part in refs[shards:-2]])
    slabs_ref[...] = (total * factor).astype(BF16)


def last_sum(factor, slabs, planes):
    parts = [*slabs, *planes]
    return pl.pallas_call(
        functools.partial(last_kernel, factor, len(slabs)),
        out_shape=[
            jax.ShapeDtypeStruct(slabs[0].shape, BF16), jax.ShapeDtypeStruct(planes[0].shape, BF16)
        ],
        in_specs=[VMEM] * len(parts),
        out_specs=[VMEM] * 2,
        compiler_params=params(32),
        cost_estimate=cost(*parts),
        name="last_sum",
    )(*parts)


def gather_kernel(count, piece, down_piece, *refs):
    near, far = refs[:count], refs[count : 2 * count]
    rest_ref, rest_far_ref, conv_ref, down_ref, conv_whole, down_whole = refs[2 * count :]
    lanes = rest_ref.shape[1]
    cut = count * piece
    high = lax.axis_index("dom") // 2
    low = lax.rem(lax.axis_index("dom"), 2)
    for side, group, rest in ((low, near, rest_ref), (1 - low, far, rest_far_ref)):
        lane = pl.ds(pl.multiple_of(side * lanes, lanes), lanes)
        for step, ref in enumerate(group):
            place = source_of(high, step, count)
            row = pl.multiple_of(place * piece, 16)
            conv_whole[pl.ds(row, piece), lane] = ref[:piece, :].astype(F32)
            row = pl.multiple_of(place * down_piece, 16)
            down_whole[pl.ds(row, down_piece), lane] = ref[piece:, :].astype(F32)
        conv_whole[cut:, lane] = rest[...].astype(F32)
    conv_ref[...] = conv_whole[...]
    down_ref[...] = down_whole[: down_ref.shape[0]]


def gather_up(conv_rows, down_rows, pieces, near, far, rest, rest_far):
    count = len(near)
    lanes = rest.shape[1]
    outs = [jax.ShapeDtypeStruct((rows, 2 * lanes), F32) for rows in (conv_rows, down_rows)]
    return pl.pallas_call(
        functools.partial(gather_kernel, count, *pieces),
        out_shape=outs,
        in_specs=[VMEM] * (2 * count + 2),
        out_specs=[VMEM] * 2,
        scratch_shapes=[
            pltpu.VMEM((conv_rows, 2 * lanes), F32),
            pltpu.VMEM((count * pieces[1], 2 * lanes), F32),
        ],
        compiler_params=params(32),
        cost_estimate=cost(*near, *far, *outs),
        name="gather_up",
    )(*near, *far, rest, rest_far)


def body(grad_out, pre_act, conv_weight, down_weight, fine_act, neighbours, octant_routes):
    own = grad_out[0]
    places = octant_routes.shape[-1]
    table = jnp.concatenate([neighbours.reshape(-1), octant_routes.reshape(-1)])
    slots, voxels, channels = own.shape
    devices = lax.axis_size("dom")
    shards = lax.axis_size("dp")
    count = devices // 2
    factor = 1.0 / math.sqrt(shards * devices * slots * voxels)

    forward = [(i, i + 1) for i in range(devices - 1)]
    backward = [(i + 1, i) for i in range(devices - 1)]
    ring = [(i, (i + 1) % devices) for i in range(devices)]
    swap = [(i, i ^ 1) for i in range(devices)]

    def spread_out(parts, axis, stride):
        return [parts[0]] + [
            exchange(parts[step], axis, step, stride) for step in range(1, len(parts))
        ]

    low = lax.ppermute(own[:, voxels - PLANE :], "dom", forward)
    high = lax.ppermute(own[:, :PLANE], "dom", backward)
    to_lower, stay, to_upper = input_gradient(
        table, places, grad_out, low, high, pre_act, conv_weight
    )
    from_upper = lax.ppermute(to_lower, "dom", [(b, a) for a, b in ring])
    from_lower = lax.ppermute(to_upper, "dom", ring)
    conv_keep, conv_send = filter_gradient(shards, table, grad_out, low, high, pre_act)
    fine_grad, down_keep, down_send = fine_gradient(
        shards, count, from_upper, stay, from_lower, down_weight, fine_act[0]
    )
    conv_got = lax.ppermute(conv_send, "dom", swap)
    down_got = lax.ppermute(down_send, "dom", swap)

    planes, slabs, pieces = pair_sum(count, conv_keep, conv_got, down_keep, down_got)
    slabs = spread_out(slabs, "dp", 1)
    planes = spread_out(planes, "dom", 2)
    to_slabs, rest = middle_sum(planes, slabs)
    to_slabs = spread_out(to_slabs, "dp", 1)
    mine, rest = last_sum(factor, to_slabs, spread_out([rest] * count, "dom", 2))
    near = spread_out([mine] * count, "dom", 2)
    far = [lax.ppermute(value, "dom", swap) for value in near]
    rest_far = lax.ppermute(rest, "dom", swap)
    conv_rows = 27 * channels // shards
    down_rows = down_weight.shape[0] * down_weight.shape[1] // shards
    conv_grad, down_grad = gather_up(conv_rows, down_rows, pieces, near, far, rest, rest_far)
    return (fine_grad[None], conv_grad, down_grad)


def solution(mesh):
    return jax.shard_map(
        body,
        mesh=mesh,
        in_specs=(
            P("dp", "dom", None, None),
            P("dp", "dom", None, None),
            P(),
            P(),
            P("dp", "dom", None, None),
            P("dp", "dom", None),
            P("dp", "dom", None, None),
        ),
        out_specs=(P("dp", "dom", None, None), P("dp", None), P("dp", None)),
        check_vma=False,
    )
```

time: 94.5 us -> 96.7 us (1.023)
  Pallas kernels: 25.1 us -> 34.6 us
  local copies, waits for them, and re-layouts: 10.1 us -> 4.13 us
  waiting for transfers between devices: 27 us -> 21.2 us
  starting transfers between devices: 31.1 us -> 33.6 us
  other arithmetic: 0 us -> 2.01 us
    ppermute x9 -> x15, starting transfers between devices: 11.4 us -> 24.3 us  [exchange(): return lax.ppermute(value, axis, pairs)]
    all_to_all x2 -> x0, starting transfers between devices: 9.39 us -> none  [the longest x1 4.87 us: body(): to_slabs = lax.all_to_all(to_slabs, 'dp', 0, 0)]
    pallas_call x5, Pallas kernels: 20.1 us -> 26.6 us  [the longest x1 12.6 us: input_gradient(): pl.pallas_call(functools.partial(input_kernel, places), out_shape=(out, o...]
    unnamed x16 -> x12, local copies, waits for them, and re-layouts: 9.15 us -> 3 us
    all_to_all x2 -> x0, waiting for transfers between devices: 5.16 us -> none  [the longest x1 3.55 us: body(): to_slabs = lax.all_to_all(to_slabs, 'dp', 0, 0)]
    pallas_call x1, Pallas kernels: 3.56 us -> 6.07 us  [fine_gradient(): pl.pallas_call(functools.partial(fine_kernel, groups), grid=(3 * groups,)...]
    unnamed x0 -> x2, other arithmetic: none -> 1.4 us
    ppermute x9 -> x15, waiting for transfers between devices: 19.3 us -> 18.2 us  [exchange(): return lax.ppermute(value, axis, pairs)]
  transfers between devices with their start and end apart: 21 -> 26, of which waited for: 12 -> 9; matrix products, arithmetic and copies ran while one was open for 1% -> 2% of each run, Pallas kernels for 12% -> 19%
where the time goes in v1:
time: 96.7 us; the launch traced here: 96.3 us
  Pallas kernels  34.6 us (36%)
  starting transfers between devices  33.6 us (35%)
  waiting for transfers between devices  21.2 us (22%)
  local copies, waits for them, and re-layouts  4.13 us (4%)
  other arithmetic  2.01 us (2%)
    ppermute x15, starting transfers between devices, exchange(): return lax.ppermute(value, axis, pairs)  24.3 us
    ppermute x15, waiting for transfers between devices, exchange(): return lax.ppermute(value, axis, pairs)  18.2 us
    pallas_call x1, Pallas kernels, input_gradient(): pl.pallas_call(functools.partial(input_kernel, places), out_shape=(out, o...  12.6 us
    pallas_call x1, Pallas kernels, filter_gradient(): pl.pallas_call(functools.partial(filter_kernel, shard_rows), out_shape=(o...  12 us
    pallas_call x1, Pallas kernels, fine_gradient(): pl.pallas_call(functools.partial(fine_kernel, groups), grid=(3 * groups,)...  6.07 us
    ppermute x1, starting transfers between devices, body(): low = lax.ppermute(own[:, voxels - PLANE:], 'dom', forward)  3.04 us
    unnamed x12, local copies, waits for them, and re-layouts  3 us
    ppermute x1, starting transfers between devices, body(): from_upper = lax.ppermute(to_lower, 'dom', [(b, a) for a, b in ring])  2.93 us
  transfers between devices with their start and end apart: 26, of which 9 were waited for; matrix products, arithmetic and copies ran while one was open for 2% of the time, Pallas kernels for 19%

profile of v1, /device:TPU:0, one launch (start us, length us, event | category | flops | bytes accessed | tf_op | source)
XLA Modules:
  0.0 96.3 jit_solution(3034277992725722849)
XLA Ops:
  0.6 1.0 fusion
  1.6 1.3 %collective-permute-start.1 = (bf16[3,64,256]{2,1,0:T(8,128)(2,1)S(1)}, bf16[3,64,256]{2,1,0:T(8,128)(2,1)S(1)}, u32[]{:S(2)}, u32[]{:S(2)}) collective-permute-start(bf16[3,64,256]{2,1,0:T(8,128)(2,1)S(1)} %get-tuple-element.53), channel_id=1, source_target_pairs={{1,0},{2,1},{3,2},{4,3},{5,4},{6,5},{7,6},{9,8},{10,9},{11,10},{12... | collective-permute-start | bytes 294920 | tf_op jit(solution)/shard_map/ppermute | solution.py:548
  2.9 3.0 %collective-permute-start = (bf16[3,64,256]{2,1,0:T(8,128)(2,1)S(1)}, bf16[3,64,256]{2,1,0:T(8,128)(2,1)S(1)}, u32[]{:S(2)}, u32[]{:S(2)}) collective-permute-start(bf16[3,64,256]{2,1,0:T(8,128)(2,1)S(1)} %get-tuple-element.54), channel_id=1, source_target_pairs={{0,1},{1,2},{2,3},{3,4},{4,5},{5,6},{6,7},{8,9},{9,10},{10,11},{11... | collective-permute-start | bytes 294920 | tf_op jit(solution)/shard_map/ppermute | solution.py:547
  5.9 0.7 reduce
  6.6 0.1 reshape.12
  6.7 0.7 reduce.1
  7.4 0.1 reshape.13
  7.5 0.6 pad_add_fusion.table_ref
  8.1 0.0 collective-permute-done.1.high_ref
  8.1 0.0 collective-permute-done.low_ref
  8.1 0.6 copy-done.4
  8.8 0.6 copy-done.5
  9.4 12.6 %input_gradient.1 = (bf16[1,512,256]{2,1,0:T(8,128)(2,1)}, bf16[1,512,256]{2,1,0:T(8,128)(2,1)}, bf16[1,512,256]{2,1,0:T(8,128)(2,1)}) custom-call(s32[105]{0:T(128)} %pad_add_fusion.table_ref, bf16[1,3,512,256]{3,2,1,0:T(8,128)(2,1)} %own_hbm.3, bf16[3,64,256]{2,1,0:T(8,128)(2,1)} %copy-done.5, bf16[3,64,256]{2,1,0:T(8,128)(2,1)} %copy-done.4, ...), custom_call_target="tpu_custom_call" | custom-call | flops 5435817984 | bytes 8388608 | tf_op jit(solution)/shard_map/input_gradient/pallas_call | solution.py:197
  22.0 2.9 %collective-permute-start.2 = (bf16[1,512,256]{2,1,0:T(8,128)(2,1)}, bf16[1,512,256]{2,1,0:T(8,128)(2,1)S(1)}, u32[]{:S(2)}, u32[]{:S(2)}) collective-permute-start(bf16[1,512,256]{2,1,0:T(8,128)(2,1)} %get-tuple-element.28), channel_id=1, source_target_pairs={{1,0},{2,1},{3,2},{4,3},{5,4},{6,5},{7,6},{0,7},{9,8},{10,9},{11,1... | collective-permute-start | bytes 786440 | tf_op jit(solution)/shard_map/ppermute | solution.py:552
  25.0 12.0 %filter_gradient.1 = (bf16[4,1728,128]{2,1,0:T(8,128)(2,1)}, bf16[4,1728,128]{2,1,0:T(8,128)(2,1)}) custom-call(s32[105]{0:T(128)} %pad_add_fusion.table_ref, bf16[1,3,512,256]{3,2,1,0:T(8,128)(2,1)} %own_hbm.3, bf16[3,64,256]{2,1,0:T(8,128)(2,1)} %copy-done.5, bf16[3,64,256]{2,1,0:T(8,128)(2,1)} %copy-done.4, bf16[1,3,512,256]{3,2,1,0:T(8,128)(2,1)} %pre_hbm.3), custom_call_target="tpu_custom_call" | custom-call | flops 5435817984 | bytes 8388608 | tf_op jit(solution)/shard_map/filter_gradient/pallas_call | solution.py:272
  37.0 1.5 %collective-permute-start.4 = (bf16[4,1728,128]{2,1,0:T(8,128)(2,1)}, bf16[4,1728,128]{2,1,0:T(8,128)(2,1)}, u32[]{:S(2)}, u32[]{:S(2)}) collective-permute-start(bf16[4,1728,128]{2,1,0:T(8,128)(2,1)} %get-tuple-element.33), channel_id=1, source_target_pairs={{0,1},{1,0},{2,3},{3,2},{4,5},{5,4},{6,7},{7,6},{8,9},{9,8},{10,11... | collective-permute-start | bytes 5308424 | tf_op jit(solution)/shard_map/ppermute | solution.py:558
  38.5 0.0 collective-permute-done.2.upper_ref
  38.5 0.0 collective-permute-done.3.lower_ref
  38.5 0.7 copy-done.2
  39.2 0.1 copy-done.3
  39.3 6.1 %fine_gradient.1 = (bf16[24,512,128]{2,1,0:T(8,128)(2,1)}, bf16[4,256,128]{2,1,0:T(8,128)(2,1)}, bf16[4,256,128]{2,1,0:T(8,128)(2,1)}) custom-call(bf16[1,512,256]{2,1,0:T(8,128)(2,1)} %copy-done.2, bf16[1,512,256]{2,1,0:T(8,128)(2,1)} %get-tuple-element.29.stay_ref, bf16[1,512,256]{2,1,0:T(8,128)(2,1)} %copy-done.3, bf16[8,128,256]{2,1,0:T(8,128)(2,1)} %weight_ref.3, ...), custom_call_target="tpu_custom_call" | custom-call | flops 25769803776 | bytes 8388608 | tf_op jit(solution)/shard_map/fine_gradient/pallas_call | solution.py:356
  45.3 0.0 collective-permute-start.5
  45.4 1.7 %collective-permute-done.5.down_got_ref = bf16[4,256,128]{2,1,0:T(8,128)(2,1)S(1)} collective-permute-done((bf16[4,256,128]{2,1,0:T(8,128)(2,1)}, bf16[4,256,128]{2,1,0:T(8,128)(2,1)S(1)}, u32[]{:S(2)}, u32[]{:S(2)}) %collective-permute-start.5) | collective-permute-done | bytes 262176 | tf_op jit(solution)/shard_map/ppermute | solution.py:559
  47.1 0.9 copy-done.1
  48.1 1.9 %pair_sum.1 = (f32[4,336,128]{2,1,0:T(8,128)S(1)}, bf16[4,336,128]{2,1,0:T(8,128)(2,1)S(1)}, bf16[4,336,128]{2,1,0:T(8,128)(2,1)S(1)}, bf16[4,336,128]{2,1,0:T(8...) custom-call(bf16[4,1728,128]{2,1,0:T(8,128)(2,1)S(1)} %copy-done, ...), custom_call_target="tpu_custom_call" | custom-call | flops 6078464 | bytes 6078464 | tf_op jit(solution)/shard_map/pair_sum/pallas_call | solution.py:427
  50.0 3.3 %collective-permute-start.6 = (bf16[4,336,128]{2,1,0:T(8,128)(2,1)S(1)}, bf16[4,336,128]{2,1,0:T(8,128)(2,1)S(1)}, u32[]{:S(2)}, u32[]{:S(2)}) collective-permute-start(bf16[4,336,128]{2,1,0:T(8,128)(2,1)S(1)} %get-tuple-element.37), channel_id=1, source_target_pairs={{0,2},{1,3},{2,0},{3,1},{4,6},{5,7},{6,4},{7,5},{8,10},{9,11},{10,... | collective-permute-start | bytes 1032200 | tf_op jit(solution)/shard_map/ppermute | solution.py:47
  53.3 1.5 %collective-permute-start.8 = (bf16[4,336,128]{2,1,0:T(8,128)(2,1)S(1)}, bf16[4,336,128]{2,1,0:T(8,128)(2,1)S(1)}, u32[]{:S(2)}, u32[]{:S(2)}) collective-permute-start(bf16[4,336,128]{2,1,0:T(8,128)(2,1)S(1)} %get-tuple-element.39), channel_id=1, source_target_pairs={{0,6},{1,7},{2,4},{3,5},{4,2},{5,3},{6,0},{7,1},{8,14},{9,15},{10,... | collective-permute-start | bytes 1032200 | tf_op jit(solution)/shard_map/ppermute | solution.py:47
  54.8 1.6 %collective-permute-start.9 = (bf16[640,128]{1,0:T(8,128)(2,1)S(1)}, bf16[640,128]{1,0:T(8,128)(2,1)S(1)}, u32[]{:S(2)}, u32[]{:S(2)}) collective-permute-start(bf16[640,128]{1,0:T(8,128)(2,1)S(1)} %get-tuple-element.41), channel_id=1, source_target_pairs={{0,8},{8,0},{16,24},{24,16},{1,9},{9,1},{17,25},{25,17},{2,10},{10... | collective-permute-start | bytes 491528 | tf_op jit(solution)/shard_map/ppermute | solution.py:47
  56.4 2.6 %collective-permute-start.10 = (bf16[640,128]{1,0:T(8,128)(2,1)S(1)}, bf16[640,128]{1,0:T(8,128)(2,1)S(1)}, u32[]{:S(2)}, u32[]{:S(2)}) collective-permute-start(bf16[640,128]{1,0:T(8,128)(2,1)S(1)} %get-tuple-element.42), channel_id=1, source_target_pairs={{0,16},{8,24},{16,0},{24,8},{1,17},{9,25},{17,1},{25,9},{2,18},{10... | collective-permute-start | bytes 491528 | tf_op jit(solution)/shard_map/ppermute | solution.py:47
  59.0 4.6 %collective-permute-done.9.refs_5_ = bf16[640,128]{1,0:T(8,128)(2,1)S(1)} collective-permute-done((bf16[640,128]{1,0:T(8,128)(2,1)S(1)}, bf16[640,128]{1,0:T(8,128)(2,1)S(1)}, u32[]{:S(2)}, u32[]{:S(2)}) %collective-permute-start.9) | collective-permute-done | bytes 163872 | tf_op jit(solution)/shard_map/ppermute | solution.py:47
  63.6 2.7 %collective-permute-start.11 = (bf16[640,128]{1,0:T(8,128)(2,1)S(1)}, bf16[640,128]{1,0:T(8,128)(2,1)S(1)}, u32[]{:S(2)}, u32[]{:S(2)}) collective-permute-start(bf16[640,128]{1,0:T(8,128)(2,1)S(1)} %get-tuple-element.43), channel_id=1, source_target_pairs={{0,24},{8,16},{16,8},{24,0},{1,25},{9,17},{17,9},{25,1},{2,26},{10... | collective-permute-start | bytes 491528 | tf_op jit(solution)/shard_map/ppermute | solution.py:47
  66.3 2.1 %collective-permute-done.10.refs_6_ = bf16[640,128]{1,0:T(8,128)(2,1)S(1)} collective-permute-done((bf16[640,128]{1,0:T(8,128)(2,1)S(1)}, bf16[640,128]{1,0:T(8,128)(2,1)S(1)}, u32[]{:S(2)}, u32[]{:S(2)}) %collective-permute-start.10) | collective-permute-done | bytes 163872 | tf_op jit(solution)/shard_map/ppermute | solution.py:47
  68.4 2.5 %collective-permute-done.11.refs_7_ = bf16[640,128]{1,0:T(8,128)(2,1)S(1)} collective-permute-done((bf16[640,128]{1,0:T(8,128)(2,1)S(1)}, bf16[640,128]{1,0:T(8,128)(2,1)S(1)}, u32[]{:S(2)}, u32[]{:S(2)}) %collective-permute-start.11) | collective-permute-done | bytes 163872 | tf_op jit(solution)/shard_map/ppermute | solution.py:47
  70.8 0.0 collective-permute-done.7.refs_2_
  70.9 0.0 collective-permute-done.8.refs_3_
  70.9 0.2 middle_sum.1
  71.1 3.1 %collective-permute-start.12 = (bf16[336,128]{1,0:T(8,128)(2,1)S(1)}, bf16[336,128]{1,0:T(8,128)(2,1)S(1)}, u32[]{:S(2)}, u32[]{:S(2)}) collective-permute-start(bf16[336,128]{1,0:T(8,128)(2,1)S(1)} %get-tuple-element.45), channel_id=1, source_target_pairs={{0,8},{8,0},{16,24},{24,16},{1,9},{9,1},{17,25},{25,17},{2,10},{10... | collective-permute-start | bytes 258056 | tf_op jit(solution)/shard_map/ppermute | solution.py:47
  74.2 1.4 %collective-permute-start.17 = (bf16[640,128]{1,0:T(8,128)(2,1)S(1)}, bf16[640,128]{1,0:T(8,128)(2,1)S(1)}, u32[]{:S(2)}, u32[]{:S(2)}) collective-permute-start(bf16[640,128]{1,0:T(8,128)(2,1)S(1)} %get-tuple-element.48.refs_4_), channel_id=1, source_target_pairs={{0,6},{1,7},{2,4},{3,5},{4,2},{5,3},{6,0},{7,1},{8,14},{9,15},{10,... | collective-permute-start | bytes 491528 | tf_op jit(solution)/shard_map/ppermute | solution.py:47
  75.6 1.7 %collective-permute-start.16 = (bf16[640,128]{1,0:T(8,128)(2,1)S(1)}, bf16[640,128]{1,0:T(8,128)(2,1)S(1)}, u32[]{:S(2)}, u32[]{:S(2)}) collective-permute-start(bf16[640,128]{1,0:T(8,128)(2,1)S(1)} %get-tuple-element.48.refs_4_), channel_id=1, source_target_pairs={{0,4},{1,5},{2,6},{3,7},{4,0},{5,1},{6,2},{7,3},{8,12},{9,13},{10,... | collective-permute-start | bytes 491528 | tf_op jit(solution)/shard_map/ppermute | solution.py:47
  77.3 0.4 collective-permute-start.15
  77.7 1.1 %collective-permute-start.13 = (bf16[336,128]{1,0:T(8,128)(2,1)S(1)}, bf16[336,128]{1,0:T(8,128)(2,1)S(1)}, u32[]{:S(2)}, u32[]{:S(2)}) collective-permute-start(bf16[336,128]{1,0:T(8,128)(2,1)S(1)} %get-tuple-element.46), channel_id=1, source_target_pairs={{0,16},{8,24},{16,0},{24,8},{1,17},{9,25},{17,1},{25,9},{2,18},{10... | collective-permute-start | bytes 258056 | tf_op jit(solution)/shard_map/ppermute | solution.py:47
  78.7 0.0 collective-permute-done.12.refs_1_
  78.7 1.4 %collective-permute-start.14 = (bf16[336,128]{1,0:T(8,128)(2,1)S(1)}, bf16[336,128]{1,0:T(8,128)(2,1)S(1)}, u32[]{:S(2)}, u32[]{:S(2)}) collective-permute-start(bf16[336,128]{1,0:T(8,128)(2,1)S(1)} %get-tuple-element.47), channel_id=1, source_target_pairs={{0,24},{8,16},{16,8},{24,0},{1,25},{9,17},{17,9},{25,1},{2,26},{10... | collective-permute-start | bytes 258056 | tf_op jit(solution)/shard_map/ppermute | solution.py:47
  80.1 5.3 %collective-permute-done.13.refs_2_ = bf16[336,128]{1,0:T(8,128)(2,1)S(1)} collective-permute-done((bf16[336,128]{1,0:T(8,128)(2,1)S(1)}, bf16[336,128]{1,0:T(8,128)(2,1)S(1)}, u32[]{:S(2)}, u32[]{:S(2)}) %collective-permute-start.13) | collective-permute-done | bytes 86048 | tf_op jit(solution)/shard_map/ppermute | solution.py:47
  85.5 0.0 collective-permute-done.16.refs_6_
  85.5 0.0 collective-permute-done.15.refs_5_
  85.5 0.1 last_sum.1
  85.6 1.5 %collective-permute-start.20 = (bf16[336,128]{1,0:T(8,128)(2,1)S(1)}, bf16[336,128]{1,0:T(8,128)(2,1)S(1)}, u32[]{:S(2)}, u32[]{:S(2)}) collective-permute-start(bf16[336,128]{1,0:T(8,128)(2,1)S(1)} %get-tuple-element.49.refs_0_), channel_id=1, source_target_pairs={{0,6},{1,7},{2,4},{3,5},{4,2},{5,3},{6,0},{7,1},{8,14},{9,15},{10,... | collective-permute-start | bytes 258056 | tf_op jit(solution)/shard_map/ppermute | solution.py:47
  87.1 1.8 %collective-permute-start.19 = (bf16[336,128]{1,0:T(8,128)(2,1)S(1)}, bf16[336,128]{1,0:T(8,128)(2,1)S(1)}, u32[]{:S(2)}, u32[]{:S(2)}) collective-permute-start(bf16[336,128]{1,0:T(8,128)(2,1)S(1)} %get-tuple-element.49.refs_0_), channel_id=1, source_target_pairs={{0,4},{1,5},{2,6},{3,7},{4,0},{5,1},{6,2},{7,3},{8,12},{9,13},{10,... | collective-permute-start | bytes 258056 | tf_op jit(solution)/shard_map/ppermute | solution.py:47
  88.9 0.3 collective-permute-start.18
  89.2 0.0 collective-permute-start.25
  89.2 0.5 collective-permute-start.21
  89.7 1.5 %collective-permute-done.20.refs_3_ = bf16[336,128]{1,0:T(8,128)(2,1)S(1)} collective-permute-done((bf16[336,128]{1,0:T(8,128)(2,1)S(1)}, bf16[336,128]{1,0:T(8,128)(2,1)S(1)}, u32[]{:S(2)}, u32[]{:S(2)}) %collective-permute-start.20) | collective-permute-done | bytes 86048 | tf_op jit(solution)/shard_map/ppermute | solution.py:47
  91.2 0.0 collective-permute-start.24
  91.2 0.9 collective-permute-done.19.refs_2_
  92.0 0.0 collective-permute-start.23
  92.0 1.3 %collective-permute-done.18.refs_1_ = bf16[336,128]{1,0:T(8,128)(2,1)S(1)} collective-permute-done((bf16[336,128]{1,0:T(8,128)(2,1)S(1)}, bf16[336,128]{1,0:T(8,128)(2,1)S(1)}, u32[]{:S(2)}, u32[]{:S(2)}) %collective-permute-start.18) | collective-permute-done | bytes 86048 | tf_op jit(solution)/shard_map/ppermute | solution.py:47
  93.4 0.0 collective-permute-start.22
  93.4 0.0 collective-permute-done.21.refs_4_
  93.4 0.0 collective-permute-done.25.refs_9_
  93.4 0.0 collective-permute-done.24.refs_7_
  93.4 0.0 collective-permute-done.23.refs_6_
  93.4 1.2 %collective-permute-done.22.refs_5_ = bf16[336,128]{1,0:T(8,128)(2,1)S(1)} collective-permute-done((bf16[336,128]{1,0:T(8,128)(2,1)S(1)}, bf16[336,128]{1,0:T(8,128)(2,1)S(1)}, u32[]{:S(2)}, u32[]{:S(2)}) %collective-permute-start.22) | collective-permute-done | bytes 86048 | tf_op jit(solution)/shard_map/ppermute | solution.py:568
  94.7 1.6 %gather_up.1 = (f32[1728,256]{1,0:T(8,128)}, f32[256,256]{1,0:T(8,128)}) custom-call(bf16[336,128]{1,0:T(8,128)(2,1)S(1)} %get-tuple-element.49.refs_0_, bf16[336,128]{1,0:T(8,128)(2,1)S(1)} %collective-permute-done.18.refs_1_, bf16[336,128]{1,0:T(8,128)(2,1)S(1)} %collective-permute-done.19.refs_2_, bf16[336,128]{1,0:T(8,128)(2,1)S(1)} %collective-permute-done.20.refs_3_, ...), custom_call_target="tpu_custom_call" | custom-call | flops 2719744 | bytes 2719744 | tf_op jit(solution)/shard_map/gather_up/pallas_call | solution.py:512
  (13 shorter events, 0.0 us)
Async XLA Ops:
  1.6 6.5 %collective-permute-start.1 = (bf16[3,64,256]{2,1,0:T(8,128)(2,1)S(1)}, bf16[3,64,256]{2,1,0:T(8,128)(2,1)S(1)}, u32[]{:S(2)}, u32[]{:S(2)}) collective-permute-start(bf16[3,64,256]{2,1,0:T(8,128)(2,1)S(1)} %get-tuple-element.53), channel_id=1, source_target_pairs={{1,0},{2,1},{3,2},{4,3},{5,4},{6,5},{7,6},{9,8},{10,9},{11,10},{12... | collective-permute-start | bytes 294920 | tf_op jit(solution)/shard_map/ppermute | solution.py:548
  2.9 5.2 %collective-permute-start = (bf16[3,64,256]{2,1,0:T(8,128)(2,1)S(1)}, bf16[3,64,256]{2,1,0:T(8,128)(2,1)S(1)}, u32[]{:S(2)}, u32[]{:S(2)}) collective-permute-start(bf16[3,64,256]{2,1,0:T(8,128)(2,1)S(1)} %get-tuple-element.54), channel_id=1, source_target_pairs={{0,1},{1,2},{2,3},{3,4},{4,5},{5,6},{6,7},{8,9},{9,10},{10,11},{11... | collective-permute-start | bytes 294920 | tf_op jit(solution)/shard_map/ppermute | solution.py:547
  8.1 0.6 copy-start.4
  8.8 0.6 copy-start.5
  22.0 16.5 %collective-permute-start.2 = (bf16[1,512,256]{2,1,0:T(8,128)(2,1)}, bf16[1,512,256]{2,1,0:T(8,128)(2,1)S(1)}, u32[]{:S(2)}, u32[]{:S(2)}) collective-permute-start(bf16[1,512,256]{2,1,0:T(8,128)(2,1)} %get-tuple-element.28), channel_id=1, source_target_pairs={{1,0},{2,1},{3,2},{4,3},{5,4},{6,5},{7,6},{0,7},{9,8},{10,9},{11,1... | collective-permute-start | bytes 786440 | tf_op jit(solution)/shard_map/ppermute | solution.py:552
  25.0 13.5 %collective-permute-start.3 = (bf16[1,512,256]{2,1,0:T(8,128)(2,1)}, bf16[1,512,256]{2,1,0:T(8,128)(2,1)S(1)}, u32[]{:S(2)}, u32[]{:S(2)}) collective-permute-start(bf16[1,512,256]{2,1,0:T(8,128)(2,1)} %get-tuple-element.30), channel_id=1, source_target_pairs={{0,1},{1,2},{2,3},{3,4},{4,5},{5,6},{6,7},{7,0},{8,9},{9,10},{10,1... | collective-permute-start | bytes 786440 | tf_op jit(solution)/shard_map/ppermute | solution.py:553
  37.0 10.1 %collective-permute-start.4 = (bf16[4,1728,128]{2,1,0:T(8,128)(2,1)}, bf16[4,1728,128]{2,1,0:T(8,128)(2,1)}, u32[]{:S(2)}, u32[]{:S(2)}) collective-permute-start(bf16[4,1728,128]{2,1,0:T(8,128)(2,1)} %get-tuple-element.33), channel_id=1, source_target_pairs={{0,1},{1,0},{2,3},{3,2},{4,5},{5,4},{6,7},{7,6},{8,9},{9,8},{10,11... | collective-permute-start | bytes 5308424 | tf_op jit(solution)/shard_map/ppermute | solution.py:558
  38.5 0.7 copy-start.2
  38.5 0.8 copy-start.3
  39.3 7.8 %copy-start = (bf16[4,1728,128]{2,1,0:T(8,128)(2,1)S(1)}, bf16[4,1728,128]{2,1,0:T(8,128)(2,1)}, u32[]{:S(2)}) copy-start(bf16[4,1728,128]{2,1,0:T(8,128)(2,1)} %get-tuple-element.32.conv_ref) | copy-start | bytes 5308420
  45.3 1.7 %collective-permute-start.5 = (bf16[4,256,128]{2,1,0:T(8,128)(2,1)}, bf16[4,256,128]{2,1,0:T(8,128)(2,1)S(1)}, u32[]{:S(2)}, u32[]{:S(2)}) collective-permute-start(bf16[4,256,128]{2,1,0:T(8,128)(2,1)} %get-tuple-element.35), channel_id=1, source_target_pairs={{0,1},{1,0},{2,3},{3,2},{4,5},{5,4},{6,7},{7,6},{8,9},{9,8},{10,11... | collective-permute-start | bytes 786440 | tf_op jit(solution)/shard_map/ppermute | solution.py:559
  47.1 1.0 copy-start.1
  50.0 20.9 %collective-permute-start.6 = (bf16[4,336,128]{2,1,0:T(8,128)(2,1)S(1)}, bf16[4,336,128]{2,1,0:T(8,128)(2,1)S(1)}, u32[]{:S(2)}, u32[]{:S(2)}) collective-permute-start(bf16[4,336,128]{2,1,0:T(8,128)(2,1)S(1)} %get-tuple-element.37), channel_id=1, source_target_pairs={{0,2},{1,3},{2,0},{3,1},{4,6},{5,7},{6,4},{7,5},{8,10},{9,11},{10,... | collective-permute-start | bytes 1032200 | tf_op jit(solution)/shard_map/ppermute | solution.py:47
  53.3 17.6 %collective-permute-start.7 = (bf16[4,336,128]{2,1,0:T(8,128)(2,1)S(1)}, bf16[4,336,128]{2,1,0:T(8,128)(2,1)S(1)}, u32[]{:S(2)}, u32[]{:S(2)}) collective-permute-start(bf16[4,336,128]{2,1,0:T(8,128)(2,1)S(1)} %get-tuple-element.38), channel_id=1, source_target_pairs={{0,4},{1,5},{2,6},{3,7},{4,0},{5,1},{6,2},{7,3},{8,12},{9,13},{10,... | collective-permute-start | bytes 1032200 | tf_op jit(solution)/shard_map/ppermute | solution.py:47
  53.3 17.6 %collective-permute-start.8 = (bf16[4,336,128]{2,1,0:T(8,128)(2,1)S(1)}, bf16[4,336,128]{2,1,0:T(8,128)(2,1)S(1)}, u32[]{:S(2)}, u32[]{:S(2)}) collective-permute-start(bf16[4,336,128]{2,1,0:T(8,128)(2,1)S(1)} %get-tuple-element.39), channel_id=1, source_target_pairs={{0,6},{1,7},{2,4},{3,5},{4,2},{5,3},{6,0},{7,1},{8,14},{9,15},{10,... | collective-permute-start | bytes 1032200 | tf_op jit(solution)/shard_map/ppermute | solution.py:47
  54.8 8.8 %collective-permute-start.9 = (bf16[640,128]{1,0:T(8,128)(2,1)S(1)}, bf16[640,128]{1,0:T(8,128)(2,1)S(1)}, u32[]{:S(2)}, u32[]{:S(2)}) collective-permute-start(bf16[640,128]{1,0:T(8,128)(2,1)S(1)} %get-tuple-element.41), channel_id=1, source_target_pairs={{0,8},{8,0},{16,24},{24,16},{1,9},{9,1},{17,25},{25,17},{2,10},{10... | collective-permute-start | bytes 491528 | tf_op jit(solution)/shard_map/ppermute | solution.py:47
  56.4 12.0 %collective-permute-start.10 = (bf16[640,128]{1,0:T(8,128)(2,1)S(1)}, bf16[640,128]{1,0:T(8,128)(2,1)S(1)}, u32[]{:S(2)}, u32[]{:S(2)}) collective-permute-start(bf16[640,128]{1,0:T(8,128)(2,1)S(1)} %get-tuple-element.42), channel_id=1, source_target_pairs={{0,16},{8,24},{16,0},{24,8},{1,17},{9,25},{17,1},{25,9},{2,18},{10... | collective-permute-start | bytes 491528 | tf_op jit(solution)/shard_map/ppermute | solution.py:47
  63.6 7.2 %collective-permute-start.11 = (bf16[640,128]{1,0:T(8,128)(2,1)S(1)}, bf16[640,128]{1,0:T(8,128)(2,1)S(1)}, u32[]{:S(2)}, u32[]{:S(2)}) collective-permute-start(bf16[640,128]{1,0:T(8,128)(2,1)S(1)} %get-tuple-element.43), channel_id=1, source_target_pairs={{0,24},{8,16},{16,8},{24,0},{1,25},{9,17},{17,9},{25,1},{2,26},{10... | collective-permute-start | bytes 491528 | tf_op jit(solution)/shard_map/ppermute | solution.py:47
  71.1 7.6 %collective-permute-start.12 = (bf16[336,128]{1,0:T(8,128)(2,1)S(1)}, bf16[336,128]{1,0:T(8,128)(2,1)S(1)}, u32[]{:S(2)}, u32[]{:S(2)}) collective-permute-start(bf16[336,128]{1,0:T(8,128)(2,1)S(1)} %get-tuple-element.45), channel_id=1, source_target_pairs={{0,8},{8,0},{16,24},{24,16},{1,9},{9,1},{17,25},{25,17},{2,10},{10... | collective-permute-start | bytes 258056 | tf_op jit(solution)/shard_map/ppermute | solution.py:47
  74.2 11.3 %collective-permute-start.17 = (bf16[640,128]{1,0:T(8,128)(2,1)S(1)}, bf16[640,128]{1,0:T(8,128)(2,1)S(1)}, u32[]{:S(2)}, u32[]{:S(2)}) collective-permute-start(bf16[640,128]{1,0:T(8,128)(2,1)S(1)} %get-tuple-element.48.refs_4_), channel_id=1, source_target_pairs={{0,6},{1,7},{2,4},{3,5},{4,2},{5,3},{6,0},{7,1},{8,14},{9,15},{10,... | collective-permute-start | bytes 491528 | tf_op jit(solution)/shard_map/ppermute | solution.py:47
  75.6 9.9 %collective-permute-start.16 = (bf16[640,128]{1,0:T(8,128)(2,1)S(1)}, bf16[640,128]{1,0:T(8,128)(2,1)S(1)}, u32[]{:S(2)}, u32[]{:S(2)}) collective-permute-start(bf16[640,128]{1,0:T(8,128)(2,1)S(1)} %get-tuple-element.48.refs_4_), channel_id=1, source_target_pairs={{0,4},{1,5},{2,6},{3,7},{4,0},{5,1},{6,2},{7,3},{8,12},{9,13},{10,... | collective-permute-start | bytes 491528 | tf_op jit(solution)/shard_map/ppermute | solution.py:47
  77.3 8.2 %collective-permute-start.15 = (bf16[640,128]{1,0:T(8,128)(2,1)S(1)}, bf16[640,128]{1,0:T(8,128)(2,1)S(1)}, u32[]{:S(2)}, u32[]{:S(2)}) collective-permute-start(bf16[640,128]{1,0:T(8,128)(2,1)S(1)} %get-tuple-element.48.refs_4_), channel_id=1, source_target_pairs={{0,2},{1,3},{2,0},{3,1},{4,6},{5,7},{6,4},{7,5},{8,10},{9,11},{10,... | collective-permute-start | bytes 491528 | tf_op jit(solution)/shard_map/ppermute | solution.py:47
  77.7 7.8 %collective-permute-start.13 = (bf16[336,128]{1,0:T(8,128)(2,1)S(1)}, bf16[336,128]{1,0:T(8,128)(2,1)S(1)}, u32[]{:S(2)}, u32[]{:S(2)}) collective-permute-start(bf16[336,128]{1,0:T(8,128)(2,1)S(1)} %get-tuple-element.46), channel_id=1, source_target_pairs={{0,16},{8,24},{16,0},{24,8},{1,17},{9,25},{17,1},{25,9},{2,18},{10... | collective-permute-start | bytes 258056 | tf_op jit(solution)/shard_map/ppermute | solution.py:47
  78.7 6.7 %collective-permute-start.14 = (bf16[336,128]{1,0:T(8,128)(2,1)S(1)}, bf16[336,128]{1,0:T(8,128)(2,1)S(1)}, u32[]{:S(2)}, u32[]{:S(2)}) collective-permute-start(bf16[336,128]{1,0:T(8,128)(2,1)S(1)} %get-tuple-element.47), channel_id=1, source_target_pairs={{0,24},{8,16},{16,8},{24,0},{1,25},{9,17},{17,9},{25,1},{2,26},{10... | collective-permute-start | bytes 258056 | tf_op jit(solution)/shard_map/ppermute | solution.py:47
  85.6 5.5 %collective-permute-start.20 = (bf16[336,128]{1,0:T(8,128)(2,1)S(1)}, bf16[336,128]{1,0:T(8,128)(2,1)S(1)}, u32[]{:S(2)}, u32[]{:S(2)}) collective-permute-start(bf16[336,128]{1,0:T(8,128)(2,1)S(1)} %get-tuple-element.49.refs_0_), channel_id=1, source_target_pairs={{0,6},{1,7},{2,4},{3,5},{4,2},{5,3},{6,0},{7,1},{8,14},{9,15},{10,... | collective-permute-start | bytes 258056 | tf_op jit(solution)/shard_map/ppermute | solution.py:47
  87.1 5.0 %collective-permute-start.19 = (bf16[336,128]{1,0:T(8,128)(2,1)S(1)}, bf16[336,128]{1,0:T(8,128)(2,1)S(1)}, u32[]{:S(2)}, u32[]{:S(2)}) collective-permute-start(bf16[336,128]{1,0:T(8,128)(2,1)S(1)} %get-tuple-element.49.refs_0_), channel_id=1, source_target_pairs={{0,4},{1,5},{2,6},{3,7},{4,0},{5,1},{6,2},{7,3},{8,12},{9,13},{10,... | collective-permute-start | bytes 258056 | tf_op jit(solution)/shard_map/ppermute | solution.py:47
  88.9 4.5 %collective-permute-start.18 = (bf16[336,128]{1,0:T(8,128)(2,1)S(1)}, bf16[336,128]{1,0:T(8,128)(2,1)S(1)}, u32[]{:S(2)}, u32[]{:S(2)}) collective-permute-start(bf16[336,128]{1,0:T(8,128)(2,1)S(1)} %get-tuple-element.49.refs_0_), channel_id=1, source_target_pairs={{0,2},{1,3},{2,0},{3,1},{4,6},{5,7},{6,4},{7,5},{8,10},{9,11},{10,... | collective-permute-start | bytes 258056 | tf_op jit(solution)/shard_map/ppermute | solution.py:47
  89.2 4.2 %collective-permute-start.25 = (bf16[640,128]{1,0:T(8,128)(2,1)S(1)}, bf16[640,128]{1,0:T(8,128)(2,1)S(1)}, u32[]{:S(2)}, u32[]{:S(2)}) collective-permute-start(bf16[640,128]{1,0:T(8,128)(2,1)S(1)} %get-tuple-element.50.refs_8_), channel_id=1, source_target_pairs={{0,1},{1,0},{2,3},{3,2},{4,5},{5,4},{6,7},{7,6},{8,9},{9,8},{10,11... | collective-permute-start | bytes 491528 | tf_op jit(solution)/shard_map/ppermute | solution.py:569
  89.2 4.2 %collective-permute-start.21 = (bf16[336,128]{1,0:T(8,128)(2,1)S(1)}, bf16[336,128]{1,0:T(8,128)(2,1)S(1)}, u32[]{:S(2)}, u32[]{:S(2)}) collective-permute-start(bf16[336,128]{1,0:T(8,128)(2,1)S(1)} %get-tuple-element.49.refs_0_), channel_id=1, source_target_pairs={{0,1},{1,0},{2,3},{3,2},{4,5},{5,4},{6,7},{7,6},{8,9},{9,8},{10,11... | collective-permute-start | bytes 258056 | tf_op jit(solution)/shard_map/ppermute | solution.py:568
  91.2 2.2 %collective-permute-start.24 = (bf16[336,128]{1,0:T(8,128)(2,1)S(1)}, bf16[336,128]{1,0:T(8,128)(2,1)S(1)}, u32[]{:S(2)}, u32[]{:S(2)}) collective-permute-start(bf16[336,128]{1,0:T(8,128)(2,1)S(1)} %collective-permute-done.20.refs_3_), channel_id=1, source_target_pairs={{0,1},{1,0},{2,3},{3,2},{4,5},{5,4},{6,7},{7,6},{8,9},{9,8},{10,11... | collective-permute-start | bytes 258056 | tf_op jit(solution)/shard_map/ppermute | solution.py:568
  92.0 1.4 %collective-permute-start.23 = (bf16[336,128]{1,0:T(8,128)(2,1)S(1)}, bf16[336,128]{1,0:T(8,128)(2,1)S(1)}, u32[]{:S(2)}, u32[]{:S(2)}) collective-permute-start(bf16[336,128]{1,0:T(8,128)(2,1)S(1)} %collective-permute-done.19.refs_2_), channel_id=1, source_target_pairs={{0,1},{1,0},{2,3},{3,2},{4,5},{5,4},{6,7},{7,6},{8,9},{9,8},{10,11... | collective-permute-start | bytes 258056 | tf_op jit(solution)/shard_map/ppermute | solution.py:568
  93.4 1.3 %collective-permute-start.22 = (bf16[336,128]{1,0:T(8,128)(2,1)S(1)}, bf16[336,128]{1,0:T(8,128)(2,1)S(1)}, u32[]{:S(2)}, u32[]{:S(2)}) collective-permute-start(bf16[336,128]{1,0:T(8,128)(2,1)S(1)} %collective-permute-done.18.refs_1_), channel_id=1, source_target_pairs={{0,1},{1,0},{2,3},{3,2},{4,5},{5,4},{6,7},{7,6},{8,9},{9,8},{10,11... | collective-permute-start | bytes 258056 | tf_op jit(solution)/shard_map/ppermute | solution.py:568

commit v2 on v1

--- a/solution.py
+++ b/solution.py
@@ -22,7 +22,7 @@
 
 
 def params(mib):
-    return pltpu.CompilerParams(vmem_limit_bytes=mib * MIB)
+    return pltpu.CompilerParams(vmem_limit_bytes=int(mib * MIB))
 
 
 def relative(index, step, count):
@@ -47,119 +47,146 @@
     return lax.ppermute(value, axis, pairs)
 
 
-def fetch(ref, slot, start, rows):
-    value = ref[jnp.maximum(slot, 0), pl.ds(start, rows), :].astype(F32)
-    return jnp.where(slot >= 0, value, 0.0)
-
-
-def spread(table_ref, ref, start, step_x, slot, row, win_ref):
-    channels = ref.shape[-1]
-
-    def link(step_y, step_z):
-        return table_ref[27 * slot + 9 * (step_x + 1) + 3 * (step_y + 1) + step_z + 1]
-
-    columns = {}
-    for step_z in (-1, 0, 1):
-        below = fetch(ref, link(-1, step_z), start + PLANE - 16, 16).reshape(2, BE, channels)[1:]
-        middle = fetch(ref, link(0, step_z), start, PLANE).reshape(BE, BE, channels)
-        above = fetch(ref, link(1, step_z), start, 16).reshape(2, BE, channels)[:1]
-        columns[step_z] = jnp.concatenate([below, middle, above], axis=0)
-    place_z = lax.broadcasted_iota(jnp.int32, columns[0].shape, 1)
-    shifted = {
-        0: columns[0],
-        -1: jnp.where(
-            place_z == 0, pltpu.roll(columns[-1], 1, axis=1), pltpu.roll(columns[0], 1, axis=1)
-        ),
-        1: jnp.where(
-            place_z == BE - 1,
-            pltpu.roll(columns[1], BE - 1, axis=1),
-            pltpu.roll(columns[0], BE - 1, axis=1),
-        ),
-    }
-    for tap_y in (-1, 0, 1):
-        for tap_z in (-1, 0, 1):
-            tap = 3 * (tap_y + 1) + tap_z + 1
-            value = shifted[-tap_z][1 - tap_y : 1 - tap_y + BE].reshape(PLANE, channels)
-            win_ref[pl.ds(row, PLANE), tap * channels : (tap + 1) * channels] = value.astype(BF16)
-
-
-def build_windows(table_ref, own_ref, low_ref, high_ref, win_ref):
-    slots = own_ref.shape[0]
-
-    def edge(slot, carry):
-        spread(table_ref, low_ref, 0, -1, slot, pl.multiple_of(slot * PLANE, PLANE), win_ref)
-        row = ((BE + 1) * slots + slot) * PLANE
-        spread(table_ref, high_ref, 0, 1, slot, pl.multiple_of(row, PLANE), win_ref)
-        return carry
-
-    def inner(step, carry):
-        x = step // slots
-        slot = step - x * slots
-        row = (x + 1) * slots * PLANE + slot * PLANE
-        start = pl.multiple_of(x * PLANE, PLANE)
-        spread(table_ref, own_ref, start, 0, slot, pl.multiple_of(row, PLANE), win_ref)
-        return carry
-
-    lax.fori_loop(0, slots, edge, 0)
-    lax.fori_loop(0, BE * slots, inner, 0)
-
-
 def started(source, target, sem):
     copy = pltpu.make_async_copy(source, target, sem)
     copy.start()
     return copy
 
 
+GROUPS = (0, -1, 1)
+
+
+def column_of(tap):
+    _, rest = divmod(tap, 9)
+    tap_y, tap_z = rest // 3 - 1, rest % 3 - 1
+    return 3 * GROUPS.index(-tap_z) + tap_y + 1
+
+
+def extend(ref, wide_ref):
+    slots = ref.shape[0]
+    wide_ref[:slots] = ref[...]
+    wide_ref[slots] = jnp.zeros(ref.shape[1:], ref.dtype)
+
+
+def spread(links_ref, ref, start, step_x, slot, row, shift, win_ref):
+    channels = ref.shape[-1]
+    empty = ref.shape[0] - 1
+
+    def fetch(step_y, step_z, first, rows):
+        found = links_ref[slot, 9 * (step_x + 1) + 3 * (step_y + 1) + step_z + 1]
+        place = jnp.where(found < 0, empty, found)
+        return ref[place, start + first : start + first + rows, :].astype(F32)
+
+    def column(step_z):
+        below = fetch(-1, step_z, PLANE - 16, 16).reshape(2, BE, channels)[1:]
+        middle = fetch(0, step_z, 0, PLANE).reshape(BE, BE, channels)
+        above = fetch(1, step_z, 0, 16).reshape(2, BE, channels)[:1]
+        return jnp.concatenate([below, middle, above], axis=0)
+
+    value = column(0)
+    if shift != 0:
+        turn = 1 if shift < 0 else BE - 1
+        edge = 0 if shift < 0 else BE - 1
+        place_z = lax.broadcasted_iota(jnp.int32, value.shape, 1)
+        value = jnp.where(
+            place_z == edge,
+            pltpu.roll(column(shift), turn, axis=1),
+            pltpu.roll(value, turn, axis=1),
+        )
+    for tap_y in (-1, 0, 1):
+        lane = (3 * GROUPS.index(shift) + tap_y + 1) * channels
+        part = value[1 - tap_y : 1 - tap_y + BE].reshape(PLANE, channels)
+        win_ref[row : row + PLANE, lane : lane + channels] = part.astype(BF16)
+
+
+def builders(links_ref, own_ref, low_ref, high_ref, win_ref, shift):
+    slots = own_ref.shape[0] - 1
+    calls = []
+    for plane in range(BE + 2):
+        if plane == 0:
+            ref, start, step_x = low_ref, 0, -1
+        elif plane == BE + 1:
+            ref, start, step_x = high_ref, 0, 1
+        else:
+            ref, start, step_x = own_ref, (plane - 1) * PLANE, 0
+        for slot in range(slots):
+            row = (plane * slots + slot) * PLANE
+            calls.append(
+                functools.partial(
+                    spread, links_ref, ref, start, step_x, slot, row, shift, win_ref
+                )
+            )
+    return calls
+
+
+def interleave(first, second):
+    done = 0
+    for index, call in enumerate(first):
+        call()
+        until = len(second) * (index + 1) // len(first)
+        for other in second[done:until]:
+            other()
+        done = until
+
+
 def input_kernel(
-    places, table_ref, own_hbm, low_ref, high_ref, pre_hbm, weight_ref,
+    links_ref, routes_ref, own_ref, low_ref, high_ref, pre_ref, weight_ref,
     to_lower_ref, stay_ref, to_upper_ref,
-    own_ref, pre_ref, win_ref, taps_ref, acc_ref, octants_ref,
-    in_sems, tap_sems, out_sems,
+    own_wide, low_wide, high_wide, win_ref, taps_ref, acc_ref, octants_ref, tap_sems, out_sems,
 ):
     slots, voxels, channels = own_ref.shape
-    groups = places // 8
-    own_copy = started(own_hbm.at[0], own_ref, in_sems.at[1])
+    groups = routes_ref.shape[1] // 8
     copies = []
     for tap in range(27):
-        index_x, rest = divmod(tap, 9)
-        lanes = slice(rest * channels, (rest + 1) * channels)
+        column = column_of(tap)
+        lanes = slice(column * channels, (column + 1) * channels)
         copies.append(
-            started(weight_ref.at[tap], taps_ref.at[index_x, :, lanes], tap_sems.at[tap])
+            started(weight_ref.at[tap], taps_ref.at[tap // 9, :, lanes], tap_sems.at[tap])
         )
-    pre_copy = started(pre_hbm.at[0], pre_ref, in_sems.at[2])
-    own_copy.wait()
-    build_windows(table_ref, own_ref, low_ref, high_ref, win_ref)
-    for copy in copies:
-        copy.wait()
+    for ref, wide in ((own_ref, own_wide), (low_ref, low_wide), (high_ref, high_wide)):
+        extend(ref, wide)
     slab = slots * PLANE
     rows = BE * slab
-    half = rows // 2
-
-    def multiply(part, carry):
-        start = part * half
+    part = rows // 2
+
+    def product(group, start):
+        lanes = slice(3 * group * channels, 3 * (group + 1) * channels)
         total = None
         for index_x in range(3):
-            offset = pl.multiple_of(start + (2 - index_x) * slab, PLANE)
+            offset = start + (2 - index_x) * slab
             term = lax.dot_general(
-                win_ref[pl.ds(offset, half), :],
-                taps_ref[index_x],
+                win_ref[offset : offset + part, lanes],
+                taps_ref[index_x, :, lanes],
                 (((1,), (1,)), ((), ())),
                 preferred_element_type=F32,
             )
             total = term if total is None else total + term
-        acc_ref[pl.ds(pl.multiple_of(start, PLANE), half), :] = total
-        return carry
-
-    lax.fori_loop(0, 2, multiply, 0)
-    pre_copy.wait()
+        if group > 0:
+            total = total + acc_ref[start : start + part, :]
+        acc_ref[start : start + part, :] = total
+
+    def products(group):
+        return [functools.partial(product, group, start) for start in range(0, rows, part)]
+
+    sources = (links_ref, own_wide, low_wide, high_wide, win_ref)
+    for call in builders(*sources, GROUPS[0]):
+        call()
+    for copy in copies:
+        copy.wait()
+    interleave(products(0), builders(*sources, GROUPS[1]))
+    interleave(products(1), builders(*sources, GROUPS[2]))
+    for call in products(2):
+        call()
+
     octants_ref[...] = jnp.zeros_like(octants_ref)
     place_z = lax.broadcasted_iota(jnp.int32, (BE // 2, BE, channels), 1)
     for slot in range(slots):
         group = jnp.int32(3 * groups)
         for row in range(3):
-            for part in range(groups):
-                entry = table_ref[27 * slots + row * places + 8 * part]
-                group = jnp.where(entry == 8 * slot, row * groups + part, group)
+            for place in range(groups):
+                group = jnp.where(
+                    routes_ref[row, 8 * place] == 8 * slot, row * groups + place, group
+                )
 
         def finish(x, carry):
             value = acc_ref[pl.ds(pl.multiple_of(x * slab + slot * PLANE, PLANE), PLANE), :]
@@ -180,113 +207,116 @@
         lax.fori_loop(0, BE, finish, 0)
     outs = []
     for row, ref in enumerate((to_lower_ref, stay_ref, to_upper_ref)):
-        copy = pltpu.make_async_copy(
-            octants_ref.at[pl.ds(row * groups, groups)], ref, out_sems.at[row]
-        )
-        copy.start()
-        outs.append(copy)
+        outs.append(started(octants_ref.at[pl.ds(row * groups, groups)], ref, out_sems.at[row]))
     for copy in outs:
         copy.wait()
 
 
-def input_gradient(table, places, own, low, high, pre, weight):
-    _, slots, voxels, channels = own.shape
-    groups = places // 8
+def wide_scratch(own, low):
+    slots, voxels, channels = own.shape
+    return [
+        pltpu.VMEM((slots + 1, voxels, channels), BF16),
+        pltpu.VMEM((slots + 1, low.shape[1], channels), BF16),
+        pltpu.VMEM((slots + 1, low.shape[1], channels), BF16),
+        pltpu.VMEM((slots * PLANE * (BE + 2), 9 * channels), BF16),
+    ]
+
+
+def input_gradient(links, routes, own, low, high, pre, weight):
+    slots, voxels, channels = own.shape
+    groups = routes.shape[1] // 8
     rows = slots * voxels
     out = jax.ShapeDtypeStruct((groups, voxels, channels), BF16)
     return pl.pallas_call(
-        functools.partial(input_kernel, places),
+        input_kernel,
         out_shape=(out, out, out),
-        in_specs=[SMEM, HBM, VMEM, VMEM, HBM, HBM],
+        in_specs=[SMEM, SMEM, VMEM, VMEM, VMEM, VMEM, ANY],
         out_specs=(ANY, ANY, ANY),
-        scratch_shapes=[
-            pltpu.VMEM(own.shape[1:], BF16),
-            pltpu.VMEM(pre.shape[1:], BF16),
-            pltpu.VMEM((slots * PLANE * (BE + 2), 9 * channels), BF16),
+        scratch_shapes=wide_scratch(own, low)
+        + [
             pltpu.VMEM((3, channels, 9 * channels), BF16),
             pltpu.VMEM((rows, channels), F32),
             pltpu.VMEM((3 * groups + 1, voxels, channels), BF16),
-            pltpu.SemaphoreType.DMA((3,)),
             pltpu.SemaphoreType.DMA((27,)),
             pltpu.SemaphoreType.DMA((3,)),
         ],
-        compiler_params=params(62),
+        compiler_params=params(40),
         cost_estimate=pl.CostEstimate(
             flops=2 * rows * 27 * channels * channels, bytes_accessed=8 * MIB, transcendentals=0
         ),
         name="input_gradient",
-    )(table, own, low, high, pre, weight)
+    )(links, routes, own, low, high, pre, weight)
 
 
 def filter_kernel(
-    shard_rows, table_ref, own_hbm, low_ref, high_ref, pre_hbm,
-    keep_ref, send_ref, own_ref, pre_ref, win_ref, act_ref, in_sems,
+    shard_rows, links_ref, own_ref, low_ref, high_ref, pre_ref,
+    keep_ref, send_ref, own_wide, low_wide, high_wide, win_ref, act_ref,
 ):
     slots, voxels, channels = own_ref.shape
     slab = slots * PLANE
     rows = BE * slab
     lanes = channels // 2
-    pre_copy = started(pre_hbm.at[0], pre_ref, in_sems.at[2])
-    own_copy = started(own_hbm.at[0], own_ref, in_sems.at[1])
-    pre_copy.wait()
-    for pair in range(BE // 2):
+    for ref, wide in ((own_ref, own_wide), (low_ref, low_wide), (high_ref, high_wide)):
+        extend(ref, wide)
+
+    def transpose(pair):
         parts = []
         for x in (2 * pair, 2 * pair + 1):
             for slot in range(slots):
                 parts.append(pre_ref[slot, x * PLANE : (x + 1) * PLANE, :])
         block = jnp.maximum(jnp.concatenate(parts, axis=0).astype(F32), 0.0)
         act_ref[:, pair * 2 * slab : (pair + 1) * 2 * slab] = block.T.astype(BF16)
-    own_copy.wait()
-    build_windows(table_ref, own_ref, low_ref, high_ref, win_ref)
+
     first = lax.rem(lax.axis_index("dom"), 2) == 0
     unit = math.gcd(channels, shard_rows)
 
-    def step(index_x, carry):
-        offset = pl.multiple_of((2 - index_x) * slab, PLANE)
-        for rest in range(9):
-            total = jnp.dot(
-                act_ref[...],
-                win_ref[pl.ds(offset, rows), rest * channels : (rest + 1) * channels],
-                preferred_element_type=F32,
-            )
-            left, right = total[:, :lanes], total[:, lanes:]
-            keep = jnp.where(first, left, right).astype(BF16)
-            send = jnp.where(first, right, left).astype(BF16)
-            for part in range(channels // unit):
-                row = (index_x * 9 + rest) * channels + part * unit
-                shard = row // shard_rows
-                start = pl.multiple_of(row - shard * shard_rows, unit)
-                span = slice(part * unit, (part + 1) * unit)
-                keep_ref[shard, pl.ds(start, unit), :] = keep[span]
-                send_ref[shard, pl.ds(start, unit), :] = send[span]
-        return carry
-
-    lax.fori_loop(0, 3, step, 0)
-
-
-def filter_gradient(shards, table, own, low, high, pre):
-    _, slots, voxels, channels = own.shape
+    def product(tap):
+        offset = (2 - tap // 9) * slab
+        column = column_of(tap) * channels
+        total = jnp.dot(
+            act_ref[...],
+            win_ref[offset : offset + rows, column : column + channels],
+            preferred_element_type=F32,
+        )
+        left, right = total[:, :lanes], total[:, lanes:]
+        keep = jnp.where(first, left, right).astype(BF16)
+        send = jnp.where(first, right, left).astype(BF16)
+        for part in range(channels // unit):
+            shard, start = divmod(tap * channels + part * unit, shard_rows)
+            span = slice(part * unit, (part + 1) * unit)
+            keep_ref[shard, start : start + unit, :] = keep[span]
+            send_ref[shard, start : start + unit, :] = send[span]
+
+    def products(group):
+        taps = [tap for tap in range(27) if column_of(tap) // 3 == group]
+        return [functools.partial(product, tap) for tap in taps]
+
+    sources = (links_ref, own_wide, low_wide, high_wide, win_ref)
+    turns = [functools.partial(transpose, pair) for pair in range(BE // 2)]
+    interleave(turns, builders(*sources, GROUPS[0]))
+    interleave(products(0), builders(*sources, GROUPS[1]))
+    interleave(products(1), builders(*sources, GROUPS[2]))
+    for call in products(2):
+        call()
+
+
+def filter_gradient(shards, links, own, low, high, pre):
+    slots, voxels, channels = own.shape
     shard_rows = 27 * channels // shards
     rows = slots * voxels
     out = jax.ShapeDtypeStruct((shards, shard_rows, channels // 2), BF16)
     return pl.pallas_call(
         functools.partial(filter_kernel, shard_rows),
         out_shape=(out, out),
-        in_specs=[SMEM, HBM, VMEM, VMEM, HBM],
+        in_specs=[SMEM, VMEM, VMEM, VMEM, VMEM],
         out_specs=(VMEM, VMEM),
-        scratch_shapes=[
-            pltpu.VMEM(own.shape[1:], BF16),
-            pltpu.VMEM(pre.shape[1:], BF16),
-            pltpu.VMEM((slots * PLANE * (BE + 2), 9 * channels), BF16),
-            pltpu.VMEM((channels, rows), BF16),
-            pltpu.SemaphoreType.DMA((3,)),
-        ],
-        compiler_params=params(62),
+        scratch_shapes=wide_scratch(own, low) + [pltpu.VMEM((channels, rows), BF16)],
+        compiler_params=params(40),
         cost_estimate=pl.CostEstimate(
             flops=2 * rows * 27 * channels * channels, bytes_accessed=8 * MIB, transcendentals=0
         ),
         name="filter_gradient",
-    )(table, own, low, high, pre)
+    )(links, own, low, high, pre)
 
 
 def fine_kernel(
@@ -364,7 +394,7 @@
         ],
         out_specs=(block, same, same),
         scratch_shapes=[pltpu.VMEM((channels, taps * fine_channels), F32)],
-        compiler_params=params(61),
+        compiler_params=params(40),
         cost_estimate=pl.CostEstimate(
             flops=64 * fine * voxels * fine_channels * channels, bytes_accessed=8 * MIB,
             transcendentals=0,
@@ -526,8 +556,9 @@
 
 def body(grad_out, pre_act, conv_weight, down_weight, fine_act, neighbours, octant_routes):
     own = grad_out[0]
-    places = octant_routes.shape[-1]
-    table = jnp.concatenate([neighbours.reshape(-1), octant_routes.reshape(-1)])
+    pre = pre_act[0]
+    links = neighbours[0]
+    routes = octant_routes[0, 0]
     slots, voxels, channels = own.shape
     devices = lax.axis_size("dom")
     shards = lax.axis_size("dp")
@@ -547,11 +578,11 @@
     low = lax.ppermute(own[:, voxels - PLANE :], "dom", forward)
     high = lax.ppermute(own[:, :PLANE], "dom", backward)
     to_lower, stay, to_upper = input_gradient(
-        table, places, grad_out, low, high, pre_act, conv_weight
+        links, routes, own, low, high, pre, conv_weight
     )
     from_upper = lax.ppermute(to_lower, "dom", [(b, a) for a, b in ring])
     from_lower = lax.ppermute(to_upper, "dom", ring)
-    conv_keep, conv_send = filter_gradient(shards, table, grad_out, low, high, pre_act)
+    conv_keep, conv_send = filter_gradient(shards, links, own, low, high, pre)
     fine_grad, down_keep, down_send = fine_gradient(
         shards, count, from_upper, stay, from_lower, down_weight, fine_act[0]
     )

time: 96.7 us -> 83.5 us (0.86)
  Pallas kernels: 34.6 us -> 20 us
  local copies, waits for them, and re-layouts: 4.13 us -> 6.61 us
  other arithmetic: 2.01 us -> 0 us
    pallas_call x1, Pallas kernels: 12 us -> 6.43 us  [filter_gradient(): pl.pallas_call(functools.partial(filter_kernel, shard_rows), out_shape=(o...]
    pallas_call x1, Pallas kernels: 12.6 us -> 7.65 us  [input_gradient(): pl.pallas_call(input_kernel, out_shape=(out, out, out), in_specs=[SMEM, S...]
    unnamed x12 -> x16, local copies, waits for them, and re-layouts: 3 us -> 5.65 us
    pallas_call x1, Pallas kernels: 6.07 us -> 3.53 us  [fine_gradient(): pl.pallas_call(functools.partial(fine_kernel, groups), grid=(3 * groups,)...]
    pallas_call x1, Pallas kernels: 1.92 us -> 0.44 us  [pair_sum(): pl.pallas_call(functools.partial(pair_kernel, count), out_shape=outs, in_...]
    unnamed x2 -> x0, other arithmetic: 1.4 us -> none
  transfers between devices with their start and end apart: 26 -> 26, of which waited for: 9 -> 10; matrix products, arithmetic and copies ran while one was open for 2% -> 2% of each run, Pallas kernels for 19% -> 12%
where the time goes in v2:
time: 83.5 us; the launch traced here: 83.1 us
  starting transfers between devices  33.8 us (40%)
  waiting for transfers between devices  21.9 us (26%)
  Pallas kernels  20 us (24%)
  local copies, waits for them, and re-layouts  6.61 us (8%)
    ppermute x15, starting transfers between devices, exchange(): return lax.ppermute(value, axis, pairs)  23.4 us
    ppermute x15, waiting for transfers between devices, exchange(): return lax.ppermute(value, axis, pairs)  18.2 us
    pallas_call x1, Pallas kernels, input_gradient(): pl.pallas_call(input_kernel, out_shape=(out, out, out), in_specs=[SMEM, S...  7.65 us
    pallas_call x1, Pallas kernels, filter_gradient(): pl.pallas_call(functools.partial(filter_kernel, shard_rows), out_shape=(o...  6.43 us
    unnamed x16, local copies, waits for them, and re-layouts  5.65 us
    pallas_call x1, Pallas kernels, fine_gradient(): pl.pallas_call(functools.partial(fine_kernel, groups), grid=(3 * groups,)...  3.53 us
    ppermute x1, starting transfers between devices, body(): from_upper = lax.ppermute(to_lower, 'dom', [(b, a) for a, b in ring])  3.45 us
    ppermute x1, starting transfers between devices, body(): low = lax.ppermute(own[:, voxels - PLANE:], 'dom', forward)  3.04 us
  transfers between devices with their start and end apart: 26, of which 10 were waited for; matrix products, arithmetic and copies ran while one was open for 2% of the time, Pallas kernels for 12%

profile of v2, /device:TPU:0, one launch (start us, length us, event | category | flops | bytes accessed | tf_op | source)
XLA Modules:
  0.0 83.1 jit_solution(2647450651662276203)
XLA Ops:
  0.6 1.0 %fusion = (bf16[3,64,256]{2,1,0:T(8,128)(2,1)S(1)}, bf16[3,64,256]{2,1,0:T(8,128)(2,1)S(1)}) fusion(bf16[3,512,256]{2,1,0:T(8,128)(2,1)} %bitcast.10), kind=kLoop, calls=%fused_computation.2 | loop fusion | bytes 393216 | tf_op jit(solution)/shard_map/slice | solution.py:579
  1.6 1.3 %collective-permute-start.1 = (bf16[3,64,256]{2,1,0:T(8,128)(2,1)S(1)}, bf16[3,64,256]{2,1,0:T(8,128)(2,1)S(1)}, u32[]{:S(2)}, u32[]{:S(2)}) collective-permute-start(bf16[3,64,256]{2,1,0:T(8,128)(2,1)S(1)} %get-tuple-element.53), channel_id=1, source_target_pairs={{1,0},{2,1},{3,2},{4,3},{5,4},{6,5},{7,6},{9,8},{10,9},{11,10},{12... | collective-permute-start | bytes 294920 | tf_op jit(solution)/shard_map/ppermute | solution.py:579
  2.9 3.0 %collective-permute-start = (bf16[3,64,256]{2,1,0:T(8,128)(2,1)S(1)}, bf16[3,64,256]{2,1,0:T(8,128)(2,1)S(1)}, u32[]{:S(2)}, u32[]{:S(2)}) collective-permute-start(bf16[3,64,256]{2,1,0:T(8,128)(2,1)S(1)} %get-tuple-element.54), channel_id=1, source_target_pairs={{0,1},{1,2},{2,3},{3,4},{4,5},{5,6},{6,7},{8,9},{9,10},{10,11},{11... | collective-permute-start | bytes 294920 | tf_op jit(solution)/shard_map/ppermute | solution.py:578
  5.9 0.7 copy.15
  6.6 0.7 copy.14
  7.3 0.0 collective-permute-done.1.high_ref
  7.3 0.0 collective-permute-done.low_ref
  7.3 1.1 %copy-done = bf16[1,3,512,256]{3,2,1,0:T(8,128)(2,1)S(1)} copy-done((bf16[1,3,512,256]{3,2,1,0:T(8,128)(2,1)S(1)}, bf16[1,3,512,256]{3,2,1,0:T(8,128)(2,1)}, u32[]{:S(2)}) %copy-start) | copy-done | bytes 786456
  8.4 2.0 %copy-done.2 = bf16[27,256,256]{2,1,0:T(8,128)(2,1)S(1)} copy-done((bf16[27,256,256]{2,1,0:T(8,128)(2,1)S(1)}, bf16[27,256,256]{2,1,0:T(8,128)(2,1)}, u32[]{:S(2)}) %copy-start.2) | copy-done | bytes 3538968
  10.4 1.1 %copy-done.4 = bf16[1,3,512,256]{3,2,1,0:T(8,128)(2,1)S(1)} copy-done((bf16[1,3,512,256]{3,2,1,0:T(8,128)(2,1)S(1)}, bf16[1,3,512,256]{3,2,1,0:T(8,128)(2,1)}, u32[]{:S(2)}) %copy-start.4) | copy-done | bytes 786456
  11.6 7.6 %input_gradient.1 = (bf16[1,512,256]{2,1,0:T(8,128)(2,1)S(1)}, bf16[1,512,256]{2,1,0:T(8,128)(2,1)S(1)}, bf16[1,512,256]{2,1,0:T(8,128)(2,1)S(1)}) custom-call(s32[3,27]{1,0:T(4,128)S(1)} %bitcast.13, s32[3,8]{1,0:T(4,128)S(1)} %bitcast.15, bf16[3,512,256]{2,1,0:T(8,128)(2,1)S(1)} %bitcast.11, bf16[3,64,256]{2,1,0:T(8,128)(2,1)S(1)} %collective-permute-done.low_ref, ...), custom_call_target="tpu_custom_call" | custom-call | flops 5435817984 | bytes 8388608 | tf_op jit(solution)/shard_map/input_gradient/pallas_call | solution.py:230
  19.2 3.5 %collective-permute-start.2 = (bf16[1,512,256]{2,1,0:T(8,128)(2,1)S(1)}, bf16[1,512,256]{2,1,0:T(8,128)(2,1)S(1)}, u32[]{:S(2)}, u32[]{:S(2)}) collective-permute-start(bf16[1,512,256]{2,1,0:T(8,128)(2,1)S(1)} %get-tuple-element.28), channel_id=1, source_target_pairs={{1,0},{2,1},{3,2},{4,3},{5,4},{6,5},{7,6},{0,7},{9,8},{10,9},{11,1... | collective-permute-start | bytes 786440 | tf_op jit(solution)/shard_map/ppermute | solution.py:583
  22.7 0.0 collective-permute-start.3
  22.7 6.4 %filter_gradient.1 = (bf16[4,1728,128]{2,1,0:T(8,128)(2,1)S(1)}, bf16[4,1728,128]{2,1,0:T(8,128)(2,1)S(1)}) custom-call(s32[3,27]{1,0:T(4,128)S(1)} %bitcast.14, bf16[3,512,256]{2,1,0:T(8,128)(2,1)S(1)} %bitcast.12, bf16[3,64,256]{2,1,0:T(8,128)(2,1)S(1)} %collective-permute-done.low_ref, bf16[3,64,256]{2,1,0:T(8,128)(2,1)S(1)} %collective-permute-done.1.high_ref, ...), custom_call_target="tpu_custom_call" | custom-call | flops 5435817984 | bytes 8388608 | tf_op jit(solution)/shard_map/filter_gradient/pallas_call | solution.py:308
  29.2 2.1 %collective-permute-start.4 = (bf16[4,1728,128]{2,1,0:T(8,128)(2,1)S(1)}, bf16[4,1728,128]{2,1,0:T(8,128)(2,1)S(1)}, u32[]{:S(2)}, u32[]{:S(2)}) collective-permute-start(bf16[4,1728,128]{2,1,0:T(8,128)(2,1)S(1)} %get-tuple-element.33), channel_id=1, source_target_pairs={{0,1},{1,0},{2,3},{3,2},{4,5},{5,4},{6,7},{7,6},{8,9},{9,8},{10,11... | collective-permute-start | bytes 5308424 | tf_op jit(solution)/shard_map/ppermute | solution.py:589
  31.3 0.0 collective-permute-done.2.upper_ref
  31.3 0.9 %collective-permute-done.3.lower_ref = bf16[1,512,256]{2,1,0:T(8,128)(2,1)S(1)} collective-permute-done((bf16[1,512,256]{2,1,0:T(8,128)(2,1)S(1)}, bf16[1,512,256]{2,1,0:T(8,128)(2,1)S(1)}, u32[]{:S(2)}, u32[]{:S(2)}) %collective-permute-start.3) | collective-permute-done | bytes 262176 | tf_op jit(solution)/shard_map/ppermute | solution.py:584
  32.1 3.5 %fine_gradient.1 = (bf16[24,512,128]{2,1,0:T(8,128)(2,1)}, bf16[4,256,128]{2,1,0:T(8,128)(2,1)S(1)}, bf16[4,256,128]{2,1,0:T(8,128)(2,1)S(1)}) custom-call(bf16[1,512,256]{2,1,0:T(8,128)(2,1)S(1)} %collective-permute-done.2.upper_ref, bf16[1,512,256]{2,1,0:T(8,128)(2,1)S(1)} %get-tuple-element.29.stay_ref, ...), custom_call_target="tpu_custom_call" | custom-call | flops 25769803776 | bytes 8388608 | tf_op jit(solution)/shard_map/fine_gradient/pallas_call | solution.py:386
  35.7 0.0 collective-permute-start.5
  35.7 1.5 %collective-permute-done.5.down_got_ref = bf16[4,256,128]{2,1,0:T(8,128)(2,1)S(1)} collective-permute-done((bf16[4,256,128]{2,1,0:T(8,128)(2,1)S(1)}, bf16[4,256,128]{2,1,0:T(8,128)(2,1)S(1)}, u32[]{:S(2)}, u32[]{:S(2)}) %collective-permute-start.5) | collective-permute-done | bytes 262176 | tf_op jit(solution)/shard_map/ppermute | solution.py:590
  37.2 0.0 collective-permute-done.4.conv_got_ref
  37.2 0.4 pair_sum.1
  37.7 2.5 %collective-permute-start.6 = (bf16[4,336,128]{2,1,0:T(8,128)(2,1)S(1)}, bf16[4,336,128]{2,1,0:T(8,128)(2,1)S(1)}, u32[]{:S(2)}, u32[]{:S(2)}) collective-permute-start(bf16[4,336,128]{2,1,0:T(8,128)(2,1)S(1)} %get-tuple-element.37), channel_id=1, source_target_pairs={{0,2},{1,3},{2,0},{3,1},{4,6},{5,7},{6,4},{7,5},{8,10},{9,11},{10,... | collective-permute-start | bytes 1032200 | tf_op jit(solution)/shard_map/ppermute | solution.py:47
  40.2 0.4 collective-permute-start.7
  40.6 1.1 %collective-permute-start.8 = (bf16[4,336,128]{2,1,0:T(8,128)(2,1)S(1)}, bf16[4,336,128]{2,1,0:T(8,128)(2,1)S(1)}, u32[]{:S(2)}, u32[]{:S(2)}) collective-permute-start(bf16[4,336,128]{2,1,0:T(8,128)(2,1)S(1)} %get-tuple-element.39), channel_id=1, source_target_pairs={{0,6},{1,7},{2,4},{3,5},{4,2},{5,3},{6,0},{7,1},{8,14},{9,15},{10,... | collective-permute-start | bytes 1032200 | tf_op jit(solution)/shard_map/ppermute | solution.py:47
  41.7 1.6 %collective-permute-start.9 = (bf16[640,128]{1,0:T(8,128)(2,1)S(1)}, bf16[640,128]{1,0:T(8,128)(2,1)S(1)}, u32[]{:S(2)}, u32[]{:S(2)}) collective-permute-start(bf16[640,128]{1,0:T(8,128)(2,1)S(1)} %get-tuple-element.41), channel_id=1, source_target_pairs={{0,8},{8,0},{16,24},{24,16},{1,9},{9,1},{17,25},{25,17},{2,10},{10... | collective-permute-start | bytes 491528 | tf_op jit(solution)/shard_map/ppermute | solution.py:47
  43.3 2.6 %collective-permute-start.10 = (bf16[640,128]{1,0:T(8,128)(2,1)S(1)}, bf16[640,128]{1,0:T(8,128)(2,1)S(1)}, u32[]{:S(2)}, u32[]{:S(2)}) collective-permute-start(bf16[640,128]{1,0:T(8,128)(2,1)S(1)} %get-tuple-element.42), channel_id=1, source_target_pairs={{0,16},{8,24},{16,0},{24,8},{1,17},{9,25},{17,1},{25,9},{2,18},{10... | collective-permute-start | bytes 491528 | tf_op jit(solution)/shard_map/ppermute | solution.py:47
  45.9 4.6 %collective-permute-done.9.refs_5_ = bf16[640,128]{1,0:T(8,128)(2,1)S(1)} collective-permute-done((bf16[640,128]{1,0:T(8,128)(2,1)S(1)}, bf16[640,128]{1,0:T(8,128)(2,1)S(1)}, u32[]{:S(2)}, u32[]{:S(2)}) %collective-permute-start.9) | collective-permute-done | bytes 163872 | tf_op jit(solution)/shard_map/ppermute | solution.py:47
  50.5 2.7 %collective-permute-start.11 = (bf16[640,128]{1,0:T(8,128)(2,1)S(1)}, bf16[640,128]{1,0:T(8,128)(2,1)S(1)}, u32[]{:S(2)}, u32[]{:S(2)}) collective-permute-start(bf16[640,128]{1,0:T(8,128)(2,1)S(1)} %get-tuple-element.43), channel_id=1, source_target_pairs={{0,24},{8,16},{16,8},{24,0},{1,25},{9,17},{17,9},{25,1},{2,26},{10... | collective-permute-start | bytes 491528 | tf_op jit(solution)/shard_map/ppermute | solution.py:47
  53.2 2.1 %collective-permute-done.10.refs_6_ = bf16[640,128]{1,0:T(8,128)(2,1)S(1)} collective-permute-done((bf16[640,128]{1,0:T(8,128)(2,1)S(1)}, bf16[640,128]{1,0:T(8,128)(2,1)S(1)}, u32[]{:S(2)}, u32[]{:S(2)}) %collective-permute-start.10) | collective-permute-done | bytes 163872 | tf_op jit(solution)/shard_map/ppermute | solution.py:47
  55.2 2.5 %collective-permute-done.11.refs_7_ = bf16[640,128]{1,0:T(8,128)(2,1)S(1)} collective-permute-done((bf16[640,128]{1,0:T(8,128)(2,1)S(1)}, bf16[640,128]{1,0:T(8,128)(2,1)S(1)}, u32[]{:S(2)}, u32[]{:S(2)}) %collective-permute-start.11) | collective-permute-done | bytes 163872 | tf_op jit(solution)/shard_map/ppermute | solution.py:47
  57.7 0.0 collective-permute-done.6.refs_1_
  57.7 0.0 collective-permute-done.7.refs_2_
  57.7 0.0 collective-permute-done.8.refs_3_
  57.7 0.2 middle_sum.1
  58.0 3.1 %collective-permute-start.12 = (bf16[336,128]{1,0:T(8,128)(2,1)S(1)}, bf16[336,128]{1,0:T(8,128)(2,1)S(1)}, u32[]{:S(2)}, u32[]{:S(2)}) collective-permute-start(bf16[336,128]{1,0:T(8,128)(2,1)S(1)} %get-tuple-element.45), channel_id=1, source_target_pairs={{0,8},{8,0},{16,24},{24,16},{1,9},{9,1},{17,25},{25,17},{2,10},{10... | collective-permute-start | bytes 258056 | tf_op jit(solution)/shard_map/ppermute | solution.py:47
  61.0 1.5 %collective-permute-start.17 = (bf16[640,128]{1,0:T(8,128)(2,1)S(1)}, bf16[640,128]{1,0:T(8,128)(2,1)S(1)}, u32[]{:S(2)}, u32[]{:S(2)}) collective-permute-start(bf16[640,128]{1,0:T(8,128)(2,1)S(1)} %get-tuple-element.48.refs_4_), channel_id=1, source_target_pairs={{0,6},{1,7},{2,4},{3,5},{4,2},{5,3},{6,0},{7,1},{8,14},{9,15},{10,... | collective-permute-start | bytes 491528 | tf_op jit(solution)/shard_map/ppermute | solution.py:47
  62.6 1.6 %collective-permute-start.16 = (bf16[640,128]{1,0:T(8,128)(2,1)S(1)}, bf16[640,128]{1,0:T(8,128)(2,1)S(1)}, u32[]{:S(2)}, u32[]{:S(2)}) collective-permute-start(bf16[640,128]{1,0:T(8,128)(2,1)S(1)} %get-tuple-element.48.refs_4_), channel_id=1, source_target_pairs={{0,4},{1,5},{2,6},{3,7},{4,0},{5,1},{6,2},{7,3},{8,12},{9,13},{10,... | collective-permute-start | bytes 491528 | tf_op jit(solution)/shard_map/ppermute | solution.py:47
  64.2 0.4 collective-permute-start.15
  64.5 1.1 %collective-permute-start.13 = (bf16[336,128]{1,0:T(8,128)(2,1)S(1)}, bf16[336,128]{1,0:T(8,128)(2,1)S(1)}, u32[]{:S(2)}, u32[]{:S(2)}) collective-permute-start(bf16[336,128]{1,0:T(8,128)(2,1)S(1)} %get-tuple-element.46), channel_id=1, source_target_pairs={{0,16},{8,24},{16,0},{24,8},{1,17},{9,25},{17,1},{25,9},{2,18},{10... | collective-permute-start | bytes 258056 | tf_op jit(solution)/shard_map/ppermute | solution.py:47
  65.6 0.0 collective-permute-done.12.refs_1_
  65.6 1.4 %collective-permute-start.14 = (bf16[336,128]{1,0:T(8,128)(2,1)S(1)}, bf16[336,128]{1,0:T(8,128)(2,1)S(1)}, u32[]{:S(2)}, u32[]{:S(2)}) collective-permute-start(bf16[336,128]{1,0:T(8,128)(2,1)S(1)} %get-tuple-element.47), channel_id=1, source_target_pairs={{0,24},{8,16},{16,8},{24,0},{1,25},{9,17},{17,9},{25,1},{2,26},{10... | collective-permute-start | bytes 258056 | tf_op jit(solution)/shard_map/ppermute | solution.py:47
  67.0 5.3 %collective-permute-done.13.refs_2_ = bf16[336,128]{1,0:T(8,128)(2,1)S(1)} collective-permute-done((bf16[336,128]{1,0:T(8,128)(2,1)S(1)}, bf16[336,128]{1,0:T(8,128)(2,1)S(1)}, u32[]{:S(2)}, u32[]{:S(2)}) %collective-permute-start.13) | collective-permute-done | bytes 86048 | tf_op jit(solution)/shard_map/ppermute | solution.py:47
  72.3 0.0 collective-permute-done.14.refs_3_
  72.3 0.0 collective-permute-done.17.refs_7_
  72.3 0.0 collective-permute-done.16.refs_6_
  72.3 0.0 collective-permute-done.15.refs_5_
  72.3 0.1 last_sum.1
  72.5 1.8 %collective-permute-start.20 = (bf16[336,128]{1,0:T(8,128)(2,1)S(1)}, bf16[336,128]{1,0:T(8,128)(2,1)S(1)}, u32[]{:S(2)}, u32[]{:S(2)}) collective-permute-start(bf16[336,128]{1,0:T(8,128)(2,1)S(1)} %get-tuple-element.49.refs_0_), channel_id=1, source_target_pairs={{0,6},{1,7},{2,4},{3,5},{4,2},{5,3},{6,0},{7,1},{8,14},{9,15},{10,... | collective-permute-start | bytes 258056 | tf_op jit(solution)/shard_map/ppermute | solution.py:47
  74.3 1.5 %collective-permute-start.19 = (bf16[336,128]{1,0:T(8,128)(2,1)S(1)}, bf16[336,128]{1,0:T(8,128)(2,1)S(1)}, u32[]{:S(2)}, u32[]{:S(2)}) collective-permute-start(bf16[336,128]{1,0:T(8,128)(2,1)S(1)} %get-tuple-element.49.refs_0_), channel_id=1, source_target_pairs={{0,4},{1,5},{2,6},{3,7},{4,0},{5,1},{6,2},{7,3},{8,12},{9,13},{10,... | collective-permute-start | bytes 258056 | tf_op jit(solution)/shard_map/ppermute | solution.py:47
  75.8 0.3 collective-permute-start.18
  76.1 0.0 collective-permute-start.25
  76.1 0.5 collective-permute-start.21
  76.6 1.4 %collective-permute-done.20.refs_3_ = bf16[336,128]{1,0:T(8,128)(2,1)S(1)} collective-permute-done((bf16[336,128]{1,0:T(8,128)(2,1)S(1)}, bf16[336,128]{1,0:T(8,128)(2,1)S(1)}, u32[]{:S(2)}, u32[]{:S(2)}) %collective-permute-start.20) | collective-permute-done | bytes 86048 | tf_op jit(solution)/shard_map/ppermute | solution.py:47
  78.0 0.0 collective-permute-start.24
  78.0 0.9 %collective-permute-done.19.refs_2_ = bf16[336,128]{1,0:T(8,128)(2,1)S(1)} collective-permute-done((bf16[336,128]{1,0:T(8,128)(2,1)S(1)}, bf16[336,128]{1,0:T(8,128)(2,1)S(1)}, u32[]{:S(2)}, u32[]{:S(2)}) %collective-permute-start.19) | collective-permute-done | bytes 86048 | tf_op jit(solution)/shard_map/ppermute | solution.py:47
  78.9 0.0 collective-permute-start.23
  78.9 1.4 %collective-permute-done.18.refs_1_ = bf16[336,128]{1,0:T(8,128)(2,1)S(1)} collective-permute-done((bf16[336,128]{1,0:T(8,128)(2,1)S(1)}, bf16[336,128]{1,0:T(8,128)(2,1)S(1)}, u32[]{:S(2)}, u32[]{:S(2)}) %collective-permute-start.18) | collective-permute-done | bytes 86048 | tf_op jit(solution)/shard_map/ppermute | solution.py:47
  80.2 0.0 collective-permute-start.22
  80.2 0.0 collective-permute-done.21.refs_4_
  80.3 0.0 collective-permute-done.25.refs_9_
  80.3 0.0 collective-permute-done.24.refs_7_
  80.3 1.2 %collective-permute-done.22.refs_5_ = bf16[336,128]{1,0:T(8,128)(2,1)S(1)} collective-permute-done((bf16[336,128]{1,0:T(8,128)(2,1)S(1)}, bf16[336,128]{1,0:T(8,128)(2,1)S(1)}, u32[]{:S(2)}, u32[]{:S(2)}) %collective-permute-start.22) | collective-permute-done | bytes 86048 | tf_op jit(solution)/shard_map/ppermute | solution.py:599
  81.5 1.6 %gather_up.1 = (f32[1728,256]{1,0:T(8,128)}, f32[256,256]{1,0:T(8,128)}) custom-call(bf16[336,128]{1,0:T(8,128)(2,1)S(1)} %get-tuple-element.49.refs_0_, bf16[336,128]{1,0:T(8,128)(2,1)S(1)} %collective-permute-done.18.refs_1_, bf16[336,128]{1,0:T(8,128)(2,1)S(1)} %collective-permute-done.19.refs_2_, bf16[336,128]{1,0:T(8,128)(2,1)S(1)} %collective-permute-done.20.refs_3_, ...), custom_call_target="tpu_custom_call" | custom-call | flops 2719744 | bytes 2719744 | tf_op jit(solution)/shard_map/gather_up/pallas_call | solution.py:542
  (12 shorter events, 0.0 us)
Async XLA Ops:
  1.6 5.7 %collective-permute-start.1 = (bf16[3,64,256]{2,1,0:T(8,128)(2,1)S(1)}, bf16[3,64,256]{2,1,0:T(8,128)(2,1)S(1)}, u32[]{:S(2)}, u32[]{:S(2)}) collective-permute-start(bf16[3,64,256]{2,1,0:T(8,128)(2,1)S(1)} %get-tuple-element.53), channel_id=1, source_target_pairs={{1,0},{2,1},{3,2},{4,3},{5,4},{6,5},{7,6},{9,8},{10,9},{11,10},{12... | collective-permute-start | bytes 294920 | tf_op jit(solution)/shard_map/ppermute | solution.py:579
  2.9 4.4 %collective-permute-start = (bf16[3,64,256]{2,1,0:T(8,128)(2,1)S(1)}, bf16[3,64,256]{2,1,0:T(8,128)(2,1)S(1)}, u32[]{:S(2)}, u32[]{:S(2)}) collective-permute-start(bf16[3,64,256]{2,1,0:T(8,128)(2,1)S(1)} %get-tuple-element.54), channel_id=1, source_target_pairs={{0,1},{1,2},{2,3},{3,4},{4,5},{5,6},{6,7},{8,9},{9,10},{10,11},{11... | collective-permute-start | bytes 294920 | tf_op jit(solution)/shard_map/ppermute | solution.py:578
  7.3 1.1 %copy-start = (bf16[1,3,512,256]{3,2,1,0:T(8,128)(2,1)S(1)}, bf16[1,3,512,256]{3,2,1,0:T(8,128)(2,1)}, u32[]{:S(2)}) copy-start(bf16[1,3,512,256]{3,2,1,0:T(8,128)(2,1)} %param.7) | copy-start | bytes 2359300
  8.4 2.0 %copy-start.2 = (bf16[27,256,256]{2,1,0:T(8,128)(2,1)S(1)}, bf16[27,256,256]{2,1,0:T(8,128)(2,1)}, u32[]{:S(2)}) copy-start(bf16[27,256,256]{2,1,0:T(8,128)(2,1)} %weight_ref.2) | copy-start | bytes 10616836
  10.4 1.1 %copy-start.4 = (bf16[1,3,512,256]{3,2,1,0:T(8,128)(2,1)S(1)}, bf16[1,3,512,256]{3,2,1,0:T(8,128)(2,1)}, u32[]{:S(2)}) copy-start(bf16[1,3,512,256]{3,2,1,0:T(8,128)(2,1)} %param.8) | copy-start | bytes 2359300
  11.6 11.1 %copy-start.1 = (bf16[1,3,512,256]{3,2,1,0:T(8,128)(2,1)S(1)}, bf16[1,3,512,256]{3,2,1,0:T(8,128)(2,1)}, u32[]{:S(2)}) copy-start(bf16[1,3,512,256]{3,2,1,0:T(8,128)(2,1)} %param.7) | copy-start | bytes 2359300
  11.6 11.1 %copy-start.5 = (bf16[1,3,512,256]{3,2,1,0:T(8,128)(2,1)S(1)}, bf16[1,3,512,256]{3,2,1,0:T(8,128)(2,1)}, u32[]{:S(2)}) copy-start(bf16[1,3,512,256]{3,2,1,0:T(8,128)(2,1)} %param.8) | copy-start | bytes 2359300
  19.2 12.0 %collective-permute-start.2 = (bf16[1,512,256]{2,1,0:T(8,128)(2,1)S(1)}, bf16[1,512,256]{2,1,0:T(8,128)(2,1)S(1)}, u32[]{:S(2)}, u32[]{:S(2)}) collective-permute-start(bf16[1,512,256]{2,1,0:T(8,128)(2,1)S(1)} %get-tuple-element.28), channel_id=1, source_target_pairs={{1,0},{2,1},{3,2},{4,3},{5,4},{6,5},{7,6},{0,7},{9,8},{10,9},{11,1... | collective-permute-start | bytes 786440 | tf_op jit(solution)/shard_map/ppermute | solution.py:583
  22.7 9.4 %copy-start.3 = (bf16[1,24,512,128]{3,2,1,0:T(8,128)(2,1)S(1)}, bf16[1,24,512,128]{3,2,1,0:T(8,128)(2,1)}, u32[]{:S(2)}) copy-start(bf16[1,24,512,128]{3,2,1,0:T(8,128)(2,1)} %param.11) | copy-start | bytes 9437188
  22.7 9.4 %copy-start.6 = (bf16[8,128,256]{2,1,0:T(8,128)(2,1)S(1)}, bf16[8,128,256]{2,1,0:T(8,128)(2,1)}, u32[]{:S(2)}) copy-start(bf16[8,128,256]{2,1,0:T(8,128)(2,1)} %weight_ref.3) | copy-start | bytes 1572868
  22.7 9.4 %collective-permute-start.3 = (bf16[1,512,256]{2,1,0:T(8,128)(2,1)S(1)}, bf16[1,512,256]{2,1,0:T(8,128)(2,1)S(1)}, u32[]{:S(2)}, u32[]{:S(2)}) collective-permute-start(bf16[1,512,256]{2,1,0:T(8,128)(2,1)S(1)} %get-tuple-element.30), channel_id=1, source_target_pairs={{0,1},{1,2},{2,3},{3,4},{4,5},{5,6},{6,7},{7,0},{8,9},{9,10},{10,1... | collective-permute-start | bytes 786440 | tf_op jit(solution)/shard_map/ppermute | solution.py:584
  29.2 8.1 %collective-permute-start.4 = (bf16[4,1728,128]{2,1,0:T(8,128)(2,1)S(1)}, bf16[4,1728,128]{2,1,0:T(8,128)(2,1)S(1)}, u32[]{:S(2)}, u32[]{:S(2)}) collective-permute-start(bf16[4,1728,128]{2,1,0:T(8,128)(2,1)S(1)} %get-tuple-element.33), channel_id=1, source_target_pairs={{0,1},{1,0},{2,3},{3,2},{4,5},{5,4},{6,7},{7,6},{8,9},{9,8},{10,11... | collective-permute-start | bytes 5308424 | tf_op jit(solution)/shard_map/ppermute | solution.py:589
  35.7 1.5 %collective-permute-start.5 = (bf16[4,256,128]{2,1,0:T(8,128)(2,1)S(1)}, bf16[4,256,128]{2,1,0:T(8,128)(2,1)S(1)}, u32[]{:S(2)}, u32[]{:S(2)}) collective-permute-start(bf16[4,256,128]{2,1,0:T(8,128)(2,1)S(1)} %get-tuple-element.35), channel_id=1, source_target_pairs={{0,1},{1,0},{2,3},{3,2},{4,5},{5,4},{6,7},{7,6},{8,9},{9,8},{10,11... | collective-permute-start | bytes 786440 | tf_op jit(solution)/shard_map/ppermute | solution.py:590
  37.7 20.1 %collective-permute-start.6 = (bf16[4,336,128]{2,1,0:T(8,128)(2,1)S(1)}, bf16[4,336,128]{2,1,0:T(8,128)(2,1)S(1)}, u32[]{:S(2)}, u32[]{:S(2)}) collective-permute-start(bf16[4,336,128]{2,1,0:T(8,128)(2,1)S(1)} %get-tuple-element.37), channel_id=1, source_target_pairs={{0,2},{1,3},{2,0},{3,1},{4,6},{5,7},{6,4},{7,5},{8,10},{9,11},{10,... | collective-permute-start | bytes 1032200 | tf_op jit(solution)/shard_map/ppermute | solution.py:47
  40.2 17.6 %collective-permute-start.7 = (bf16[4,336,128]{2,1,0:T(8,128)(2,1)S(1)}, bf16[4,336,128]{2,1,0:T(8,128)(2,1)S(1)}, u32[]{:S(2)}, u32[]{:S(2)}) collective-permute-start(bf16[4,336,128]{2,1,0:T(8,128)(2,1)S(1)} %get-tuple-element.38), channel_id=1, source_target_pairs={{0,4},{1,5},{2,6},{3,7},{4,0},{5,1},{6,2},{7,3},{8,12},{9,13},{10,... | collective-permute-start | bytes 1032200 | tf_op jit(solution)/shard_map/ppermute | solution.py:47
  40.6 17.1 %collective-permute-start.8 = (bf16[4,336,128]{2,1,0:T(8,128)(2,1)S(1)}, bf16[4,336,128]{2,1,0:T(8,128)(2,1)S(1)}, u32[]{:S(2)}, u32[]{:S(2)}) collective-permute-start(bf16[4,336,128]{2,1,0:T(8,128)(2,1)S(1)} %get-tuple-element.39), channel_id=1, source_target_pairs={{0,6},{1,7},{2,4},{3,5},{4,2},{5,3},{6,0},{7,1},{8,14},{9,15},{10,... | collective-permute-start | bytes 1032200 | tf_op jit(solution)/shard_map/ppermute | solution.py:47
  41.7 8.8 %collective-permute-start.9 = (bf16[640,128]{1,0:T(8,128)(2,1)S(1)}, bf16[640,128]{1,0:T(8,128)(2,1)S(1)}, u32[]{:S(2)}, u32[]{:S(2)}) collective-permute-start(bf16[640,128]{1,0:T(8,128)(2,1)S(1)} %get-tuple-element.41), channel_id=1, source_target_pairs={{0,8},{8,0},{16,24},{24,16},{1,9},{9,1},{17,25},{25,17},{2,10},{10... | collective-permute-start | bytes 491528 | tf_op jit(solution)/shard_map/ppermute | solution.py:47
  43.3 12.0 %collective-permute-start.10 = (bf16[640,128]{1,0:T(8,128)(2,1)S(1)}, bf16[640,128]{1,0:T(8,128)(2,1)S(1)}, u32[]{:S(2)}, u32[]{:S(2)}) collective-permute-start(bf16[640,128]{1,0:T(8,128)(2,1)S(1)} %get-tuple-element.42), channel_id=1, source_target_pairs={{0,16},{8,24},{16,0},{24,8},{1,17},{9,25},{17,1},{25,9},{2,18},{10... | collective-permute-start | bytes 491528 | tf_op jit(solution)/shard_map/ppermute | solution.py:47
  50.5 7.2 %collective-permute-start.11 = (bf16[640,128]{1,0:T(8,128)(2,1)S(1)}, bf16[640,128]{1,0:T(8,128)(2,1)S(1)}, u32[]{:S(2)}, u32[]{:S(2)}) collective-permute-start(bf16[640,128]{1,0:T(8,128)(2,1)S(1)} %get-tuple-element.43), channel_id=1, source_target_pairs={{0,24},{8,16},{16,8},{24,0},{1,25},{9,17},{17,9},{25,1},{2,26},{10... | collective-permute-start | bytes 491528 | tf_op jit(solution)/shard_map/ppermute | solution.py:47
  58.0 7.6 %collective-permute-start.12 = (bf16[336,128]{1,0:T(8,128)(2,1)S(1)}, bf16[336,128]{1,0:T(8,128)(2,1)S(1)}, u32[]{:S(2)}, u32[]{:S(2)}) collective-permute-start(bf16[336,128]{1,0:T(8,128)(2,1)S(1)} %get-tuple-element.45), channel_id=1, source_target_pairs={{0,8},{8,0},{16,24},{24,16},{1,9},{9,1},{17,25},{25,17},{2,10},{10... | collective-permute-start | bytes 258056 | tf_op jit(solution)/shard_map/ppermute | solution.py:47
  61.0 11.3 %collective-permute-start.17 = (bf16[640,128]{1,0:T(8,128)(2,1)S(1)}, bf16[640,128]{1,0:T(8,128)(2,1)S(1)}, u32[]{:S(2)}, u32[]{:S(2)}) collective-permute-start(bf16[640,128]{1,0:T(8,128)(2,1)S(1)} %get-tuple-element.48.refs_4_), channel_id=1, source_target_pairs={{0,6},{1,7},{2,4},{3,5},{4,2},{5,3},{6,0},{7,1},{8,14},{9,15},{10,... | collective-permute-start | bytes 491528 | tf_op jit(solution)/shard_map/ppermute | solution.py:47
  62.6 9.8 %collective-permute-start.16 = (bf16[640,128]{1,0:T(8,128)(2,1)S(1)}, bf16[640,128]{1,0:T(8,128)(2,1)S(1)}, u32[]{:S(2)}, u32[]{:S(2)}) collective-permute-start(bf16[640,128]{1,0:T(8,128)(2,1)S(1)} %get-tuple-element.48.refs_4_), channel_id=1, source_target_pairs={{0,4},{1,5},{2,6},{3,7},{4,0},{5,1},{6,2},{7,3},{8,12},{9,13},{10,... | collective-permute-start | bytes 491528 | tf_op jit(solution)/shard_map/ppermute | solution.py:47
  64.2 8.2 %collective-permute-start.15 = (bf16[640,128]{1,0:T(8,128)(2,1)S(1)}, bf16[640,128]{1,0:T(8,128)(2,1)S(1)}, u32[]{:S(2)}, u32[]{:S(2)}) collective-permute-start(bf16[640,128]{1,0:T(8,128)(2,1)S(1)} %get-tuple-element.48.refs_4_), channel_id=1, source_target_pairs={{0,2},{1,3},{2,0},{3,1},{4,6},{5,7},{6,4},{7,5},{8,10},{9,11},{10,... | collective-permute-start | bytes 491528 | tf_op jit(solution)/shard_map/ppermute | solution.py:47
  64.5 7.8 %collective-permute-start.13 = (bf16[336,128]{1,0:T(8,128)(2,1)S(1)}, bf16[336,128]{1,0:T(8,128)(2,1)S(1)}, u32[]{:S(2)}, u32[]{:S(2)}) collective-permute-start(bf16[336,128]{1,0:T(8,128)(2,1)S(1)} %get-tuple-element.46), channel_id=1, source_target_pairs={{0,16},{8,24},{16,0},{24,8},{1,17},{9,25},{17,1},{25,9},{2,18},{10... | collective-permute-start | bytes 258056 | tf_op jit(solution)/shard_map/ppermute | solution.py:47
  65.6 6.7 %collective-permute-start.14 = (bf16[336,128]{1,0:T(8,128)(2,1)S(1)}, bf16[336,128]{1,0:T(8,128)(2,1)S(1)}, u32[]{:S(2)}, u32[]{:S(2)}) collective-permute-start(bf16[336,128]{1,0:T(8,128)(2,1)S(1)} %get-tuple-element.47), channel_id=1, source_target_pairs={{0,24},{8,16},{16,8},{24,0},{1,25},{9,17},{17,9},{25,1},{2,26},{10... | collective-permute-start | bytes 258056 | tf_op jit(solution)/shard_map/ppermute | solution.py:47
  72.5 5.5 %collective-permute-start.20 = (bf16[336,128]{1,0:T(8,128)(2,1)S(1)}, bf16[336,128]{1,0:T(8,128)(2,1)S(1)}, u32[]{:S(2)}, u32[]{:S(2)}) collective-permute-start(bf16[336,128]{1,0:T(8,128)(2,1)S(1)} %get-tuple-element.49.refs_0_), channel_id=1, source_target_pairs={{0,6},{1,7},{2,4},{3,5},{4,2},{5,3},{6,0},{7,1},{8,14},{9,15},{10,... | collective-permute-start | bytes 258056 | tf_op jit(solution)/shard_map/ppermute | solution.py:47
  74.3 4.6 %collective-permute-start.19 = (bf16[336,128]{1,0:T(8,128)(2,1)S(1)}, bf16[336,128]{1,0:T(8,128)(2,1)S(1)}, u32[]{:S(2)}, u32[]{:S(2)}) collective-permute-start(bf16[336,128]{1,0:T(8,128)(2,1)S(1)} %get-tuple-element.49.refs_0_), channel_id=1, source_target_pairs={{0,4},{1,5},{2,6},{3,7},{4,0},{5,1},{6,2},{7,3},{8,12},{9,13},{10,... | collective-permute-start | bytes 258056 | tf_op jit(solution)/shard_map/ppermute | solution.py:47
  75.8 4.5 %collective-permute-start.18 = (bf16[336,128]{1,0:T(8,128)(2,1)S(1)}, bf16[336,128]{1,0:T(8,128)(2,1)S(1)}, u32[]{:S(2)}, u32[]{:S(2)}) collective-permute-start(bf16[336,128]{1,0:T(8,128)(2,1)S(1)} %get-tuple-element.49.refs_0_), channel_id=1, source_target_pairs={{0,2},{1,3},{2,0},{3,1},{4,6},{5,7},{6,4},{7,5},{8,10},{9,11},{10,... | collective-permute-start | bytes 258056 | tf_op jit(solution)/shard_map/ppermute | solution.py:47
  76.1 4.2 %collective-permute-start.25 = (bf16[640,128]{1,0:T(8,128)(2,1)S(1)}, bf16[640,128]{1,0:T(8,128)(2,1)S(1)}, u32[]{:S(2)}, u32[]{:S(2)}) collective-permute-start(bf16[640,128]{1,0:T(8,128)(2,1)S(1)} %get-tuple-element.50.refs_8_), channel_id=1, source_target_pairs={{0,1},{1,0},{2,3},{3,2},{4,5},{5,4},{6,7},{7,6},{8,9},{9,8},{10,11... | collective-permute-start | bytes 491528 | tf_op jit(solution)/shard_map/ppermute | solution.py:600
  76.1 4.2 %collective-permute-start.21 = (bf16[336,128]{1,0:T(8,128)(2,1)S(1)}, bf16[336,128]{1,0:T(8,128)(2,1)S(1)}, u32[]{:S(2)}, u32[]{:S(2)}) collective-permute-start(bf16[336,128]{1,0:T(8,128)(2,1)S(1)} %get-tuple-element.49.refs_0_), channel_id=1, source_target_pairs={{0,1},{1,0},{2,3},{3,2},{4,5},{5,4},{6,7},{7,6},{8,9},{9,8},{10,11... | collective-permute-start | bytes 258056 | tf_op jit(solution)/shard_map/ppermute | solution.py:599
  78.0 2.3 %collective-permute-start.24 = (bf16[336,128]{1,0:T(8,128)(2,1)S(1)}, bf16[336,128]{1,0:T(8,128)(2,1)S(1)}, u32[]{:S(2)}, u32[]{:S(2)}) collective-permute-start(bf16[336,128]{1,0:T(8,128)(2,1)S(1)} %collective-permute-done.20.refs_3_), channel_id=1, source_target_pairs={{0,1},{1,0},{2,3},{3,2},{4,5},{5,4},{6,7},{7,6},{8,9},{9,8},{10,11... | collective-permute-start | bytes 258056 | tf_op jit(solution)/shard_map/ppermute | solution.py:599
  78.9 1.4 %collective-permute-start.23 = (bf16[336,128]{1,0:T(8,128)(2,1)S(1)}, bf16[336,128]{1,0:T(8,128)(2,1)S(1)}, u32[]{:S(2)}, u32[]{:S(2)}) collective-permute-start(bf16[336,128]{1,0:T(8,128)(2,1)S(1)} %collective-permute-done.19.refs_2_), channel_id=1, source_target_pairs={{0,1},{1,0},{2,3},{3,2},{4,5},{5,4},{6,7},{7,6},{8,9},{9,8},{10,11... | collective-permute-start | bytes 258056 | tf_op jit(solution)/shard_map/ppermute | solution.py:599
  80.2 1.3 %collective-permute-start.22 = (bf16[336,128]{1,0:T(8,128)(2,1)S(1)}, bf16[336,128]{1,0:T(8,128)(2,1)S(1)}, u32[]{:S(2)}, u32[]{:S(2)}) collective-permute-start(bf16[336,128]{1,0:T(8,128)(2,1)S(1)} %collective-permute-done.18.refs_1_), channel_id=1, source_target_pairs={{0,1},{1,0},{2,3},{3,2},{4,5},{5,4},{6,7},{7,6},{8,9},{9,8},{10,11... | collective-permute-start | bytes 258056 | tf_op jit(solution)/shard_map/ppermute | solution.py:599

commit v3 on v2

--- a/solution.py
+++ b/solution.py
@@ -37,14 +37,8 @@
     return (index - step) % count if isinstance(index, int) else lax.rem(index + count - step, count)
 
 
-def exchange(value, axis, step, stride):
-    count = lax.axis_size(axis) // stride
-    pairs = []
-    for index in range(lax.axis_size(axis)):
-        high, low = divmod(index, stride)
-        other = high ^ step if count & (count - 1) == 0 else (high + step) % count
-        pairs.append((index, other * stride + low))
-    return lax.ppermute(value, axis, pairs)
+def partner(index, step, count):
+    return index ^ step if count & (count - 1) == 0 else (index + step) % count
 
 
 def started(source, target, sem):
@@ -250,12 +244,11 @@
 
 def filter_kernel(
     shard_rows, links_ref, own_ref, low_ref, high_ref, pre_ref,
-    keep_ref, send_ref, own_wide, low_wide, high_wide, win_ref, act_ref,
+    early_ref, late_ref, own_wide, low_wide, high_wide, win_ref, act_ref,
 ):
     slots, voxels, channels = own_ref.shape
     slab = slots * PLANE
     rows = BE * slab
-    lanes = channels // 2
     for ref, wide in ((own_ref, own_wide), (low_ref, low_wide), (high_ref, high_wide)):
         extend(ref, wide)
 
@@ -267,8 +260,8 @@
         block = jnp.maximum(jnp.concatenate(parts, axis=0).astype(F32), 0.0)
         act_ref[:, pair * 2 * slab : (pair + 1) * 2 * slab] = block.T.astype(BF16)
 
-    first = lax.rem(lax.axis_index("dom"), 2) == 0
     unit = math.gcd(channels, shard_rows)
+    cut = early_ref.shape[1]
 
     def product(tap):
         offset = (2 - tap // 9) * slab
@@ -278,14 +271,13 @@
             win_ref[offset : offset + rows, column : column + channels],
             preferred_element_type=F32,
         )
-        left, right = total[:, :lanes], total[:, lanes:]
-        keep = jnp.where(first, left, right).astype(BF16)
-        send = jnp.where(first, right, left).astype(BF16)
+        total = total.astype(BF16)
         for part in range(channels // unit):
             shard, start = divmod(tap * channels + part * unit, shard_rows)
-            span = slice(part * unit, (part + 1) * unit)
-            keep_ref[shard, start : start + unit, :] = keep[span]
-            send_ref[shard, start : start + unit, :] = send[span]
+            ref = early_ref
+            if start >= cut:
+                ref, start = late_ref, start - cut
+            ref[shard, start : start + unit, :] = total[part * unit : (part + 1) * unit]
 
     def products(group):
         taps = [tap for tap in range(27) if column_of(tap) // 3 == group]
@@ -300,14 +292,15 @@
         call()
 
 
-def filter_gradient(shards, links, own, low, high, pre):
+def filter_gradient(shards, cut, links, own, low, high, pre):
     slots, voxels, channels = own.shape
     shard_rows = 27 * channels // shards
     rows = slots * voxels
-    out = jax.ShapeDtypeStruct((shards, shard_rows, channels // 2), BF16)
+    early = jax.ShapeDtypeStruct((shards, cut, channels), BF16)
+    late = jax.ShapeDtypeStruct((shards, shard_rows - cut, channels), BF16)
     return pl.pallas_call(
         functools.partial(filter_kernel, shard_rows),
-        out_shape=(out, out),
+        out_shape=(early, late),
         in_specs=[SMEM, VMEM, VMEM, VMEM, VMEM],
         out_specs=(VMEM, VMEM),
         scratch_shapes=wide_scratch(own, low) + [pltpu.VMEM((channels, rows), BF16)],
@@ -321,7 +314,7 @@
 
 def fine_kernel(
     groups, upper_ref, stay_ref, lower_ref, weight_ref, act_ref,
-    grad_ref, keep_ref, send_ref, acc_ref,
+    grad_ref, down_ref, acc_ref,
 ):
     step = pl.program_id(0)
     fine, voxels, fine_channels = act_ref.shape
@@ -363,15 +356,10 @@
 
     @pl.when(step == pl.num_programs(0) - 1)
     def _():
-        total = acc_ref[...].T
-        first = lax.rem(lax.axis_index("dom"), 2) == 0
-        lanes = channels // 2
-        shards = keep_ref.shape[0]
+        total = acc_ref[...].T.astype(BF16)
+        shards = down_ref.shape[0]
         rows = total.shape[0] // shards
-        left = total[:, :lanes].reshape(shards, rows, lanes)
-        right = total[:, lanes:].reshape(shards, rows, lanes)
-        keep_ref[:, :rows, :] = jnp.where(first, left, right).astype(BF16)
-        send_ref[:, :rows, :] = jnp.where(first, right, left).astype(BF16)
+        down_ref[:, :rows, :] = total.reshape(shards, rows, channels)
 
 
 def fine_gradient(shards, count, from_upper, stay, from_lower, weight, fine_act):
@@ -380,19 +368,19 @@
     taps = weight.shape[0]
     whole = pl.BlockSpec((1, voxels, channels), lambda i: (i % groups, 0, 0))
     rows = count * piece_rows(taps * fine_channels // shards, count)
-    down = jax.ShapeDtypeStruct((shards, rows, channels // 2), BF16)
+    down = jax.ShapeDtypeStruct((shards, rows, channels), BF16)
     same = pl.BlockSpec(down.shape, lambda i: (0, 0, 0))
     block = pl.BlockSpec((8, voxels, fine_channels), lambda i: (i, 0, 0))
     return pl.pallas_call(
         functools.partial(fine_kernel, groups),
         grid=(3 * groups,),
-        out_shape=(jax.ShapeDtypeStruct(fine_act.shape, BF16), down, down),
+        out_shape=(jax.ShapeDtypeStruct(fine_act.shape, BF16), down),
         in_specs=[
             whole, whole, whole,
             pl.BlockSpec(weight.shape, lambda i: (0, 0, 0)),
             block,
         ],
-        out_specs=(block, same, same),
+        out_specs=(block, same),
         scratch_shapes=[pltpu.VMEM((channels, taps * fine_channels), F32)],
         compiler_params=params(40),
         cost_estimate=pl.CostEstimate(
@@ -425,67 +413,81 @@
     return [jax.ShapeDtypeStruct(shape, F32 if step == 0 else BF16) for step in range(count)]
 
 
-def pair_kernel(count, conv_ref, conv_got_ref, down_ref, down_got_ref, *outs):
+def parity():
+    return lax.rem(lax.axis_index("dom"), 2)
+
+
+def pair_kernel(count, early, down, late, *outs):
     planes, slabs = outs[:count], outs[count:]
-    shards, rows, _ = conv_ref.shape
-    down_piece = down_ref.shape[1] // count
-    piece = planes[0].shape[1] - down_piece
-    cut = count * piece
-    for step, ref in enumerate(slabs):
-        shard = relative(lax.axis_index("dp"), step, shards)
-        total = conv_ref[shard, cut:, :].astype(F32) + conv_got_ref[shard, cut:, :].astype(F32)
-        ref[...] = total.astype(ref.dtype)
-    high = lax.axis_index("dom") // 2
-    for step, ref in enumerate(planes):
-        place = relative(high, step, count)
-        for keep_ref, got_ref, size, start in (
-            (conv_ref, conv_got_ref, piece, 0),
-            (down_ref, down_got_ref, down_piece, piece),
-        ):
-            span = pl.ds(pl.multiple_of(place * size, 16), size)
-            total = keep_ref[:, span, :].astype(F32) + got_ref[:, span, :].astype(F32)
-            ref[:, start : start + size, :] = total.astype(ref.dtype)
-
-
-def pair_sum(count, conv, conv_got, down, down_got):
-    shards, rows, lanes = conv.shape
-    down_piece = down.shape[1] // count
-    unit = 16 * count
-    piece = 16 * round((2 * (rows + down.shape[1]) / 3 - down.shape[1]) / unit)
-    outs = shapes_of(count, (shards, piece + down_piece, lanes))
-    outs += shapes_of(shards, (rows - count * piece, lanes))
+    shards, cut, _ = early[0].shape
+    piece = cut // count
+    down_piece = down[0].shape[1] // count
+
+    @pl.when(parity() == 0)
+    def _():
+        high = lax.axis_index("dom") // 2
+        for step, ref in enumerate(planes):
+            place = relative(high, step, count)
+            for refs, size, start in ((early, piece, 0), (down, down_piece, piece)):
+                span = pl.ds(pl.multiple_of(place * size, 16), size)
+                total = refs[0][:, span, :].astype(F32) + refs[1][:, span, :].astype(F32)
+                ref[:, start : start + size, :] = total.astype(ref.dtype)
+
+    @pl.when(parity() == 1)
+    def _():
+        for step, ref in enumerate(slabs):
+            shard = relative(lax.axis_index("dp"), step, shards)
+            total = late[0][shard].astype(F32) + late[1][shard].astype(F32)
+            ref[...] = total.astype(ref.dtype)
+
+
+def pair_sum(count, early, down, late):
+    shards, cut, channels = early[0].shape
+    outs = shapes_of(count, (shards, (cut + down[0].shape[1]) // count, channels))
+    outs += shapes_of(shards, late[0].shape[1:])
+    parts = [*early, *down, *late]
+
+    def kernel(*refs):
+        pair_kernel(count, refs[:2], refs[2:4], refs[4:6], *refs[6:])
+
     outs = pl.pallas_call(
-        functools.partial(pair_kernel, count),
+        kernel,
         out_shape=outs,
-        in_specs=[VMEM] * 4,
+        in_specs=[VMEM] * 6,
         out_specs=[VMEM] * len(outs),
-        compiler_params=params(32),
-        cost_estimate=cost(conv, conv_got, *outs),
+        compiler_params=params(24),
+        cost_estimate=cost(*parts, *outs),
         name="pair_sum",
-    )(conv, conv_got, down, down_got)
-    return outs[:count], outs[count:], (piece, down_piece)
+    )(*parts)
+    return outs[:count], outs[count:]
 
 
 def middle_kernel(count, shards, *refs):
     planes, slabs = refs[:count], refs[count : count + shards]
     to_slabs, mine_ref = refs[count + shards : -1], refs[-1]
-    mine_ref[...] = tree([part[...].astype(F32) for part in slabs]).astype(BF16)
-    for step, ref in enumerate(to_slabs):
-        shard = relative(lax.axis_index("dp"), step, shards)
-        ref[...] = tree([part[shard].astype(F32) for part in planes]).astype(ref.dtype)
+
+    @pl.when(parity() == 0)
+    def _():
+        for step, ref in enumerate(to_slabs):
+            shard = relative(lax.axis_index("dp"), step, shards)
+            ref[...] = tree([part[shard].astype(F32) for part in planes]).astype(ref.dtype)
+
+    @pl.when(parity() == 1)
+    def _():
+        mine_ref[...] = tree([part[...].astype(F32) for part in slabs]).astype(BF16)
 
 
 def middle_sum(planes, slabs):
     count, shards = len(planes), len(slabs)
-    _, piece, lanes = planes[0].shape
-    outs = shapes_of(shards, (piece, lanes)) + [jax.ShapeDtypeStruct(slabs[0].shape, BF16)]
+    outs = shapes_of(shards, planes[0].shape[1:])
+    outs += [jax.ShapeDtypeStruct(slabs[0].shape, BF16)]
     parts = [*planes, *slabs]
     outs = pl.pallas_call(
         functools.partial(middle_kernel, count, shards),
         out_shape=outs,
         in_specs=[VMEM] * len(parts),
         out_specs=[VMEM] * len(outs),
-        compiler_params=params(32),
+        compiler_params=params(24),
         cost_estimate=cost(*parts, *outs),
         name="middle_sum",
     )(*parts)
@@ -493,11 +495,13 @@
 
 
 def last_kernel(factor, shards, *refs):
-    planes_ref, slabs_ref = refs[-2:]
-    total = tree([part[...].astype(F32) for part in refs[:shards]])
-    planes_ref[...] = (total * factor).astype(BF16)
-    total = tree([part[...].astype(F32) for part in refs[shards:-2]])
-    slabs_ref[...] = (total * factor).astype(BF16)
+    slabs, planes = refs[:shards], refs[shards:-2]
+    for side, group, ref in ((0, slabs, refs[-2]), (1, planes, refs[-1])):
+
+        @pl.when(parity() == side)
+        def _():
+            total = tree([part[...].astype(F32) for part in group])
+            ref[...] = (total * factor).astype(BF16)
 
 
 def last_sum(factor, slabs, planes):
@@ -509,7 +513,7 @@
         ],
         in_specs=[VMEM] * len(parts),
         out_specs=[VMEM] * 2,
-        compiler_params=params(32),
+        compiler_params=params(24),
         cost_estimate=cost(*parts),
         name="last_sum",
     )(*parts)
@@ -517,38 +521,35 @@
 
 def gather_kernel(count, piece, down_piece, *refs):
     near, far = refs[:count], refs[count : 2 * count]
-    rest_ref, rest_far_ref, conv_ref, down_ref, conv_whole, down_whole = refs[2 * count :]
-    lanes = rest_ref.shape[1]
-    cut = count * piece
+    rest_ref, rest_far_ref, conv_ref, down_ref, down_whole = refs[2 * count :]
     high = lax.axis_index("dom") // 2
-    low = lax.rem(lax.axis_index("dom"), 2)
-    for side, group, rest in ((low, near, rest_ref), (1 - low, far, rest_far_ref)):
-        lane = pl.ds(pl.multiple_of(side * lanes, lanes), lanes)
-        for step, ref in enumerate(group):
-            place = source_of(high, step, count)
-            row = pl.multiple_of(place * piece, 16)
-            conv_whole[pl.ds(row, piece), lane] = ref[:piece, :].astype(F32)
-            row = pl.multiple_of(place * down_piece, 16)
-            down_whole[pl.ds(row, down_piece), lane] = ref[piece:, :].astype(F32)
-        conv_whole[cut:, lane] = rest[...].astype(F32)
-    conv_ref[...] = conv_whole[...]
+    for side, group, rest in ((0, near, rest_far_ref), (1, far, rest_ref)):
+
+        @pl.when(parity() == side)
+        def _():
+            for step, ref in enumerate(group):
+                place = source_of(high, step, count)
+                row = pl.multiple_of(place * piece, 16)
+                conv_ref[pl.ds(row, piece), :] = ref[:piece, :].astype(F32)
+                row = pl.multiple_of(place * down_piece, 16)
+                down_whole[pl.ds(row, down_piece), :] = ref[piece:, :].astype(F32)
+            conv_ref[count * piece :, :] = rest[...].astype(F32)
+
     down_ref[...] = down_whole[: down_ref.shape[0]]
 
 
-def gather_up(conv_rows, down_rows, pieces, near, far, rest, rest_far):
+def gather_up(conv_rows, down_rows, piece, near, far, rest, rest_far):
     count = len(near)
-    lanes = rest.shape[1]
-    outs = [jax.ShapeDtypeStruct((rows, 2 * lanes), F32) for rows in (conv_rows, down_rows)]
+    channels = rest.shape[1]
+    down_piece = near[0].shape[0] - piece
+    outs = [jax.ShapeDtypeStruct((rows, channels), F32) for rows in (conv_rows, down_rows)]
     return pl.pallas_call(
-        functools.partial(gather_kernel, count, *pieces),
+        functools.partial(gather_kernel, count, piece, down_piece),
         out_shape=outs,
         in_specs=[VMEM] * (2 * count + 2),
         out_specs=[VMEM] * 2,
-        scratch_shapes=[
-            pltpu.VMEM((conv_rows, 2 * lanes), F32),
-            pltpu.VMEM((count * pieces[1], 2 * lanes), F32),
-        ],
-        compiler_params=params(32),
+        scratch_shapes=[pltpu.VMEM((count * down_piece, channels), F32)],
+        compiler_params=params(24),
         cost_estimate=cost(*near, *far, *outs),
         name="gather_up",
     )(*near, *far, rest, rest_far)
@@ -568,12 +569,29 @@
     forward = [(i, i + 1) for i in range(devices - 1)]
     backward = [(i + 1, i) for i in range(devices - 1)]
     ring = [(i, (i + 1) % devices) for i in range(devices)]
-    swap = [(i, i ^ 1) for i in range(devices)]
-
-    def spread_out(parts, axis, stride):
-        return [parts[0]] + [
-            exchange(parts[step], axis, step, stride) for step in range(1, len(parts))
-        ]
+
+    to_even = [(i + 1, i) for i in range(0, devices, 2)]
+    to_odd = [(i, i + 1) for i in range(0, devices, 2)]
+
+    def over_plane(parts, side):
+        moved = [parts[0]]
+        for step in range(1, count):
+            pairs = [
+                (2 * high + side, 2 * partner(high, step, count) + side) for high in range(count)
+            ]
+            moved.append(lax.ppermute(parts[step], "dom", pairs))
+        return moved
+
+    def over_shards(parts, side):
+        moved = [parts[0]]
+        for step in range(1, shards):
+            pairs = [
+                (shard * devices + index, partner(shard, step, shards) * devices + index)
+                for shard in range(shards)
+                for index in range(side, devices, 2)
+            ]
+            moved.append(lax.ppermute(parts[step], ("dp", "dom"), pairs))
+        return moved
 
     low = lax.ppermute(own[:, voxels - PLANE :], "dom", forward)
     high = lax.ppermute(own[:, :PLANE], "dom", backward)
@@ -582,25 +600,27 @@
     )
     from_upper = lax.ppermute(to_lower, "dom", [(b, a) for a, b in ring])
     from_lower = lax.ppermute(to_upper, "dom", ring)
-    conv_keep, conv_send = filter_gradient(shards, links, own, low, high, pre)
-    fine_grad, down_keep, down_send = fine_gradient(
+    conv_rows = 27 * channels // shards
+    down_rows = down_weight.shape[0] * down_weight.shape[1] // shards
+    piece = 16 * round((2 * (conv_rows + down_rows) / 3 - down_rows) / (16 * count))
+    early, late = filter_gradient(shards, count * piece, links, own, low, high, pre)
+    fine_grad, down = fine_gradient(
         shards, count, from_upper, stay, from_lower, down_weight, fine_act[0]
     )
-    conv_got = lax.ppermute(conv_send, "dom", swap)
-    down_got = lax.ppermute(down_send, "dom", swap)
-
-    planes, slabs, pieces = pair_sum(count, conv_keep, conv_got, down_keep, down_got)
-    slabs = spread_out(slabs, "dp", 1)
-    planes = spread_out(planes, "dom", 2)
+    early = (early, lax.ppermute(early, "dom", to_even))
+    late = (late, lax.ppermute(late, "dom", to_odd))
+    down = (down, lax.ppermute(down, "dom", to_even))
+
+    planes, slabs = pair_sum(count, early, down, late)
+    slabs = over_shards(slabs, 1)
+    planes = over_plane(planes, 0)
     to_slabs, rest = middle_sum(planes, slabs)
-    to_slabs = spread_out(to_slabs, "dp", 1)
-    mine, rest = last_sum(factor, to_slabs, spread_out([rest] * count, "dom", 2))
-    near = spread_out([mine] * count, "dom", 2)
-    far = [lax.ppermute(value, "dom", swap) for value in near]
-    rest_far = lax.ppermute(rest, "dom", swap)
-    conv_rows = 27 * channels // shards
-    down_rows = down_weight.shape[0] * down_weight.shape[1] // shards
-    conv_grad, down_grad = gather_up(conv_rows, down_rows, pieces, near, far, rest, rest_far)
+    to_slabs = over_shards(to_slabs, 0)
+    mine, rest = last_sum(factor, to_slabs, over_plane([rest] * count, 1))
+    near = over_plane([mine] * count, 0)
+    far = [lax.ppermute(value, "dom", to_odd) for value in near]
+    rest_far = lax.ppermute(rest, "dom", to_even)
+    conv_grad, down_grad = gather_up(conv_rows, down_rows, piece, near, far, rest, rest_far)
     return (fine_grad[None], conv_grad, down_grad)
 
 

time: 83.5 us -> 108 us (1.29)
  starting transfers between devices: 33.8 us -> 57.1 us
    ppermute x22 -> x23, starting transfers between devices: 26.1 us -> 49.3 us  [the longest x9 21.7 us: over_plane(): moved.append(lax.ppermute(parts[step], 'dom', pairs))]
    ppermute x22 -> x23, waiting for transfers between devices: 21 us -> 22.8 us  [the longest x9 12.8 us: over_plane(): moved.append(lax.ppermute(parts[step], 'dom', pairs))]
    unnamed x16 -> x14, local copies, waits for them, and re-layouts: 5.65 us -> 5.64 us
  transfers between devices with their start and end apart: 26 -> 27, of which waited for: 10 -> 6; matrix products, arithmetic and copies ran while one was open for 2% -> 1% of each run, Pallas kernels for 12% -> 9%
where the time goes in v3:
time: 108 us
  starting transfers between devices  57.1 us (53%)
  waiting for transfers between devices  22.8 us (21%)
  Pallas kernels  20.1 us (19%)
  local copies, waits for them, and re-layouts  6.6 us (6%)
    ppermute x9, starting transfers between devices, over_plane(): moved.append(lax.ppermute(parts[step], 'dom', pairs))  21.7 us
    ppermute x9, waiting for transfers between devices, over_plane(): moved.append(lax.ppermute(parts[step], 'dom', pairs))  12.8 us
    ppermute x6, starting transfers between devices, over_shards(): moved.append(lax.ppermute(parts[step], ('dp', 'dom'), pairs))  12.7 us
    pallas_call x1, Pallas kernels, input_gradient(): pl.pallas_call(input_kernel, out_shape=(out, out, out), in_specs=[SMEM, S...  7.65 us
    ppermute x4, starting transfers between devices, body(): far = [lax.ppermute(value, 'dom', to_odd) for value in near]  6.96 us
    pallas_call x1, Pallas kernels, filter_gradient(): pl.pallas_call(functools.partial(filter_kernel, shard_rows), out_shape=(e...  6.42 us
    ppermute x6, waiting for transfers between devices, over_shards(): moved.append(lax.ppermute(parts[step], ('dp', 'dom'), pairs))  6.4 us
    unnamed x14, local copies, waits for them, and re-layouts  5.64 us
  transfers between devices with their start and end apart: 27, of which 6 were waited for; matrix products, arithmetic and copies ran while one was open for 1% of the time, Pallas kernels for 9%

profile of v3, /device:TPU:0, one launch (start us, length us, event | category | flops | bytes accessed | tf_op | source)
XLA Modules:
  0.0 107.6 jit_solution(12532959397407636434)
XLA Ops:
  0.6 1.0 fusion
  1.6 1.3 %collective-permute-start.1 = (bf16[3,64,256]{2,1,0:T(8,128)(2,1)S(1)}, bf16[3,64,256]{2,1,0:T(8,128)(2,1)S(1)}, u32[]{:S(2)}, u32[]{:S(2)}) collective-permute-start(bf16[3,64,256]{2,1,0:T(8,128)(2,1)S(1)} %get-tuple-element.51), channel_id=1, source_target_pairs={{1,0},{2,1},{3,2},{4,3},{5,4},{6,5},{7,6},{9,8},{10,9},{11,10},{12... | collective-permute-start | bytes 294920 | tf_op jit(solution)/shard_map/ppermute | solution.py:597
  2.9 3.0 %collective-permute-start = (bf16[3,64,256]{2,1,0:T(8,128)(2,1)S(1)}, bf16[3,64,256]{2,1,0:T(8,128)(2,1)S(1)}, u32[]{:S(2)}, u32[]{:S(2)}) collective-permute-start(bf16[3,64,256]{2,1,0:T(8,128)(2,1)S(1)} %get-tuple-element.52), channel_id=1, source_target_pairs={{0,1},{1,2},{2,3},{3,4},{4,5},{5,6},{6,7},{8,9},{9,10},{10,11},{11... | collective-permute-start | bytes 294920 | tf_op jit(solution)/shard_map/ppermute | solution.py:596
  5.9 0.7 copy.15
  6.6 0.7 copy.14
  7.3 0.0 collective-permute-done.1.high_ref
  7.3 0.0 collective-permute-done.low_ref
  7.3 1.1 %copy-done = bf16[1,3,512,256]{3,2,1,0:T(8,128)(2,1)S(1)} copy-done((bf16[1,3,512,256]{3,2,1,0:T(8,128)(2,1)S(1)}, bf16[1,3,512,256]{3,2,1,0:T(8,128)(2,1)}, u32[]{:S(2)}) %copy-start) | copy-done | bytes 786456
  8.4 2.0 %copy-done.2 = bf16[27,256,256]{2,1,0:T(8,128)(2,1)S(1)} copy-done((bf16[27,256,256]{2,1,0:T(8,128)(2,1)S(1)}, bf16[27,256,256]{2,1,0:T(8,128)(2,1)}, u32[]{:S(2)}) %copy-start.2) | copy-done | bytes 3538968
  10.4 1.1 %copy-done.4 = bf16[1,3,512,256]{3,2,1,0:T(8,128)(2,1)S(1)} copy-done((bf16[1,3,512,256]{3,2,1,0:T(8,128)(2,1)S(1)}, bf16[1,3,512,256]{3,2,1,0:T(8,128)(2,1)}, u32[]{:S(2)}) %copy-start.4) | copy-done | bytes 786456
  11.6 7.6 %input_gradient.1 = (bf16[1,512,256]{2,1,0:T(8,128)(2,1)S(1)}, bf16[1,512,256]{2,1,0:T(8,128)(2,1)S(1)}, bf16[1,512,256]{2,1,0:T(8,128)(2,1)S(1)}) custom-call(s32[3,27]{1,0:T(4,128)S(1)} %bitcast.13, s32[3,8]{1,0:T(4,128)S(1)} %bitcast.15, bf16[3,512,256]{2,1,0:T(8,128)(2,1)S(1)} %bitcast.11, bf16[3,64,256]{2,1,0:T(8,128)(2,1)S(1)} %collective-permute-done.low_ref, ...), custom_call_target="tpu_custom_call" | custom-call | flops 5435817984 | bytes 8388608 | tf_op jit(solution)/shard_map/input_gradient/pallas_call | solution.py:224
  19.2 3.5 %collective-permute-start.2 = (bf16[1,512,256]{2,1,0:T(8,128)(2,1)S(1)}, bf16[1,512,256]{2,1,0:T(8,128)(2,1)S(1)}, u32[]{:S(2)}, u32[]{:S(2)}) collective-permute-start(bf16[1,512,256]{2,1,0:T(8,128)(2,1)S(1)} %get-tuple-element.27), channel_id=1, source_target_pairs={{1,0},{2,1},{3,2},{4,3},{5,4},{6,5},{7,6},{0,7},{9,8},{10,9},{11,1... | collective-permute-start | bytes 786440 | tf_op jit(solution)/shard_map/ppermute | solution.py:601
  22.7 0.0 collective-permute-start.3
  22.7 6.4 %filter_gradient.1 = (bf16[4,1088,256]{2,1,0:T(8,128)(2,1)S(1)}, bf16[4,640,256]{2,1,0:T(8,128)(2,1)S(1)}) custom-call(s32[3,27]{1,0:T(4,128)S(1)} %bitcast.14, bf16[3,512,256]{2,1,0:T(8,128)(2,1)S(1)} %bitcast.12, bf16[3,64,256]{2,1,0:T(8,128)(2,1)S(1)} %collective-permute-done.low_ref, bf16[3,64,256]{2,1,0:T(8,128)(2,1)S(1)} %collective-permute-done.1.high_ref, ...), custom_call_target="tpu_custom_call" | custom-call | flops 5435817984 | bytes 8388608 | tf_op jit(solution)/shard_map/filter_gradient/pallas_call | solution.py:301
  29.1 3.9 %collective-permute-start.6 = (bf16[4,640,256]{2,1,0:T(8,128)(2,1)S(1)}, bf16[4,640,256]{2,1,0:T(8,128)(2,1)S(1)}, u32[]{:S(2)}, u32[]{:S(2)}) collective-permute-start(bf16[4,640,256]{2,1,0:T(8,128)(2,1)S(1)} %get-tuple-element.33.refs_4_), channel_id=1, source_target_pairs={{0,1},{2,3},{4,5},{6,7},{8,9},{10,11},{12,13},{14,15},{16,17},{18,... | collective-permute-start | bytes 3932168 | tf_op jit(solution)/shard_map/ppermute | solution.py:611
  33.0 1.5 %collective-permute-start.4 = (bf16[4,1088,256]{2,1,0:T(8,128)(2,1)S(1)}, bf16[4,1088,256]{2,1,0:T(8,128)(2,1)S(1)}, u32[]{:S(2)}, u32[]{:S(2)}) collective-permute-start(bf16[4,1088,256]{2,1,0:T(8,128)(2,1)S(1)} %get-tuple-element.31.refs_0_), channel_id=1, source_target_pairs={{1,0},{3,2},{5,4},{7,6},{9,8},{11,10},{13,12},{15,14},{17,16},{19,... | collective-permute-start | bytes 6684680 | tf_op jit(solution)/shard_map/ppermute | solution.py:610
  34.5 0.0 collective-permute-done.2.upper_ref
  34.5 0.0 collective-permute-done.3.lower_ref
  34.5 3.6 %fine_gradient.1 = (bf16[24,512,128]{2,1,0:T(8,128)(2,1)}, bf16[4,256,256]{2,1,0:T(8,128)(2,1)S(1)}) custom-call(bf16[1,512,256]{2,1,0:T(8,128)(2,1)S(1)} %collective-permute-done.2.upper_ref, bf16[1,512,256]{2,1,0:T(8,128)(2,1)S(1)} %get-tuple-element.28.stay_ref, bf16[1,512,256]{2,1,0:T(8,128)(2,1)S(1)} %collective-permute-done.3.lower_ref, ...), custom_call_target="tpu_custom_call" | custom-call | flops 25769803776 | bytes 8388608 | tf_op jit(solution)/shard_map/fine_gradient/pallas_call | solution.py:374
  38.1 1.3 %collective-permute-start.5 = (bf16[4,256,256]{2,1,0:T(8,128)(2,1)S(1)}, bf16[4,256,256]{2,1,0:T(8,128)(2,1)S(1)}, u32[]{:S(2)}, u32[]{:S(2)}) collective-permute-start(bf16[4,256,256]{2,1,0:T(8,128)(2,1)S(1)} %get-tuple-element.32.refs_2_), channel_id=1, source_target_pairs={{1,0},{3,2},{5,4},{7,6},{9,8},{11,10},{13,12},{15,14},{17,16},{19,... | collective-permute-start | bytes 1572872 | tf_op jit(solution)/shard_map/ppermute | solution.py:612
  39.4 2.6 %collective-permute-done.5.refs_3_ = bf16[4,256,256]{2,1,0:T(8,128)(2,1)S(1)} collective-permute-done((bf16[4,256,256]{2,1,0:T(8,128)(2,1)S(1)}, bf16[4,256,256]{2,1,0:T(8,128)(2,1)S(1)}, u32[]{:S(2)}, u32[]{:S(2)}) %collective-permute-start.5) | collective-permute-done | bytes 524320 | tf_op jit(solution)/shard_map/ppermute | solution.py:612
  42.0 0.0 collective-permute-done.6.refs_5_
  42.0 0.0 collective-permute-done.4.refs_1_
  42.0 0.6 pair_sum.1
  42.6 5.2 %collective-permute-start.7 = (bf16[4,336,256]{2,1,0:T(8,128)(2,1)S(1)}, bf16[4,336,256]{2,1,0:T(8,128)(2,1)S(1)}, u32[]{:S(2)}, u32[]{:S(2)}) collective-permute-start(bf16[4,336,256]{2,1,0:T(8,128)(2,1)S(1)} %get-tuple-element.35), channel_id=1, source_target_pairs={{0,2},{2,0},{4,6},{6,4},{8,10},{10,8},{12,14},{14,12},{16,18},{18,... | collective-permute-start | bytes 2064392 | tf_op jit(solution)/shard_map/ppermute | solution.py:582
  47.8 1.9 %collective-permute-start.8 = (bf16[4,336,256]{2,1,0:T(8,128)(2,1)S(1)}, bf16[4,336,256]{2,1,0:T(8,128)(2,1)S(1)}, u32[]{:S(2)}, u32[]{:S(2)}) collective-permute-start(bf16[4,336,256]{2,1,0:T(8,128)(2,1)S(1)} %get-tuple-element.36), channel_id=1, source_target_pairs={{0,4},{2,6},{4,0},{6,2},{8,12},{10,14},{12,8},{14,10},{16,20},{18,... | collective-permute-start | bytes 2064392 | tf_op jit(solution)/shard_map/ppermute | solution.py:582
  49.7 3.4 %collective-permute-start.9 = (bf16[4,336,256]{2,1,0:T(8,128)(2,1)S(1)}, bf16[4,336,256]{2,1,0:T(8,128)(2,1)S(1)}, u32[]{:S(2)}, u32[]{:S(2)}) collective-permute-start(bf16[4,336,256]{2,1,0:T(8,128)(2,1)S(1)} %get-tuple-element.37), channel_id=1, source_target_pairs={{0,6},{2,4},{4,2},{6,0},{8,14},{10,12},{12,10},{14,8},{16,22},{18,... | collective-permute-start | bytes 2064392 | tf_op jit(solution)/shard_map/ppermute | solution.py:582
  53.1 0.7 collective-permute-start.10
  53.8 0.7 collective-permute-start.11
  54.5 0.0 collective-permute-done.10.refs_5_
  54.5 0.7 collective-permute-start.12
  55.2 0.0 collective-permute-done.11.refs_6_
  55.2 0.0 collective-permute-done.12.refs_7_
  55.2 1.5 %collective-permute-done.7.refs_1_ = bf16[4,336,256]{2,1,0:T(8,128)(2,1)S(1)} collective-permute-done((bf16[4,336,256]{2,1,0:T(8,128)(2,1)S(1)}, bf16[4,336,256]{2,1,0:T(8,128)(2,1)S(1)}, u32[]{:S(2)}, u32[]{:S(2)}) %collective-permute-start.7) | collective-permute-done | bytes 688160 | tf_op jit(solution)/shard_map/ppermute | solution.py:582
  56.7 11.3 %collective-permute-done.8.refs_2_ = bf16[4,336,256]{2,1,0:T(8,128)(2,1)S(1)} collective-permute-done((bf16[4,336,256]{2,1,0:T(8,128)(2,1)S(1)}, bf16[4,336,256]{2,1,0:T(8,128)(2,1)S(1)}, u32[]{:S(2)}, u32[]{:S(2)}) %collective-permute-start.8) | collective-permute-done | bytes 688160 | tf_op jit(solution)/shard_map/ppermute | solution.py:582
  68.0 0.0 collective-permute-done.9.refs_3_
  68.0 0.3 middle_sum.1
  68.3 3.5 %collective-permute-start.13 = (bf16[336,256]{1,0:T(8,128)(2,1)S(1)}, bf16[336,256]{1,0:T(8,128)(2,1)S(1)}, u32[]{:S(2)}, u32[]{:S(2)}) collective-permute-start(bf16[336,256]{1,0:T(8,128)(2,1)S(1)} %get-tuple-element.43), channel_id=1, source_target_pairs={{0,8},{2,10},{4,12},{6,14},{8,0},{10,2},{12,4},{14,6},{16,24},{18,... | collective-permute-start | bytes 516104 | tf_op jit(solution)/shard_map/ppermute | solution.py:593
  71.8 0.7 collective-permute-start.18
  72.5 0.7 collective-permute-start.17
  73.2 0.7 collective-permute-start.16
  73.9 4.5 %collective-permute-start.14 = (bf16[336,256]{1,0:T(8,128)(2,1)S(1)}, bf16[336,256]{1,0:T(8,128)(2,1)S(1)}, u32[]{:S(2)}, u32[]{:S(2)}) collective-permute-start(bf16[336,256]{1,0:T(8,128)(2,1)S(1)} %get-tuple-element.44), channel_id=1, source_target_pairs={{0,16},{2,18},{4,20},{6,22},{8,24},{10,26},{12,28},{14,30},{16,0},... | collective-permute-start | bytes 516104 | tf_op jit(solution)/shard_map/ppermute | solution.py:593
  78.4 0.0 collective-permute-done.13.refs_1_
  78.4 2.7 %collective-permute-start.15 = (bf16[336,256]{1,0:T(8,128)(2,1)S(1)}, bf16[336,256]{1,0:T(8,128)(2,1)S(1)}, u32[]{:S(2)}, u32[]{:S(2)}) collective-permute-start(bf16[336,256]{1,0:T(8,128)(2,1)S(1)} %get-tuple-element.45), channel_id=1, source_target_pairs={{0,24},{2,26},{4,28},{6,30},{8,16},{10,18},{12,20},{14,22},{16,8},... | collective-permute-start | bytes 516104 | tf_op jit(solution)/shard_map/ppermute | solution.py:593
  81.1 2.7 %collective-permute-done.14.refs_2_ = bf16[336,256]{1,0:T(8,128)(2,1)S(1)} collective-permute-done((bf16[336,256]{1,0:T(8,128)(2,1)S(1)}, bf16[336,256]{1,0:T(8,128)(2,1)S(1)}, u32[]{:S(2)}, u32[]{:S(2)}) %collective-permute-start.14) | collective-permute-done | bytes 172064 | tf_op jit(solution)/shard_map/ppermute | solution.py:593
  83.8 3.7 %collective-permute-done.15.refs_3_ = bf16[336,256]{1,0:T(8,128)(2,1)S(1)} collective-permute-done((bf16[336,256]{1,0:T(8,128)(2,1)S(1)}, bf16[336,256]{1,0:T(8,128)(2,1)S(1)}, u32[]{:S(2)}, u32[]{:S(2)}) %collective-permute-start.15) | collective-permute-done | bytes 172064 | tf_op jit(solution)/shard_map/ppermute | solution.py:593
  87.5 0.0 collective-permute-done.18.refs_7_
  87.5 0.0 collective-permute-done.17.refs_6_
  87.5 0.0 collective-permute-done.16.refs_5_
  87.5 0.1 last_sum.1
  87.6 2.2 %collective-permute-start.21 = (bf16[336,256]{1,0:T(8,128)(2,1)S(1)}, bf16[336,256]{1,0:T(8,128)(2,1)S(1)}, u32[]{:S(2)}, u32[]{:S(2)}) collective-permute-start(bf16[336,256]{1,0:T(8,128)(2,1)S(1)} %get-tuple-element.47.refs_0_), channel_id=1, source_target_pairs={{0,6},{2,4},{4,2},{6,0},{8,14},{10,12},{12,10},{14,8},{16,22},{18,... | collective-permute-start | bytes 516104 | tf_op jit(solution)/shard_map/ppermute | solution.py:582
  89.9 3.1 %collective-permute-start.20 = (bf16[336,256]{1,0:T(8,128)(2,1)S(1)}, bf16[336,256]{1,0:T(8,128)(2,1)S(1)}, u32[]{:S(2)}, u32[]{:S(2)}) collective-permute-start(bf16[336,256]{1,0:T(8,128)(2,1)S(1)} %get-tuple-element.47.refs_0_), channel_id=1, source_target_pairs={{0,4},{2,6},{4,0},{6,2},{8,12},{10,14},{12,8},{14,10},{16,20},{18,... | collective-permute-start | bytes 516104 | tf_op jit(solution)/shard_map/ppermute | solution.py:582
  93.0 3.9 %collective-permute-start.19 = (bf16[336,256]{1,0:T(8,128)(2,1)S(1)}, bf16[336,256]{1,0:T(8,128)(2,1)S(1)}, u32[]{:S(2)}, u32[]{:S(2)}) collective-permute-start(bf16[336,256]{1,0:T(8,128)(2,1)S(1)} %get-tuple-element.47.refs_0_), channel_id=1, source_target_pairs={{0,2},{2,0},{4,6},{6,4},{8,10},{10,8},{12,14},{14,12},{16,18},{18,... | collective-permute-start | bytes 516104 | tf_op jit(solution)/shard_map/ppermute | solution.py:582
  96.9 1.3 %collective-permute-start.26 = (bf16[640,256]{1,0:T(8,128)(2,1)S(1)}, bf16[640,256]{1,0:T(8,128)(2,1)S(1)}, u32[]{:S(2)}, u32[]{:S(2)}) collective-permute-start(bf16[640,256]{1,0:T(8,128)(2,1)S(1)} %get-tuple-element.48.refs_8_), channel_id=1, source_target_pairs={{1,0},{3,2},{5,4},{7,6},{9,8},{11,10},{13,12},{15,14},{17,16},{19,... | collective-permute-start | bytes 983048 | tf_op jit(solution)/shard_map/ppermute | solution.py:622
  98.2 3.1 %collective-permute-start.22 = (bf16[336,256]{1,0:T(8,128)(2,1)S(1)}, bf16[336,256]{1,0:T(8,128)(2,1)S(1)}, u32[]{:S(2)}, u32[]{:S(2)}) collective-permute-start(bf16[336,256]{1,0:T(8,128)(2,1)S(1)} %get-tuple-element.47.refs_0_), channel_id=1, source_target_pairs={{0,1},{2,3},{4,5},{6,7},{8,9},{10,11},{12,13},{14,15},{16,17},{18,... | collective-permute-start | bytes 516104 | tf_op jit(solution)/shard_map/ppermute | solution.py:621
  101.3 1.3 %collective-permute-start.25 = (bf16[336,256]{1,0:T(8,128)(2,1)S(1)}, bf16[336,256]{1,0:T(8,128)(2,1)S(1)}, u32[]{:S(2)}, u32[]{:S(2)}) collective-permute-start(bf16[336,256]{1,0:T(8,128)(2,1)S(1)} %collective-permute-done.21.refs_3_), channel_id=1, source_target_pairs={{0,1},{2,3},{4,5},{6,7},{8,9},{10,11},{12,13},{14,15},{16,17},{18,... | collective-permute-start | bytes 516104 | tf_op jit(solution)/shard_map/ppermute | solution.py:621
  102.6 1.3 %collective-permute-start.24 = (bf16[336,256]{1,0:T(8,128)(2,1)S(1)}, bf16[336,256]{1,0:T(8,128)(2,1)S(1)}, u32[]{:S(2)}, u32[]{:S(2)}) collective-permute-start(bf16[336,256]{1,0:T(8,128)(2,1)S(1)} %collective-permute-done.20.refs_2_), channel_id=1, source_target_pairs={{0,1},{2,3},{4,5},{6,7},{8,9},{10,11},{12,13},{14,15},{16,17},{18,... | collective-permute-start | bytes 516104 | tf_op jit(solution)/shard_map/ppermute | solution.py:621
  103.9 0.0 collective-permute-done.19.refs_1_
  103.9 1.3 %collective-permute-start.23 = (bf16[336,256]{1,0:T(8,128)(2,1)S(1)}, bf16[336,256]{1,0:T(8,128)(2,1)S(1)}, u32[]{:S(2)}, u32[]{:S(2)}) collective-permute-start(bf16[336,256]{1,0:T(8,128)(2,1)S(1)} %collective-permute-done.19.refs_1_), channel_id=1, source_target_pairs={{0,1},{2,3},{4,5},{6,7},{8,9},{10,11},{12,13},{14,15},{16,17},{18,... | collective-permute-start | bytes 516104 | tf_op jit(solution)/shard_map/ppermute | solution.py:621
  105.2 0.0 collective-permute-done.22.refs_4_
  105.2 0.0 collective-permute-done.26.refs_9_
  105.2 0.0 collective-permute-done.24.refs_6_
  105.2 1.0 collective-permute-done.23.refs_5_
  106.2 1.4 %gather_up.1 = (f32[1728,256]{1,0:T(8,128)}, f32[256,256]{1,0:T(8,128)}) custom-call(bf16[336,256]{1,0:T(8,128)(2,1)S(1)} %get-tuple-element.47.refs_0_, bf16[336,256]{1,0:T(8,128)(2,1)S(1)} %collective-permute-done.19.refs_1_, bf16[336,256]{1,0:T(8,128)(2,1)S(1)} %collective-permute-done.20.refs_2_, bf16[336,256]{1,0:T(8,128)(2,1)S(1)} %collective-permute-done.21.refs_3_, ...), custom_call_target="tpu_custom_call" | custom-call | flops 3407872 | bytes 3407872 | tf_op jit(solution)/shard_map/gather_up/pallas_call | solution.py:546
  (12 shorter events, 0.0 us)
Async XLA Ops:
  1.6 5.7 %collective-permute-start.1 = (bf16[3,64,256]{2,1,0:T(8,128)(2,1)S(1)}, bf16[3,64,256]{2,1,0:T(8,128)(2,1)S(1)}, u32[]{:S(2)}, u32[]{:S(2)}) collective-permute-start(bf16[3,64,256]{2,1,0:T(8,128)(2,1)S(1)} %get-tuple-element.51), channel_id=1, source_target_pairs={{1,0},{2,1},{3,2},{4,3},{5,4},{6,5},{7,6},{9,8},{10,9},{11,10},{12... | collective-permute-start | bytes 294920 | tf_op jit(solution)/shard_map/ppermute | solution.py:597
  2.9 4.4 %collective-permute-start = (bf16[3,64,256]{2,1,0:T(8,128)(2,1)S(1)}, bf16[3,64,256]{2,1,0:T(8,128)(2,1)S(1)}, u32[]{:S(2)}, u32[]{:S(2)}) collective-permute-start(bf16[3,64,256]{2,1,0:T(8,128)(2,1)S(1)} %get-tuple-element.52), channel_id=1, source_target_pairs={{0,1},{1,2},{2,3},{3,4},{4,5},{5,6},{6,7},{8,9},{9,10},{10,11},{11... | collective-permute-start | bytes 294920 | tf_op jit(solution)/shard_map/ppermute | solution.py:596
  7.3 1.1 %copy-start = (bf16[1,3,512,256]{3,2,1,0:T(8,128)(2,1)S(1)}, bf16[1,3,512,256]{3,2,1,0:T(8,128)(2,1)}, u32[]{:S(2)}) copy-start(bf16[1,3,512,256]{3,2,1,0:T(8,128)(2,1)} %param.7) | copy-start | bytes 2359300
  8.4 2.0 %copy-start.2 = (bf16[27,256,256]{2,1,0:T(8,128)(2,1)S(1)}, bf16[27,256,256]{2,1,0:T(8,128)(2,1)}, u32[]{:S(2)}) copy-start(bf16[27,256,256]{2,1,0:T(8,128)(2,1)} %weight_ref.2) | copy-start | bytes 10616836
  10.4 1.1 %copy-start.4 = (bf16[1,3,512,256]{3,2,1,0:T(8,128)(2,1)S(1)}, bf16[1,3,512,256]{3,2,1,0:T(8,128)(2,1)}, u32[]{:S(2)}) copy-start(bf16[1,3,512,256]{3,2,1,0:T(8,128)(2,1)} %param.8) | copy-start | bytes 2359300
  11.6 11.1 %copy-start.1 = (bf16[1,3,512,256]{3,2,1,0:T(8,128)(2,1)S(1)}, bf16[1,3,512,256]{3,2,1,0:T(8,128)(2,1)}, u32[]{:S(2)}) copy-start(bf16[1,3,512,256]{3,2,1,0:T(8,128)(2,1)} %param.7) | copy-start | bytes 2359300
  19.2 15.3 %collective-permute-start.2 = (bf16[1,512,256]{2,1,0:T(8,128)(2,1)S(1)}, bf16[1,512,256]{2,1,0:T(8,128)(2,1)S(1)}, u32[]{:S(2)}, u32[]{:S(2)}) collective-permute-start(bf16[1,512,256]{2,1,0:T(8,128)(2,1)S(1)} %get-tuple-element.27), channel_id=1, source_target_pairs={{1,0},{2,1},{3,2},{4,3},{5,4},{6,5},{7,6},{0,7},{9,8},{10,9},{11,1... | collective-permute-start | bytes 786440 | tf_op jit(solution)/shard_map/ppermute | solution.py:601
  22.7 11.8 %copy-start.3 = (bf16[1,24,512,128]{3,2,1,0:T(8,128)(2,1)S(1)}, bf16[1,24,512,128]{3,2,1,0:T(8,128)(2,1)}, u32[]{:S(2)}) copy-start(bf16[1,24,512,128]{3,2,1,0:T(8,128)(2,1)} %param.11) | copy-start | bytes 9437188
  22.7 11.8 %copy-start.5 = (bf16[8,128,256]{2,1,0:T(8,128)(2,1)S(1)}, bf16[8,128,256]{2,1,0:T(8,128)(2,1)}, u32[]{:S(2)}) copy-start(bf16[8,128,256]{2,1,0:T(8,128)(2,1)} %weight_ref.3) | copy-start | bytes 1572868
  22.7 11.8 %collective-permute-start.3 = (bf16[1,512,256]{2,1,0:T(8,128)(2,1)S(1)}, bf16[1,512,256]{2,1,0:T(8,128)(2,1)S(1)}, u32[]{:S(2)}, u32[]{:S(2)}) collective-permute-start(bf16[1,512,256]{2,1,0:T(8,128)(2,1)S(1)} %get-tuple-element.29), channel_id=1, source_target_pairs={{0,1},{1,2},{2,3},{3,4},{4,5},{5,6},{6,7},{7,0},{8,9},{9,10},{10,1... | collective-permute-start | bytes 786440 | tf_op jit(solution)/shard_map/ppermute | solution.py:602
  29.1 12.9 %collective-permute-start.6 = (bf16[4,640,256]{2,1,0:T(8,128)(2,1)S(1)}, bf16[4,640,256]{2,1,0:T(8,128)(2,1)S(1)}, u32[]{:S(2)}, u32[]{:S(2)}) collective-permute-start(bf16[4,640,256]{2,1,0:T(8,128)(2,1)S(1)} %get-tuple-element.33.refs_4_), channel_id=1, source_target_pairs={{0,1},{2,3},{4,5},{6,7},{8,9},{10,11},{12,13},{14,15},{16,17},{18,... | collective-permute-start | bytes 3932168 | tf_op jit(solution)/shard_map/ppermute | solution.py:611
  33.0 9.0 %collective-permute-start.4 = (bf16[4,1088,256]{2,1,0:T(8,128)(2,1)S(1)}, bf16[4,1088,256]{2,1,0:T(8,128)(2,1)S(1)}, u32[]{:S(2)}, u32[]{:S(2)}) collective-permute-start(bf16[4,1088,256]{2,1,0:T(8,128)(2,1)S(1)} %get-tuple-element.31.refs_0_), channel_id=1, source_target_pairs={{1,0},{3,2},{5,4},{7,6},{9,8},{11,10},{13,12},{15,14},{17,16},{19,... | collective-permute-start | bytes 6684680 | tf_op jit(solution)/shard_map/ppermute | solution.py:610
  38.1 3.9 %collective-permute-start.5 = (bf16[4,256,256]{2,1,0:T(8,128)(2,1)S(1)}, bf16[4,256,256]{2,1,0:T(8,128)(2,1)S(1)}, u32[]{:S(2)}, u32[]{:S(2)}) collective-permute-start(bf16[4,256,256]{2,1,0:T(8,128)(2,1)S(1)} %get-tuple-element.32.refs_2_), channel_id=1, source_target_pairs={{1,0},{3,2},{5,4},{7,6},{9,8},{11,10},{13,12},{15,14},{17,16},{19,... | collective-permute-start | bytes 1572872 | tf_op jit(solution)/shard_map/ppermute | solution.py:612
  42.6 14.1 %collective-permute-start.7 = (bf16[4,336,256]{2,1,0:T(8,128)(2,1)S(1)}, bf16[4,336,256]{2,1,0:T(8,128)(2,1)S(1)}, u32[]{:S(2)}, u32[]{:S(2)}) collective-permute-start(bf16[4,336,256]{2,1,0:T(8,128)(2,1)S(1)} %get-tuple-element.35), channel_id=1, source_target_pairs={{0,2},{2,0},{4,6},{6,4},{8,10},{10,8},{12,14},{14,12},{16,18},{18,... | collective-permute-start | bytes 2064392 | tf_op jit(solution)/shard_map/ppermute | solution.py:582
  47.8 20.2 %collective-permute-start.8 = (bf16[4,336,256]{2,1,0:T(8,128)(2,1)S(1)}, bf16[4,336,256]{2,1,0:T(8,128)(2,1)S(1)}, u32[]{:S(2)}, u32[]{:S(2)}) collective-permute-start(bf16[4,336,256]{2,1,0:T(8,128)(2,1)S(1)} %get-tuple-element.36), channel_id=1, source_target_pairs={{0,4},{2,6},{4,0},{6,2},{8,12},{10,14},{12,8},{14,10},{16,20},{18,... | collective-permute-start | bytes 2064392 | tf_op jit(solution)/shard_map/ppermute | solution.py:582
  49.7 18.3 %collective-permute-start.9 = (bf16[4,336,256]{2,1,0:T(8,128)(2,1)S(1)}, bf16[4,336,256]{2,1,0:T(8,128)(2,1)S(1)}, u32[]{:S(2)}, u32[]{:S(2)}) collective-permute-start(bf16[4,336,256]{2,1,0:T(8,128)(2,1)S(1)} %get-tuple-element.37), channel_id=1, source_target_pairs={{0,6},{2,4},{4,2},{6,0},{8,14},{10,12},{12,10},{14,8},{16,22},{18,... | collective-permute-start | bytes 2064392 | tf_op jit(solution)/shard_map/ppermute | solution.py:582
  53.1 1.4 %collective-permute-start.10 = (bf16[640,256]{1,0:T(8,128)(2,1)S(1)}, bf16[640,256]{1,0:T(8,128)(2,1)S(1)}, u32[]{:S(2)}, u32[]{:S(2)}) collective-permute-start(bf16[640,256]{1,0:T(8,128)(2,1)S(1)} %get-tuple-element.39), channel_id=1, source_target_pairs={{1,9},{3,11},{5,13},{7,15},{9,1},{11,3},{13,5},{15,7},{17,25},{19,... | collective-permute-start | bytes 983048 | tf_op jit(solution)/shard_map/ppermute | solution.py:593
  53.8 1.4 %collective-permute-start.11 = (bf16[640,256]{1,0:T(8,128)(2,1)S(1)}, bf16[640,256]{1,0:T(8,128)(2,1)S(1)}, u32[]{:S(2)}, u32[]{:S(2)}) collective-permute-start(bf16[640,256]{1,0:T(8,128)(2,1)S(1)} %get-tuple-element.40), channel_id=1, source_target_pairs={{1,17},{3,19},{5,21},{7,23},{9,25},{11,27},{13,29},{15,31},{17,1},... | collective-permute-start | bytes 983048 | tf_op jit(solution)/shard_map/ppermute | solution.py:593
  54.5 0.7 collective-permute-start.12
  68.3 10.1 %collective-permute-start.13 = (bf16[336,256]{1,0:T(8,128)(2,1)S(1)}, bf16[336,256]{1,0:T(8,128)(2,1)S(1)}, u32[]{:S(2)}, u32[]{:S(2)}) collective-permute-start(bf16[336,256]{1,0:T(8,128)(2,1)S(1)} %get-tuple-element.43), channel_id=1, source_target_pairs={{0,8},{2,10},{4,12},{6,14},{8,0},{10,2},{12,4},{14,6},{16,24},{18,... | collective-permute-start | bytes 516104 | tf_op jit(solution)/shard_map/ppermute | solution.py:593
  71.8 15.7 %collective-permute-start.18 = (bf16[640,256]{1,0:T(8,128)(2,1)S(1)}, bf16[640,256]{1,0:T(8,128)(2,1)S(1)}, u32[]{:S(2)}, u32[]{:S(2)}) collective-permute-start(bf16[640,256]{1,0:T(8,128)(2,1)S(1)} %get-tuple-element.46.refs_4_), channel_id=1, source_target_pairs={{1,7},{3,5},{5,3},{7,1},{9,15},{11,13},{13,11},{15,9},{17,23},{19,... | collective-permute-start | bytes 983048 | tf_op jit(solution)/shard_map/ppermute | solution.py:582
  72.5 15.0 %collective-permute-start.17 = (bf16[640,256]{1,0:T(8,128)(2,1)S(1)}, bf16[640,256]{1,0:T(8,128)(2,1)S(1)}, u32[]{:S(2)}, u32[]{:S(2)}) collective-permute-start(bf16[640,256]{1,0:T(8,128)(2,1)S(1)} %get-tuple-element.46.refs_4_), channel_id=1, source_target_pairs={{1,5},{3,7},{5,1},{7,3},{9,13},{11,15},{13,9},{15,11},{17,21},{19,... | collective-permute-start | bytes 983048 | tf_op jit(solution)/shard_map/ppermute | solution.py:582
  73.2 14.3 %collective-permute-start.16 = (bf16[640,256]{1,0:T(8,128)(2,1)S(1)}, bf16[640,256]{1,0:T(8,128)(2,1)S(1)}, u32[]{:S(2)}, u32[]{:S(2)}) collective-permute-start(bf16[640,256]{1,0:T(8,128)(2,1)S(1)} %get-tuple-element.46.refs_4_), channel_id=1, source_target_pairs={{1,3},{3,1},{5,7},{7,5},{9,11},{11,9},{13,15},{15,13},{17,19},{19,... | collective-permute-start | bytes 983048 | tf_op jit(solution)/shard_map/ppermute | solution.py:582
  73.9 9.9 %collective-permute-start.14 = (bf16[336,256]{1,0:T(8,128)(2,1)S(1)}, bf16[336,256]{1,0:T(8,128)(2,1)S(1)}, u32[]{:S(2)}, u32[]{:S(2)}) collective-permute-start(bf16[336,256]{1,0:T(8,128)(2,1)S(1)} %get-tuple-element.44), channel_id=1, source_target_pairs={{0,16},{2,18},{4,20},{6,22},{8,24},{10,26},{12,28},{14,30},{16,0},... | collective-permute-start | bytes 516104 | tf_op jit(solution)/shard_map/ppermute | solution.py:593
  78.4 9.1 %collective-permute-start.15 = (bf16[336,256]{1,0:T(8,128)(2,1)S(1)}, bf16[336,256]{1,0:T(8,128)(2,1)S(1)}, u32[]{:S(2)}, u32[]{:S(2)}) collective-permute-start(bf16[336,256]{1,0:T(8,128)(2,1)S(1)} %get-tuple-element.45), channel_id=1, source_target_pairs={{0,24},{2,26},{4,28},{6,30},{8,16},{10,18},{12,20},{14,22},{16,8},... | collective-permute-start | bytes 516104 | tf_op jit(solution)/shard_map/ppermute | solution.py:593
  87.6 13.6 %collective-permute-start.21 = (bf16[336,256]{1,0:T(8,128)(2,1)S(1)}, bf16[336,256]{1,0:T(8,128)(2,1)S(1)}, u32[]{:S(2)}, u32[]{:S(2)}) collective-permute-start(bf16[336,256]{1,0:T(8,128)(2,1)S(1)} %get-tuple-element.47.refs_0_), channel_id=1, source_target_pairs={{0,6},{2,4},{4,2},{6,0},{8,14},{10,12},{12,10},{14,8},{16,22},{18,... | collective-permute-start | bytes 516104 | tf_op jit(solution)/shard_map/ppermute | solution.py:582
  89.9 12.7 %collective-permute-start.20 = (bf16[336,256]{1,0:T(8,128)(2,1)S(1)}, bf16[336,256]{1,0:T(8,128)(2,1)S(1)}, u32[]{:S(2)}, u32[]{:S(2)}) collective-permute-start(bf16[336,256]{1,0:T(8,128)(2,1)S(1)} %get-tuple-element.47.refs_0_), channel_id=1, source_target_pairs={{0,4},{2,6},{4,0},{6,2},{8,12},{10,14},{12,8},{14,10},{16,20},{18,... | collective-permute-start | bytes 516104 | tf_op jit(solution)/shard_map/ppermute | solution.py:582
  93.0 10.9 %collective-permute-start.19 = (bf16[336,256]{1,0:T(8,128)(2,1)S(1)}, bf16[336,256]{1,0:T(8,128)(2,1)S(1)}, u32[]{:S(2)}, u32[]{:S(2)}) collective-permute-start(bf16[336,256]{1,0:T(8,128)(2,1)S(1)} %get-tuple-element.47.refs_0_), channel_id=1, source_target_pairs={{0,2},{2,0},{4,6},{6,4},{8,10},{10,8},{12,14},{14,12},{16,18},{18,... | collective-permute-start | bytes 516104 | tf_op jit(solution)/shard_map/ppermute | solution.py:582
  96.9 8.3 %collective-permute-start.26 = (bf16[640,256]{1,0:T(8,128)(2,1)S(1)}, bf16[640,256]{1,0:T(8,128)(2,1)S(1)}, u32[]{:S(2)}, u32[]{:S(2)}) collective-permute-start(bf16[640,256]{1,0:T(8,128)(2,1)S(1)} %get-tuple-element.48.refs_8_), channel_id=1, source_target_pairs={{1,0},{3,2},{5,4},{7,6},{9,8},{11,10},{13,12},{15,14},{17,16},{19,... | collective-permute-start | bytes 983048 | tf_op jit(solution)/shard_map/ppermute | solution.py:622
  98.2 7.0 %collective-permute-start.22 = (bf16[336,256]{1,0:T(8,128)(2,1)S(1)}, bf16[336,256]{1,0:T(8,128)(2,1)S(1)}, u32[]{:S(2)}, u32[]{:S(2)}) collective-permute-start(bf16[336,256]{1,0:T(8,128)(2,1)S(1)} %get-tuple-element.47.refs_0_), channel_id=1, source_target_pairs={{0,1},{2,3},{4,5},{6,7},{8,9},{10,11},{12,13},{14,15},{16,17},{18,... | collective-permute-start | bytes 516104 | tf_op jit(solution)/shard_map/ppermute | solution.py:621
  101.3 4.0 %collective-permute-start.25 = (bf16[336,256]{1,0:T(8,128)(2,1)S(1)}, bf16[336,256]{1,0:T(8,128)(2,1)S(1)}, u32[]{:S(2)}, u32[]{:S(2)}) collective-permute-start(bf16[336,256]{1,0:T(8,128)(2,1)S(1)} %collective-permute-done.21.refs_3_), channel_id=1, source_target_pairs={{0,1},{2,3},{4,5},{6,7},{8,9},{10,11},{12,13},{14,15},{16,17},{18,... | collective-permute-start | bytes 516104 | tf_op jit(solution)/shard_map/ppermute | solution.py:621
  102.6 2.7 %collective-permute-start.24 = (bf16[336,256]{1,0:T(8,128)(2,1)S(1)}, bf16[336,256]{1,0:T(8,128)(2,1)S(1)}, u32[]{:S(2)}, u32[]{:S(2)}) collective-permute-start(bf16[336,256]{1,0:T(8,128)(2,1)S(1)} %collective-permute-done.20.refs_2_), channel_id=1, source_target_pairs={{0,1},{2,3},{4,5},{6,7},{8,9},{10,11},{12,13},{14,15},{16,17},{18,... | collective-permute-start | bytes 516104 | tf_op jit(solution)/shard_map/ppermute | solution.py:621
  103.9 2.3 %collective-permute-start.23 = (bf16[336,256]{1,0:T(8,128)(2,1)S(1)}, bf16[336,256]{1,0:T(8,128)(2,1)S(1)}, u32[]{:S(2)}, u32[]{:S(2)}) collective-permute-start(bf16[336,256]{1,0:T(8,128)(2,1)S(1)} %collective-permute-done.19.refs_1_), channel_id=1, source_target_pairs={{0,1},{2,3},{4,5},{6,7},{8,9},{10,11},{12,13},{14,15},{16,17},{18,... | collective-permute-start | bytes 516104 | tf_op jit(solution)/shard_map/ppermute | solution.py:621

commit v4 on v2

--- a/solution.py
+++ b/solution.py
@@ -45,6 +45,10 @@
         other = high ^ step if count & (count - 1) == 0 else (high + step) % count
         pairs.append((index, other * stride + low))
     return lax.ppermute(value, axis, pairs)
+
+
+def in_hbm(value):
+    return pltpu.with_memory_space_constraint(value, pltpu.HBM)
 
 
 def started(source, target, sem):
@@ -130,21 +134,28 @@
 
 
 def input_kernel(
-    links_ref, routes_ref, own_ref, low_ref, high_ref, pre_ref, weight_ref,
+    links_ref, routes_ref, own_hbm, low_ref, high_ref, pre_hbm, weight_ref,
     to_lower_ref, stay_ref, to_upper_ref,
-    own_wide, low_wide, high_wide, win_ref, taps_ref, acc_ref, octants_ref, tap_sems, out_sems,
+    own_wide, low_wide, high_wide, win_ref, taps_ref, acc_ref, octants_ref,
+    pre_ref, tap_sems, out_sems, in_sems,
 ):
-    slots, voxels, channels = own_ref.shape
+    slots, voxels, channels = pre_ref.shape
     groups = routes_ref.shape[1] // 8
-    copies = []
-    for tap in range(27):
+    own_copies = [
+        started(own_hbm.at[0, slot], own_wide.at[slot], in_sems.at[slot]) for slot in range(slots)
+    ]
+    copies = {}
+    for tap in sorted(range(27), key=column_of):
         column = column_of(tap)
         lanes = slice(column * channels, (column + 1) * channels)
-        copies.append(
-            started(weight_ref.at[tap], taps_ref.at[tap // 9, :, lanes], tap_sems.at[tap])
+        copies[tap] = started(
+            weight_ref.at[tap], taps_ref.at[tap // 9, :, lanes], tap_sems.at[tap]
         )
-    for ref, wide in ((own_ref, own_wide), (low_ref, low_wide), (high_ref, high_wide)):
+    pre_copy = started(pre_hbm.at[0], pre_ref, in_sems.at[slots])
+    for ref, wide in ((low_ref, low_wide), (high_ref, high_wide)):
         extend(ref, wide)
+    own_wide[slots] = jnp.zeros((voxels, channels), BF16)
+    octants_ref[...] = jnp.zeros_like(octants_ref)
     slab = slots * PLANE
     rows = BE * slab
     part = rows // 2
@@ -168,17 +179,25 @@
     def products(group):
         return [functools.partial(product, group, start) for start in range(0, rows, part)]
 
+    def arrive(group):
+        for tap, copy in copies.items():
+            if column_of(tap) // 3 == group:
+                copy.wait()
+
     sources = (links_ref, own_wide, low_wide, high_wide, win_ref)
+    for copy in own_copies:
+        copy.wait()
     for call in builders(*sources, GROUPS[0]):
         call()
-    for copy in copies:
-        copy.wait()
+    arrive(0)
     interleave(products(0), builders(*sources, GROUPS[1]))
+    arrive(1)
     interleave(products(1), builders(*sources, GROUPS[2]))
+    arrive(2)
     for call in products(2):
         call()
-
-    octants_ref[...] = jnp.zeros_like(octants_ref)
+    pre_copy.wait()
+
     place_z = lax.broadcasted_iota(jnp.int32, (BE // 2, BE, channels), 1)
     for slot in range(slots):
         group = jnp.int32(3 * groups)
@@ -213,7 +232,7 @@
 
 
 def wide_scratch(own, low):
-    slots, voxels, channels = own.shape
+    *_, slots, voxels, channels = own.shape
     return [
         pltpu.VMEM((slots + 1, voxels, channels), BF16),
         pltpu.VMEM((slots + 1, low.shape[1], channels), BF16),
@@ -223,29 +242,31 @@
 
 
 def input_gradient(links, routes, own, low, high, pre, weight):
-    slots, voxels, channels = own.shape
-    groups = routes.shape[1] // 8
+    _, slots, voxels, channels = own.shape
+    groups = routes.shape[-1] // 8
     rows = slots * voxels
     out = jax.ShapeDtypeStruct((groups, voxels, channels), BF16)
     return pl.pallas_call(
         input_kernel,
         out_shape=(out, out, out),
-        in_specs=[SMEM, SMEM, VMEM, VMEM, VMEM, VMEM, ANY],
+        in_specs=[SMEM, SMEM, HBM, VMEM, VMEM, HBM, HBM],
         out_specs=(ANY, ANY, ANY),
         scratch_shapes=wide_scratch(own, low)
         + [
             pltpu.VMEM((3, channels, 9 * channels), BF16),
             pltpu.VMEM((rows, channels), F32),
             pltpu.VMEM((3 * groups + 1, voxels, channels), BF16),
+            pltpu.VMEM((slots, voxels, channels), BF16),
             pltpu.SemaphoreType.DMA((27,)),
             pltpu.SemaphoreType.DMA((3,)),
+            pltpu.SemaphoreType.DMA((slots + 1,)),
         ],
         compiler_params=params(40),
         cost_estimate=pl.CostEstimate(
             flops=2 * rows * 27 * channels * channels, bytes_accessed=8 * MIB, transcendentals=0
         ),
         name="input_gradient",
-    )(links, routes, own, low, high, pre, weight)
+    )(links, routes, in_hbm(own), low, high, in_hbm(pre), in_hbm(weight))
 
 
 def filter_kernel(
@@ -319,35 +340,22 @@
     )(links, own, low, high, pre)
 
 
-def fine_kernel(
-    groups, upper_ref, stay_ref, lower_ref, weight_ref, act_ref,
-    grad_ref, keep_ref, send_ref, acc_ref,
+def down_kernel(
+    groups, upper_ref, stay_ref, lower_ref, act_ref, keep_ref, send_ref, acc_ref
 ):
     step = pl.program_id(0)
-    fine, voxels, fine_channels = act_ref.shape
+    fine = act_ref.shape[0]
     channels = upper_ref.shape[-1]
-    taps = weight_ref.shape[0]
-    cells = voxels // taps
+    cells = upper_ref.shape[1] // fine
+    taps = act_ref.shape[1] // cells
 
     @pl.when(step == 0)
     def _():
         acc_ref[...] = jnp.zeros_like(acc_ref)
 
     def work(ref):
-        octants = ref[0]
-        product = lax.dot_general(
-            octants,
-            weight_ref[...].reshape(taps * fine_channels, channels),
-            (((1,), (1,)), ((), ())),
-            preferred_element_type=F32,
-        ).astype(BF16)
         wide = []
         for place in range(fine):
-            for tap in range(taps):
-                grad_ref[place, tap * cells : (tap + 1) * cells, :] = product[
-                    place * cells : (place + 1) * cells,
-                    tap * fine_channels : (tap + 1) * fine_channels,
-                ]
             wide.append(
                 jnp.concatenate(
                     [act_ref[place, tap * cells : (tap + 1) * cells, :] for tap in range(taps)],
@@ -355,7 +363,7 @@
                 )
             )
         acc_ref[...] += jnp.dot(
-            octants.T, jnp.concatenate(wide, axis=0), preferred_element_type=F32
+            ref[0].T, jnp.concatenate(wide, axis=0), preferred_element_type=F32
         )
 
     for row, ref in enumerate((upper_ref, stay_ref, lower_ref)):
@@ -374,33 +382,71 @@
         send_ref[:, :rows, :] = jnp.where(first, right, left).astype(BF16)
 
 
-def fine_gradient(shards, count, from_upper, stay, from_lower, weight, fine_act):
+def down_gradient(shards, count, from_upper, stay, from_lower, taps, fine_act):
     fine, voxels, fine_channels = fine_act.shape
     groups, _, channels = stay.shape
-    taps = weight.shape[0]
     whole = pl.BlockSpec((1, voxels, channels), lambda i: (i % groups, 0, 0))
     rows = count * piece_rows(taps * fine_channels // shards, count)
     down = jax.ShapeDtypeStruct((shards, rows, channels // 2), BF16)
     same = pl.BlockSpec(down.shape, lambda i: (0, 0, 0))
-    block = pl.BlockSpec((8, voxels, fine_channels), lambda i: (i, 0, 0))
     return pl.pallas_call(
-        functools.partial(fine_kernel, groups),
+        functools.partial(down_kernel, groups),
         grid=(3 * groups,),
-        out_shape=(jax.ShapeDtypeStruct(fine_act.shape, BF16), down, down),
+        out_shape=(down, down),
         in_specs=[
-            whole, whole, whole,
-            pl.BlockSpec(weight.shape, lambda i: (0, 0, 0)),
-            block,
+            whole, whole, whole, pl.BlockSpec((8, voxels, fine_channels), lambda i: (i, 0, 0))
         ],
-        out_specs=(block, same, same),
+        out_specs=(same, same),
         scratch_shapes=[pltpu.VMEM((channels, taps * fine_channels), F32)],
         compiler_params=params(40),
         cost_estimate=pl.CostEstimate(
             flops=64 * fine * voxels * fine_channels * channels, bytes_accessed=8 * MIB,
             transcendentals=0,
         ),
+        name="down_gradient",
+    )(from_upper, stay, from_lower, fine_act)
+
+
+def fine_kernel(groups, upper_ref, stay_ref, lower_ref, weight_ref, grad_ref):
+    step = pl.program_id(0)
+    taps, fine_channels, channels = weight_ref.shape
+    fine, voxels, _ = grad_ref.shape
+    cells = voxels // taps
+
+    def work(ref):
+        product = lax.dot_general(
+            ref[0],
+            weight_ref[...].reshape(taps * fine_channels, channels),
+            (((1,), (1,)), ((), ())),
+            preferred_element_type=F32,
+        ).astype(BF16)
+        for place in range(fine):
+            for tap in range(taps):
+                grad_ref[place, tap * cells : (tap + 1) * cells, :] = product[
+                    place * cells : (place + 1) * cells,
+                    tap * fine_channels : (tap + 1) * fine_channels,
+                ]
+
+    for row, ref in enumerate((upper_ref, stay_ref, lower_ref)):
+        pl.when(step // groups == row)(functools.partial(work, ref))
+
+
+def fine_gradient(from_upper, stay, from_lower, weight):
+    groups, voxels, channels = stay.shape
+    whole = pl.BlockSpec((1, voxels, channels), lambda i: (i % groups, 0, 0))
+    return pl.pallas_call(
+        functools.partial(fine_kernel, groups),
+        grid=(3 * groups,),
+        out_shape=jax.ShapeDtypeStruct((24 * groups, voxels, weight.shape[1]), BF16),
+        in_specs=[whole, whole, whole, pl.BlockSpec(weight.shape, lambda i: (0, 0, 0))],
+        out_specs=pl.BlockSpec((8, voxels, weight.shape[1]), lambda i: (i, 0, 0)),
+        compiler_params=params(40),
+        cost_estimate=pl.CostEstimate(
+            flops=2 * 24 * groups * voxels * weight.shape[1] * channels, bytes_accessed=4 * MIB,
+            transcendentals=0,
+        ),
         name="fine_gradient",
-    )(from_upper, stay, from_lower, weight, fine_act)
+    )(from_upper, stay, from_lower, weight)
 
 
 def piece_rows(rows, count):
@@ -466,11 +512,15 @@
     return outs[:count], outs[count:], (piece, down_piece)
 
 
+def far_first(count):
+    return [0, *range(count - 1, 0, -1)]
+
+
 def middle_kernel(count, shards, *refs):
     planes, slabs = refs[:count], refs[count : count + shards]
     to_slabs, mine_ref = refs[count + shards : -1], refs[-1]
     mine_ref[...] = tree([part[...].astype(F32) for part in slabs]).astype(BF16)
-    for step, ref in enumerate(to_slabs):
+    for step, ref in zip(far_first(shards), to_slabs):
         shard = relative(lax.axis_index("dp"), step, shards)
         ref[...] = tree([part[shard].astype(F32) for part in planes]).astype(ref.dtype)
 
@@ -493,26 +543,26 @@
 
 
 def last_kernel(factor, shards, *refs):
-    planes_ref, slabs_ref = refs[-2:]
+    *refs, _, planes_ref, slabs_ref = refs
     total = tree([part[...].astype(F32) for part in refs[:shards]])
     planes_ref[...] = (total * factor).astype(BF16)
-    total = tree([part[...].astype(F32) for part in refs[shards:-2]])
+    total = tree([part[...].astype(F32) for part in refs[shards:]])
     slabs_ref[...] = (total * factor).astype(BF16)
 
 
-def last_sum(factor, slabs, planes):
+def last_sum(factor, slabs, planes, after):
     parts = [*slabs, *planes]
     return pl.pallas_call(
         functools.partial(last_kernel, factor, len(slabs)),
         out_shape=[
             jax.ShapeDtypeStruct(slabs[0].shape, BF16), jax.ShapeDtypeStruct(planes[0].shape, BF16)
         ],
-        in_specs=[VMEM] * len(parts),
+        in_specs=[VMEM] * len(parts) + [HBM],
         out_specs=[VMEM] * 2,
         compiler_params=params(32),
         cost_estimate=cost(*parts),
         name="last_sum",
-    )(*parts)
+    )(*parts, in_hbm(after))
 
 
 def gather_kernel(count, piece, down_piece, *refs):
@@ -570,22 +620,24 @@
     ring = [(i, (i + 1) % devices) for i in range(devices)]
     swap = [(i, i ^ 1) for i in range(devices)]
 
-    def spread_out(parts, axis, stride):
+    def spread_out(parts, axis, stride, steps=None):
+        steps = steps or list(range(len(parts)))
         return [parts[0]] + [
-            exchange(parts[step], axis, step, stride) for step in range(1, len(parts))
+            exchange(part, axis, step, stride) for step, part in zip(steps[1:], parts[1:])
         ]
 
     low = lax.ppermute(own[:, voxels - PLANE :], "dom", forward)
     high = lax.ppermute(own[:, :PLANE], "dom", backward)
     to_lower, stay, to_upper = input_gradient(
-        links, routes, own, low, high, pre, conv_weight
+        links, routes, grad_out, low, high, pre_act, conv_weight
     )
     from_upper = lax.ppermute(to_lower, "dom", [(b, a) for a, b in ring])
     from_lower = lax.ppermute(to_upper, "dom", ring)
     conv_keep, conv_send = filter_gradient(shards, links, own, low, high, pre)
-    fine_grad, down_keep, down_send = fine_gradient(
-        shards, count, from_upper, stay, from_lower, down_weight, fine_act[0]
+    down_keep, down_send = down_gradient(
+        shards, count, from_upper, stay, from_lower, down_weight.shape[0], fine_act[0]
     )
+    fine_grad = fine_gradient(from_upper, stay, from_lower, down_weight)
     conv_got = lax.ppermute(conv_send, "dom", swap)
     down_got = lax.ppermute(down_send, "dom", swap)
 
@@ -593,8 +645,8 @@
     slabs = spread_out(slabs, "dp", 1)
     planes = spread_out(planes, "dom", 2)
     to_slabs, rest = middle_sum(planes, slabs)
-    to_slabs = spread_out(to_slabs, "dp", 1)
-    mine, rest = last_sum(factor, to_slabs, spread_out([rest] * count, "dom", 2))
+    to_slabs = spread_out(to_slabs, "dp", 1, far_first(shards))
+    mine, rest = last_sum(factor, to_slabs, spread_out([rest] * count, "dom", 2), fine_grad)
     near = spread_out([mine] * count, "dom", 2)
     far = [lax.ppermute(value, "dom", swap) for value in near]
     rest_far = lax.ppermute(rest, "dom", swap)

time: 83.5 us -> 84.2 us (level)
  waiting for transfers between devices: 21.9 us -> 27.6 us
  local copies, waits for them, and re-layouts: 6.61 us -> 2.34 us
  starting transfers between devices: 33.8 us -> 29.7 us
  Pallas kernels: 20 us -> 23.6 us
    unnamed x16 -> x10, local copies, waits for them, and re-layouts: 5.65 us -> 1.38 us
    ppermute x15, waiting for transfers between devices: 18.2 us -> 21.6 us  [exchange(): return lax.ppermute(value, axis, pairs)]
    ppermute x15, starting transfers between devices: 23.4 us -> 20.3 us  [exchange(): return lax.ppermute(value, axis, pairs)]
    pallas_call x1, Pallas kernels: 7.65 us -> 10.4 us  [input_gradient(): pl.pallas_call(input_kernel, out_shape=(out, out, out), in_specs=[SMEM, S...]
    ppermute x1, waiting for transfers between devices: 0.01 us -> 2.63 us  [body(): high = lax.ppermute(own[:, :PLANE], 'dom', backward)]
    ppermute x1, starting transfers between devices: 0.01 us -> 1.91 us  [body(): from_lower = lax.ppermute(to_upper, 'dom', ring)]
    ppermute x1, starting transfers between devices: 3.45 us -> 1.63 us  [body(): from_upper = lax.ppermute(to_lower, 'dom', [(b, a) for a, b in ring])]
    pallas_call x0 -> x1, Pallas kernels: none -> 1.54 us  [down_gradient(): pl.pallas_call(functools.partial(down_kernel, groups), grid=(3 * groups,)...]
  transfers between devices with their start and end apart: 26 -> 26, of which waited for: 10 -> 10; matrix products, arithmetic and copies ran while one was open for 2% -> 2% of each run, Pallas kernels for 12% -> 13%
where the time goes in v4:
time: 84.2 us; the launch traced here: 84 us
  starting transfers between devices  29.7 us (35%)
  waiting for transfers between devices  27.6 us (33%)
  Pallas kernels  23.6 us (28%)
  local copies, waits for them, and re-layouts  2.34 us (3%)
    ppermute x15, waiting for transfers between devices, exchange(): return lax.ppermute(value, axis, pairs)  21.6 us
    ppermute x15, starting transfers between devices, exchange(): return lax.ppermute(value, axis, pairs)  20.3 us
    pallas_call x1, Pallas kernels, input_gradient(): pl.pallas_call(input_kernel, out_shape=(out, out, out), in_specs=[SMEM, S...  10.4 us
    pallas_call x1, Pallas kernels, filter_gradient(): pl.pallas_call(functools.partial(filter_kernel, shard_rows), out_shape=(o...  6.41 us
    pallas_call x1, Pallas kernels, fine_gradient(): pl.pallas_call(functools.partial(fine_kernel, groups), grid=(3 * groups,)...  2.89 us
    ppermute x1, waiting for transfers between devices, body(): high = lax.ppermute(own[:, :PLANE], 'dom', backward)  2.63 us
    ppermute x1, starting transfers between devices, body(): low = lax.ppermute(own[:, voxels - PLANE:], 'dom', forward)  2.36 us
    ppermute x1, waiting for transfers between devices, body(): down_got = lax.ppermute(down_send, 'dom', swap)  2.03 us
  transfers between devices with their start and end apart: 26, of which 10 were waited for; matrix products, arithmetic and copies ran while one was open for 2% of the time, Pallas kernels for 13%

profile of v4, /device:TPU:0, one launch (start us, length us, event | category | flops | bytes accessed | tf_op | source)
XLA Modules:
  0.0 84.0 jit_solution(6402057852840143601)
XLA Ops:
  0.6 1.0 %fusion = (bf16[3,64,256]{2,1,0:T(8,128)(2,1)S(1)}, bf16[3,64,256]{2,1,0:T(8,128)(2,1)S(1)}) fusion(bf16[3,512,256]{2,1,0:T(8,128)(2,1)} %bitcast.10), kind=kLoop, calls=%fused_computation.2 | loop fusion | bytes 393216 | tf_op jit(solution)/shard_map/slice | solution.py:630
  1.6 2.4 %collective-permute-start = (bf16[3,64,256]{2,1,0:T(8,128)(2,1)S(1)}, bf16[3,64,256]{2,1,0:T(8,128)(2,1)S(1)}, u32[]{:S(2)}, u32[]{:S(2)}) collective-permute-start(bf16[3,64,256]{2,1,0:T(8,128)(2,1)S(1)} %get-tuple-element.52), channel_id=1, source_target_pairs={{0,1},{1,2},{2,3},{3,4},{4,5},{5,6},{6,7},{8,9},{9,10},{10,11},{11... | collective-permute-start | bytes 294920 | tf_op jit(solution)/shard_map/ppermute | solution.py:629
  4.0 1.3 %collective-permute-start.1 = (bf16[3,64,256]{2,1,0:T(8,128)(2,1)S(1)}, bf16[3,64,256]{2,1,0:T(8,128)(2,1)S(1)}, u32[]{:S(2)}, u32[]{:S(2)}) collective-permute-start(bf16[3,64,256]{2,1,0:T(8,128)(2,1)S(1)} %get-tuple-element.51), channel_id=1, source_target_pairs={{1,0},{2,1},{3,2},{4,3},{5,4},{6,5},{7,6},{9,8},{10,9},{11,10},{12... | collective-permute-start | bytes 294920 | tf_op jit(solution)/shard_map/ppermute | solution.py:630
  5.3 0.7 copy.15
  5.9 0.7 copy.14
  6.6 0.0 collective-permute-done.low_ref
  6.6 2.6 %collective-permute-done.1.high_ref = bf16[3,64,256]{2,1,0:T(8,128)(2,1)S(1)} collective-permute-done((bf16[3,64,256]{2,1,0:T(8,128)(2,1)S(1)}, bf16[3,64,256]{2,1,0:T(8,128)(2,1)S(1)}, u32[]{:S(2)}, u32[]{:S(2)}) %collective-permute-start.1) | collective-permute-done | bytes 98336 | tf_op jit(solution)/shard_map/ppermute | solution.py:630
  9.3 10.4 %input_gradient.1 = (bf16[1,512,256]{2,1,0:T(8,128)(2,1)S(1)}, bf16[1,512,256]{2,1,0:T(8,128)(2,1)S(1)}, bf16[1,512,256]{2,1,0:T(8,128)(2,1)S(1)}) custom-call(s32[3,27]{1,0:T(4,128)S(1)} %bitcast.12, s32[3,8]{1,0:T(4,128)S(1)} %bitcast.14, bf16[1,3,512,256]{3,2,1,0:T(8,128)(2,1)} %own_hbm.1, bf16[3,64,256]{2,1,0:T(8,128)(2,1)S(1)} %collective-permute-done.low_ref, ...), custom_call_target="tpu_custom_call" | custom-call | flops 5435817984 | bytes 8388608 | tf_op jit(solution)/shard_map/input_gradient/pallas_call | solution.py:249
  19.6 1.6 %collective-permute-start.2 = (bf16[1,512,256]{2,1,0:T(8,128)(2,1)S(1)}, bf16[1,512,256]{2,1,0:T(8,128)(2,1)S(1)}, u32[]{:S(2)}, u32[]{:S(2)}) collective-permute-start(bf16[1,512,256]{2,1,0:T(8,128)(2,1)S(1)} %get-tuple-element.27), channel_id=1, source_target_pairs={{1,0},{2,1},{3,2},{4,3},{5,4},{6,5},{7,6},{0,7},{9,8},{10,9},{11,1... | collective-permute-start | bytes 786440 | tf_op jit(solution)/shard_map/ppermute | solution.py:634
  21.3 1.9 %collective-permute-start.3 = (bf16[1,512,256]{2,1,0:T(8,128)(2,1)S(1)}, bf16[1,512,256]{2,1,0:T(8,128)(2,1)S(1)}, u32[]{:S(2)}, u32[]{:S(2)}) collective-permute-start(bf16[1,512,256]{2,1,0:T(8,128)(2,1)S(1)} %get-tuple-element.29), channel_id=1, source_target_pairs={{0,1},{1,2},{2,3},{3,4},{4,5},{5,6},{6,7},{7,0},{8,9},{9,10},{10,1... | collective-permute-start | bytes 786440 | tf_op jit(solution)/shard_map/ppermute | solution.py:635
  23.2 6.4 %filter_gradient.1 = (bf16[4,1728,128]{2,1,0:T(8,128)(2,1)S(1)}, bf16[4,1728,128]{2,1,0:T(8,128)(2,1)S(1)}) custom-call(s32[3,27]{1,0:T(4,128)S(1)} %bitcast.13, bf16[3,512,256]{2,1,0:T(8,128)(2,1)S(1)} %bitcast.11, bf16[3,64,256]{2,1,0:T(8,128)(2,1)S(1)} %collective-permute-done.low_ref, bf16[3,64,256]{2,1,0:T(8,128)(2,1)S(1)} %collective-permute-done.1.high_ref, ...), custom_call_target="tpu_custom_call" | custom-call | flops 5435817984 | bytes 8388608 | tf_op jit(solution)/shard_map/filter_gradient/pallas_call | solution.py:329
  29.6 1.6 %collective-permute-start.4 = (bf16[4,1728,128]{2,1,0:T(8,128)(2,1)S(1)}, bf16[4,1728,128]{2,1,0:T(8,128)(2,1)S(1)}, u32[]{:S(2)}, u32[]{:S(2)}) collective-permute-start(bf16[4,1728,128]{2,1,0:T(8,128)(2,1)S(1)} %get-tuple-element.31), channel_id=1, source_target_pairs={{0,1},{1,0},{2,3},{3,2},{4,5},{5,4},{6,7},{7,6},{8,9},{9,8},{10,11... | collective-permute-start | bytes 5308424 | tf_op jit(solution)/shard_map/ppermute | solution.py:641
  31.2 0.0 collective-permute-done.2.upper_ref
  31.2 0.0 collective-permute-done.3.lower_ref
  31.2 1.5 %down_gradient.1 = (bf16[4,256,128]{2,1,0:T(8,128)(2,1)S(1)}, bf16[4,256,128]{2,1,0:T(8,128)(2,1)S(1)}) custom-call(bf16[1,512,256]{2,1,0:T(8,128)(2,1)S(1)} %collective-permute-done.2.upper_ref, bf16[1,512,256]{2,1,0:T(8,128)(2,1)S(1)} %get-tuple-element.28.stay_ref, bf16[1,512,256]{2,1,0:T(8,128)(2,1)S(1)} %collective-permute-done.3.lower_ref, ...), custom_call_target="tpu_custom_call" | custom-call | flops 25769803776 | bytes 8388608 | tf_op jit(solution)/shard_map/down_gradient/pallas_call | solution.py:392
  32.7 0.1 collective-permute-start.5
  32.8 2.0 %collective-permute-done.5.down_got_ref = bf16[4,256,128]{2,1,0:T(8,128)(2,1)S(1)} collective-permute-done((bf16[4,256,128]{2,1,0:T(8,128)(2,1)S(1)}, bf16[4,256,128]{2,1,0:T(8,128)(2,1)S(1)}, u32[]{:S(2)}, u32[]{:S(2)}) %collective-permute-start.5) | collective-permute-done | bytes 262176 | tf_op jit(solution)/shard_map/ppermute | solution.py:642
  34.9 0.0 collective-permute-done.4.conv_got_ref
  34.9 0.4 pair_sum.1
  35.3 0.0 copy-start
  35.3 3.4 %collective-permute-start.6 = (bf16[4,336,128]{2,1,0:T(8,128)(2,1)S(1)}, bf16[4,336,128]{2,1,0:T(8,128)(2,1)S(1)}, u32[]{:S(2)}, u32[]{:S(2)}) collective-permute-start(bf16[4,336,128]{2,1,0:T(8,128)(2,1)S(1)} %get-tuple-element.35), channel_id=1, source_target_pairs={{0,2},{1,3},{2,0},{3,1},{4,6},{5,7},{6,4},{7,5},{8,10},{9,11},{10,... | collective-permute-start | bytes 1032200 | tf_op jit(solution)/shard_map/ppermute | solution.py:47
  38.7 0.0 collective-permute-start.7
  38.7 1.5 %collective-permute-start.8 = (bf16[4,336,128]{2,1,0:T(8,128)(2,1)S(1)}, bf16[4,336,128]{2,1,0:T(8,128)(2,1)S(1)}, u32[]{:S(2)}, u32[]{:S(2)}) collective-permute-start(bf16[4,336,128]{2,1,0:T(8,128)(2,1)S(1)} %get-tuple-element.37), channel_id=1, source_target_pairs={{0,6},{1,7},{2,4},{3,5},{4,2},{5,3},{6,0},{7,1},{8,14},{9,15},{10,... | collective-permute-start | bytes 1032200 | tf_op jit(solution)/shard_map/ppermute | solution.py:47
  40.2 2.6 %collective-permute-start.10 = (bf16[640,128]{1,0:T(8,128)(2,1)S(1)}, bf16[640,128]{1,0:T(8,128)(2,1)S(1)}, u32[]{:S(2)}, u32[]{:S(2)}) collective-permute-start(bf16[640,128]{1,0:T(8,128)(2,1)S(1)} %get-tuple-element.40), channel_id=1, source_target_pairs={{0,16},{8,24},{16,0},{24,8},{1,17},{9,25},{17,1},{25,9},{2,18},{10... | collective-permute-start | bytes 491528 | tf_op jit(solution)/shard_map/ppermute | solution.py:47
  42.8 1.3 %collective-permute-start.11 = (bf16[640,128]{1,0:T(8,128)(2,1)S(1)}, bf16[640,128]{1,0:T(8,128)(2,1)S(1)}, u32[]{:S(2)}, u32[]{:S(2)}) collective-permute-start(bf16[640,128]{1,0:T(8,128)(2,1)S(1)} %get-tuple-element.41), channel_id=1, source_target_pairs={{0,24},{8,16},{16,8},{24,0},{1,25},{9,17},{17,9},{25,1},{2,26},{10... | collective-permute-start | bytes 491528 | tf_op jit(solution)/shard_map/ppermute | solution.py:47
  44.2 11.0 %collective-permute-done.10.refs_6_ = bf16[640,128]{1,0:T(8,128)(2,1)S(1)} collective-permute-done((bf16[640,128]{1,0:T(8,128)(2,1)S(1)}, bf16[640,128]{1,0:T(8,128)(2,1)S(1)}, u32[]{:S(2)}, u32[]{:S(2)}) %collective-permute-start.10) | collective-permute-done | bytes 163872 | tf_op jit(solution)/shard_map/ppermute | solution.py:47
  55.2 0.0 collective-permute-start.9
  55.2 0.0 collective-permute-done.11.refs_7_
  55.2 5.3 %collective-permute-done.9.refs_5_ = bf16[640,128]{1,0:T(8,128)(2,1)S(1)} collective-permute-done((bf16[640,128]{1,0:T(8,128)(2,1)S(1)}, bf16[640,128]{1,0:T(8,128)(2,1)S(1)}, u32[]{:S(2)}, u32[]{:S(2)}) %collective-permute-start.9) | collective-permute-done | bytes 163872 | tf_op jit(solution)/shard_map/ppermute | solution.py:47
  60.5 0.0 collective-permute-done.6.refs_1_
  60.5 0.0 collective-permute-done.7.refs_2_
  60.5 0.0 collective-permute-done.8.refs_3_
  60.5 0.2 middle_sum.1
  60.8 3.2 %collective-permute-start.12 = (bf16[336,128]{1,0:T(8,128)(2,1)S(1)}, bf16[336,128]{1,0:T(8,128)(2,1)S(1)}, u32[]{:S(2)}, u32[]{:S(2)}) collective-permute-start(bf16[336,128]{1,0:T(8,128)(2,1)S(1)} %get-tuple-element.43), channel_id=1, source_target_pairs={{0,24},{8,16},{16,8},{24,0},{1,25},{9,17},{17,9},{25,1},{2,26},{10... | collective-permute-start | bytes 258056 | tf_op jit(solution)/shard_map/ppermute | solution.py:47
  64.0 1.7 %collective-permute-start.15 = (bf16[640,128]{1,0:T(8,128)(2,1)S(1)}, bf16[640,128]{1,0:T(8,128)(2,1)S(1)}, u32[]{:S(2)}, u32[]{:S(2)}) collective-permute-start(bf16[640,128]{1,0:T(8,128)(2,1)S(1)} %get-tuple-element.46.refs_4_), channel_id=1, source_target_pairs={{0,2},{1,3},{2,0},{3,1},{4,6},{5,7},{6,4},{7,5},{8,10},{9,11},{10,... | collective-permute-start | bytes 491528 | tf_op jit(solution)/shard_map/ppermute | solution.py:47
  65.7 0.3 collective-permute-start.16
  66.0 1.5 %collective-permute-start.17 = (bf16[640,128]{1,0:T(8,128)(2,1)S(1)}, bf16[640,128]{1,0:T(8,128)(2,1)S(1)}, u32[]{:S(2)}, u32[]{:S(2)}) collective-permute-start(bf16[640,128]{1,0:T(8,128)(2,1)S(1)} %get-tuple-element.46.refs_4_), channel_id=1, source_target_pairs={{0,6},{1,7},{2,4},{3,5},{4,2},{5,3},{6,0},{7,1},{8,14},{9,15},{10,... | collective-permute-start | bytes 491528 | tf_op jit(solution)/shard_map/ppermute | solution.py:47
  67.5 0.0 collective-permute-start.13
  67.5 0.0 collective-permute-done.12.refs_1_
  67.5 1.2 %collective-permute-start.14 = (bf16[336,128]{1,0:T(8,128)(2,1)S(1)}, bf16[336,128]{1,0:T(8,128)(2,1)S(1)}, u32[]{:S(2)}, u32[]{:S(2)}) collective-permute-start(bf16[336,128]{1,0:T(8,128)(2,1)S(1)} %get-tuple-element.45), channel_id=1, source_target_pairs={{0,8},{8,0},{16,24},{24,16},{1,9},{9,1},{17,25},{25,17},{2,10},{10... | collective-permute-start | bytes 258056 | tf_op jit(solution)/shard_map/ppermute | solution.py:47
  68.7 2.9 %fine_gradient.1.refs_8_ = bf16[24,512,128]{2,1,0:T(8,128)(2,1)} custom-call(bf16[1,512,256]{2,1,0:T(8,128)(2,1)S(1)} %collective-permute-done.2.upper_ref, bf16[1,512,256]{2,1,0:T(8,128)(2,1)S(1)} %get-tuple-element.28.stay_ref, bf16[1,512,256]{2,1,0:T(8,128)(2,1)S(1)} %collective-permute-done.3.lower_ref, bf16[8,128,256]{2,1,0:T(8,128)(2,1)S(1)} %copy-done), custom_call_target="tpu_custom_call" | custom-call | flops 805306368 | bytes 4194304 | tf_op jit(solution)/shard_map/fine_gradient/pallas_call | solution.py:437
  71.6 1.3 %collective-permute-done.13.refs_2_ = bf16[336,128]{1,0:T(8,128)(2,1)S(1)} collective-permute-done((bf16[336,128]{1,0:T(8,128)(2,1)S(1)}, bf16[336,128]{1,0:T(8,128)(2,1)S(1)}, u32[]{:S(2)}, u32[]{:S(2)}) %collective-permute-start.13) | collective-permute-done | bytes 86048 | tf_op jit(solution)/shard_map/ppermute | solution.py:47
  72.9 0.0 collective-permute-done.14.refs_3_
  72.9 0.0 collective-permute-done.15.refs_5_
  72.9 0.9 %collective-permute-done.16.refs_6_ = bf16[640,128]{1,0:T(8,128)(2,1)S(1)} collective-permute-done((bf16[640,128]{1,0:T(8,128)(2,1)S(1)}, bf16[640,128]{1,0:T(8,128)(2,1)S(1)}, u32[]{:S(2)}, u32[]{:S(2)}) %collective-permute-start.16) | collective-permute-done | bytes 163872 | tf_op jit(solution)/shard_map/ppermute | solution.py:47
  73.8 0.0 collective-permute-done.17.refs_7_
  73.8 0.1 last_sum.1
  73.9 0.9 %collective-permute-start.18 = (bf16[336,128]{1,0:T(8,128)(2,1)S(1)}, bf16[336,128]{1,0:T(8,128)(2,1)S(1)}, u32[]{:S(2)}, u32[]{:S(2)}) collective-permute-start(bf16[336,128]{1,0:T(8,128)(2,1)S(1)} %get-tuple-element.47.refs_0_), channel_id=1, source_target_pairs={{0,2},{1,3},{2,0},{3,1},{4,6},{5,7},{6,4},{7,5},{8,10},{9,11},{10,... | collective-permute-start | bytes 258056 | tf_op jit(solution)/shard_map/ppermute | solution.py:47
  74.8 0.9 %collective-permute-start.19 = (bf16[336,128]{1,0:T(8,128)(2,1)S(1)}, bf16[336,128]{1,0:T(8,128)(2,1)S(1)}, u32[]{:S(2)}, u32[]{:S(2)}) collective-permute-start(bf16[336,128]{1,0:T(8,128)(2,1)S(1)} %get-tuple-element.47.refs_0_), channel_id=1, source_target_pairs={{0,4},{1,5},{2,6},{3,7},{4,0},{5,1},{6,2},{7,3},{8,12},{9,13},{10,... | collective-permute-start | bytes 258056 | tf_op jit(solution)/shard_map/ppermute | solution.py:47
  75.7 1.8 %collective-permute-start.20 = (bf16[336,128]{1,0:T(8,128)(2,1)S(1)}, bf16[336,128]{1,0:T(8,128)(2,1)S(1)}, u32[]{:S(2)}, u32[]{:S(2)}) collective-permute-start(bf16[336,128]{1,0:T(8,128)(2,1)S(1)} %get-tuple-element.47.refs_0_), channel_id=1, source_target_pairs={{0,6},{1,7},{2,4},{3,5},{4,2},{5,3},{6,0},{7,1},{8,14},{9,15},{10,... | collective-permute-start | bytes 258056 | tf_op jit(solution)/shard_map/ppermute | solution.py:47
  77.5 0.0 collective-permute-start.25
  77.5 0.5 collective-permute-start.21
  78.0 0.5 collective-permute-done.18.refs_1_
  78.5 0.0 collective-permute-start.22
  78.5 0.8 collective-permute-done.19.refs_2_
  79.3 0.0 collective-permute-start.23
  79.3 1.8 %collective-permute-done.20.refs_3_ = bf16[336,128]{1,0:T(8,128)(2,1)S(1)} collective-permute-done((bf16[336,128]{1,0:T(8,128)(2,1)S(1)}, bf16[336,128]{1,0:T(8,128)(2,1)S(1)}, u32[]{:S(2)}, u32[]{:S(2)}) %collective-permute-start.20) | collective-permute-done | bytes 86048 | tf_op jit(solution)/shard_map/ppermute | solution.py:47
  81.1 0.0 collective-permute-start.24
  81.1 0.0 collective-permute-done.21.refs_4_
  81.1 0.0 collective-permute-done.25.refs_9_
  81.1 0.0 collective-permute-done.22.refs_5_
  81.1 0.0 collective-permute-done.23.refs_6_
  81.2 1.2 %collective-permute-done.24.refs_7_ = bf16[336,128]{1,0:T(8,128)(2,1)S(1)} collective-permute-done((bf16[336,128]{1,0:T(8,128)(2,1)S(1)}, bf16[336,128]{1,0:T(8,128)(2,1)S(1)}, u32[]{:S(2)}, u32[]{:S(2)}) %collective-permute-start.24) | collective-permute-done | bytes 86048 | tf_op jit(solution)/shard_map/ppermute | solution.py:651
  82.4 1.6 %gather_up.1 = (f32[1728,256]{1,0:T(8,128)}, f32[256,256]{1,0:T(8,128)}) custom-call(bf16[336,128]{1,0:T(8,128)(2,1)S(1)} %get-tuple-element.47.refs_0_, bf16[336,128]{1,0:T(8,128)(2,1)S(1)} %collective-permute-done.18.refs_1_, bf16[336,128]{1,0:T(8,128)(2,1)S(1)} %collective-permute-done.19.refs_2_, bf16[336,128]{1,0:T(8,128)(2,1)S(1)} %collective-permute-done.20.refs_3_, ...), custom_call_target="tpu_custom_call" | custom-call | flops 2719744 | bytes 2719744 | tf_op jit(solution)/shard_map/gather_up/pallas_call | solution.py:592
  (7 shorter events, 0.0 us)
Async XLA Ops:
  1.6 5.0 %collective-permute-start = (bf16[3,64,256]{2,1,0:T(8,128)(2,1)S(1)}, bf16[3,64,256]{2,1,0:T(8,128)(2,1)S(1)}, u32[]{:S(2)}, u32[]{:S(2)}) collective-permute-start(bf16[3,64,256]{2,1,0:T(8,128)(2,1)S(1)} %get-tuple-element.52), channel_id=1, source_target_pairs={{0,1},{1,2},{2,3},{3,4},{4,5},{5,6},{6,7},{8,9},{9,10},{10,11},{11... | collective-permute-start | bytes 294920 | tf_op jit(solution)/shard_map/ppermute | solution.py:629
  4.0 5.3 %collective-permute-start.1 = (bf16[3,64,256]{2,1,0:T(8,128)(2,1)S(1)}, bf16[3,64,256]{2,1,0:T(8,128)(2,1)S(1)}, u32[]{:S(2)}, u32[]{:S(2)}) collective-permute-start(bf16[3,64,256]{2,1,0:T(8,128)(2,1)S(1)} %get-tuple-element.51), channel_id=1, source_target_pairs={{1,0},{2,1},{3,2},{4,3},{5,4},{6,5},{7,6},{9,8},{10,9},{11,10},{12... | collective-permute-start | bytes 294920 | tf_op jit(solution)/shard_map/ppermute | solution.py:630
  9.3 13.9 %copy-start.1 = (bf16[1,3,512,256]{3,2,1,0:T(8,128)(2,1)S(1)}, bf16[1,3,512,256]{3,2,1,0:T(8,128)(2,1)}, u32[]{:S(2)}) copy-start(bf16[1,3,512,256]{3,2,1,0:T(8,128)(2,1)} %own_hbm.1) | copy-start | bytes 2359300
  9.3 13.9 %copy-start.3 = (bf16[1,3,512,256]{3,2,1,0:T(8,128)(2,1)S(1)}, bf16[1,3,512,256]{3,2,1,0:T(8,128)(2,1)}, u32[]{:S(2)}) copy-start(bf16[1,3,512,256]{3,2,1,0:T(8,128)(2,1)} %pre_hbm.1) | copy-start | bytes 2359300
  19.6 11.5 %collective-permute-start.2 = (bf16[1,512,256]{2,1,0:T(8,128)(2,1)S(1)}, bf16[1,512,256]{2,1,0:T(8,128)(2,1)S(1)}, u32[]{:S(2)}, u32[]{:S(2)}) collective-permute-start(bf16[1,512,256]{2,1,0:T(8,128)(2,1)S(1)} %get-tuple-element.27), channel_id=1, source_target_pairs={{1,0},{2,1},{3,2},{4,3},{5,4},{6,5},{7,6},{0,7},{9,8},{10,9},{11,1... | collective-permute-start | bytes 786440 | tf_op jit(solution)/shard_map/ppermute | solution.py:634
  21.3 9.9 %collective-permute-start.3 = (bf16[1,512,256]{2,1,0:T(8,128)(2,1)S(1)}, bf16[1,512,256]{2,1,0:T(8,128)(2,1)S(1)}, u32[]{:S(2)}, u32[]{:S(2)}) collective-permute-start(bf16[1,512,256]{2,1,0:T(8,128)(2,1)S(1)} %get-tuple-element.29), channel_id=1, source_target_pairs={{0,1},{1,2},{2,3},{3,4},{4,5},{5,6},{6,7},{7,0},{8,9},{9,10},{10,1... | collective-permute-start | bytes 786440 | tf_op jit(solution)/shard_map/ppermute | solution.py:635
  23.2 8.0 %copy-start.2 = (bf16[1,24,512,128]{3,2,1,0:T(8,128)(2,1)S(1)}, bf16[1,24,512,128]{3,2,1,0:T(8,128)(2,1)}, u32[]{:S(2)}) copy-start(bf16[1,24,512,128]{3,2,1,0:T(8,128)(2,1)} %param.11) | copy-start | bytes 9437188
  29.6 5.3 %collective-permute-start.4 = (bf16[4,1728,128]{2,1,0:T(8,128)(2,1)S(1)}, bf16[4,1728,128]{2,1,0:T(8,128)(2,1)S(1)}, u32[]{:S(2)}, u32[]{:S(2)}) collective-permute-start(bf16[4,1728,128]{2,1,0:T(8,128)(2,1)S(1)} %get-tuple-element.31), channel_id=1, source_target_pairs={{0,1},{1,0},{2,3},{3,2},{4,5},{5,4},{6,7},{7,6},{8,9},{9,8},{10,11... | collective-permute-start | bytes 5308424 | tf_op jit(solution)/shard_map/ppermute | solution.py:641
  32.7 2.1 %collective-permute-start.5 = (bf16[4,256,128]{2,1,0:T(8,128)(2,1)S(1)}, bf16[4,256,128]{2,1,0:T(8,128)(2,1)S(1)}, u32[]{:S(2)}, u32[]{:S(2)}) collective-permute-start(bf16[4,256,128]{2,1,0:T(8,128)(2,1)S(1)} %get-tuple-element.33), channel_id=1, source_target_pairs={{0,1},{1,0},{2,3},{3,2},{4,5},{5,4},{6,7},{7,6},{8,9},{9,8},{10,11... | collective-permute-start | bytes 786440 | tf_op jit(solution)/shard_map/ppermute | solution.py:642
  35.3 33.4 %copy-start = (bf16[8,128,256]{2,1,0:T(8,128)(2,1)S(1)}, bf16[8,128,256]{2,1,0:T(8,128)(2,1)}, u32[]{:S(2)}) copy-start(bf16[8,128,256]{2,1,0:T(8,128)(2,1)} %weight_ref.3) | copy-start | bytes 1572868
  35.3 25.2 %collective-permute-start.6 = (bf16[4,336,128]{2,1,0:T(8,128)(2,1)S(1)}, bf16[4,336,128]{2,1,0:T(8,128)(2,1)S(1)}, u32[]{:S(2)}, u32[]{:S(2)}) collective-permute-start(bf16[4,336,128]{2,1,0:T(8,128)(2,1)S(1)} %get-tuple-element.35), channel_id=1, source_target_pairs={{0,2},{1,3},{2,0},{3,1},{4,6},{5,7},{6,4},{7,5},{8,10},{9,11},{10,... | collective-permute-start | bytes 1032200 | tf_op jit(solution)/shard_map/ppermute | solution.py:47
  38.7 21.8 %collective-permute-start.7 = (bf16[4,336,128]{2,1,0:T(8,128)(2,1)S(1)}, bf16[4,336,128]{2,1,0:T(8,128)(2,1)S(1)}, u32[]{:S(2)}, u32[]{:S(2)}) collective-permute-start(bf16[4,336,128]{2,1,0:T(8,128)(2,1)S(1)} %get-tuple-element.36), channel_id=1, source_target_pairs={{0,4},{1,5},{2,6},{3,7},{4,0},{5,1},{6,2},{7,3},{8,12},{9,13},{10,... | collective-permute-start | bytes 1032200 | tf_op jit(solution)/shard_map/ppermute | solution.py:47
  38.7 21.8 %collective-permute-start.8 = (bf16[4,336,128]{2,1,0:T(8,128)(2,1)S(1)}, bf16[4,336,128]{2,1,0:T(8,128)(2,1)S(1)}, u32[]{:S(2)}, u32[]{:S(2)}) collective-permute-start(bf16[4,336,128]{2,1,0:T(8,128)(2,1)S(1)} %get-tuple-element.37), channel_id=1, source_target_pairs={{0,6},{1,7},{2,4},{3,5},{4,2},{5,3},{6,0},{7,1},{8,14},{9,15},{10,... | collective-permute-start | bytes 1032200 | tf_op jit(solution)/shard_map/ppermute | solution.py:47
  40.2 15.0 %collective-permute-start.10 = (bf16[640,128]{1,0:T(8,128)(2,1)S(1)}, bf16[640,128]{1,0:T(8,128)(2,1)S(1)}, u32[]{:S(2)}, u32[]{:S(2)}) collective-permute-start(bf16[640,128]{1,0:T(8,128)(2,1)S(1)} %get-tuple-element.40), channel_id=1, source_target_pairs={{0,16},{8,24},{16,0},{24,8},{1,17},{9,25},{17,1},{25,9},{2,18},{10... | collective-permute-start | bytes 491528 | tf_op jit(solution)/shard_map/ppermute | solution.py:47
  42.8 12.4 %collective-permute-start.11 = (bf16[640,128]{1,0:T(8,128)(2,1)S(1)}, bf16[640,128]{1,0:T(8,128)(2,1)S(1)}, u32[]{:S(2)}, u32[]{:S(2)}) collective-permute-start(bf16[640,128]{1,0:T(8,128)(2,1)S(1)} %get-tuple-element.41), channel_id=1, source_target_pairs={{0,24},{8,16},{16,8},{24,0},{1,25},{9,17},{17,9},{25,1},{2,26},{10... | collective-permute-start | bytes 491528 | tf_op jit(solution)/shard_map/ppermute | solution.py:47
  55.2 5.3 %collective-permute-start.9 = (bf16[640,128]{1,0:T(8,128)(2,1)S(1)}, bf16[640,128]{1,0:T(8,128)(2,1)S(1)}, u32[]{:S(2)}, u32[]{:S(2)}) collective-permute-start(bf16[640,128]{1,0:T(8,128)(2,1)S(1)} %get-tuple-element.39), channel_id=1, source_target_pairs={{0,8},{8,0},{16,24},{24,16},{1,9},{9,1},{17,25},{25,17},{2,10},{10... | collective-permute-start | bytes 491528 | tf_op jit(solution)/shard_map/ppermute | solution.py:47
  60.8 6.7 %collective-permute-start.12 = (bf16[336,128]{1,0:T(8,128)(2,1)S(1)}, bf16[336,128]{1,0:T(8,128)(2,1)S(1)}, u32[]{:S(2)}, u32[]{:S(2)}) collective-permute-start(bf16[336,128]{1,0:T(8,128)(2,1)S(1)} %get-tuple-element.43), channel_id=1, source_target_pairs={{0,24},{8,16},{16,8},{24,0},{1,25},{9,17},{17,9},{25,1},{2,26},{10... | collective-permute-start | bytes 258056 | tf_op jit(solution)/shard_map/ppermute | solution.py:47
  64.0 8.9 %collective-permute-start.15 = (bf16[640,128]{1,0:T(8,128)(2,1)S(1)}, bf16[640,128]{1,0:T(8,128)(2,1)S(1)}, u32[]{:S(2)}, u32[]{:S(2)}) collective-permute-start(bf16[640,128]{1,0:T(8,128)(2,1)S(1)} %get-tuple-element.46.refs_4_), channel_id=1, source_target_pairs={{0,2},{1,3},{2,0},{3,1},{4,6},{5,7},{6,4},{7,5},{8,10},{9,11},{10,... | collective-permute-start | bytes 491528 | tf_op jit(solution)/shard_map/ppermute | solution.py:47
  65.7 8.1 %collective-permute-start.16 = (bf16[640,128]{1,0:T(8,128)(2,1)S(1)}, bf16[640,128]{1,0:T(8,128)(2,1)S(1)}, u32[]{:S(2)}, u32[]{:S(2)}) collective-permute-start(bf16[640,128]{1,0:T(8,128)(2,1)S(1)} %get-tuple-element.46.refs_4_), channel_id=1, source_target_pairs={{0,4},{1,5},{2,6},{3,7},{4,0},{5,1},{6,2},{7,3},{8,12},{9,13},{10,... | collective-permute-start | bytes 491528 | tf_op jit(solution)/shard_map/ppermute | solution.py:47
  66.0 7.8 %collective-permute-start.17 = (bf16[640,128]{1,0:T(8,128)(2,1)S(1)}, bf16[640,128]{1,0:T(8,128)(2,1)S(1)}, u32[]{:S(2)}, u32[]{:S(2)}) collective-permute-start(bf16[640,128]{1,0:T(8,128)(2,1)S(1)} %get-tuple-element.46.refs_4_), channel_id=1, source_target_pairs={{0,6},{1,7},{2,4},{3,5},{4,2},{5,3},{6,0},{7,1},{8,14},{9,15},{10,... | collective-permute-start | bytes 491528 | tf_op jit(solution)/shard_map/ppermute | solution.py:47
  67.5 5.4 %collective-permute-start.13 = (bf16[336,128]{1,0:T(8,128)(2,1)S(1)}, bf16[336,128]{1,0:T(8,128)(2,1)S(1)}, u32[]{:S(2)}, u32[]{:S(2)}) collective-permute-start(bf16[336,128]{1,0:T(8,128)(2,1)S(1)} %get-tuple-element.44), channel_id=1, source_target_pairs={{0,16},{8,24},{16,0},{24,8},{1,17},{9,25},{17,1},{25,9},{2,18},{10... | collective-permute-start | bytes 258056 | tf_op jit(solution)/shard_map/ppermute | solution.py:47
  67.5 5.4 %collective-permute-start.14 = (bf16[336,128]{1,0:T(8,128)(2,1)S(1)}, bf16[336,128]{1,0:T(8,128)(2,1)S(1)}, u32[]{:S(2)}, u32[]{:S(2)}) collective-permute-start(bf16[336,128]{1,0:T(8,128)(2,1)S(1)} %get-tuple-element.45), channel_id=1, source_target_pairs={{0,8},{8,0},{16,24},{24,16},{1,9},{9,1},{17,25},{25,17},{2,10},{10... | collective-permute-start | bytes 258056 | tf_op jit(solution)/shard_map/ppermute | solution.py:47
  73.9 4.6 %collective-permute-start.18 = (bf16[336,128]{1,0:T(8,128)(2,1)S(1)}, bf16[336,128]{1,0:T(8,128)(2,1)S(1)}, u32[]{:S(2)}, u32[]{:S(2)}) collective-permute-start(bf16[336,128]{1,0:T(8,128)(2,1)S(1)} %get-tuple-element.47.refs_0_), channel_id=1, source_target_pairs={{0,2},{1,3},{2,0},{3,1},{4,6},{5,7},{6,4},{7,5},{8,10},{9,11},{10,... | collective-permute-start | bytes 258056 | tf_op jit(solution)/shard_map/ppermute | solution.py:47
  74.8 4.5 %collective-permute-start.19 = (bf16[336,128]{1,0:T(8,128)(2,1)S(1)}, bf16[336,128]{1,0:T(8,128)(2,1)S(1)}, u32[]{:S(2)}, u32[]{:S(2)}) collective-permute-start(bf16[336,128]{1,0:T(8,128)(2,1)S(1)} %get-tuple-element.47.refs_0_), channel_id=1, source_target_pairs={{0,4},{1,5},{2,6},{3,7},{4,0},{5,1},{6,2},{7,3},{8,12},{9,13},{10,... | collective-permute-start | bytes 258056 | tf_op jit(solution)/shard_map/ppermute | solution.py:47
  75.7 5.4 %collective-permute-start.20 = (bf16[336,128]{1,0:T(8,128)(2,1)S(1)}, bf16[336,128]{1,0:T(8,128)(2,1)S(1)}, u32[]{:S(2)}, u32[]{:S(2)}) collective-permute-start(bf16[336,128]{1,0:T(8,128)(2,1)S(1)} %get-tuple-element.47.refs_0_), channel_id=1, source_target_pairs={{0,6},{1,7},{2,4},{3,5},{4,2},{5,3},{6,0},{7,1},{8,14},{9,15},{10,... | collective-permute-start | bytes 258056 | tf_op jit(solution)/shard_map/ppermute | solution.py:47
  77.5 3.6 %collective-permute-start.25 = (bf16[640,128]{1,0:T(8,128)(2,1)S(1)}, bf16[640,128]{1,0:T(8,128)(2,1)S(1)}, u32[]{:S(2)}, u32[]{:S(2)}) collective-permute-start(bf16[640,128]{1,0:T(8,128)(2,1)S(1)} %get-tuple-element.48.refs_8_), channel_id=1, source_target_pairs={{0,1},{1,0},{2,3},{3,2},{4,5},{5,4},{6,7},{7,6},{8,9},{9,8},{10,11... | collective-permute-start | bytes 491528 | tf_op jit(solution)/shard_map/ppermute | solution.py:652
  77.5 3.6 %collective-permute-start.21 = (bf16[336,128]{1,0:T(8,128)(2,1)S(1)}, bf16[336,128]{1,0:T(8,128)(2,1)S(1)}, u32[]{:S(2)}, u32[]{:S(2)}) collective-permute-start(bf16[336,128]{1,0:T(8,128)(2,1)S(1)} %get-tuple-element.47.refs_0_), channel_id=1, source_target_pairs={{0,1},{1,0},{2,3},{3,2},{4,5},{5,4},{6,7},{7,6},{8,9},{9,8},{10,11... | collective-permute-start | bytes 258056 | tf_op jit(solution)/shard_map/ppermute | solution.py:651
  78.5 2.7 %collective-permute-start.22 = (bf16[336,128]{1,0:T(8,128)(2,1)S(1)}, bf16[336,128]{1,0:T(8,128)(2,1)S(1)}, u32[]{:S(2)}, u32[]{:S(2)}) collective-permute-start(bf16[336,128]{1,0:T(8,128)(2,1)S(1)} %collective-permute-done.18.refs_1_), channel_id=1, source_target_pairs={{0,1},{1,0},{2,3},{3,2},{4,5},{5,4},{6,7},{7,6},{8,9},{9,8},{10,11... | collective-permute-start | bytes 258056 | tf_op jit(solution)/shard_map/ppermute | solution.py:651
  79.3 1.9 %collective-permute-start.23 = (bf16[336,128]{1,0:T(8,128)(2,1)S(1)}, bf16[336,128]{1,0:T(8,128)(2,1)S(1)}, u32[]{:S(2)}, u32[]{:S(2)}) collective-permute-start(bf16[336,128]{1,0:T(8,128)(2,1)S(1)} %collective-permute-done.19.refs_2_), channel_id=1, source_target_pairs={{0,1},{1,0},{2,3},{3,2},{4,5},{5,4},{6,7},{7,6},{8,9},{9,8},{10,11... | collective-permute-start | bytes 258056 | tf_op jit(solution)/shard_map/ppermute | solution.py:651
  81.1 1.3 %collective-permute-start.24 = (bf16[336,128]{1,0:T(8,128)(2,1)S(1)}, bf16[336,128]{1,0:T(8,128)(2,1)S(1)}, u32[]{:S(2)}, u32[]{:S(2)}) collective-permute-start(bf16[336,128]{1,0:T(8,128)(2,1)S(1)} %collective-permute-done.20.refs_3_), channel_id=1, source_target_pairs={{0,1},{1,0},{2,3},{3,2},{4,5},{5,4},{6,7},{7,6},{8,9},{9,8},{10,11... | collective-permute-start | bytes 258056 | tf_op jit(solution)/shard_map/ppermute | solution.py:651

commit v5 on v4

--- a/solution.py
+++ b/solution.py
@@ -133,28 +133,60 @@
         done = until
 
 
+def prepare_kernel(own_hbm, pre_hbm, weight_hbm, own_wide, act_ref, taps_ref, pre_ref, sems):
+    _, slots, voxels, channels = own_hbm.shape
+    slab = slots * PLANE
+    pre_copy = started(pre_hbm.at[0], pre_ref, sems.at[27])
+    copies = [started(own_hbm.at[0], own_wide.at[pl.ds(0, slots)], sems.at[28])]
+    for tap in range(27):
+        lanes = slice(column_of(tap) * channels, (column_of(tap) + 1) * channels)
+        copies.append(started(weight_hbm.at[tap], taps_ref.at[tap // 9, :, lanes], sems.at[tap]))
+    own_wide[slots] = jnp.zeros((voxels, channels), BF16)
+    pre_copy.wait()
+    for pair in range(BE // 2):
+        parts = []
+        for x in (2 * pair, 2 * pair + 1):
+            for slot in range(slots):
+                parts.append(pre_ref[slot, x * PLANE : (x + 1) * PLANE, :])
+        block = jnp.maximum(jnp.concatenate(parts, axis=0).astype(F32), 0.0)
+        act_ref[:, pair * 2 * slab : (pair + 1) * 2 * slab] = block.T.astype(BF16)
+    for copy in copies:
+        copy.wait()
+
+
+def prepare(own, pre, weight):
+    _, slots, voxels, channels = own.shape
+    return pl.pallas_call(
+        prepare_kernel,
+        out_shape=(
+            jax.ShapeDtypeStruct((slots + 1, voxels, channels), BF16),
+            jax.ShapeDtypeStruct((channels, slots * voxels), BF16),
+            jax.ShapeDtypeStruct((3, channels, 9 * channels), BF16),
+        ),
+        in_specs=[HBM] * 3,
+        out_specs=[VMEM] * 3,
+        scratch_shapes=[
+            pltpu.VMEM((slots, voxels, channels), BF16),
+            pltpu.SemaphoreType.DMA((29,)),
+        ],
+        compiler_params=params(24),
+        cost_estimate=pl.CostEstimate(
+            flops=4 * MIB, bytes_accessed=12 * MIB, transcendentals=0
+        ),
+        name="prepare",
+    )(in_hbm(own), in_hbm(pre), in_hbm(weight))
+
+
 def input_kernel(
-    links_ref, routes_ref, own_hbm, low_ref, high_ref, pre_hbm, weight_ref,
+    links_ref, routes_ref, own_wide, low_ref, high_ref, pre_hbm, taps_ref,
     to_lower_ref, stay_ref, to_upper_ref,
-    own_wide, low_wide, high_wide, win_ref, taps_ref, acc_ref, octants_ref,
-    pre_ref, tap_sems, out_sems, in_sems,
+    low_wide, high_wide, win_ref, acc_ref, octants_ref, pre_ref, out_sems, pre_sem,
 ):
     slots, voxels, channels = pre_ref.shape
     groups = routes_ref.shape[1] // 8
-    own_copies = [
-        started(own_hbm.at[0, slot], own_wide.at[slot], in_sems.at[slot]) for slot in range(slots)
-    ]
-    copies = {}
-    for tap in sorted(range(27), key=column_of):
-        column = column_of(tap)
-        lanes = slice(column * channels, (column + 1) * channels)
-        copies[tap] = started(
-            weight_ref.at[tap], taps_ref.at[tap // 9, :, lanes], tap_sems.at[tap]
-        )
-    pre_copy = started(pre_hbm.at[0], pre_ref, in_sems.at[slots])
+    pre_copy = started(pre_hbm.at[0], pre_ref, pre_sem)
     for ref, wide in ((low_ref, low_wide), (high_ref, high_wide)):
         extend(ref, wide)
-    own_wide[slots] = jnp.zeros((voxels, channels), BF16)
     octants_ref[...] = jnp.zeros_like(octants_ref)
     slab = slots * PLANE
     rows = BE * slab
@@ -179,21 +211,11 @@
     def products(group):
         return [functools.partial(product, group, start) for start in range(0, rows, part)]
 
-    def arrive(group):
-        for tap, copy in copies.items():
-            if column_of(tap) // 3 == group:
-                copy.wait()
-
     sources = (links_ref, own_wide, low_wide, high_wide, win_ref)
-    for copy in own_copies:
-        copy.wait()
     for call in builders(*sources, GROUPS[0]):
         call()
-    arrive(0)
     interleave(products(0), builders(*sources, GROUPS[1]))
-    arrive(1)
     interleave(products(1), builders(*sources, GROUPS[2]))
-    arrive(2)
     for call in products(2):
         call()
     pre_copy.wait()
@@ -231,63 +253,51 @@
         copy.wait()
 
 
-def wide_scratch(own, low):
-    *_, slots, voxels, channels = own.shape
+def window_scratch(slots, low):
+    _, rows, channels = low.shape
     return [
-        pltpu.VMEM((slots + 1, voxels, channels), BF16),
-        pltpu.VMEM((slots + 1, low.shape[1], channels), BF16),
-        pltpu.VMEM((slots + 1, low.shape[1], channels), BF16),
+        pltpu.VMEM((slots + 1, rows, channels), BF16),
+        pltpu.VMEM((slots + 1, rows, channels), BF16),
         pltpu.VMEM((slots * PLANE * (BE + 2), 9 * channels), BF16),
     ]
 
 
-def input_gradient(links, routes, own, low, high, pre, weight):
-    _, slots, voxels, channels = own.shape
+def input_gradient(links, routes, own_wide, low, high, pre, taps):
+    _, slots, voxels, channels = pre.shape
     groups = routes.shape[-1] // 8
     rows = slots * voxels
     out = jax.ShapeDtypeStruct((groups, voxels, channels), BF16)
     return pl.pallas_call(
         input_kernel,
         out_shape=(out, out, out),
-        in_specs=[SMEM, SMEM, HBM, VMEM, VMEM, HBM, HBM],
+        in_specs=[SMEM, SMEM, VMEM, VMEM, VMEM, HBM, VMEM],
         out_specs=(ANY, ANY, ANY),
-        scratch_shapes=wide_scratch(own, low)
+        scratch_shapes=window_scratch(slots, low)
         + [
-            pltpu.VMEM((3, channels, 9 * channels), BF16),
             pltpu.VMEM((rows, channels), F32),
             pltpu.VMEM((3 * groups + 1, voxels, channels), BF16),
             pltpu.VMEM((slots, voxels, channels), BF16),
-            pltpu.SemaphoreType.DMA((27,)),
             pltpu.SemaphoreType.DMA((3,)),
-            pltpu.SemaphoreType.DMA((slots + 1,)),
+            pltpu.SemaphoreType.DMA,
         ],
-        compiler_params=params(40),
+        compiler_params=params(36),
         cost_estimate=pl.CostEstimate(
             flops=2 * rows * 27 * channels * channels, bytes_accessed=8 * MIB, transcendentals=0
         ),
         name="input_gradient",
-    )(links, routes, in_hbm(own), low, high, in_hbm(pre), in_hbm(weight))
+    )(links, routes, own_wide, low, high, in_hbm(pre), taps)
 
 
 def filter_kernel(
-    shard_rows, links_ref, own_ref, low_ref, high_ref, pre_ref,
-    keep_ref, send_ref, own_wide, low_wide, high_wide, win_ref, act_ref,
+    shard_rows, links_ref, own_wide, low_ref, high_ref, act_ref,
+    keep_ref, send_ref, low_wide, high_wide, win_ref,
 ):
-    slots, voxels, channels = own_ref.shape
+    slots = low_ref.shape[0]
+    channels, rows = act_ref.shape
     slab = slots * PLANE
-    rows = BE * slab
     lanes = channels // 2
-    for ref, wide in ((own_ref, own_wide), (low_ref, low_wide), (high_ref, high_wide)):
+    for ref, wide in ((low_ref, low_wide), (high_ref, high_wide)):
         extend(ref, wide)
-
-    def transpose(pair):
-        parts = []
-        for x in (2 * pair, 2 * pair + 1):
-            for slot in range(slots):
-                parts.append(pre_ref[slot, x * PLANE : (x + 1) * PLANE, :])
-        block = jnp.maximum(jnp.concatenate(parts, axis=0).astype(F32), 0.0)
-        act_ref[:, pair * 2 * slab : (pair + 1) * 2 * slab] = block.T.astype(BF16)
-
     first = lax.rem(lax.axis_index("dom"), 2) == 0
     unit = math.gcd(channels, shard_rows)
 
@@ -313,31 +323,30 @@
         return [functools.partial(product, tap) for tap in taps]
 
     sources = (links_ref, own_wide, low_wide, high_wide, win_ref)
-    turns = [functools.partial(transpose, pair) for pair in range(BE // 2)]
-    interleave(turns, builders(*sources, GROUPS[0]))
+    for call in builders(*sources, GROUPS[0]):
+        call()
     interleave(products(0), builders(*sources, GROUPS[1]))
     interleave(products(1), builders(*sources, GROUPS[2]))
     for call in products(2):
         call()
 
 
-def filter_gradient(shards, links, own, low, high, pre):
-    slots, voxels, channels = own.shape
+def filter_gradient(shards, links, own_wide, low, high, act):
+    channels, rows = act.shape
     shard_rows = 27 * channels // shards
-    rows = slots * voxels
     out = jax.ShapeDtypeStruct((shards, shard_rows, channels // 2), BF16)
     return pl.pallas_call(
         functools.partial(filter_kernel, shard_rows),
         out_shape=(out, out),
         in_specs=[SMEM, VMEM, VMEM, VMEM, VMEM],
         out_specs=(VMEM, VMEM),
-        scratch_shapes=wide_scratch(own, low) + [pltpu.VMEM((channels, rows), BF16)],
-        compiler_params=params(40),
+        scratch_shapes=window_scratch(low.shape[0], low),
+        compiler_params=params(36),
         cost_estimate=pl.CostEstimate(
             flops=2 * rows * 27 * channels * channels, bytes_accessed=8 * MIB, transcendentals=0
         ),
         name="filter_gradient",
-    )(links, own, low, high, pre)
+    )(links, own_wide, low, high, act)
 
 
 def down_kernel(
@@ -606,7 +615,6 @@
 
 def body(grad_out, pre_act, conv_weight, down_weight, fine_act, neighbours, octant_routes):
     own = grad_out[0]
-    pre = pre_act[0]
     links = neighbours[0]
     routes = octant_routes[0, 0]
     slots, voxels, channels = own.shape
@@ -628,12 +636,13 @@
 
     low = lax.ppermute(own[:, voxels - PLANE :], "dom", forward)
     high = lax.ppermute(own[:, :PLANE], "dom", backward)
+    own_wide, act, taps = prepare(grad_out, pre_act, conv_weight)
     to_lower, stay, to_upper = input_gradient(
-        links, routes, grad_out, low, high, pre_act, conv_weight
+        links, routes, own_wide, low, high, pre_act, taps
     )
     from_upper = lax.ppermute(to_lower, "dom", [(b, a) for a, b in ring])
     from_lower = lax.ppermute(to_upper, "dom", ring)
-    conv_keep, conv_send = filter_gradient(shards, links, own, low, high, pre)
+    conv_keep, conv_send = filter_gradient(shards, links, own_wide, low, high, act)
     down_keep, down_send = down_gradient(
         shards, count, from_upper, stay, from_lower, down_weight.shape[0], fine_act[0]
     )

time: 84.2 us -> 77.3 us (0.918)
  waiting for transfers between devices: 27.6 us -> 18.8 us
  starting transfers between devices: 29.7 us -> 31.8 us
    ppermute x15, waiting for transfers between devices: 21.6 us -> 14.4 us  [exchange(): return lax.ppermute(value, axis, pairs)]
    pallas_call x1, Pallas kernels: 10.4 us -> 7.43 us  [input_gradient(): pl.pallas_call(input_kernel, out_shape=(out, out, out), in_specs=[SMEM, S...]
    pallas_call x0 -> x1, Pallas kernels: none -> 2.73 us  [prepare(): pl.pallas_call(prepare_kernel, out_shape=(jax.ShapeDtypeStruct((slots + 1...]
    ppermute x1, waiting for transfers between devices: 2.63 us -> 0.01 us  [body(): high = lax.ppermute(own[:, :PLANE], 'dom', backward)]
    ppermute x1, starting transfers between devices: 1.91 us -> 0.01 us  [body(): from_lower = lax.ppermute(to_upper, 'dom', ring)]
    ppermute x15, starting transfers between devices: 20.3 us -> 22.2 us  [exchange(): return lax.ppermute(value, axis, pairs)]
    ppermute x1, waiting for transfers between devices: 0.01 us -> 1.6 us  [body(): from_lower = lax.ppermute(to_upper, 'dom', ring)]
    ppermute x1, starting transfers between devices: 1.63 us -> 2.93 us  [body(): from_upper = lax.ppermute(to_lower, 'dom', [(b, a) for a, b in ring])]
  transfers between devices with their start and end apart: 26 -> 26, of which waited for: 10 -> 12; matrix products, arithmetic and copies ran while one was open for 2% -> 2% of each run, Pallas kernels for 13% -> 17%
where the time goes in v5:
time: 77.3 us; the launch traced here: 77 us
  starting transfers between devices  31.8 us (41%)
  Pallas kernels  23.3 us (30%)
  waiting for transfers between devices  18.8 us (24%)
  local copies, waits for them, and re-layouts  2.33 us (3%)
    ppermute x15, starting transfers between devices, exchange(): return lax.ppermute(value, axis, pairs)  22.2 us
    ppermute x15, waiting for transfers between devices, exchange(): return lax.ppermute(value, axis, pairs)  14.4 us
    pallas_call x1, Pallas kernels, input_gradient(): pl.pallas_call(input_kernel, out_shape=(out, out, out), in_specs=[SMEM, S...  7.43 us
    pallas_call x1, Pallas kernels, filter_gradient(): pl.pallas_call(functools.partial(filter_kernel, shard_rows), out_shape=(o...  6.31 us
    ppermute x1, starting transfers between devices, body(): low = lax.ppermute(own[:, voxels - PLANE:], 'dom', forward)  3.04 us
    ppermute x1, starting transfers between devices, body(): from_upper = lax.ppermute(to_lower, 'dom', [(b, a) for a, b in ring])  2.93 us
    pallas_call x1, Pallas kernels, fine_gradient(): pl.pallas_call(functools.partial(fine_kernel, groups), grid=(3 * groups,)...  2.89 us
    pallas_call x1, Pallas kernels, prepare(): pl.pallas_call(prepare_kernel, out_shape=(jax.ShapeDtypeStruct((slots + 1...  2.73 us
  transfers between devices with their start and end apart: 26, of which 12 were waited for; matrix products, arithmetic and copies ran while one was open for 2% of the time, Pallas kernels for 17%

profile of v5, /device:TPU:0, one launch (start us, length us, event | category | flops | bytes accessed | tf_op | source)
XLA Modules:
  0.0 77.0 jit_solution(17012765479500861073)
XLA Ops:
  0.6 1.0 %fusion = (bf16[3,64,256]{2,1,0:T(8,128)(2,1)S(1)}, bf16[3,64,256]{2,1,0:T(8,128)(2,1)S(1)}) fusion(bf16[3,512,256]{2,1,0:T(8,128)(2,1)} %bitcast.14), kind=kLoop, calls=%fused_computation.2 | loop fusion | bytes 393216 | tf_op jit(solution)/shard_map/slice | solution.py:638
  1.6 1.3 %collective-permute-start.1 = (bf16[3,64,256]{2,1,0:T(8,128)(2,1)S(1)}, bf16[3,64,256]{2,1,0:T(8,128)(2,1)S(1)}, u32[]{:S(2)}, u32[]{:S(2)}) collective-permute-start(bf16[3,64,256]{2,1,0:T(8,128)(2,1)S(1)} %get-tuple-element.57), channel_id=1, source_target_pairs={{1,0},{2,1},{3,2},{4,3},{5,4},{6,5},{7,6},{9,8},{10,9},{11,10},{12... | collective-permute-start | bytes 294920 | tf_op jit(solution)/shard_map/ppermute | solution.py:638
  2.9 3.0 %collective-permute-start = (bf16[3,64,256]{2,1,0:T(8,128)(2,1)S(1)}, bf16[3,64,256]{2,1,0:T(8,128)(2,1)S(1)}, u32[]{:S(2)}, u32[]{:S(2)}) collective-permute-start(bf16[3,64,256]{2,1,0:T(8,128)(2,1)S(1)} %get-tuple-element.58), channel_id=1, source_target_pairs={{0,1},{1,2},{2,3},{3,4},{4,5},{5,6},{6,7},{8,9},{9,10},{10,11},{11... | collective-permute-start | bytes 294920 | tf_op jit(solution)/shard_map/ppermute | solution.py:637
  5.9 0.7 copy.15
  6.6 0.7 copy.14
  7.3 2.7 %prepare.1 = (bf16[4,512,256]{2,1,0:T(8,128)(2,1)S(1)}, bf16[256,1536]{1,0:T(8,128)(2,1)S(1)}, bf16[3,256,2304]{2,1,0:T(8,128)(2,1)S(1)}) custom-call(bf16[1,3,512,256]{3,2,1,0:T(8,128)(2,1)} %own_hbm.1, bf16[1,3,512,256]{3,2,1,0:T(8,128)(2,1)} %pre_hbm.3, bf16[27,256,256]{2,1,0:T(8,128)(2,1)} %weight_hbm.1), custom_call_target="tpu_custom_call" | custom-call | flops 4194304 | bytes 12582912 | tf_op jit(solution)/shard_map/prepare/pallas_call | solution.py:159
  10.0 0.0 collective-permute-done.1.high_ref
  10.0 0.0 collective-permute-done.low_ref
  10.1 7.4 %input_gradient.1 = (bf16[1,512,256]{2,1,0:T(8,128)(2,1)S(1)}, bf16[1,512,256]{2,1,0:T(8,128)(2,1)S(1)}, bf16[1,512,256]{2,1,0:T(8,128)(2,1)S(1)}) custom-call(s32[3,27]{1,0:T(4,128)S(1)} %bitcast.9, s32[3,8]{1,0:T(4,128)S(1)} %bitcast.11, bf16[4,512,256]{2,1,0:T(8,128)(2,1)S(1)} %get-tuple-element.30.own_wide, ...), custom_call_target="tpu_custom_call" | custom-call | flops 5435817984 | bytes 8388608 | tf_op jit(solution)/shard_map/input_gradient/pallas_call | solution.py:270
  17.5 2.9 %collective-permute-start.2 = (bf16[1,512,256]{2,1,0:T(8,128)(2,1)S(1)}, bf16[1,512,256]{2,1,0:T(8,128)(2,1)S(1)}, u32[]{:S(2)}, u32[]{:S(2)}) collective-permute-start(bf16[1,512,256]{2,1,0:T(8,128)(2,1)S(1)} %get-tuple-element.32), channel_id=1, source_target_pairs={{1,0},{2,1},{3,2},{4,3},{5,4},{6,5},{7,6},{0,7},{9,8},{10,9},{11,1... | collective-permute-start | bytes 786440 | tf_op jit(solution)/shard_map/ppermute | solution.py:643
  20.4 0.0 collective-permute-start.3
  20.4 6.3 %filter_gradient.1 = (bf16[4,1728,128]{2,1,0:T(8,128)(2,1)S(1)}, bf16[4,1728,128]{2,1,0:T(8,128)(2,1)S(1)}) custom-call(s32[3,27]{1,0:T(4,128)S(1)} %bitcast.10, bf16[4,512,256]{2,1,0:T(8,128)(2,1)S(1)} %get-tuple-element.30.own_wide, bf16[3,64,256]{2,1,0:T(8,128)(2,1)S(1)} %collective-permute-done.low_ref, ...), custom_call_target="tpu_custom_call" | custom-call | flops 5435817984 | bytes 8388608 | tf_op jit(solution)/shard_map/filter_gradient/pallas_call | solution.py:338
  26.8 1.5 %collective-permute-start.4 = (bf16[4,1728,128]{2,1,0:T(8,128)(2,1)S(1)}, bf16[4,1728,128]{2,1,0:T(8,128)(2,1)S(1)}, u32[]{:S(2)}, u32[]{:S(2)}) collective-permute-start(bf16[4,1728,128]{2,1,0:T(8,128)(2,1)S(1)} %get-tuple-element.37), channel_id=1, source_target_pairs={{0,1},{1,0},{2,3},{3,2},{4,5},{5,4},{6,7},{7,6},{8,9},{9,8},{10,11... | collective-permute-start | bytes 5308424 | tf_op jit(solution)/shard_map/ppermute | solution.py:650
  28.2 0.0 collective-permute-done.2.upper_ref
  28.2 1.6 %collective-permute-done.3.lower_ref = bf16[1,512,256]{2,1,0:T(8,128)(2,1)S(1)} collective-permute-done((bf16[1,512,256]{2,1,0:T(8,128)(2,1)S(1)}, bf16[1,512,256]{2,1,0:T(8,128)(2,1)S(1)}, u32[]{:S(2)}, u32[]{:S(2)}) %collective-permute-start.3) | collective-permute-done | bytes 262176 | tf_op jit(solution)/shard_map/ppermute | solution.py:644
  29.9 1.5 %down_gradient.1 = (bf16[4,256,128]{2,1,0:T(8,128)(2,1)S(1)}, bf16[4,256,128]{2,1,0:T(8,128)(2,1)S(1)}) custom-call(bf16[1,512,256]{2,1,0:T(8,128)(2,1)S(1)} %collective-permute-done.2.upper_ref, bf16[1,512,256]{2,1,0:T(8,128)(2,1)S(1)} %get-tuple-element.33.stay_ref, bf16[1,512,256]{2,1,0:T(8,128)(2,1)S(1)} %collective-permute-done.3.lower_ref, ...), custom_call_target="tpu_custom_call" | custom-call | flops 25769803776 | bytes 8388608 | tf_op jit(solution)/shard_map/down_gradient/pallas_call | solution.py:401
  31.4 0.1 collective-permute-start.5
  31.5 1.5 %collective-permute-done.5.down_got_ref = bf16[4,256,128]{2,1,0:T(8,128)(2,1)S(1)} collective-permute-done((bf16[4,256,128]{2,1,0:T(8,128)(2,1)S(1)}, bf16[4,256,128]{2,1,0:T(8,128)(2,1)S(1)}, u32[]{:S(2)}, u32[]{:S(2)}) %collective-permute-start.5) | collective-permute-done | bytes 262176 | tf_op jit(solution)/shard_map/ppermute | solution.py:651
  33.0 0.0 collective-permute-done.4.conv_got_ref
  33.0 0.4 pair_sum.1
  33.4 2.3 %collective-permute-start.6 = (bf16[4,336,128]{2,1,0:T(8,128)(2,1)S(1)}, bf16[4,336,128]{2,1,0:T(8,128)(2,1)S(1)}, u32[]{:S(2)}, u32[]{:S(2)}) collective-permute-start(bf16[4,336,128]{2,1,0:T(8,128)(2,1)S(1)} %get-tuple-element.41), channel_id=1, source_target_pairs={{0,2},{1,3},{2,0},{3,1},{4,6},{5,7},{6,4},{7,5},{8,10},{9,11},{10,... | collective-permute-start | bytes 1032200 | tf_op jit(solution)/shard_map/ppermute | solution.py:47
  35.7 0.0 collective-permute-start.7
  35.7 1.5 %collective-permute-start.8 = (bf16[4,336,128]{2,1,0:T(8,128)(2,1)S(1)}, bf16[4,336,128]{2,1,0:T(8,128)(2,1)S(1)}, u32[]{:S(2)}, u32[]{:S(2)}) collective-permute-start(bf16[4,336,128]{2,1,0:T(8,128)(2,1)S(1)} %get-tuple-element.43), channel_id=1, source_target_pairs={{0,6},{1,7},{2,4},{3,5},{4,2},{5,3},{6,0},{7,1},{8,14},{9,15},{10,... | collective-permute-start | bytes 1032200 | tf_op jit(solution)/shard_map/ppermute | solution.py:47
  37.3 1.6 %collective-permute-start.9 = (bf16[640,128]{1,0:T(8,128)(2,1)S(1)}, bf16[640,128]{1,0:T(8,128)(2,1)S(1)}, u32[]{:S(2)}, u32[]{:S(2)}) collective-permute-start(bf16[640,128]{1,0:T(8,128)(2,1)S(1)} %get-tuple-element.45), channel_id=1, source_target_pairs={{0,8},{8,0},{16,24},{24,16},{1,9},{9,1},{17,25},{25,17},{2,10},{10... | collective-permute-start | bytes 491528 | tf_op jit(solution)/shard_map/ppermute | solution.py:47
  38.8 2.6 %collective-permute-start.10 = (bf16[640,128]{1,0:T(8,128)(2,1)S(1)}, bf16[640,128]{1,0:T(8,128)(2,1)S(1)}, u32[]{:S(2)}, u32[]{:S(2)}) collective-permute-start(bf16[640,128]{1,0:T(8,128)(2,1)S(1)} %get-tuple-element.46), channel_id=1, source_target_pairs={{0,16},{8,24},{16,0},{24,8},{1,17},{9,25},{17,1},{25,9},{2,18},{10... | collective-permute-start | bytes 491528 | tf_op jit(solution)/shard_map/ppermute | solution.py:47
  41.4 5.1 %collective-permute-done.9.refs_5_ = bf16[640,128]{1,0:T(8,128)(2,1)S(1)} collective-permute-done((bf16[640,128]{1,0:T(8,128)(2,1)S(1)}, bf16[640,128]{1,0:T(8,128)(2,1)S(1)}, u32[]{:S(2)}, u32[]{:S(2)}) %collective-permute-start.9) | collective-permute-done | bytes 163872 | tf_op jit(solution)/shard_map/ppermute | solution.py:47
  46.5 2.5 %collective-permute-start.11 = (bf16[640,128]{1,0:T(8,128)(2,1)S(1)}, bf16[640,128]{1,0:T(8,128)(2,1)S(1)}, u32[]{:S(2)}, u32[]{:S(2)}) collective-permute-start(bf16[640,128]{1,0:T(8,128)(2,1)S(1)} %get-tuple-element.47), channel_id=1, source_target_pairs={{0,24},{8,16},{16,8},{24,0},{1,25},{9,17},{17,9},{25,1},{2,26},{10... | collective-permute-start | bytes 491528 | tf_op jit(solution)/shard_map/ppermute | solution.py:47
  49.0 1.8 %collective-permute-done.10.refs_6_ = bf16[640,128]{1,0:T(8,128)(2,1)S(1)} collective-permute-done((bf16[640,128]{1,0:T(8,128)(2,1)S(1)}, bf16[640,128]{1,0:T(8,128)(2,1)S(1)}, u32[]{:S(2)}, u32[]{:S(2)}) %collective-permute-start.10) | collective-permute-done | bytes 163872 | tf_op jit(solution)/shard_map/ppermute | solution.py:47
  50.8 2.9 %collective-permute-done.11.refs_7_ = bf16[640,128]{1,0:T(8,128)(2,1)S(1)} collective-permute-done((bf16[640,128]{1,0:T(8,128)(2,1)S(1)}, bf16[640,128]{1,0:T(8,128)(2,1)S(1)}, u32[]{:S(2)}, u32[]{:S(2)}) %collective-permute-start.11) | collective-permute-done | bytes 163872 | tf_op jit(solution)/shard_map/ppermute | solution.py:47
  53.8 0.0 collective-permute-done.6.refs_1_
  53.8 0.0 collective-permute-done.7.refs_2_
  53.8 0.0 collective-permute-done.8.refs_3_
  53.8 0.2 middle_sum.1
  54.0 3.0 %collective-permute-start.12 = (bf16[336,128]{1,0:T(8,128)(2,1)S(1)}, bf16[336,128]{1,0:T(8,128)(2,1)S(1)}, u32[]{:S(2)}, u32[]{:S(2)}) collective-permute-start(bf16[336,128]{1,0:T(8,128)(2,1)S(1)} %get-tuple-element.49), channel_id=1, source_target_pairs={{0,24},{8,16},{16,8},{24,0},{1,25},{9,17},{17,9},{25,1},{2,26},{10... | collective-permute-start | bytes 258056 | tf_op jit(solution)/shard_map/ppermute | solution.py:47
  57.1 1.2 %collective-permute-start.17 = (bf16[640,128]{1,0:T(8,128)(2,1)S(1)}, bf16[640,128]{1,0:T(8,128)(2,1)S(1)}, u32[]{:S(2)}, u32[]{:S(2)}) collective-permute-start(bf16[640,128]{1,0:T(8,128)(2,1)S(1)} %get-tuple-element.52.refs_4_), channel_id=1, source_target_pairs={{0,6},{1,7},{2,4},{3,5},{4,2},{5,3},{6,0},{7,1},{8,14},{9,15},{10,... | collective-permute-start | bytes 491528 | tf_op jit(solution)/shard_map/ppermute | solution.py:47
  58.2 1.4 %collective-permute-start.16 = (bf16[640,128]{1,0:T(8,128)(2,1)S(1)}, bf16[640,128]{1,0:T(8,128)(2,1)S(1)}, u32[]{:S(2)}, u32[]{:S(2)}) collective-permute-start(bf16[640,128]{1,0:T(8,128)(2,1)S(1)} %get-tuple-element.52.refs_4_), channel_id=1, source_target_pairs={{0,4},{1,5},{2,6},{3,7},{4,0},{5,1},{6,2},{7,3},{8,12},{9,13},{10,... | collective-permute-start | bytes 491528 | tf_op jit(solution)/shard_map/ppermute | solution.py:47
  59.6 0.9 %collective-permute-start.15 = (bf16[640,128]{1,0:T(8,128)(2,1)S(1)}, bf16[640,128]{1,0:T(8,128)(2,1)S(1)}, u32[]{:S(2)}, u32[]{:S(2)}) collective-permute-start(bf16[640,128]{1,0:T(8,128)(2,1)S(1)} %get-tuple-element.52.refs_4_), channel_id=1, source_target_pairs={{0,2},{1,3},{2,0},{3,1},{4,6},{5,7},{6,4},{7,5},{8,10},{9,11},{10,... | collective-permute-start | bytes 491528 | tf_op jit(solution)/shard_map/ppermute | solution.py:47
  60.6 1.2 %collective-permute-start.13 = (bf16[336,128]{1,0:T(8,128)(2,1)S(1)}, bf16[336,128]{1,0:T(8,128)(2,1)S(1)}, u32[]{:S(2)}, u32[]{:S(2)}) collective-permute-start(bf16[336,128]{1,0:T(8,128)(2,1)S(1)} %get-tuple-element.50), channel_id=1, source_target_pairs={{0,16},{8,24},{16,0},{24,8},{1,17},{9,25},{17,1},{25,9},{2,18},{10... | collective-permute-start | bytes 258056 | tf_op jit(solution)/shard_map/ppermute | solution.py:47
  61.8 0.0 collective-permute-done.12.refs_1_
  61.8 0.3 collective-permute-start.14
  62.1 2.9 %fine_gradient.1.refs_8_ = bf16[24,512,128]{2,1,0:T(8,128)(2,1)} custom-call(bf16[1,512,256]{2,1,0:T(8,128)(2,1)S(1)} %collective-permute-done.2.upper_ref, bf16[1,512,256]{2,1,0:T(8,128)(2,1)S(1)} %get-tuple-element.33.stay_ref, bf16[1,512,256]{2,1,0:T(8,128)(2,1)S(1)} %collective-permute-done.3.lower_ref, bf16[8,128,256]{2,1,0:T(8,128)(2,1)S(1)} %copy-done), custom_call_target="tpu_custom_call" | custom-call | flops 805306368 | bytes 4194304 | tf_op jit(solution)/shard_map/fine_gradient/pallas_call | solution.py:446
  65.0 1.8 %collective-permute-done.13.refs_2_ = bf16[336,128]{1,0:T(8,128)(2,1)S(1)} collective-permute-done((bf16[336,128]{1,0:T(8,128)(2,1)S(1)}, bf16[336,128]{1,0:T(8,128)(2,1)S(1)}, u32[]{:S(2)}, u32[]{:S(2)}) %collective-permute-start.13) | collective-permute-done | bytes 86048 | tf_op jit(solution)/shard_map/ppermute | solution.py:47
  66.9 0.0 collective-permute-done.14.refs_3_
  66.9 0.0 collective-permute-done.17.refs_7_
  66.9 0.0 collective-permute-done.16.refs_6_
  66.9 0.0 collective-permute-done.15.refs_5_
  66.9 0.1 last_sum.1
  67.0 1.2 %collective-permute-start.20 = (bf16[336,128]{1,0:T(8,128)(2,1)S(1)}, bf16[336,128]{1,0:T(8,128)(2,1)S(1)}, u32[]{:S(2)}, u32[]{:S(2)}) collective-permute-start(bf16[336,128]{1,0:T(8,128)(2,1)S(1)} %get-tuple-element.53.refs_0_), channel_id=1, source_target_pairs={{0,6},{1,7},{2,4},{3,5},{4,2},{5,3},{6,0},{7,1},{8,14},{9,15},{10,... | collective-permute-start | bytes 258056 | tf_op jit(solution)/shard_map/ppermute | solution.py:47
  68.3 1.4 %collective-permute-start.19 = (bf16[336,128]{1,0:T(8,128)(2,1)S(1)}, bf16[336,128]{1,0:T(8,128)(2,1)S(1)}, u32[]{:S(2)}, u32[]{:S(2)}) collective-permute-start(bf16[336,128]{1,0:T(8,128)(2,1)S(1)} %get-tuple-element.53.refs_0_), channel_id=1, source_target_pairs={{0,4},{1,5},{2,6},{3,7},{4,0},{5,1},{6,2},{7,3},{8,12},{9,13},{10,... | collective-permute-start | bytes 258056 | tf_op jit(solution)/shard_map/ppermute | solution.py:47
  69.7 0.9 %collective-permute-start.18 = (bf16[336,128]{1,0:T(8,128)(2,1)S(1)}, bf16[336,128]{1,0:T(8,128)(2,1)S(1)}, u32[]{:S(2)}, u32[]{:S(2)}) collective-permute-start(bf16[336,128]{1,0:T(8,128)(2,1)S(1)} %get-tuple-element.53.refs_0_), channel_id=1, source_target_pairs={{0,2},{1,3},{2,0},{3,1},{4,6},{5,7},{6,4},{7,5},{8,10},{9,11},{10,... | collective-permute-start | bytes 258056 | tf_op jit(solution)/shard_map/ppermute | solution.py:47
  70.6 0.0 collective-permute-start.25
  70.6 0.5 collective-permute-start.21
  71.1 2.2 %collective-permute-done.20.refs_3_ = bf16[336,128]{1,0:T(8,128)(2,1)S(1)} collective-permute-done((bf16[336,128]{1,0:T(8,128)(2,1)S(1)}, bf16[336,128]{1,0:T(8,128)(2,1)S(1)}, u32[]{:S(2)}, u32[]{:S(2)}) %collective-permute-start.20) | collective-permute-done | bytes 86048 | tf_op jit(solution)/shard_map/ppermute | solution.py:47
  73.3 0.0 collective-permute-start.24
  73.3 0.2 collective-permute-done.19.refs_2_
  73.5 0.3 collective-permute-start.23
  73.8 0.3 collective-permute-done.18.refs_1_
  74.2 0.0 collective-permute-start.22
  74.2 0.0 collective-permute-done.21.refs_4_
  74.2 0.0 collective-permute-done.25.refs_9_
  74.2 0.4 collective-permute-done.24.refs_7_
  74.6 0.2 collective-permute-done.23.refs_6_
  74.8 0.6 collective-permute-done.22.refs_5_
  75.4 1.6 %gather_up.1 = (f32[1728,256]{1,0:T(8,128)}, f32[256,256]{1,0:T(8,128)}) custom-call(bf16[336,128]{1,0:T(8,128)(2,1)S(1)} %get-tuple-element.53.refs_0_, bf16[336,128]{1,0:T(8,128)(2,1)S(1)} %collective-permute-done.18.refs_1_, bf16[336,128]{1,0:T(8,128)(2,1)S(1)} %collective-permute-done.19.refs_2_, bf16[336,128]{1,0:T(8,128)(2,1)S(1)} %collective-permute-done.20.refs_3_, ...), custom_call_target="tpu_custom_call" | custom-call | flops 2719744 | bytes 2719744 | tf_op jit(solution)/shard_map/gather_up/pallas_call | solution.py:601
  (4 shorter events, 0.0 us)
Async XLA Ops:
  1.6 8.4 %collective-permute-start.1 = (bf16[3,64,256]{2,1,0:T(8,128)(2,1)S(1)}, bf16[3,64,256]{2,1,0:T(8,128)(2,1)S(1)}, u32[]{:S(2)}, u32[]{:S(2)}) collective-permute-start(bf16[3,64,256]{2,1,0:T(8,128)(2,1)S(1)} %get-tuple-element.57), channel_id=1, source_target_pairs={{1,0},{2,1},{3,2},{4,3},{5,4},{6,5},{7,6},{9,8},{10,9},{11,10},{12... | collective-permute-start | bytes 294920 | tf_op jit(solution)/shard_map/ppermute | solution.py:638
  2.9 7.2 %collective-permute-start = (bf16[3,64,256]{2,1,0:T(8,128)(2,1)S(1)}, bf16[3,64,256]{2,1,0:T(8,128)(2,1)S(1)}, u32[]{:S(2)}, u32[]{:S(2)}) collective-permute-start(bf16[3,64,256]{2,1,0:T(8,128)(2,1)S(1)} %get-tuple-element.58), channel_id=1, source_target_pairs={{0,1},{1,2},{2,3},{3,4},{4,5},{5,6},{6,7},{8,9},{9,10},{10,11},{11... | collective-permute-start | bytes 294920 | tf_op jit(solution)/shard_map/ppermute | solution.py:637
  17.5 10.7 %collective-permute-start.2 = (bf16[1,512,256]{2,1,0:T(8,128)(2,1)S(1)}, bf16[1,512,256]{2,1,0:T(8,128)(2,1)S(1)}, u32[]{:S(2)}, u32[]{:S(2)}) collective-permute-start(bf16[1,512,256]{2,1,0:T(8,128)(2,1)S(1)} %get-tuple-element.32), channel_id=1, source_target_pairs={{1,0},{2,1},{3,2},{4,3},{5,4},{6,5},{7,6},{0,7},{9,8},{10,9},{11,1... | collective-permute-start | bytes 786440 | tf_op jit(solution)/shard_map/ppermute | solution.py:643
  20.4 9.4 %collective-permute-start.3 = (bf16[1,512,256]{2,1,0:T(8,128)(2,1)S(1)}, bf16[1,512,256]{2,1,0:T(8,128)(2,1)S(1)}, u32[]{:S(2)}, u32[]{:S(2)}) collective-permute-start(bf16[1,512,256]{2,1,0:T(8,128)(2,1)S(1)} %get-tuple-element.34), channel_id=1, source_target_pairs={{0,1},{1,2},{2,3},{3,4},{4,5},{5,6},{6,7},{7,0},{8,9},{9,10},{10,1... | collective-permute-start | bytes 786440 | tf_op jit(solution)/shard_map/ppermute | solution.py:644
  20.4 9.4 %copy-start.1 = (bf16[1,24,512,128]{3,2,1,0:T(8,128)(2,1)S(1)}, bf16[1,24,512,128]{3,2,1,0:T(8,128)(2,1)}, u32[]{:S(2)}) copy-start(bf16[1,24,512,128]{3,2,1,0:T(8,128)(2,1)} %param.11) | copy-start | bytes 9437188
  26.8 6.2 %collective-permute-start.4 = (bf16[4,1728,128]{2,1,0:T(8,128)(2,1)S(1)}, bf16[4,1728,128]{2,1,0:T(8,128)(2,1)S(1)}, u32[]{:S(2)}, u32[]{:S(2)}) collective-permute-start(bf16[4,1728,128]{2,1,0:T(8,128)(2,1)S(1)} %get-tuple-element.37), channel_id=1, source_target_pairs={{0,1},{1,0},{2,3},{3,2},{4,5},{5,4},{6,7},{7,6},{8,9},{9,8},{10,11... | collective-permute-start | bytes 5308424 | tf_op jit(solution)/shard_map/ppermute | solution.py:650
  31.4 1.6 %collective-permute-start.5 = (bf16[4,256,128]{2,1,0:T(8,128)(2,1)S(1)}, bf16[4,256,128]{2,1,0:T(8,128)(2,1)S(1)}, u32[]{:S(2)}, u32[]{:S(2)}) collective-permute-start(bf16[4,256,128]{2,1,0:T(8,128)(2,1)S(1)} %get-tuple-element.39), channel_id=1, source_target_pairs={{0,1},{1,0},{2,3},{3,2},{4,5},{5,4},{6,7},{7,6},{8,9},{9,8},{10,11... | collective-permute-start | bytes 786440 | tf_op jit(solution)/shard_map/ppermute | solution.py:651
  33.0 29.2 %copy-start = (bf16[8,128,256]{2,1,0:T(8,128)(2,1)S(1)}, bf16[8,128,256]{2,1,0:T(8,128)(2,1)}, u32[]{:S(2)}) copy-start(bf16[8,128,256]{2,1,0:T(8,128)(2,1)} %weight_ref.1) | copy-start | bytes 1572868
  33.4 20.3 %collective-permute-start.6 = (bf16[4,336,128]{2,1,0:T(8,128)(2,1)S(1)}, bf16[4,336,128]{2,1,0:T(8,128)(2,1)S(1)}, u32[]{:S(2)}, u32[]{:S(2)}) collective-permute-start(bf16[4,336,128]{2,1,0:T(8,128)(2,1)S(1)} %get-tuple-element.41), channel_id=1, source_target_pairs={{0,2},{1,3},{2,0},{3,1},{4,6},{5,7},{6,4},{7,5},{8,10},{9,11},{10,... | collective-permute-start | bytes 1032200 | tf_op jit(solution)/shard_map/ppermute | solution.py:47
  35.7 18.0 %collective-permute-start.7 = (bf16[4,336,128]{2,1,0:T(8,128)(2,1)S(1)}, bf16[4,336,128]{2,1,0:T(8,128)(2,1)S(1)}, u32[]{:S(2)}, u32[]{:S(2)}) collective-permute-start(bf16[4,336,128]{2,1,0:T(8,128)(2,1)S(1)} %get-tuple-element.42), channel_id=1, source_target_pairs={{0,4},{1,5},{2,6},{3,7},{4,0},{5,1},{6,2},{7,3},{8,12},{9,13},{10,... | collective-permute-start | bytes 1032200 | tf_op jit(solution)/shard_map/ppermute | solution.py:47
  35.7 18.0 %collective-permute-start.8 = (bf16[4,336,128]{2,1,0:T(8,128)(2,1)S(1)}, bf16[4,336,128]{2,1,0:T(8,128)(2,1)S(1)}, u32[]{:S(2)}, u32[]{:S(2)}) collective-permute-start(bf16[4,336,128]{2,1,0:T(8,128)(2,1)S(1)} %get-tuple-element.43), channel_id=1, source_target_pairs={{0,6},{1,7},{2,4},{3,5},{4,2},{5,3},{6,0},{7,1},{8,14},{9,15},{10,... | collective-permute-start | bytes 1032200 | tf_op jit(solution)/shard_map/ppermute | solution.py:47
  37.3 9.3 %collective-permute-start.9 = (bf16[640,128]{1,0:T(8,128)(2,1)S(1)}, bf16[640,128]{1,0:T(8,128)(2,1)S(1)}, u32[]{:S(2)}, u32[]{:S(2)}) collective-permute-start(bf16[640,128]{1,0:T(8,128)(2,1)S(1)} %get-tuple-element.45), channel_id=1, source_target_pairs={{0,8},{8,0},{16,24},{24,16},{1,9},{9,1},{17,25},{25,17},{2,10},{10... | collective-permute-start | bytes 491528 | tf_op jit(solution)/shard_map/ppermute | solution.py:47
  38.8 12.0 %collective-permute-start.10 = (bf16[640,128]{1,0:T(8,128)(2,1)S(1)}, bf16[640,128]{1,0:T(8,128)(2,1)S(1)}, u32[]{:S(2)}, u32[]{:S(2)}) collective-permute-start(bf16[640,128]{1,0:T(8,128)(2,1)S(1)} %get-tuple-element.46), channel_id=1, source_target_pairs={{0,16},{8,24},{16,0},{24,8},{1,17},{9,25},{17,1},{25,9},{2,18},{10... | collective-permute-start | bytes 491528 | tf_op jit(solution)/shard_map/ppermute | solution.py:47
  46.5 7.2 %collective-permute-start.11 = (bf16[640,128]{1,0:T(8,128)(2,1)S(1)}, bf16[640,128]{1,0:T(8,128)(2,1)S(1)}, u32[]{:S(2)}, u32[]{:S(2)}) collective-permute-start(bf16[640,128]{1,0:T(8,128)(2,1)S(1)} %get-tuple-element.47), channel_id=1, source_target_pairs={{0,24},{8,16},{16,8},{24,0},{1,25},{9,17},{17,9},{25,1},{2,26},{10... | collective-permute-start | bytes 491528 | tf_op jit(solution)/shard_map/ppermute | solution.py:47
  54.0 7.8 %collective-permute-start.12 = (bf16[336,128]{1,0:T(8,128)(2,1)S(1)}, bf16[336,128]{1,0:T(8,128)(2,1)S(1)}, u32[]{:S(2)}, u32[]{:S(2)}) collective-permute-start(bf16[336,128]{1,0:T(8,128)(2,1)S(1)} %get-tuple-element.49), channel_id=1, source_target_pairs={{0,24},{8,16},{16,8},{24,0},{1,25},{9,17},{17,9},{25,1},{2,26},{10... | collective-permute-start | bytes 258056 | tf_op jit(solution)/shard_map/ppermute | solution.py:47
  57.1 9.8 %collective-permute-start.17 = (bf16[640,128]{1,0:T(8,128)(2,1)S(1)}, bf16[640,128]{1,0:T(8,128)(2,1)S(1)}, u32[]{:S(2)}, u32[]{:S(2)}) collective-permute-start(bf16[640,128]{1,0:T(8,128)(2,1)S(1)} %get-tuple-element.52.refs_4_), channel_id=1, source_target_pairs={{0,6},{1,7},{2,4},{3,5},{4,2},{5,3},{6,0},{7,1},{8,14},{9,15},{10,... | collective-permute-start | bytes 491528 | tf_op jit(solution)/shard_map/ppermute | solution.py:47
  58.2 8.6 %collective-permute-start.16 = (bf16[640,128]{1,0:T(8,128)(2,1)S(1)}, bf16[640,128]{1,0:T(8,128)(2,1)S(1)}, u32[]{:S(2)}, u32[]{:S(2)}) collective-permute-start(bf16[640,128]{1,0:T(8,128)(2,1)S(1)} %get-tuple-element.52.refs_4_), channel_id=1, source_target_pairs={{0,4},{1,5},{2,6},{3,7},{4,0},{5,1},{6,2},{7,3},{8,12},{9,13},{10,... | collective-permute-start | bytes 491528 | tf_op jit(solution)/shard_map/ppermute | solution.py:47
  59.6 7.2 %collective-permute-start.15 = (bf16[640,128]{1,0:T(8,128)(2,1)S(1)}, bf16[640,128]{1,0:T(8,128)(2,1)S(1)}, u32[]{:S(2)}, u32[]{:S(2)}) collective-permute-start(bf16[640,128]{1,0:T(8,128)(2,1)S(1)} %get-tuple-element.52.refs_4_), channel_id=1, source_target_pairs={{0,2},{1,3},{2,0},{3,1},{4,6},{5,7},{6,4},{7,5},{8,10},{9,11},{10,... | collective-permute-start | bytes 491528 | tf_op jit(solution)/shard_map/ppermute | solution.py:47
  60.6 6.3 %collective-permute-start.13 = (bf16[336,128]{1,0:T(8,128)(2,1)S(1)}, bf16[336,128]{1,0:T(8,128)(2,1)S(1)}, u32[]{:S(2)}, u32[]{:S(2)}) collective-permute-start(bf16[336,128]{1,0:T(8,128)(2,1)S(1)} %get-tuple-element.50), channel_id=1, source_target_pairs={{0,16},{8,24},{16,0},{24,8},{1,17},{9,25},{17,1},{25,9},{2,18},{10... | collective-permute-start | bytes 258056 | tf_op jit(solution)/shard_map/ppermute | solution.py:47
  61.8 5.1 %collective-permute-start.14 = (bf16[336,128]{1,0:T(8,128)(2,1)S(1)}, bf16[336,128]{1,0:T(8,128)(2,1)S(1)}, u32[]{:S(2)}, u32[]{:S(2)}) collective-permute-start(bf16[336,128]{1,0:T(8,128)(2,1)S(1)} %get-tuple-element.51), channel_id=1, source_target_pairs={{0,8},{8,0},{16,24},{24,16},{1,9},{9,1},{17,25},{25,17},{2,10},{10... | collective-permute-start | bytes 258056 | tf_op jit(solution)/shard_map/ppermute | solution.py:47
  67.0 6.3 %collective-permute-start.20 = (bf16[336,128]{1,0:T(8,128)(2,1)S(1)}, bf16[336,128]{1,0:T(8,128)(2,1)S(1)}, u32[]{:S(2)}, u32[]{:S(2)}) collective-permute-start(bf16[336,128]{1,0:T(8,128)(2,1)S(1)} %get-tuple-element.53.refs_0_), channel_id=1, source_target_pairs={{0,6},{1,7},{2,4},{3,5},{4,2},{5,3},{6,0},{7,1},{8,14},{9,15},{10,... | collective-permute-start | bytes 258056 | tf_op jit(solution)/shard_map/ppermute | solution.py:47
  68.3 5.3 %collective-permute-start.19 = (bf16[336,128]{1,0:T(8,128)(2,1)S(1)}, bf16[336,128]{1,0:T(8,128)(2,1)S(1)}, u32[]{:S(2)}, u32[]{:S(2)}) collective-permute-start(bf16[336,128]{1,0:T(8,128)(2,1)S(1)} %get-tuple-element.53.refs_0_), channel_id=1, source_target_pairs={{0,4},{1,5},{2,6},{3,7},{4,0},{5,1},{6,2},{7,3},{8,12},{9,13},{10,... | collective-permute-start | bytes 258056 | tf_op jit(solution)/shard_map/ppermute | solution.py:47
  69.7 4.5 %collective-permute-start.18 = (bf16[336,128]{1,0:T(8,128)(2,1)S(1)}, bf16[336,128]{1,0:T(8,128)(2,1)S(1)}, u32[]{:S(2)}, u32[]{:S(2)}) collective-permute-start(bf16[336,128]{1,0:T(8,128)(2,1)S(1)} %get-tuple-element.53.refs_0_), channel_id=1, source_target_pairs={{0,2},{1,3},{2,0},{3,1},{4,6},{5,7},{6,4},{7,5},{8,10},{9,11},{10,... | collective-permute-start | bytes 258056 | tf_op jit(solution)/shard_map/ppermute | solution.py:47
  70.6 3.6 %collective-permute-start.25 = (bf16[640,128]{1,0:T(8,128)(2,1)S(1)}, bf16[640,128]{1,0:T(8,128)(2,1)S(1)}, u32[]{:S(2)}, u32[]{:S(2)}) collective-permute-start(bf16[640,128]{1,0:T(8,128)(2,1)S(1)} %get-tuple-element.54.refs_8_), channel_id=1, source_target_pairs={{0,1},{1,0},{2,3},{3,2},{4,5},{5,4},{6,7},{7,6},{8,9},{9,8},{10,11... | collective-permute-start | bytes 491528 | tf_op jit(solution)/shard_map/ppermute | solution.py:661
  70.6 3.6 %collective-permute-start.21 = (bf16[336,128]{1,0:T(8,128)(2,1)S(1)}, bf16[336,128]{1,0:T(8,128)(2,1)S(1)}, u32[]{:S(2)}, u32[]{:S(2)}) collective-permute-start(bf16[336,128]{1,0:T(8,128)(2,1)S(1)} %get-tuple-element.53.refs_0_), channel_id=1, source_target_pairs={{0,1},{1,0},{2,3},{3,2},{4,5},{5,4},{6,7},{7,6},{8,9},{9,8},{10,11... | collective-permute-start | bytes 258056 | tf_op jit(solution)/shard_map/ppermute | solution.py:660
  73.3 1.3 %collective-permute-start.24 = (bf16[336,128]{1,0:T(8,128)(2,1)S(1)}, bf16[336,128]{1,0:T(8,128)(2,1)S(1)}, u32[]{:S(2)}, u32[]{:S(2)}) collective-permute-start(bf16[336,128]{1,0:T(8,128)(2,1)S(1)} %collective-permute-done.20.refs_3_), channel_id=1, source_target_pairs={{0,1},{1,0},{2,3},{3,2},{4,5},{5,4},{6,7},{7,6},{8,9},{9,8},{10,11... | collective-permute-start | bytes 258056 | tf_op jit(solution)/shard_map/ppermute | solution.py:660
  73.5 1.3 %collective-permute-start.23 = (bf16[336,128]{1,0:T(8,128)(2,1)S(1)}, bf16[336,128]{1,0:T(8,128)(2,1)S(1)}, u32[]{:S(2)}, u32[]{:S(2)}) collective-permute-start(bf16[336,128]{1,0:T(8,128)(2,1)S(1)} %collective-permute-done.19.refs_2_), channel_id=1, source_target_pairs={{0,1},{1,0},{2,3},{3,2},{4,5},{5,4},{6,7},{7,6},{8,9},{9,8},{10,11... | collective-permute-start | bytes 258056 | tf_op jit(solution)/shard_map/ppermute | solution.py:660
  74.2 1.3 %collective-permute-start.22 = (bf16[336,128]{1,0:T(8,128)(2,1)S(1)}, bf16[336,128]{1,0:T(8,128)(2,1)S(1)}, u32[]{:S(2)}, u32[]{:S(2)}) collective-permute-start(bf16[336,128]{1,0:T(8,128)(2,1)S(1)} %collective-permute-done.18.refs_1_), channel_id=1, source_target_pairs={{0,1},{1,0},{2,3},{3,2},{4,5},{5,4},{6,7},{7,6},{8,9},{9,8},{10,11... | collective-permute-start | bytes 258056 | tf_op jit(solution)/shard_map/ppermute | solution.py:660

commit v6 on v5

--- a/solution.py
+++ b/solution.py
@@ -14,6 +14,7 @@
 F32 = jnp.float32
 BF16 = jnp.bfloat16
 MIB = 1 << 20
+PLANE_FIRST = 0.74
 
 VMEM = pl.BlockSpec(memory_space=pltpu.VMEM)
 SMEM = pl.BlockSpec(memory_space=pltpu.SMEM)
@@ -77,7 +78,7 @@
     empty = ref.shape[0] - 1
 
     def fetch(step_y, step_z, first, rows):
-        found = links_ref[slot, 9 * (step_x + 1) + 3 * (step_y + 1) + step_z + 1]
+        found = links_ref[slot, 0, 9 * (step_x + 1) + 3 * (step_y + 1) + step_z + 1]
         place = jnp.where(found < 0, empty, found)
         return ref[place, start + first : start + first + rows, :].astype(F32)
 
@@ -179,11 +180,11 @@
 
 def input_kernel(
     links_ref, routes_ref, own_wide, low_ref, high_ref, pre_hbm, taps_ref,
-    to_lower_ref, stay_ref, to_upper_ref,
-    low_wide, high_wide, win_ref, acc_ref, octants_ref, pre_ref, out_sems, pre_sem,
+    to_lower_ref, stay_ref, to_upper_ref, win_ref,
+    low_wide, high_wide, acc_ref, octants_ref, pre_ref, out_sems, pre_sem,
 ):
     slots, voxels, channels = pre_ref.shape
-    groups = routes_ref.shape[1] // 8
+    groups = routes_ref.shape[-1] // 8
     pre_copy = started(pre_hbm.at[0], pre_ref, pre_sem)
     for ref, wide in ((low_ref, low_wide), (high_ref, high_wide)):
         extend(ref, wide)
@@ -212,40 +213,45 @@
         return [functools.partial(product, group, start) for start in range(0, rows, part)]
 
     sources = (links_ref, own_wide, low_wide, high_wide, win_ref)
-    for call in builders(*sources, GROUPS[0]):
-        call()
-    interleave(products(0), builders(*sources, GROUPS[1]))
-    interleave(products(1), builders(*sources, GROUPS[2]))
-    for call in products(2):
-        call()
-    pre_copy.wait()
-
     place_z = lax.broadcasted_iota(jnp.int32, (BE // 2, BE, channels), 1)
+    targets = []
     for slot in range(slots):
         group = jnp.int32(3 * groups)
         for row in range(3):
             for place in range(groups):
                 group = jnp.where(
-                    routes_ref[row, 8 * place] == 8 * slot, row * groups + place, group
+                    routes_ref[row, 0, 8 * place] == 8 * slot, row * groups + place, group
                 )
-
-        def finish(x, carry):
-            value = acc_ref[pl.ds(pl.multiple_of(x * slab + slot * PLANE, PLANE), PLANE), :]
-            pre = pre_ref[slot, pl.ds(pl.multiple_of(x * PLANE, PLANE), PLANE), :].astype(F32)
-            value = jnp.where(pre > 0, value, 0.0).reshape(BE // 2, 2, BE, channels)
-            even, odd = value[:, 0], value[:, 1]
-            near = jnp.where(place_z < HALF, even, pltpu.roll(odd, HALF, axis=1))
-            far = jnp.where(place_z < HALF, pltpu.roll(even, HALF, axis=1), odd)
-            side = x // HALF
-            row = (x - side * HALF) * 16
-            for side_y in range(2):
-                for side_z, piece in enumerate((near, far)):
-                    block = piece[2 * side_y : 2 * side_y + 2].reshape(16, channels).astype(BF16)
-                    start = (4 * side + 2 * side_y + side_z) * PLANE + row
-                    octants_ref[group, pl.ds(pl.multiple_of(start, 16), 16), :] = block
-            return carry
-
-        lax.fori_loop(0, BE, finish, 0)
+        targets.append(group)
+
+    def finish(x, slot):
+        start = x * slab + slot * PLANE
+        value = acc_ref[start : start + PLANE, :]
+        pre = pre_ref[slot, x * PLANE : (x + 1) * PLANE, :].astype(F32)
+        value = jnp.where(pre > 0, value, 0.0).reshape(BE // 2, 2, BE, channels)
+        even, odd = value[:, 0], value[:, 1]
+        near = jnp.where(place_z < HALF, even, pltpu.roll(odd, HALF, axis=1))
+        far = jnp.where(place_z < HALF, pltpu.roll(even, HALF, axis=1), odd)
+        side, row = x // HALF, x % HALF * 16
+        for side_y in range(2):
+            for side_z, piece in enumerate((near, far)):
+                block = piece[2 * side_y : 2 * side_y + 2].reshape(16, channels).astype(BF16)
+                start = (4 * side + 2 * side_y + side_z) * PLANE + row
+                octants_ref[targets[slot], start : start + 16, :] = block
+
+    def finishes(planes):
+        return [functools.partial(finish, x, slot) for x in planes for slot in range(slots)]
+
+    for call in builders(*sources, GROUPS[0]):
+        call()
+    pre_copy.wait()
+    interleave(products(0), builders(*sources, GROUPS[1]))
+    interleave(products(1), builders(*sources, GROUPS[2]))
+    last = products(2)
+    last[0]()
+    interleave(last[1:], finishes(range(HALF)))
+    for call in finishes(range(HALF, BE)):
+        call()
     outs = []
     for row, ref in enumerate((to_lower_ref, stay_ref, to_upper_ref)):
         outs.append(started(octants_ref.at[pl.ds(row * groups, groups)], ref, out_sems.at[row]))
@@ -253,34 +259,27 @@
         copy.wait()
 
 
-def window_scratch(slots, low):
-    _, rows, channels = low.shape
-    return [
-        pltpu.VMEM((slots + 1, rows, channels), BF16),
-        pltpu.VMEM((slots + 1, rows, channels), BF16),
-        pltpu.VMEM((slots * PLANE * (BE + 2), 9 * channels), BF16),
-    ]
-
-
 def input_gradient(links, routes, own_wide, low, high, pre, taps):
     _, slots, voxels, channels = pre.shape
     groups = routes.shape[-1] // 8
     rows = slots * voxels
     out = jax.ShapeDtypeStruct((groups, voxels, channels), BF16)
+    windows = jax.ShapeDtypeStruct((slots * PLANE * (BE + 2), 9 * channels), BF16)
     return pl.pallas_call(
         input_kernel,
-        out_shape=(out, out, out),
+        out_shape=(out, out, out, windows),
         in_specs=[SMEM, SMEM, VMEM, VMEM, VMEM, HBM, VMEM],
-        out_specs=(ANY, ANY, ANY),
-        scratch_shapes=window_scratch(slots, low)
-        + [
+        out_specs=(ANY, ANY, ANY, VMEM),
+        scratch_shapes=[
+            pltpu.VMEM((slots + 1, *low.shape[1:]), BF16),
+            pltpu.VMEM((slots + 1, *low.shape[1:]), BF16),
             pltpu.VMEM((rows, channels), F32),
             pltpu.VMEM((3 * groups + 1, voxels, channels), BF16),
             pltpu.VMEM((slots, voxels, channels), BF16),
             pltpu.SemaphoreType.DMA((3,)),
             pltpu.SemaphoreType.DMA,
         ],
-        compiler_params=params(36),
+        compiler_params=params(20),
         cost_estimate=pl.CostEstimate(
             flops=2 * rows * 27 * channels * channels, bytes_accessed=8 * MIB, transcendentals=0
         ),
@@ -289,15 +288,11 @@
 
 
 def filter_kernel(
-    shard_rows, links_ref, own_wide, low_ref, high_ref, act_ref,
-    keep_ref, send_ref, low_wide, high_wide, win_ref,
+    shard_rows, win_ref, act_ref, keep_ref, send_ref
 ):
-    slots = low_ref.shape[0]
     channels, rows = act_ref.shape
-    slab = slots * PLANE
+    slab = rows // BE
     lanes = channels // 2
-    for ref, wide in ((low_ref, low_wide), (high_ref, high_wide)):
-        extend(ref, wide)
     first = lax.rem(lax.axis_index("dom"), 2) == 0
     unit = math.gcd(channels, shard_rows)
 
@@ -318,35 +313,25 @@
             keep_ref[shard, start : start + unit, :] = keep[span]
             send_ref[shard, start : start + unit, :] = send[span]
 
-    def products(group):
-        taps = [tap for tap in range(27) if column_of(tap) // 3 == group]
-        return [functools.partial(product, tap) for tap in taps]
-
-    sources = (links_ref, own_wide, low_wide, high_wide, win_ref)
-    for call in builders(*sources, GROUPS[0]):
-        call()
-    interleave(products(0), builders(*sources, GROUPS[1]))
-    interleave(products(1), builders(*sources, GROUPS[2]))
-    for call in products(2):
-        call()
-
-
-def filter_gradient(shards, links, own_wide, low, high, act):
+    for tap in sorted(range(27), key=column_of):
+        product(tap)
+
+
+def filter_gradient(shards, windows, act):
     channels, rows = act.shape
     shard_rows = 27 * channels // shards
     out = jax.ShapeDtypeStruct((shards, shard_rows, channels // 2), BF16)
     return pl.pallas_call(
         functools.partial(filter_kernel, shard_rows),
         out_shape=(out, out),
-        in_specs=[SMEM, VMEM, VMEM, VMEM, VMEM],
+        in_specs=[VMEM, VMEM],
         out_specs=(VMEM, VMEM),
-        scratch_shapes=window_scratch(low.shape[0], low),
-        compiler_params=params(36),
+        compiler_params=params(12),
         cost_estimate=pl.CostEstimate(
             flops=2 * rows * 27 * channels * channels, bytes_accessed=8 * MIB, transcendentals=0
         ),
         name="filter_gradient",
-    )(links, own_wide, low, high, act)
+    )(windows, act)
 
 
 def down_kernel(
@@ -480,13 +465,21 @@
     return [jax.ShapeDtypeStruct(shape, F32 if step == 0 else BF16) for step in range(count)]
 
 
+def farthest_then_nearest(count):
+    return [0, count - 1, *range(1, count - 1)]
+
+
+def far_first(count):
+    return [0, *range(count - 1, 0, -1)]
+
+
 def pair_kernel(count, conv_ref, conv_got_ref, down_ref, down_got_ref, *outs):
     planes, slabs = outs[:count], outs[count:]
     shards, rows, _ = conv_ref.shape
     down_piece = down_ref.shape[1] // count
     piece = planes[0].shape[1] - down_piece
     cut = count * piece
-    for step, ref in enumerate(slabs):
+    for step, ref in zip(farthest_then_nearest(shards), slabs):
         shard = relative(lax.axis_index("dp"), step, shards)
         total = conv_ref[shard, cut:, :].astype(F32) + conv_got_ref[shard, cut:, :].astype(F32)
         ref[...] = total.astype(ref.dtype)
@@ -506,7 +499,7 @@
     shards, rows, lanes = conv.shape
     down_piece = down.shape[1] // count
     unit = 16 * count
-    piece = 16 * round((2 * (rows + down.shape[1]) / 3 - down.shape[1]) / unit)
+    piece = 16 * round((PLANE_FIRST * (rows + down.shape[1]) - down.shape[1]) / unit)
     outs = shapes_of(count, (shards, piece + down_piece, lanes))
     outs += shapes_of(shards, (rows - count * piece, lanes))
     outs = pl.pallas_call(
@@ -519,10 +512,6 @@
         name="pair_sum",
     )(conv, conv_got, down, down_got)
     return outs[:count], outs[count:], (piece, down_piece)
-
-
-def far_first(count):
-    return [0, *range(count - 1, 0, -1)]
 
 
 def middle_kernel(count, shards, *refs):
@@ -583,7 +572,7 @@
     low = lax.rem(lax.axis_index("dom"), 2)
     for side, group, rest in ((low, near, rest_ref), (1 - low, far, rest_far_ref)):
         lane = pl.ds(pl.multiple_of(side * lanes, lanes), lanes)
-        for step, ref in enumerate(group):
+        for step, ref in zip(far_first(count), group):
             place = source_of(high, step, count)
             row = pl.multiple_of(place * piece, 16)
             conv_whole[pl.ds(row, piece), lane] = ref[:piece, :].astype(F32)
@@ -615,8 +604,8 @@
 
 def body(grad_out, pre_act, conv_weight, down_weight, fine_act, neighbours, octant_routes):
     own = grad_out[0]
-    links = neighbours[0]
-    routes = octant_routes[0, 0]
+    links = neighbours.transpose(1, 0, 2)
+    routes = octant_routes.transpose(0, 2, 1, 3)[0]
     slots, voxels, channels = own.shape
     devices = lax.axis_size("dom")
     shards = lax.axis_size("dp")
@@ -637,12 +626,12 @@
     low = lax.ppermute(own[:, voxels - PLANE :], "dom", forward)
     high = lax.ppermute(own[:, :PLANE], "dom", backward)
     own_wide, act, taps = prepare(grad_out, pre_act, conv_weight)
-    to_lower, stay, to_upper = input_gradient(
+    to_lower, stay, to_upper, windows = input_gradient(
         links, routes, own_wide, low, high, pre_act, taps
     )
     from_upper = lax.ppermute(to_lower, "dom", [(b, a) for a, b in ring])
     from_lower = lax.ppermute(to_upper, "dom", ring)
-    conv_keep, conv_send = filter_gradient(shards, links, own_wide, low, high, act)
+    conv_keep, conv_send = filter_gradient(shards, windows, act)
     down_keep, down_send = down_gradient(
         shards, count, from_upper, stay, from_lower, down_weight.shape[0], fine_act[0]
     )
@@ -651,12 +640,12 @@
     down_got = lax.ppermute(down_send, "dom", swap)
 
     planes, slabs, pieces = pair_sum(count, conv_keep, conv_got, down_keep, down_got)
-    slabs = spread_out(slabs, "dp", 1)
+    slabs = spread_out(slabs, "dp", 1, farthest_then_nearest(shards))
     planes = spread_out(planes, "dom", 2)
     to_slabs, rest = middle_sum(planes, slabs)
     to_slabs = spread_out(to_slabs, "dp", 1, far_first(shards))
     mine, rest = last_sum(factor, to_slabs, spread_out([rest] * count, "dom", 2), fine_grad)
-    near = spread_out([mine] * count, "dom", 2)
+    near = spread_out([mine] * count, "dom", 2, far_first(count))
     far = [lax.ppermute(value, "dom", swap) for value in near]
     rest_far = lax.ppermute(rest, "dom", swap)
     conv_rows = 27 * channels // shards

time: 77.3 us -> 77.3 us (level)
  local copies, waits for them, and re-layouts: 2.33 us -> 0.98 us
  starting transfers between devices: 31.8 us -> 32.8 us
  waiting for transfers between devices: 18.8 us -> 19.6 us
    unnamed x6 -> x8, local copies, waits for them, and re-layouts: 1.37 us -> 0.02 us
    ppermute x1, waiting for transfers between devices: 0.01 us -> 1.25 us  [body(): high = lax.ppermute(own[:, :PLANE], 'dom', backward)]
    ppermute x15, starting transfers between devices: 22.2 us -> 23 us  [exchange(): return lax.ppermute(value, axis, pairs)]
  transfers between devices with their start and end apart: 26 -> 26, of which waited for: 12 -> 13; matrix products, arithmetic and copies ran while one was open for 2% -> 0% of each run, Pallas kernels for 17% -> 17%
where the time goes in v6:
time: 77.3 us; the launch traced here: 77 us
  starting transfers between devices  32.8 us (42%)
  Pallas kernels  22.8 us (29%)
  waiting for transfers between devices  19.6 us (25%)
  local copies, waits for them, and re-layouts  0.98 us (1%)
    ppermute x15, starting transfers between devices, exchange(): return lax.ppermute(value, axis, pairs)  23 us
    ppermute x15, waiting for transfers between devices, exchange(): return lax.ppermute(value, axis, pairs)  14.6 us
    pallas_call x1, Pallas kernels, input_gradient(): pl.pallas_call(input_kernel, out_shape=(out, out, out, windows), in_specs...  7.64 us
    pallas_call x1, Pallas kernels, filter_gradient(): pl.pallas_call(functools.partial(filter_kernel, shard_rows), out_shape=(o...  5.64 us
    ppermute x1, starting transfers between devices, body(): from_upper = lax.ppermute(to_lower, 'dom', [(b, a) for a, b in ring])  3.03 us
    pallas_call x1, Pallas kernels, fine_gradient(): pl.pallas_call(functools.partial(fine_kernel, groups), grid=(3 * groups,)...  2.88 us
    pallas_call x1, Pallas kernels, prepare(): pl.pallas_call(prepare_kernel, out_shape=(jax.ShapeDtypeStruct((slots + 1...  2.73 us
    ppermute x1, starting transfers between devices, body(): low = lax.ppermute(own[:, voxels - PLANE:], 'dom', forward)  2.36 us
  transfers between devices with their start and end apart: 26, of which 13 were waited for; matrix products, arithmetic and copies ran while one was open for 0% of the time, Pallas kernels for 17%

profile of v6, /device:TPU:0, one launch (start us, length us, event | category | flops | bytes accessed | tf_op | source)
XLA Modules:
  0.0 77.0 jit_solution(16613279632268073426)
XLA Ops:
  0.7 1.0 %fusion = (bf16[3,64,256]{2,1,0:T(8,128)(2,1)S(1)}, bf16[3,64,256]{2,1,0:T(8,128)(2,1)S(1)}) fusion(bf16[3,512,256]{2,1,0:T(8,128)(2,1)} %bitcast.9), kind=kLoop, calls=%fused_computation | loop fusion | bytes 393216 | tf_op jit(solution)/shard_map/slice | solution.py:627
  1.6 2.4 %collective-permute-start = (bf16[3,64,256]{2,1,0:T(8,128)(2,1)S(1)}, bf16[3,64,256]{2,1,0:T(8,128)(2,1)S(1)}, u32[]{:S(2)}, u32[]{:S(2)}) collective-permute-start(bf16[3,64,256]{2,1,0:T(8,128)(2,1)S(1)} %get-tuple-element.60), channel_id=1, source_target_pairs={{0,1},{1,2},{2,3},{3,4},{4,5},{5,6},{6,7},{8,9},{9,10},{10,11},{11... | collective-permute-start | bytes 294920 | tf_op jit(solution)/shard_map/ppermute | solution.py:626
  4.0 1.3 %collective-permute-start.1 = (bf16[3,64,256]{2,1,0:T(8,128)(2,1)S(1)}, bf16[3,64,256]{2,1,0:T(8,128)(2,1)S(1)}, u32[]{:S(2)}, u32[]{:S(2)}) collective-permute-start(bf16[3,64,256]{2,1,0:T(8,128)(2,1)S(1)} %get-tuple-element.59), channel_id=1, source_target_pairs={{1,0},{2,1},{3,2},{4,3},{5,4},{6,5},{7,6},{9,8},{10,9},{11,10},{12... | collective-permute-start | bytes 294920 | tf_op jit(solution)/shard_map/ppermute | solution.py:627
  5.3 2.7 %prepare.1 = (bf16[4,512,256]{2,1,0:T(8,128)(2,1)S(1)}, bf16[256,1536]{1,0:T(8,128)(2,1)S(1)}, bf16[3,256,2304]{2,1,0:T(8,128)(2,1)S(1)}) custom-call(bf16[1,3,512,256]{3,2,1,0:T(8,128)(2,1)} %own_hbm.1, bf16[1,3,512,256]{3,2,1,0:T(8,128)(2,1)} %pre_hbm.3, bf16[27,256,256]{2,1,0:T(8,128)(2,1)} %weight_hbm.1), custom_call_target="tpu_custom_call" | custom-call | flops 4194304 | bytes 12582912 | tf_op jit(solution)/shard_map/prepare/pallas_call | solution.py:160
  8.0 0.0 collective-permute-done.low_ref
  8.0 1.2 %collective-permute-done.1.high_ref = bf16[3,64,256]{2,1,0:T(8,128)(2,1)S(1)} collective-permute-done((bf16[3,64,256]{2,1,0:T(8,128)(2,1)S(1)}, bf16[3,64,256]{2,1,0:T(8,128)(2,1)S(1)}, u32[]{:S(2)}, u32[]{:S(2)}) %collective-permute-start.1) | collective-permute-done | bytes 98336 | tf_op jit(solution)/shard_map/ppermute | solution.py:627
  9.3 7.6 %input_gradient.1 = (bf16[1,512,256]{2,1,0:T(8,128)(2,1)S(1)}, bf16[1,512,256]{2,1,0:T(8,128)(2,1)S(1)}, bf16[1,512,256]{2,1,0:T(8,128)(2,1)S(1)}, bf16[1920,2304]{1,0:T(8,128)(2,1)S(1)}) custom-call(s32[3,1,27]{2,1,0:T(1,128)S(1)} %bitcast.6, s32[3,1,8]{2,1,0:T(1,128)S(1)} %bitcast.7, bf16[4,512,256]{2,1,0:T(8,128)(2,1)S(1)} %get-tuple-element.31.own_wide, ...), custom_call_target="tpu_custom_call" | custom-call | flops 5435817984 | bytes 8388608 | tf_op jit(solution)/shard_map/input_gradient/pallas_call | solution.py:268
  16.9 3.0 %collective-permute-start.2 = (bf16[1,512,256]{2,1,0:T(8,128)(2,1)S(1)}, bf16[1,512,256]{2,1,0:T(8,128)(2,1)S(1)}, u32[]{:S(2)}, u32[]{:S(2)}) collective-permute-start(bf16[1,512,256]{2,1,0:T(8,128)(2,1)S(1)} %get-tuple-element.33), channel_id=1, source_target_pairs={{1,0},{2,1},{3,2},{4,3},{5,4},{6,5},{7,6},{0,7},{9,8},{10,9},{11,1... | collective-permute-start | bytes 786440 | tf_op jit(solution)/shard_map/ppermute | solution.py:632
  20.0 0.5 collective-permute-start.3
  20.5 5.6 %filter_gradient.1 = (bf16[4,1728,128]{2,1,0:T(8,128)(2,1)S(1)}, bf16[4,1728,128]{2,1,0:T(8,128)(2,1)S(1)}) custom-call(bf16[1920,2304]{1,0:T(8,128)(2,1)S(1)} %get-tuple-element.36.win_ref, bf16[256,1536]{1,0:T(8,128)(2,1)S(1)} %get-tuple-element.37.act_ref), custom_call_target="tpu_custom_call" | custom-call | flops 5435817984 | bytes 8388608 | tf_op jit(solution)/shard_map/filter_gradient/pallas_call | solution.py:324
  26.1 1.6 %collective-permute-start.4 = (bf16[4,1728,128]{2,1,0:T(8,128)(2,1)S(1)}, bf16[4,1728,128]{2,1,0:T(8,128)(2,1)S(1)}, u32[]{:S(2)}, u32[]{:S(2)}) collective-permute-start(bf16[4,1728,128]{2,1,0:T(8,128)(2,1)S(1)} %get-tuple-element.39), channel_id=1, source_target_pairs={{0,1},{1,0},{2,3},{3,2},{4,5},{5,4},{6,7},{7,6},{8,9},{9,8},{10,11... | collective-permute-start | bytes 5308424 | tf_op jit(solution)/shard_map/ppermute | solution.py:639
  27.7 0.0 collective-permute-done.2.upper_ref
  27.7 1.3 %collective-permute-done.3.lower_ref = bf16[1,512,256]{2,1,0:T(8,128)(2,1)S(1)} collective-permute-done((bf16[1,512,256]{2,1,0:T(8,128)(2,1)S(1)}, bf16[1,512,256]{2,1,0:T(8,128)(2,1)S(1)}, u32[]{:S(2)}, u32[]{:S(2)}) %collective-permute-start.3) | collective-permute-done | bytes 262176 | tf_op jit(solution)/shard_map/ppermute | solution.py:633
  29.0 0.0 copy-done.1
  29.0 1.5 %down_gradient.1 = (bf16[4,256,128]{2,1,0:T(8,128)(2,1)S(1)}, bf16[4,256,128]{2,1,0:T(8,128)(2,1)S(1)}) custom-call(bf16[1,512,256]{2,1,0:T(8,128)(2,1)S(1)} %collective-permute-done.2.upper_ref, bf16[1,512,256]{2,1,0:T(8,128)(2,1)S(1)} %get-tuple-element.34.stay_ref, bf16[1,512,256]{2,1,0:T(8,128)(2,1)S(1)} %collective-permute-done.3.lower_ref, ...), custom_call_target="tpu_custom_call" | custom-call | flops 25769803776 | bytes 8388608 | tf_op jit(solution)/shard_map/down_gradient/pallas_call | solution.py:386
  30.6 0.1 collective-permute-start.5
  30.6 1.5 %collective-permute-done.5.down_got_ref = bf16[4,256,128]{2,1,0:T(8,128)(2,1)S(1)} collective-permute-done((bf16[4,256,128]{2,1,0:T(8,128)(2,1)S(1)}, bf16[4,256,128]{2,1,0:T(8,128)(2,1)S(1)}, u32[]{:S(2)}, u32[]{:S(2)}) %collective-permute-start.5) | collective-permute-done | bytes 262176 | tf_op jit(solution)/shard_map/ppermute | solution.py:640
  32.2 0.0 collective-permute-done.4.conv_got_ref
  32.2 0.4 pair_sum.1
  32.6 2.6 %collective-permute-start.6 = (bf16[4,368,128]{2,1,0:T(8,128)(2,1)S(1)}, bf16[4,368,128]{2,1,0:T(8,128)(2,1)S(1)}, u32[]{:S(2)}, u32[]{:S(2)}) collective-permute-start(bf16[4,368,128]{2,1,0:T(8,128)(2,1)S(1)} %get-tuple-element.43), channel_id=1, source_target_pairs={{0,2},{1,3},{2,0},{3,1},{4,6},{5,7},{6,4},{7,5},{8,10},{9,11},{10,... | collective-permute-start | bytes 1130504 | tf_op jit(solution)/shard_map/ppermute | solution.py:48
  35.2 0.0 collective-permute-start.7
  35.2 1.5 %collective-permute-start.8 = (bf16[4,368,128]{2,1,0:T(8,128)(2,1)S(1)}, bf16[4,368,128]{2,1,0:T(8,128)(2,1)S(1)}, u32[]{:S(2)}, u32[]{:S(2)}) collective-permute-start(bf16[4,368,128]{2,1,0:T(8,128)(2,1)S(1)} %get-tuple-element.45), channel_id=1, source_target_pairs={{0,6},{1,7},{2,4},{3,5},{4,2},{5,3},{6,0},{7,1},{8,14},{9,15},{10,... | collective-permute-start | bytes 1130504 | tf_op jit(solution)/shard_map/ppermute | solution.py:48
  36.8 1.6 %collective-permute-start.10 = (bf16[512,128]{1,0:T(8,128)(2,1)S(1)}, bf16[512,128]{1,0:T(8,128)(2,1)S(1)}, u32[]{:S(2)}, u32[]{:S(2)}) collective-permute-start(bf16[512,128]{1,0:T(8,128)(2,1)S(1)} %get-tuple-element.48), channel_id=1, source_target_pairs={{0,8},{8,0},{16,24},{24,16},{1,9},{9,1},{17,25},{25,17},{2,10},{10... | collective-permute-start | bytes 393224 | tf_op jit(solution)/shard_map/ppermute | solution.py:48
  38.3 2.6 %collective-permute-start.11 = (bf16[512,128]{1,0:T(8,128)(2,1)S(1)}, bf16[512,128]{1,0:T(8,128)(2,1)S(1)}, u32[]{:S(2)}, u32[]{:S(2)}) collective-permute-start(bf16[512,128]{1,0:T(8,128)(2,1)S(1)} %get-tuple-element.49), channel_id=1, source_target_pairs={{0,16},{8,24},{16,0},{24,8},{1,17},{9,25},{17,1},{25,9},{2,18},{10... | collective-permute-start | bytes 393224 | tf_op jit(solution)/shard_map/ppermute | solution.py:48
  40.9 3.0 %collective-permute-done.10.refs_6_ = bf16[512,128]{1,0:T(8,128)(2,1)S(1)} collective-permute-done((bf16[512,128]{1,0:T(8,128)(2,1)S(1)}, bf16[512,128]{1,0:T(8,128)(2,1)S(1)}, u32[]{:S(2)}, u32[]{:S(2)}) %collective-permute-start.10) | collective-permute-done | bytes 131104 | tf_op jit(solution)/shard_map/ppermute | solution.py:48
  43.9 3.2 %collective-permute-start.9 = (bf16[512,128]{1,0:T(8,128)(2,1)S(1)}, bf16[512,128]{1,0:T(8,128)(2,1)S(1)}, u32[]{:S(2)}, u32[]{:S(2)}) collective-permute-start(bf16[512,128]{1,0:T(8,128)(2,1)S(1)} %get-tuple-element.47), channel_id=1, source_target_pairs={{0,24},{8,16},{16,8},{24,0},{1,25},{9,17},{17,9},{25,1},{2,26},{10... | collective-permute-start | bytes 393224 | tf_op jit(solution)/shard_map/ppermute | solution.py:48
  47.1 1.8 %collective-permute-done.11.refs_7_ = bf16[512,128]{1,0:T(8,128)(2,1)S(1)} collective-permute-done((bf16[512,128]{1,0:T(8,128)(2,1)S(1)}, bf16[512,128]{1,0:T(8,128)(2,1)S(1)}, u32[]{:S(2)}, u32[]{:S(2)}) %collective-permute-start.11) | collective-permute-done | bytes 131104 | tf_op jit(solution)/shard_map/ppermute | solution.py:48
  48.9 1.9 %collective-permute-done.9.refs_5_ = bf16[512,128]{1,0:T(8,128)(2,1)S(1)} collective-permute-done((bf16[512,128]{1,0:T(8,128)(2,1)S(1)}, bf16[512,128]{1,0:T(8,128)(2,1)S(1)}, u32[]{:S(2)}, u32[]{:S(2)}) %collective-permute-start.9) | collective-permute-done | bytes 131104 | tf_op jit(solution)/shard_map/ppermute | solution.py:48
  50.8 0.0 collective-permute-done.6.refs_1_
  50.8 3.2 %collective-permute-done.7.refs_2_ = bf16[4,368,128]{2,1,0:T(8,128)(2,1)S(1)} collective-permute-done((bf16[4,368,128]{2,1,0:T(8,128)(2,1)S(1)}, bf16[4,368,128]{2,1,0:T(8,128)(2,1)S(1)}, u32[]{:S(2)}, u32[]{:S(2)}) %collective-permute-start.7) | collective-permute-done | bytes 376864 | tf_op jit(solution)/shard_map/ppermute | solution.py:48
  54.0 0.0 collective-permute-done.8.refs_3_
  54.0 0.3 middle_sum.1
  54.3 3.7 %collective-permute-start.12 = (bf16[368,128]{1,0:T(8,128)(2,1)S(1)}, bf16[368,128]{1,0:T(8,128)(2,1)S(1)}, u32[]{:S(2)}, u32[]{:S(2)}) collective-permute-start(bf16[368,128]{1,0:T(8,128)(2,1)S(1)} %get-tuple-element.51), channel_id=1, source_target_pairs={{0,24},{8,16},{16,8},{24,0},{1,25},{9,17},{17,9},{25,1},{2,26},{10... | collective-permute-start | bytes 282632 | tf_op jit(solution)/shard_map/ppermute | solution.py:48
  58.0 0.4 collective-permute-start.15
  58.3 1.4 %collective-permute-start.16 = (bf16[512,128]{1,0:T(8,128)(2,1)S(1)}, bf16[512,128]{1,0:T(8,128)(2,1)S(1)}, u32[]{:S(2)}, u32[]{:S(2)}) collective-permute-start(bf16[512,128]{1,0:T(8,128)(2,1)S(1)} %get-tuple-element.54.refs_4_), channel_id=1, source_target_pairs={{0,4},{1,5},{2,6},{3,7},{4,0},{5,1},{6,2},{7,3},{8,12},{9,13},{10,... | collective-permute-start | bytes 393224 | tf_op jit(solution)/shard_map/ppermute | solution.py:48
  59.7 1.8 %collective-permute-start.17 = (bf16[512,128]{1,0:T(8,128)(2,1)S(1)}, bf16[512,128]{1,0:T(8,128)(2,1)S(1)}, u32[]{:S(2)}, u32[]{:S(2)}) collective-permute-start(bf16[512,128]{1,0:T(8,128)(2,1)S(1)} %get-tuple-element.54.refs_4_), channel_id=1, source_target_pairs={{0,6},{1,7},{2,4},{3,5},{4,2},{5,3},{6,0},{7,1},{8,14},{9,15},{10,... | collective-permute-start | bytes 393224 | tf_op jit(solution)/shard_map/ppermute | solution.py:48
  61.5 0.0 collective-permute-start.13
  61.5 0.0 collective-permute-done.12.refs_1_
  61.5 0.8 %collective-permute-start.14 = (bf16[368,128]{1,0:T(8,128)(2,1)S(1)}, bf16[368,128]{1,0:T(8,128)(2,1)S(1)}, u32[]{:S(2)}, u32[]{:S(2)}) collective-permute-start(bf16[368,128]{1,0:T(8,128)(2,1)S(1)} %get-tuple-element.53), channel_id=1, source_target_pairs={{0,8},{8,0},{16,24},{24,16},{1,9},{9,1},{17,25},{25,17},{2,10},{10... | collective-permute-start | bytes 282632 | tf_op jit(solution)/shard_map/ppermute | solution.py:48
  62.2 0.0 copy-done
  62.2 2.9 %fine_gradient.1.refs_8_ = bf16[24,512,128]{2,1,0:T(8,128)(2,1)} custom-call(bf16[1,512,256]{2,1,0:T(8,128)(2,1)S(1)} %collective-permute-done.2.upper_ref, bf16[1,512,256]{2,1,0:T(8,128)(2,1)S(1)} %get-tuple-element.34.stay_ref, bf16[1,512,256]{2,1,0:T(8,128)(2,1)S(1)} %collective-permute-done.3.lower_ref, bf16[8,128,256]{2,1,0:T(8,128)(2,1)S(1)} %copy-done), custom_call_target="tpu_custom_call" | custom-call | flops 805306368 | bytes 4194304 | tf_op jit(solution)/shard_map/fine_gradient/pallas_call | solution.py:431
  65.1 2.2 %collective-permute-done.13.refs_2_ = bf16[368,128]{1,0:T(8,128)(2,1)S(1)} collective-permute-done((bf16[368,128]{1,0:T(8,128)(2,1)S(1)}, bf16[368,128]{1,0:T(8,128)(2,1)S(1)}, u32[]{:S(2)}, u32[]{:S(2)}) %collective-permute-start.13) | collective-permute-done | bytes 94240 | tf_op jit(solution)/shard_map/ppermute | solution.py:48
  67.3 0.0 collective-permute-done.14.refs_3_
  67.3 0.0 collective-permute-done.15.refs_5_
  67.3 0.0 collective-permute-done.16.refs_6_
  67.3 0.0 collective-permute-done.17.refs_7_
  67.3 0.1 last_sum.1
  67.4 1.4 %collective-permute-start.18 = (bf16[368,128]{1,0:T(8,128)(2,1)S(1)}, bf16[368,128]{1,0:T(8,128)(2,1)S(1)}, u32[]{:S(2)}, u32[]{:S(2)}) collective-permute-start(bf16[368,128]{1,0:T(8,128)(2,1)S(1)} %get-tuple-element.55.refs_0_), channel_id=1, source_target_pairs={{0,6},{1,7},{2,4},{3,5},{4,2},{5,3},{6,0},{7,1},{8,14},{9,15},{10,... | collective-permute-start | bytes 282632 | tf_op jit(solution)/shard_map/ppermute | solution.py:48
  68.8 0.6 collective-permute-start.19
  69.5 1.5 %collective-permute-start.20 = (bf16[368,128]{1,0:T(8,128)(2,1)S(1)}, bf16[368,128]{1,0:T(8,128)(2,1)S(1)}, u32[]{:S(2)}, u32[]{:S(2)}) collective-permute-start(bf16[368,128]{1,0:T(8,128)(2,1)S(1)} %get-tuple-element.55.refs_0_), channel_id=1, source_target_pairs={{0,2},{1,3},{2,0},{3,1},{4,6},{5,7},{6,4},{7,5},{8,10},{9,11},{10,... | collective-permute-start | bytes 282632 | tf_op jit(solution)/shard_map/ppermute | solution.py:48
  71.0 0.0 collective-permute-start.25
  71.0 0.5 collective-permute-start.21
  71.5 1.5 %collective-permute-done.18.refs_1_ = bf16[368,128]{1,0:T(8,128)(2,1)S(1)} collective-permute-done((bf16[368,128]{1,0:T(8,128)(2,1)S(1)}, bf16[368,128]{1,0:T(8,128)(2,1)S(1)}, u32[]{:S(2)}, u32[]{:S(2)}) %collective-permute-start.18) | collective-permute-done | bytes 94240 | tf_op jit(solution)/shard_map/ppermute | solution.py:48
  73.0 0.0 collective-permute-start.22
  73.0 0.9 %collective-permute-done.19.refs_2_ = bf16[368,128]{1,0:T(8,128)(2,1)S(1)} collective-permute-done((bf16[368,128]{1,0:T(8,128)(2,1)S(1)}, bf16[368,128]{1,0:T(8,128)(2,1)S(1)}, u32[]{:S(2)}, u32[]{:S(2)}) %collective-permute-start.19) | collective-permute-done | bytes 94240 | tf_op jit(solution)/shard_map/ppermute | solution.py:48
  74.0 0.0 collective-permute-start.23
  74.0 0.1 collective-permute-done.20.refs_3_
  74.0 0.5 collective-permute-start.24
  74.5 0.0 collective-permute-done.21.refs_4_
  74.5 0.0 collective-permute-done.25.refs_9_
  74.5 0.0 collective-permute-done.22.refs_5_
  74.5 0.8 collective-permute-done.23.refs_6_
  75.3 0.2 collective-permute-done.24.refs_7_
  75.4 1.6 %gather_up.1 = (f32[1728,256]{1,0:T(8,128)}, f32[256,256]{1,0:T(8,128)}) custom-call(bf16[368,128]{1,0:T(8,128)(2,1)S(1)} %get-tuple-element.55.refs_0_, bf16[368,128]{1,0:T(8,128)(2,1)S(1)} %collective-permute-done.18.refs_1_, bf16[368,128]{1,0:T(8,128)(2,1)S(1)} %collective-permute-done.19.refs_2_, bf16[368,128]{1,0:T(8,128)(2,1)S(1)} %collective-permute-done.20.refs_3_, ...), custom_call_target="tpu_custom_call" | custom-call | flops 2785280 | bytes 2785280 | tf_op jit(solution)/shard_map/gather_up/pallas_call | solution.py:590
  (6 shorter events, 0.0 us)
Async XLA Ops:
  0.6 8.7 %copy-start.2 = (s32[1,3,27]{2,0,1:T(1,128)S(1)}, s32[1,3,27]{2,0,1:T(1,128)}, u32[]{:S(2)}) copy-start(s32[1,3,27]{2,0,1:T(1,128)} %param.12) | copy-start | bytes 976
  0.6 8.7 %copy-start.3 = (s32[1,1,3,8]{3,1,2,0:T(1,128)S(1)}, s32[1,1,3,8]{3,1,2,0:T(1,128)}, u32[]{:S(2)}) copy-start(s32[1,1,3,8]{3,1,2,0:T(1,128)} %param.13) | copy-start | bytes 292
  1.6 6.4 %collective-permute-start = (bf16[3,64,256]{2,1,0:T(8,128)(2,1)S(1)}, bf16[3,64,256]{2,1,0:T(8,128)(2,1)S(1)}, u32[]{:S(2)}, u32[]{:S(2)}) collective-permute-start(bf16[3,64,256]{2,1,0:T(8,128)(2,1)S(1)} %get-tuple-element.60), channel_id=1, source_target_pairs={{0,1},{1,2},{2,3},{3,4},{4,5},{5,6},{6,7},{8,9},{9,10},{10,11},{11... | collective-permute-start | bytes 294920 | tf_op jit(solution)/shard_map/ppermute | solution.py:626
  4.0 5.3 %collective-permute-start.1 = (bf16[3,64,256]{2,1,0:T(8,128)(2,1)S(1)}, bf16[3,64,256]{2,1,0:T(8,128)(2,1)S(1)}, u32[]{:S(2)}, u32[]{:S(2)}) collective-permute-start(bf16[3,64,256]{2,1,0:T(8,128)(2,1)S(1)} %get-tuple-element.59), channel_id=1, source_target_pairs={{1,0},{2,1},{3,2},{4,3},{5,4},{6,5},{7,6},{9,8},{10,9},{11,10},{12... | collective-permute-start | bytes 294920 | tf_op jit(solution)/shard_map/ppermute | solution.py:627
  16.9 10.8 %collective-permute-start.2 = (bf16[1,512,256]{2,1,0:T(8,128)(2,1)S(1)}, bf16[1,512,256]{2,1,0:T(8,128)(2,1)S(1)}, u32[]{:S(2)}, u32[]{:S(2)}) collective-permute-start(bf16[1,512,256]{2,1,0:T(8,128)(2,1)S(1)} %get-tuple-element.33), channel_id=1, source_target_pairs={{1,0},{2,1},{3,2},{4,3},{5,4},{6,5},{7,6},{0,7},{9,8},{10,9},{11,1... | collective-permute-start | bytes 786440 | tf_op jit(solution)/shard_map/ppermute | solution.py:632
  20.0 9.1 %collective-permute-start.3 = (bf16[1,512,256]{2,1,0:T(8,128)(2,1)S(1)}, bf16[1,512,256]{2,1,0:T(8,128)(2,1)S(1)}, u32[]{:S(2)}, u32[]{:S(2)}) collective-permute-start(bf16[1,512,256]{2,1,0:T(8,128)(2,1)S(1)} %get-tuple-element.35), channel_id=1, source_target_pairs={{0,1},{1,2},{2,3},{3,4},{4,5},{5,6},{6,7},{7,0},{8,9},{9,10},{10,1... | collective-permute-start | bytes 786440 | tf_op jit(solution)/shard_map/ppermute | solution.py:633
  20.5 8.6 %copy-start.1 = (bf16[1,24,512,128]{3,2,1,0:T(8,128)(2,1)S(1)}, bf16[1,24,512,128]{3,2,1,0:T(8,128)(2,1)}, u32[]{:S(2)}) copy-start(bf16[1,24,512,128]{3,2,1,0:T(8,128)(2,1)} %param.11) | copy-start | bytes 9437188
  26.1 6.0 %collective-permute-start.4 = (bf16[4,1728,128]{2,1,0:T(8,128)(2,1)S(1)}, bf16[4,1728,128]{2,1,0:T(8,128)(2,1)S(1)}, u32[]{:S(2)}, u32[]{:S(2)}) collective-permute-start(bf16[4,1728,128]{2,1,0:T(8,128)(2,1)S(1)} %get-tuple-element.39), channel_id=1, source_target_pairs={{0,1},{1,0},{2,3},{3,2},{4,5},{5,4},{6,7},{7,6},{8,9},{9,8},{10,11... | collective-permute-start | bytes 5308424 | tf_op jit(solution)/shard_map/ppermute | solution.py:639
  30.6 1.6 %collective-permute-start.5 = (bf16[4,256,128]{2,1,0:T(8,128)(2,1)S(1)}, bf16[4,256,128]{2,1,0:T(8,128)(2,1)S(1)}, u32[]{:S(2)}, u32[]{:S(2)}) collective-permute-start(bf16[4,256,128]{2,1,0:T(8,128)(2,1)S(1)} %get-tuple-element.41), channel_id=1, source_target_pairs={{0,1},{1,0},{2,3},{3,2},{4,5},{5,4},{6,7},{7,6},{8,9},{9,8},{10,11... | collective-permute-start | bytes 786440 | tf_op jit(solution)/shard_map/ppermute | solution.py:640
  32.2 30.1 %copy-start = (bf16[8,128,256]{2,1,0:T(8,128)(2,1)S(1)}, bf16[8,128,256]{2,1,0:T(8,128)(2,1)}, u32[]{:S(2)}) copy-start(bf16[8,128,256]{2,1,0:T(8,128)(2,1)} %weight_ref.1) | copy-start | bytes 1572868
  32.6 18.2 %collective-permute-start.6 = (bf16[4,368,128]{2,1,0:T(8,128)(2,1)S(1)}, bf16[4,368,128]{2,1,0:T(8,128)(2,1)S(1)}, u32[]{:S(2)}, u32[]{:S(2)}) collective-permute-start(bf16[4,368,128]{2,1,0:T(8,128)(2,1)S(1)} %get-tuple-element.43), channel_id=1, source_target_pairs={{0,2},{1,3},{2,0},{3,1},{4,6},{5,7},{6,4},{7,5},{8,10},{9,11},{10,... | collective-permute-start | bytes 1130504 | tf_op jit(solution)/shard_map/ppermute | solution.py:48
  35.2 18.8 %collective-permute-start.7 = (bf16[4,368,128]{2,1,0:T(8,128)(2,1)S(1)}, bf16[4,368,128]{2,1,0:T(8,128)(2,1)S(1)}, u32[]{:S(2)}, u32[]{:S(2)}) collective-permute-start(bf16[4,368,128]{2,1,0:T(8,128)(2,1)S(1)} %get-tuple-element.44), channel_id=1, source_target_pairs={{0,4},{1,5},{2,6},{3,7},{4,0},{5,1},{6,2},{7,3},{8,12},{9,13},{10,... | collective-permute-start | bytes 1130504 | tf_op jit(solution)/shard_map/ppermute | solution.py:48
  35.2 18.8 %collective-permute-start.8 = (bf16[4,368,128]{2,1,0:T(8,128)(2,1)S(1)}, bf16[4,368,128]{2,1,0:T(8,128)(2,1)S(1)}, u32[]{:S(2)}, u32[]{:S(2)}) collective-permute-start(bf16[4,368,128]{2,1,0:T(8,128)(2,1)S(1)} %get-tuple-element.45), channel_id=1, source_target_pairs={{0,6},{1,7},{2,4},{3,5},{4,2},{5,3},{6,0},{7,1},{8,14},{9,15},{10,... | collective-permute-start | bytes 1130504 | tf_op jit(solution)/shard_map/ppermute | solution.py:48
  36.8 7.2 %collective-permute-start.10 = (bf16[512,128]{1,0:T(8,128)(2,1)S(1)}, bf16[512,128]{1,0:T(8,128)(2,1)S(1)}, u32[]{:S(2)}, u32[]{:S(2)}) collective-permute-start(bf16[512,128]{1,0:T(8,128)(2,1)S(1)} %get-tuple-element.48), channel_id=1, source_target_pairs={{0,8},{8,0},{16,24},{24,16},{1,9},{9,1},{17,25},{25,17},{2,10},{10... | collective-permute-start | bytes 393224 | tf_op jit(solution)/shard_map/ppermute | solution.py:48
  38.3 10.6 %collective-permute-start.11 = (bf16[512,128]{1,0:T(8,128)(2,1)S(1)}, bf16[512,128]{1,0:T(8,128)(2,1)S(1)}, u32[]{:S(2)}, u32[]{:S(2)}) collective-permute-start(bf16[512,128]{1,0:T(8,128)(2,1)S(1)} %get-tuple-element.49), channel_id=1, source_target_pairs={{0,16},{8,24},{16,0},{24,8},{1,17},{9,25},{17,1},{25,9},{2,18},{10... | collective-permute-start | bytes 393224 | tf_op jit(solution)/shard_map/ppermute | solution.py:48
  43.9 6.9 %collective-permute-start.9 = (bf16[512,128]{1,0:T(8,128)(2,1)S(1)}, bf16[512,128]{1,0:T(8,128)(2,1)S(1)}, u32[]{:S(2)}, u32[]{:S(2)}) collective-permute-start(bf16[512,128]{1,0:T(8,128)(2,1)S(1)} %get-tuple-element.47), channel_id=1, source_target_pairs={{0,24},{8,16},{16,8},{24,0},{1,25},{9,17},{17,9},{25,1},{2,26},{10... | collective-permute-start | bytes 393224 | tf_op jit(solution)/shard_map/ppermute | solution.py:48
  54.3 7.2 %collective-permute-start.12 = (bf16[368,128]{1,0:T(8,128)(2,1)S(1)}, bf16[368,128]{1,0:T(8,128)(2,1)S(1)}, u32[]{:S(2)}, u32[]{:S(2)}) collective-permute-start(bf16[368,128]{1,0:T(8,128)(2,1)S(1)} %get-tuple-element.51), channel_id=1, source_target_pairs={{0,24},{8,16},{16,8},{24,0},{1,25},{9,17},{17,9},{25,1},{2,26},{10... | collective-permute-start | bytes 282632 | tf_op jit(solution)/shard_map/ppermute | solution.py:48
  58.0 9.3 %collective-permute-start.15 = (bf16[512,128]{1,0:T(8,128)(2,1)S(1)}, bf16[512,128]{1,0:T(8,128)(2,1)S(1)}, u32[]{:S(2)}, u32[]{:S(2)}) collective-permute-start(bf16[512,128]{1,0:T(8,128)(2,1)S(1)} %get-tuple-element.54.refs_4_), channel_id=1, source_target_pairs={{0,2},{1,3},{2,0},{3,1},{4,6},{5,7},{6,4},{7,5},{8,10},{9,11},{10,... | collective-permute-start | bytes 393224 | tf_op jit(solution)/shard_map/ppermute | solution.py:48
  58.3 9.0 %collective-permute-start.16 = (bf16[512,128]{1,0:T(8,128)(2,1)S(1)}, bf16[512,128]{1,0:T(8,128)(2,1)S(1)}, u32[]{:S(2)}, u32[]{:S(2)}) collective-permute-start(bf16[512,128]{1,0:T(8,128)(2,1)S(1)} %get-tuple-element.54.refs_4_), channel_id=1, source_target_pairs={{0,4},{1,5},{2,6},{3,7},{4,0},{5,1},{6,2},{7,3},{8,12},{9,13},{10,... | collective-permute-start | bytes 393224 | tf_op jit(solution)/shard_map/ppermute | solution.py:48
  59.7 7.6 %collective-permute-start.17 = (bf16[512,128]{1,0:T(8,128)(2,1)S(1)}, bf16[512,128]{1,0:T(8,128)(2,1)S(1)}, u32[]{:S(2)}, u32[]{:S(2)}) collective-permute-start(bf16[512,128]{1,0:T(8,128)(2,1)S(1)} %get-tuple-element.54.refs_4_), channel_id=1, source_target_pairs={{0,6},{1,7},{2,4},{3,5},{4,2},{5,3},{6,0},{7,1},{8,14},{9,15},{10,... | collective-permute-start | bytes 393224 | tf_op jit(solution)/shard_map/ppermute | solution.py:48
  61.5 5.8 %collective-permute-start.13 = (bf16[368,128]{1,0:T(8,128)(2,1)S(1)}, bf16[368,128]{1,0:T(8,128)(2,1)S(1)}, u32[]{:S(2)}, u32[]{:S(2)}) collective-permute-start(bf16[368,128]{1,0:T(8,128)(2,1)S(1)} %get-tuple-element.52), channel_id=1, source_target_pairs={{0,16},{8,24},{16,0},{24,8},{1,17},{9,25},{17,1},{25,9},{2,18},{10... | collective-permute-start | bytes 282632 | tf_op jit(solution)/shard_map/ppermute | solution.py:48
  61.5 5.8 %collective-permute-start.14 = (bf16[368,128]{1,0:T(8,128)(2,1)S(1)}, bf16[368,128]{1,0:T(8,128)(2,1)S(1)}, u32[]{:S(2)}, u32[]{:S(2)}) collective-permute-start(bf16[368,128]{1,0:T(8,128)(2,1)S(1)} %get-tuple-element.53), channel_id=1, source_target_pairs={{0,8},{8,0},{16,24},{24,16},{1,9},{9,1},{17,25},{25,17},{2,10},{10... | collective-permute-start | bytes 282632 | tf_op jit(solution)/shard_map/ppermute | solution.py:48
  67.4 5.6 %collective-permute-start.18 = (bf16[368,128]{1,0:T(8,128)(2,1)S(1)}, bf16[368,128]{1,0:T(8,128)(2,1)S(1)}, u32[]{:S(2)}, u32[]{:S(2)}) collective-permute-start(bf16[368,128]{1,0:T(8,128)(2,1)S(1)} %get-tuple-element.55.refs_0_), channel_id=1, source_target_pairs={{0,6},{1,7},{2,4},{3,5},{4,2},{5,3},{6,0},{7,1},{8,14},{9,15},{10,... | collective-permute-start | bytes 282632 | tf_op jit(solution)/shard_map/ppermute | solution.py:48
  68.8 5.2 %collective-permute-start.19 = (bf16[368,128]{1,0:T(8,128)(2,1)S(1)}, bf16[368,128]{1,0:T(8,128)(2,1)S(1)}, u32[]{:S(2)}, u32[]{:S(2)}) collective-permute-start(bf16[368,128]{1,0:T(8,128)(2,1)S(1)} %get-tuple-element.55.refs_0_), channel_id=1, source_target_pairs={{0,4},{1,5},{2,6},{3,7},{4,0},{5,1},{6,2},{7,3},{8,12},{9,13},{10,... | collective-permute-start | bytes 282632 | tf_op jit(solution)/shard_map/ppermute | solution.py:48
  69.5 4.6 %collective-permute-start.20 = (bf16[368,128]{1,0:T(8,128)(2,1)S(1)}, bf16[368,128]{1,0:T(8,128)(2,1)S(1)}, u32[]{:S(2)}, u32[]{:S(2)}) collective-permute-start(bf16[368,128]{1,0:T(8,128)(2,1)S(1)} %get-tuple-element.55.refs_0_), channel_id=1, source_target_pairs={{0,2},{1,3},{2,0},{3,1},{4,6},{5,7},{6,4},{7,5},{8,10},{9,11},{10,... | collective-permute-start | bytes 282632 | tf_op jit(solution)/shard_map/ppermute | solution.py:48
  71.0 3.5 %collective-permute-start.25 = (bf16[512,128]{1,0:T(8,128)(2,1)S(1)}, bf16[512,128]{1,0:T(8,128)(2,1)S(1)}, u32[]{:S(2)}, u32[]{:S(2)}) collective-permute-start(bf16[512,128]{1,0:T(8,128)(2,1)S(1)} %get-tuple-element.56.refs_8_), channel_id=1, source_target_pairs={{0,1},{1,0},{2,3},{3,2},{4,5},{5,4},{6,7},{7,6},{8,9},{9,8},{10,11... | collective-permute-start | bytes 393224 | tf_op jit(solution)/shard_map/ppermute | solution.py:650
  71.0 3.5 %collective-permute-start.21 = (bf16[368,128]{1,0:T(8,128)(2,1)S(1)}, bf16[368,128]{1,0:T(8,128)(2,1)S(1)}, u32[]{:S(2)}, u32[]{:S(2)}) collective-permute-start(bf16[368,128]{1,0:T(8,128)(2,1)S(1)} %get-tuple-element.55.refs_0_), channel_id=1, source_target_pairs={{0,1},{1,0},{2,3},{3,2},{4,5},{5,4},{6,7},{7,6},{8,9},{9,8},{10,11... | collective-permute-start | bytes 282632 | tf_op jit(solution)/shard_map/ppermute | solution.py:649
  73.0 1.5 %collective-permute-start.22 = (bf16[368,128]{1,0:T(8,128)(2,1)S(1)}, bf16[368,128]{1,0:T(8,128)(2,1)S(1)}, u32[]{:S(2)}, u32[]{:S(2)}) collective-permute-start(bf16[368,128]{1,0:T(8,128)(2,1)S(1)} %collective-permute-done.18.refs_1_), channel_id=1, source_target_pairs={{0,1},{1,0},{2,3},{3,2},{4,5},{5,4},{6,7},{7,6},{8,9},{9,8},{10,11... | collective-permute-start | bytes 282632 | tf_op jit(solution)/shard_map/ppermute | solution.py:649
  74.0 1.3 %collective-permute-start.23 = (bf16[368,128]{1,0:T(8,128)(2,1)S(1)}, bf16[368,128]{1,0:T(8,128)(2,1)S(1)}, u32[]{:S(2)}, u32[]{:S(2)}) collective-permute-start(bf16[368,128]{1,0:T(8,128)(2,1)S(1)} %collective-permute-done.19.refs_2_), channel_id=1, source_target_pairs={{0,1},{1,0},{2,3},{3,2},{4,5},{5,4},{6,7},{7,6},{8,9},{9,8},{10,11... | collective-permute-start | bytes 282632 | tf_op jit(solution)/shard_map/ppermute | solution.py:649
  74.0 1.4 %collective-permute-start.24 = (bf16[368,128]{1,0:T(8,128)(2,1)S(1)}, bf16[368,128]{1,0:T(8,128)(2,1)S(1)}, u32[]{:S(2)}, u32[]{:S(2)}) collective-permute-start(bf16[368,128]{1,0:T(8,128)(2,1)S(1)} %collective-permute-done.20.refs_3_), channel_id=1, source_target_pairs={{0,1},{1,0},{2,3},{3,2},{4,5},{5,4},{6,7},{7,6},{8,9},{9,8},{10,11... | collective-permute-start | bytes 282632 | tf_op jit(solution)/shard_map/ppermute | solution.py:649

commit v7 on v6

--- a/solution.py
+++ b/solution.py
@@ -14,7 +14,7 @@
 F32 = jnp.float32
 BF16 = jnp.bfloat16
 MIB = 1 << 20
-PLANE_FIRST = 0.74
+PLANE_FIRST = 0.7
 
 VMEM = pl.BlockSpec(memory_space=pltpu.VMEM)
 SMEM = pl.BlockSpec(memory_space=pltpu.SMEM)
@@ -250,11 +250,23 @@
     last = products(2)
     last[0]()
     interleave(last[1:], finishes(range(HALF)))
+    outs = []
+
+    def leave(side):
+        rows = pl.ds(side * 4 * PLANE, 4 * PLANE)
+        for row, ref in enumerate((to_lower_ref, stay_ref, to_upper_ref)):
+            outs.append(
+                started(
+                    octants_ref.at[pl.ds(row * groups, groups), rows],
+                    ref.at[:, rows],
+                    out_sems.at[3 * side + row],
+                )
+            )
+
+    leave(0)
     for call in finishes(range(HALF, BE)):
         call()
-    outs = []
-    for row, ref in enumerate((to_lower_ref, stay_ref, to_upper_ref)):
-        outs.append(started(octants_ref.at[pl.ds(row * groups, groups)], ref, out_sems.at[row]))
+    leave(1)
     for copy in outs:
         copy.wait()
 
@@ -276,7 +288,7 @@
             pltpu.VMEM((rows, channels), F32),
             pltpu.VMEM((3 * groups + 1, voxels, channels), BF16),
             pltpu.VMEM((slots, voxels, channels), BF16),
-            pltpu.SemaphoreType.DMA((3,)),
+            pltpu.SemaphoreType.DMA((6,)),
             pltpu.SemaphoreType.DMA,
         ],
         compiler_params=params(20),
@@ -484,7 +496,7 @@
         total = conv_ref[shard, cut:, :].astype(F32) + conv_got_ref[shard, cut:, :].astype(F32)
         ref[...] = total.astype(ref.dtype)
     high = lax.axis_index("dom") // 2
-    for step, ref in enumerate(planes):
+    for step, ref in zip(far_first(count), planes):
         place = relative(high, step, count)
         for keep_ref, got_ref, size, start in (
             (conv_ref, conv_got_ref, piece, 0),
@@ -565,22 +577,30 @@
 
 def gather_kernel(count, piece, down_piece, *refs):
     near, far = refs[:count], refs[count : 2 * count]
-    rest_ref, rest_far_ref, conv_ref, down_ref, conv_whole, down_whole = refs[2 * count :]
+    rest_ref, rest_far_ref, conv_ref, down_ref, conv_whole, down_whole, sems = refs[2 * count :]
     lanes = rest_ref.shape[1]
     cut = count * piece
     high = lax.axis_index("dom") // 2
     low = lax.rem(lax.axis_index("dom"), 2)
-    for side, group, rest in ((low, near, rest_ref), (1 - low, far, rest_far_ref)):
-        lane = pl.ds(pl.multiple_of(side * lanes, lanes), lanes)
-        for step, ref in zip(far_first(count), group):
-            place = source_of(high, step, count)
-            row = pl.multiple_of(place * piece, 16)
-            conv_whole[pl.ds(row, piece), lane] = ref[:piece, :].astype(F32)
-            row = pl.multiple_of(place * down_piece, 16)
-            down_whole[pl.ds(row, down_piece), lane] = ref[piece:, :].astype(F32)
-        conv_whole[cut:, lane] = rest[...].astype(F32)
-    conv_ref[...] = conv_whole[...]
-    down_ref[...] = down_whole[: down_ref.shape[0]]
+    own = pl.ds(pl.multiple_of(low * lanes, lanes), lanes)
+    other = pl.ds(pl.multiple_of((1 - low) * lanes, lanes), lanes)
+    conv_whole[cut:, own] = rest_ref[...].astype(F32)
+    conv_whole[cut:, other] = rest_far_ref[...].astype(F32)
+    tail = pl.ds(cut, conv_ref.shape[0] - cut)
+    copies = [started(conv_whole.at[tail], conv_ref.at[tail], sems.at[0])]
+    for index, step in enumerate(far_first(count)):
+        place = source_of(high, step, count)
+        rows = pl.ds(pl.multiple_of(place * piece, 16), piece)
+        down_rows = pl.ds(pl.multiple_of(place * down_piece, 16), down_piece)
+        for lane, ref in ((own, near[index]), (other, far[index])):
+            conv_whole[rows, lane] = ref[:piece, :].astype(F32)
+            down_whole[down_rows, lane] = ref[piece:, :].astype(F32)
+        copies.append(started(conv_whole.at[rows], conv_ref.at[rows], sems.at[index + 1]))
+    copies.append(
+        started(down_whole.at[pl.ds(0, down_ref.shape[0])], down_ref, sems.at[count + 1])
+    )
+    for copy in copies:
+        copy.wait()
 
 
 def gather_up(conv_rows, down_rows, pieces, near, far, rest, rest_far):
@@ -591,10 +611,11 @@
         functools.partial(gather_kernel, count, *pieces),
         out_shape=outs,
         in_specs=[VMEM] * (2 * count + 2),
-        out_specs=[VMEM] * 2,
+        out_specs=[ANY] * 2,
         scratch_shapes=[
             pltpu.VMEM((conv_rows, 2 * lanes), F32),
             pltpu.VMEM((count * pieces[1], 2 * lanes), F32),
+            pltpu.SemaphoreType.DMA((count + 2,)),
         ],
         compiler_params=params(32),
         cost_estimate=cost(*near, *far, *outs),
@@ -641,7 +662,7 @@
 
     planes, slabs, pieces = pair_sum(count, conv_keep, conv_got, down_keep, down_got)
     slabs = spread_out(slabs, "dp", 1, farthest_then_nearest(shards))
-    planes = spread_out(planes, "dom", 2)
+    planes = spread_out(planes, "dom", 2, far_first(count))
     to_slabs, rest = middle_sum(planes, slabs)
     to_slabs = spread_out(to_slabs, "dp", 1, far_first(shards))
     mine, rest = last_sum(factor, to_slabs, spread_out([rest] * count, "dom", 2), fine_grad)

time: 77.3 us -> 78.1 us (1.010)
  waiting for transfers between devices: 19.6 us -> 18.2 us
  Pallas kernels: 22.8 us -> 23.9 us
  starting transfers between devices: 32.8 us -> 33.8 us
    ppermute x15, waiting for transfers between devices: 14.6 us -> 12.9 us  [exchange(): return lax.ppermute(value, axis, pairs)]
    ppermute x15, starting transfers between devices: 23 us -> 24.4 us  [exchange(): return lax.ppermute(value, axis, pairs)]
    pallas_call x1, Pallas kernels: 7.64 us -> 8.9 us  [input_gradient(): pl.pallas_call(input_kernel, out_shape=(out, out, out, windows), in_specs...]
  transfers between devices with their start and end apart: 26 -> 26, of which waited for: 13 -> 13; matrix products, arithmetic and copies ran while one was open for 0% -> 0% of each run, Pallas kernels for 17% -> 16%
where the time goes in v7:
time: 78.1 us; the launch traced here: 77.9 us
  starting transfers between devices  33.8 us (43%)
  Pallas kernels  23.9 us (31%)
  waiting for transfers between devices  18.2 us (23%)
  local copies, waits for them, and re-layouts  0.98 us (1%)
  between operations  0.93 us (1%)
    ppermute x15, starting transfers between devices, exchange(): return lax.ppermute(value, axis, pairs)  24.4 us
    ppermute x15, waiting for transfers between devices, exchange(): return lax.ppermute(value, axis, pairs)  12.9 us
    pallas_call x1, Pallas kernels, input_gradient(): pl.pallas_call(input_kernel, out_shape=(out, out, out, windows), in_specs...  8.9 us
    pallas_call x1, Pallas kernels, filter_gradient(): pl.pallas_call(functools.partial(filter_kernel, shard_rows), out_shape=(o...  5.64 us
    ppermute x1, starting transfers between devices, body(): from_upper = lax.ppermute(to_lower, 'dom', [(b, a) for a, b in ring])  3.03 us
    pallas_call x1, Pallas kernels, fine_gradient(): pl.pallas_call(functools.partial(fine_kernel, groups), grid=(3 * groups,)...  2.89 us
    pallas_call x1, Pallas kernels, prepare(): pl.pallas_call(prepare_kernel, out_shape=(jax.ShapeDtypeStruct((slots + 1...  2.73 us
    ppermute x1, starting transfers between devices, body(): low = lax.ppermute(own[:, voxels - PLANE:], 'dom', forward)  2.36 us
  transfers between devices with their start and end apart: 26, of which 13 were waited for; matrix products, arithmetic and copies ran while one was open for 0% of the time, Pallas kernels for 16%

profile of v7, /device:TPU:0, one launch (start us, length us, event | category | flops | bytes accessed | tf_op | source)
XLA Modules:
  0.0 77.9 jit_solution(13060852382603809960)
XLA Ops:
  0.6 0.0 copy-start.2
  0.7 1.0 %fusion = (bf16[3,64,256]{2,1,0:T(8,128)(2,1)S(1)}, bf16[3,64,256]{2,1,0:T(8,128)(2,1)S(1)}) fusion(bf16[3,512,256]{2,1,0:T(8,128)(2,1)} %bitcast.9), kind=kLoop, calls=%fused_computation | loop fusion | bytes 393216 | tf_op jit(solution)/shard_map/slice | solution.py:648
  1.6 2.4 %collective-permute-start = (bf16[3,64,256]{2,1,0:T(8,128)(2,1)S(1)}, bf16[3,64,256]{2,1,0:T(8,128)(2,1)S(1)}, u32[]{:S(2)}, u32[]{:S(2)}) collective-permute-start(bf16[3,64,256]{2,1,0:T(8,128)(2,1)S(1)} %get-tuple-element.60), channel_id=1, source_target_pairs={{0,1},{1,2},{2,3},{3,4},{4,5},{5,6},{6,7},{8,9},{9,10},{10,11},{11... | collective-permute-start | bytes 294920 | tf_op jit(solution)/shard_map/ppermute | solution.py:647
  4.0 1.3 %collective-permute-start.1 = (bf16[3,64,256]{2,1,0:T(8,128)(2,1)S(1)}, bf16[3,64,256]{2,1,0:T(8,128)(2,1)S(1)}, u32[]{:S(2)}, u32[]{:S(2)}) collective-permute-start(bf16[3,64,256]{2,1,0:T(8,128)(2,1)S(1)} %get-tuple-element.59), channel_id=1, source_target_pairs={{1,0},{2,1},{3,2},{4,3},{5,4},{6,5},{7,6},{9,8},{10,9},{11,10},{12... | collective-permute-start | bytes 294920 | tf_op jit(solution)/shard_map/ppermute | solution.py:648
  5.3 2.7 %prepare.1 = (bf16[4,512,256]{2,1,0:T(8,128)(2,1)S(1)}, bf16[256,1536]{1,0:T(8,128)(2,1)S(1)}, bf16[3,256,2304]{2,1,0:T(8,128)(2,1)S(1)}) custom-call(bf16[1,3,512,256]{3,2,1,0:T(8,128)(2,1)} %own_hbm.1, bf16[1,3,512,256]{3,2,1,0:T(8,128)(2,1)} %pre_hbm.3, bf16[27,256,256]{2,1,0:T(8,128)(2,1)} %weight_hbm.1), custom_call_target="tpu_custom_call" | custom-call | flops 4194304 | bytes 12582912 | tf_op jit(solution)/shard_map/prepare/pallas_call | solution.py:160
  8.0 0.0 collective-permute-done.low_ref
  8.0 1.2 %collective-permute-done.1.high_ref = bf16[3,64,256]{2,1,0:T(8,128)(2,1)S(1)} collective-permute-done((bf16[3,64,256]{2,1,0:T(8,128)(2,1)S(1)}, bf16[3,64,256]{2,1,0:T(8,128)(2,1)S(1)}, u32[]{:S(2)}, u32[]{:S(2)}) %collective-permute-start.1) | collective-permute-done | bytes 98336 | tf_op jit(solution)/shard_map/ppermute | solution.py:648
  9.3 0.0 copy-done.2
  9.3 8.9 %input_gradient.1 = (bf16[1,512,256]{2,1,0:T(8,128)(2,1)S(1)}, bf16[1,512,256]{2,1,0:T(8,128)(2,1)S(1)}, bf16[1,512,256]{2,1,0:T(8,128)(2,1)S(1)}, bf16[1920,2304]{1,0:T(8,128)(2,1)S(1)}) custom-call(s32[3,1,27]{2,1,0:T(1,128)S(1)} %bitcast.6, s32[3,1,8]{2,1,0:T(1,128)S(1)} %bitcast.7, bf16[4,512,256]{2,1,0:T(8,128)(2,1)S(1)} %get-tuple-element.31.own_wide, ...), custom_call_target="tpu_custom_call" | custom-call | flops 5435817984 | bytes 8388608 | tf_op jit(solution)/shard_map/input_gradient/pallas_call | solution.py:280
  18.2 3.0 %collective-permute-start.2 = (bf16[1,512,256]{2,1,0:T(8,128)(2,1)S(1)}, bf16[1,512,256]{2,1,0:T(8,128)(2,1)S(1)}, u32[]{:S(2)}, u32[]{:S(2)}) collective-permute-start(bf16[1,512,256]{2,1,0:T(8,128)(2,1)S(1)} %get-tuple-element.33), channel_id=1, source_target_pairs={{1,0},{2,1},{3,2},{4,3},{5,4},{6,5},{7,6},{0,7},{9,8},{10,9},{11,1... | collective-permute-start | bytes 786440 | tf_op jit(solution)/shard_map/ppermute | solution.py:653
  21.2 0.5 collective-permute-start.3
  21.7 5.6 %filter_gradient.1 = (bf16[4,1728,128]{2,1,0:T(8,128)(2,1)S(1)}, bf16[4,1728,128]{2,1,0:T(8,128)(2,1)S(1)}) custom-call(bf16[1920,2304]{1,0:T(8,128)(2,1)S(1)} %get-tuple-element.36.win_ref, bf16[256,1536]{1,0:T(8,128)(2,1)S(1)} %get-tuple-element.37.act_ref), custom_call_target="tpu_custom_call" | custom-call | flops 5435817984 | bytes 8388608 | tf_op jit(solution)/shard_map/filter_gradient/pallas_call | solution.py:336
  27.4 1.6 %collective-permute-start.4 = (bf16[4,1728,128]{2,1,0:T(8,128)(2,1)S(1)}, bf16[4,1728,128]{2,1,0:T(8,128)(2,1)S(1)}, u32[]{:S(2)}, u32[]{:S(2)}) collective-permute-start(bf16[4,1728,128]{2,1,0:T(8,128)(2,1)S(1)} %get-tuple-element.39), channel_id=1, source_target_pairs={{0,1},{1,0},{2,3},{3,2},{4,5},{5,4},{6,7},{7,6},{8,9},{9,8},{10,11... | collective-permute-start | bytes 5308424 | tf_op jit(solution)/shard_map/ppermute | solution.py:660
  29.0 0.0 collective-permute-done.2.upper_ref
  29.0 1.3 %collective-permute-done.3.lower_ref = bf16[1,512,256]{2,1,0:T(8,128)(2,1)S(1)} collective-permute-done((bf16[1,512,256]{2,1,0:T(8,128)(2,1)S(1)}, bf16[1,512,256]{2,1,0:T(8,128)(2,1)S(1)}, u32[]{:S(2)}, u32[]{:S(2)}) %collective-permute-start.3) | collective-permute-done | bytes 262176 | tf_op jit(solution)/shard_map/ppermute | solution.py:654
  30.3 1.5 %down_gradient.1 = (bf16[4,256,128]{2,1,0:T(8,128)(2,1)S(1)}, bf16[4,256,128]{2,1,0:T(8,128)(2,1)S(1)}) custom-call(bf16[1,512,256]{2,1,0:T(8,128)(2,1)S(1)} %collective-permute-done.2.upper_ref, bf16[1,512,256]{2,1,0:T(8,128)(2,1)S(1)} %get-tuple-element.34.stay_ref, bf16[1,512,256]{2,1,0:T(8,128)(2,1)S(1)} %collective-permute-done.3.lower_ref, ...), custom_call_target="tpu_custom_call" | custom-call | flops 25769803776 | bytes 8388608 | tf_op jit(solution)/shard_map/down_gradient/pallas_call | solution.py:398
  31.8 0.1 collective-permute-start.5
  31.9 1.5 %collective-permute-done.5.down_got_ref = bf16[4,256,128]{2,1,0:T(8,128)(2,1)S(1)} collective-permute-done((bf16[4,256,128]{2,1,0:T(8,128)(2,1)S(1)}, bf16[4,256,128]{2,1,0:T(8,128)(2,1)S(1)}, u32[]{:S(2)}, u32[]{:S(2)}) %collective-permute-start.5) | collective-permute-done | bytes 262176 | tf_op jit(solution)/shard_map/ppermute | solution.py:661
  33.4 0.0 collective-permute-done.4.conv_got_ref
  33.4 0.4 pair_sum.1
  33.9 1.6 %collective-permute-start.6 = (bf16[4,352,128]{2,1,0:T(8,128)(2,1)S(1)}, bf16[4,352,128]{2,1,0:T(8,128)(2,1)S(1)}, u32[]{:S(2)}, u32[]{:S(2)}) collective-permute-start(bf16[4,352,128]{2,1,0:T(8,128)(2,1)S(1)} %get-tuple-element.43), channel_id=1, source_target_pairs={{0,6},{1,7},{2,4},{3,5},{4,2},{5,3},{6,0},{7,1},{8,14},{9,15},{10,... | collective-permute-start | bytes 1081352 | tf_op jit(solution)/shard_map/ppermute | solution.py:48
  35.5 2.4 %collective-permute-start.7 = (bf16[4,352,128]{2,1,0:T(8,128)(2,1)S(1)}, bf16[4,352,128]{2,1,0:T(8,128)(2,1)S(1)}, u32[]{:S(2)}, u32[]{:S(2)}) collective-permute-start(bf16[4,352,128]{2,1,0:T(8,128)(2,1)S(1)} %get-tuple-element.44), channel_id=1, source_target_pairs={{0,4},{1,5},{2,6},{3,7},{4,0},{5,1},{6,2},{7,3},{8,12},{9,13},{10,... | collective-permute-start | bytes 1081352 | tf_op jit(solution)/shard_map/ppermute | solution.py:48
  37.9 0.0 collective-permute-start.8
  37.9 1.6 %collective-permute-start.10 = (bf16[576,128]{1,0:T(8,128)(2,1)S(1)}, bf16[576,128]{1,0:T(8,128)(2,1)S(1)}, u32[]{:S(2)}, u32[]{:S(2)}) collective-permute-start(bf16[576,128]{1,0:T(8,128)(2,1)S(1)} %get-tuple-element.48), channel_id=1, source_target_pairs={{0,8},{8,0},{16,24},{24,16},{1,9},{9,1},{17,25},{25,17},{2,10},{10... | collective-permute-start | bytes 442376 | tf_op jit(solution)/shard_map/ppermute | solution.py:48
  39.5 2.6 %collective-permute-start.11 = (bf16[576,128]{1,0:T(8,128)(2,1)S(1)}, bf16[576,128]{1,0:T(8,128)(2,1)S(1)}, u32[]{:S(2)}, u32[]{:S(2)}) collective-permute-start(bf16[576,128]{1,0:T(8,128)(2,1)S(1)} %get-tuple-element.49), channel_id=1, source_target_pairs={{0,16},{8,24},{16,0},{24,8},{1,17},{9,25},{17,1},{25,9},{2,18},{10... | collective-permute-start | bytes 442376 | tf_op jit(solution)/shard_map/ppermute | solution.py:48
  42.1 4.1 %collective-permute-done.10.refs_6_ = bf16[576,128]{1,0:T(8,128)(2,1)S(1)} collective-permute-done((bf16[576,128]{1,0:T(8,128)(2,1)S(1)}, bf16[576,128]{1,0:T(8,128)(2,1)S(1)}, u32[]{:S(2)}, u32[]{:S(2)}) %collective-permute-start.10) | collective-permute-done | bytes 147488 | tf_op jit(solution)/shard_map/ppermute | solution.py:48
  46.2 2.9 %collective-permute-start.9 = (bf16[576,128]{1,0:T(8,128)(2,1)S(1)}, bf16[576,128]{1,0:T(8,128)(2,1)S(1)}, u32[]{:S(2)}, u32[]{:S(2)}) collective-permute-start(bf16[576,128]{1,0:T(8,128)(2,1)S(1)} %get-tuple-element.47), channel_id=1, source_target_pairs={{0,24},{8,16},{16,8},{24,0},{1,25},{9,17},{17,9},{25,1},{2,26},{10... | collective-permute-start | bytes 442376 | tf_op jit(solution)/shard_map/ppermute | solution.py:48
  49.0 1.8 %collective-permute-done.11.refs_7_ = bf16[576,128]{1,0:T(8,128)(2,1)S(1)} collective-permute-done((bf16[576,128]{1,0:T(8,128)(2,1)S(1)}, bf16[576,128]{1,0:T(8,128)(2,1)S(1)}, u32[]{:S(2)}, u32[]{:S(2)}) %collective-permute-start.11) | collective-permute-done | bytes 147488 | tf_op jit(solution)/shard_map/ppermute | solution.py:48
  50.8 2.4 %collective-permute-done.9.refs_5_ = bf16[576,128]{1,0:T(8,128)(2,1)S(1)} collective-permute-done((bf16[576,128]{1,0:T(8,128)(2,1)S(1)}, bf16[576,128]{1,0:T(8,128)(2,1)S(1)}, u32[]{:S(2)}, u32[]{:S(2)}) %collective-permute-start.9) | collective-permute-done | bytes 147488 | tf_op jit(solution)/shard_map/ppermute | solution.py:48
  53.2 0.0 collective-permute-done.6.refs_1_
  53.2 0.0 collective-permute-done.7.refs_2_
  53.2 0.0 collective-permute-done.8.refs_3_
  53.2 0.2 middle_sum.1
  53.5 3.6 %collective-permute-start.12 = (bf16[352,128]{1,0:T(8,128)(2,1)S(1)}, bf16[352,128]{1,0:T(8,128)(2,1)S(1)}, u32[]{:S(2)}, u32[]{:S(2)}) collective-permute-start(bf16[352,128]{1,0:T(8,128)(2,1)S(1)} %get-tuple-element.51), channel_id=1, source_target_pairs={{0,24},{8,16},{16,8},{24,0},{1,25},{9,17},{17,9},{25,1},{2,26},{10... | collective-permute-start | bytes 270344 | tf_op jit(solution)/shard_map/ppermute | solution.py:48
  57.1 1.8 %collective-permute-start.15 = (bf16[576,128]{1,0:T(8,128)(2,1)S(1)}, bf16[576,128]{1,0:T(8,128)(2,1)S(1)}, u32[]{:S(2)}, u32[]{:S(2)}) collective-permute-start(bf16[576,128]{1,0:T(8,128)(2,1)S(1)} %get-tuple-element.54.refs_4_), channel_id=1, source_target_pairs={{0,2},{1,3},{2,0},{3,1},{4,6},{5,7},{6,4},{7,5},{8,10},{9,11},{10,... | collective-permute-start | bytes 442376 | tf_op jit(solution)/shard_map/ppermute | solution.py:48
  58.9 1.4 %collective-permute-start.16 = (bf16[576,128]{1,0:T(8,128)(2,1)S(1)}, bf16[576,128]{1,0:T(8,128)(2,1)S(1)}, u32[]{:S(2)}, u32[]{:S(2)}) collective-permute-start(bf16[576,128]{1,0:T(8,128)(2,1)S(1)} %get-tuple-element.54.refs_4_), channel_id=1, source_target_pairs={{0,4},{1,5},{2,6},{3,7},{4,0},{5,1},{6,2},{7,3},{8,12},{9,13},{10,... | collective-permute-start | bytes 442376 | tf_op jit(solution)/shard_map/ppermute | solution.py:48
  60.3 0.3 collective-permute-start.17
  60.6 0.5 collective-permute-start.13
  61.0 0.0 collective-permute-done.12.refs_1_
  61.0 2.2 %collective-permute-start.14 = (bf16[352,128]{1,0:T(8,128)(2,1)S(1)}, bf16[352,128]{1,0:T(8,128)(2,1)S(1)}, u32[]{:S(2)}, u32[]{:S(2)}) collective-permute-start(bf16[352,128]{1,0:T(8,128)(2,1)S(1)} %get-tuple-element.53), channel_id=1, source_target_pairs={{0,8},{8,0},{16,24},{24,16},{1,9},{9,1},{17,25},{25,17},{2,10},{10... | collective-permute-start | bytes 270344 | tf_op jit(solution)/shard_map/ppermute | solution.py:48
  63.3 2.9 %fine_gradient.1.refs_8_ = bf16[24,512,128]{2,1,0:T(8,128)(2,1)} custom-call(bf16[1,512,256]{2,1,0:T(8,128)(2,1)S(1)} %collective-permute-done.2.upper_ref, bf16[1,512,256]{2,1,0:T(8,128)(2,1)S(1)} %get-tuple-element.34.stay_ref, bf16[1,512,256]{2,1,0:T(8,128)(2,1)S(1)} %collective-permute-done.3.lower_ref, bf16[8,128,256]{2,1,0:T(8,128)(2,1)S(1)} %copy-done), custom_call_target="tpu_custom_call" | custom-call | flops 805306368 | bytes 4194304 | tf_op jit(solution)/shard_map/fine_gradient/pallas_call | solution.py:443
  66.1 0.8 %collective-permute-done.13.refs_2_ = bf16[352,128]{1,0:T(8,128)(2,1)S(1)} collective-permute-done((bf16[352,128]{1,0:T(8,128)(2,1)S(1)}, bf16[352,128]{1,0:T(8,128)(2,1)S(1)}, u32[]{:S(2)}, u32[]{:S(2)}) %collective-permute-start.13) | collective-permute-done | bytes 90144 | tf_op jit(solution)/shard_map/ppermute | solution.py:48
  67.0 0.0 collective-permute-done.14.refs_3_
  67.0 0.0 collective-permute-done.15.refs_5_
  67.0 0.2 collective-permute-done.16.refs_6_
  67.2 0.0 collective-permute-done.17.refs_7_
  67.2 0.1 last_sum.1
  67.3 2.0 %collective-permute-start.18 = (bf16[352,128]{1,0:T(8,128)(2,1)S(1)}, bf16[352,128]{1,0:T(8,128)(2,1)S(1)}, u32[]{:S(2)}, u32[]{:S(2)}) collective-permute-start(bf16[352,128]{1,0:T(8,128)(2,1)S(1)} %get-tuple-element.55.refs_0_), channel_id=1, source_target_pairs={{0,6},{1,7},{2,4},{3,5},{4,2},{5,3},{6,0},{7,1},{8,14},{9,15},{10,... | collective-permute-start | bytes 270344 | tf_op jit(solution)/shard_map/ppermute | solution.py:48
  69.3 1.1 %collective-permute-start.19 = (bf16[352,128]{1,0:T(8,128)(2,1)S(1)}, bf16[352,128]{1,0:T(8,128)(2,1)S(1)}, u32[]{:S(2)}, u32[]{:S(2)}) collective-permute-start(bf16[352,128]{1,0:T(8,128)(2,1)S(1)} %get-tuple-element.55.refs_0_), channel_id=1, source_target_pairs={{0,4},{1,5},{2,6},{3,7},{4,0},{5,1},{6,2},{7,3},{8,12},{9,13},{10,... | collective-permute-start | bytes 270344 | tf_op jit(solution)/shard_map/ppermute | solution.py:48
  70.4 0.4 collective-permute-start.20
  70.9 0.0 collective-permute-start.25
  70.9 0.5 collective-permute-start.21
  71.4 1.4 %collective-permute-done.18.refs_1_ = bf16[352,128]{1,0:T(8,128)(2,1)S(1)} collective-permute-done((bf16[352,128]{1,0:T(8,128)(2,1)S(1)}, bf16[352,128]{1,0:T(8,128)(2,1)S(1)}, u32[]{:S(2)}, u32[]{:S(2)}) %collective-permute-start.18) | collective-permute-done | bytes 90144 | tf_op jit(solution)/shard_map/ppermute | solution.py:48
  72.8 0.0 collective-permute-start.22
  72.8 1.0 %collective-permute-done.19.refs_2_ = bf16[352,128]{1,0:T(8,128)(2,1)S(1)} collective-permute-done((bf16[352,128]{1,0:T(8,128)(2,1)S(1)}, bf16[352,128]{1,0:T(8,128)(2,1)S(1)}, u32[]{:S(2)}, u32[]{:S(2)}) %collective-permute-start.19) | collective-permute-done | bytes 90144 | tf_op jit(solution)/shard_map/ppermute | solution.py:48
  73.9 0.0 collective-permute-start.23
  73.9 1.1 %collective-permute-done.20.refs_3_ = bf16[352,128]{1,0:T(8,128)(2,1)S(1)} collective-permute-done((bf16[352,128]{1,0:T(8,128)(2,1)S(1)}, bf16[352,128]{1,0:T(8,128)(2,1)S(1)}, u32[]{:S(2)}, u32[]{:S(2)}) %collective-permute-start.20) | collective-permute-done | bytes 90144 | tf_op jit(solution)/shard_map/ppermute | solution.py:48
  74.9 0.0 collective-permute-start.24
  75.0 0.0 collective-permute-done.21.refs_4_
  75.0 0.0 collective-permute-done.25.refs_9_
  75.0 0.0 collective-permute-done.22.refs_5_
  75.0 0.2 collective-permute-done.23.refs_6_
  75.1 1.1 %collective-permute-done.24.refs_7_ = bf16[352,128]{1,0:T(8,128)(2,1)S(1)} collective-permute-done((bf16[352,128]{1,0:T(8,128)(2,1)S(1)}, bf16[352,128]{1,0:T(8,128)(2,1)S(1)}, u32[]{:S(2)}, u32[]{:S(2)}) %collective-permute-start.24) | collective-permute-done | bytes 90144 | tf_op jit(solution)/shard_map/ppermute | solution.py:670
  76.2 1.5 %gather_up.1 = (f32[1728,256]{1,0:T(8,128)}, f32[256,256]{1,0:T(8,128)}) custom-call(bf16[352,128]{1,0:T(8,128)(2,1)S(1)} %get-tuple-element.55.refs_0_, bf16[352,128]{1,0:T(8,128)(2,1)S(1)} %collective-permute-done.18.refs_1_, bf16[352,128]{1,0:T(8,128)(2,1)S(1)} %collective-permute-done.19.refs_2_, bf16[352,128]{1,0:T(8,128)(2,1)S(1)} %collective-permute-done.20.refs_3_, ...), custom_call_target="tpu_custom_call" | custom-call | flops 2752512 | bytes 2752512 | tf_op jit(solution)/shard_map/gather_up/pallas_call | solution.py:610
  (6 shorter events, 0.0 us)
Async XLA Ops:
  0.6 8.7 %copy-start.2 = (s32[1,3,27]{2,0,1:T(1,128)S(1)}, s32[1,3,27]{2,0,1:T(1,128)}, u32[]{:S(2)}) copy-start(s32[1,3,27]{2,0,1:T(1,128)} %param.12) | copy-start | bytes 976
  0.6 8.7 %copy-start.3 = (s32[1,1,3,8]{3,1,2,0:T(1,128)S(1)}, s32[1,1,3,8]{3,1,2,0:T(1,128)}, u32[]{:S(2)}) copy-start(s32[1,1,3,8]{3,1,2,0:T(1,128)} %param.13) | copy-start | bytes 292
  1.6 6.4 %collective-permute-start = (bf16[3,64,256]{2,1,0:T(8,128)(2,1)S(1)}, bf16[3,64,256]{2,1,0:T(8,128)(2,1)S(1)}, u32[]{:S(2)}, u32[]{:S(2)}) collective-permute-start(bf16[3,64,256]{2,1,0:T(8,128)(2,1)S(1)} %get-tuple-element.60), channel_id=1, source_target_pairs={{0,1},{1,2},{2,3},{3,4},{4,5},{5,6},{6,7},{8,9},{9,10},{10,11},{11... | collective-permute-start | bytes 294920 | tf_op jit(solution)/shard_map/ppermute | solution.py:647
  4.0 5.3 %collective-permute-start.1 = (bf16[3,64,256]{2,1,0:T(8,128)(2,1)S(1)}, bf16[3,64,256]{2,1,0:T(8,128)(2,1)S(1)}, u32[]{:S(2)}, u32[]{:S(2)}) collective-permute-start(bf16[3,64,256]{2,1,0:T(8,128)(2,1)S(1)} %get-tuple-element.59), channel_id=1, source_target_pairs={{1,0},{2,1},{3,2},{4,3},{5,4},{6,5},{7,6},{9,8},{10,9},{11,10},{12... | collective-permute-start | bytes 294920 | tf_op jit(solution)/shard_map/ppermute | solution.py:648
  18.2 10.8 %collective-permute-start.2 = (bf16[1,512,256]{2,1,0:T(8,128)(2,1)S(1)}, bf16[1,512,256]{2,1,0:T(8,128)(2,1)S(1)}, u32[]{:S(2)}, u32[]{:S(2)}) collective-permute-start(bf16[1,512,256]{2,1,0:T(8,128)(2,1)S(1)} %get-tuple-element.33), channel_id=1, source_target_pairs={{1,0},{2,1},{3,2},{4,3},{5,4},{6,5},{7,6},{0,7},{9,8},{10,9},{11,1... | collective-permute-start | bytes 786440 | tf_op jit(solution)/shard_map/ppermute | solution.py:653
  21.2 9.1 %collective-permute-start.3 = (bf16[1,512,256]{2,1,0:T(8,128)(2,1)S(1)}, bf16[1,512,256]{2,1,0:T(8,128)(2,1)S(1)}, u32[]{:S(2)}, u32[]{:S(2)}) collective-permute-start(bf16[1,512,256]{2,1,0:T(8,128)(2,1)S(1)} %get-tuple-element.35), channel_id=1, source_target_pairs={{0,1},{1,2},{2,3},{3,4},{4,5},{5,6},{6,7},{7,0},{8,9},{9,10},{10,1... | collective-permute-start | bytes 786440 | tf_op jit(solution)/shard_map/ppermute | solution.py:654
  21.7 8.6 %copy-start.1 = (bf16[1,24,512,128]{3,2,1,0:T(8,128)(2,1)S(1)}, bf16[1,24,512,128]{3,2,1,0:T(8,128)(2,1)}, u32[]{:S(2)}) copy-start(bf16[1,24,512,128]{3,2,1,0:T(8,128)(2,1)} %param.11) | copy-start | bytes 9437188
  27.4 6.0 %collective-permute-start.4 = (bf16[4,1728,128]{2,1,0:T(8,128)(2,1)S(1)}, bf16[4,1728,128]{2,1,0:T(8,128)(2,1)S(1)}, u32[]{:S(2)}, u32[]{:S(2)}) collective-permute-start(bf16[4,1728,128]{2,1,0:T(8,128)(2,1)S(1)} %get-tuple-element.39), channel_id=1, source_target_pairs={{0,1},{1,0},{2,3},{3,2},{4,5},{5,4},{6,7},{7,6},{8,9},{9,8},{10,11... | collective-permute-start | bytes 5308424 | tf_op jit(solution)/shard_map/ppermute | solution.py:660
  31.8 1.6 %collective-permute-start.5 = (bf16[4,256,128]{2,1,0:T(8,128)(2,1)S(1)}, bf16[4,256,128]{2,1,0:T(8,128)(2,1)S(1)}, u32[]{:S(2)}, u32[]{:S(2)}) collective-permute-start(bf16[4,256,128]{2,1,0:T(8,128)(2,1)S(1)} %get-tuple-element.41), channel_id=1, source_target_pairs={{0,1},{1,0},{2,3},{3,2},{4,5},{5,4},{6,7},{7,6},{8,9},{9,8},{10,11... | collective-permute-start | bytes 786440 | tf_op jit(solution)/shard_map/ppermute | solution.py:661
  33.4 29.8 %copy-start = (bf16[8,128,256]{2,1,0:T(8,128)(2,1)S(1)}, bf16[8,128,256]{2,1,0:T(8,128)(2,1)}, u32[]{:S(2)}) copy-start(bf16[8,128,256]{2,1,0:T(8,128)(2,1)} %weight_ref.1) | copy-start | bytes 1572868
  33.9 19.3 %collective-permute-start.6 = (bf16[4,352,128]{2,1,0:T(8,128)(2,1)S(1)}, bf16[4,352,128]{2,1,0:T(8,128)(2,1)S(1)}, u32[]{:S(2)}, u32[]{:S(2)}) collective-permute-start(bf16[4,352,128]{2,1,0:T(8,128)(2,1)S(1)} %get-tuple-element.43), channel_id=1, source_target_pairs={{0,6},{1,7},{2,4},{3,5},{4,2},{5,3},{6,0},{7,1},{8,14},{9,15},{10,... | collective-permute-start | bytes 1081352 | tf_op jit(solution)/shard_map/ppermute | solution.py:48
  35.5 17.7 %collective-permute-start.7 = (bf16[4,352,128]{2,1,0:T(8,128)(2,1)S(1)}, bf16[4,352,128]{2,1,0:T(8,128)(2,1)S(1)}, u32[]{:S(2)}, u32[]{:S(2)}) collective-permute-start(bf16[4,352,128]{2,1,0:T(8,128)(2,1)S(1)} %get-tuple-element.44), channel_id=1, source_target_pairs={{0,4},{1,5},{2,6},{3,7},{4,0},{5,1},{6,2},{7,3},{8,12},{9,13},{10,... | collective-permute-start | bytes 1081352 | tf_op jit(solution)/shard_map/ppermute | solution.py:48
  37.9 15.3 %collective-permute-start.8 = (bf16[4,352,128]{2,1,0:T(8,128)(2,1)S(1)}, bf16[4,352,128]{2,1,0:T(8,128)(2,1)S(1)}, u32[]{:S(2)}, u32[]{:S(2)}) collective-permute-start(bf16[4,352,128]{2,1,0:T(8,128)(2,1)S(1)} %get-tuple-element.45), channel_id=1, source_target_pairs={{0,2},{1,3},{2,0},{3,1},{4,6},{5,7},{6,4},{7,5},{8,10},{9,11},{10,... | collective-permute-start | bytes 1081352 | tf_op jit(solution)/shard_map/ppermute | solution.py:48
  37.9 8.2 %collective-permute-start.10 = (bf16[576,128]{1,0:T(8,128)(2,1)S(1)}, bf16[576,128]{1,0:T(8,128)(2,1)S(1)}, u32[]{:S(2)}, u32[]{:S(2)}) collective-permute-start(bf16[576,128]{1,0:T(8,128)(2,1)S(1)} %get-tuple-element.48), channel_id=1, source_target_pairs={{0,8},{8,0},{16,24},{24,16},{1,9},{9,1},{17,25},{25,17},{2,10},{10... | collective-permute-start | bytes 442376 | tf_op jit(solution)/shard_map/ppermute | solution.py:48
  39.5 11.3 %collective-permute-start.11 = (bf16[576,128]{1,0:T(8,128)(2,1)S(1)}, bf16[576,128]{1,0:T(8,128)(2,1)S(1)}, u32[]{:S(2)}, u32[]{:S(2)}) collective-permute-start(bf16[576,128]{1,0:T(8,128)(2,1)S(1)} %get-tuple-element.49), channel_id=1, source_target_pairs={{0,16},{8,24},{16,0},{24,8},{1,17},{9,25},{17,1},{25,9},{2,18},{10... | collective-permute-start | bytes 442376 | tf_op jit(solution)/shard_map/ppermute | solution.py:48
  46.2 7.0 %collective-permute-start.9 = (bf16[576,128]{1,0:T(8,128)(2,1)S(1)}, bf16[576,128]{1,0:T(8,128)(2,1)S(1)}, u32[]{:S(2)}, u32[]{:S(2)}) collective-permute-start(bf16[576,128]{1,0:T(8,128)(2,1)S(1)} %get-tuple-element.47), channel_id=1, source_target_pairs={{0,24},{8,16},{16,8},{24,0},{1,25},{9,17},{17,9},{25,1},{2,26},{10... | collective-permute-start | bytes 442376 | tf_op jit(solution)/shard_map/ppermute | solution.py:48
  53.5 7.6 %collective-permute-start.12 = (bf16[352,128]{1,0:T(8,128)(2,1)S(1)}, bf16[352,128]{1,0:T(8,128)(2,1)S(1)}, u32[]{:S(2)}, u32[]{:S(2)}) collective-permute-start(bf16[352,128]{1,0:T(8,128)(2,1)S(1)} %get-tuple-element.51), channel_id=1, source_target_pairs={{0,24},{8,16},{16,8},{24,0},{1,25},{9,17},{17,9},{25,1},{2,26},{10... | collective-permute-start | bytes 270344 | tf_op jit(solution)/shard_map/ppermute | solution.py:48
  57.1 9.9 %collective-permute-start.15 = (bf16[576,128]{1,0:T(8,128)(2,1)S(1)}, bf16[576,128]{1,0:T(8,128)(2,1)S(1)}, u32[]{:S(2)}, u32[]{:S(2)}) collective-permute-start(bf16[576,128]{1,0:T(8,128)(2,1)S(1)} %get-tuple-element.54.refs_4_), channel_id=1, source_target_pairs={{0,2},{1,3},{2,0},{3,1},{4,6},{5,7},{6,4},{7,5},{8,10},{9,11},{10,... | collective-permute-start | bytes 442376 | tf_op jit(solution)/shard_map/ppermute | solution.py:48
  58.9 8.3 %collective-permute-start.16 = (bf16[576,128]{1,0:T(8,128)(2,1)S(1)}, bf16[576,128]{1,0:T(8,128)(2,1)S(1)}, u32[]{:S(2)}, u32[]{:S(2)}) collective-permute-start(bf16[576,128]{1,0:T(8,128)(2,1)S(1)} %get-tuple-element.54.refs_4_), channel_id=1, source_target_pairs={{0,4},{1,5},{2,6},{3,7},{4,0},{5,1},{6,2},{7,3},{8,12},{9,13},{10,... | collective-permute-start | bytes 442376 | tf_op jit(solution)/shard_map/ppermute | solution.py:48
  60.3 6.9 %collective-permute-start.17 = (bf16[576,128]{1,0:T(8,128)(2,1)S(1)}, bf16[576,128]{1,0:T(8,128)(2,1)S(1)}, u32[]{:S(2)}, u32[]{:S(2)}) collective-permute-start(bf16[576,128]{1,0:T(8,128)(2,1)S(1)} %get-tuple-element.54.refs_4_), channel_id=1, source_target_pairs={{0,6},{1,7},{2,4},{3,5},{4,2},{5,3},{6,0},{7,1},{8,14},{9,15},{10,... | collective-permute-start | bytes 442376 | tf_op jit(solution)/shard_map/ppermute | solution.py:48
  60.6 6.4 %collective-permute-start.13 = (bf16[352,128]{1,0:T(8,128)(2,1)S(1)}, bf16[352,128]{1,0:T(8,128)(2,1)S(1)}, u32[]{:S(2)}, u32[]{:S(2)}) collective-permute-start(bf16[352,128]{1,0:T(8,128)(2,1)S(1)} %get-tuple-element.52), channel_id=1, source_target_pairs={{0,16},{8,24},{16,0},{24,8},{1,17},{9,25},{17,1},{25,9},{2,18},{10... | collective-permute-start | bytes 270344 | tf_op jit(solution)/shard_map/ppermute | solution.py:48
  61.0 5.9 %collective-permute-start.14 = (bf16[352,128]{1,0:T(8,128)(2,1)S(1)}, bf16[352,128]{1,0:T(8,128)(2,1)S(1)}, u32[]{:S(2)}, u32[]{:S(2)}) collective-permute-start(bf16[352,128]{1,0:T(8,128)(2,1)S(1)} %get-tuple-element.53), channel_id=1, source_target_pairs={{0,8},{8,0},{16,24},{24,16},{1,9},{9,1},{17,25},{25,17},{2,10},{10... | collective-permute-start | bytes 270344 | tf_op jit(solution)/shard_map/ppermute | solution.py:48
  67.3 5.5 %collective-permute-start.18 = (bf16[352,128]{1,0:T(8,128)(2,1)S(1)}, bf16[352,128]{1,0:T(8,128)(2,1)S(1)}, u32[]{:S(2)}, u32[]{:S(2)}) collective-permute-start(bf16[352,128]{1,0:T(8,128)(2,1)S(1)} %get-tuple-element.55.refs_0_), channel_id=1, source_target_pairs={{0,6},{1,7},{2,4},{3,5},{4,2},{5,3},{6,0},{7,1},{8,14},{9,15},{10,... | collective-permute-start | bytes 270344 | tf_op jit(solution)/shard_map/ppermute | solution.py:48
  69.3 4.5 %collective-permute-start.19 = (bf16[352,128]{1,0:T(8,128)(2,1)S(1)}, bf16[352,128]{1,0:T(8,128)(2,1)S(1)}, u32[]{:S(2)}, u32[]{:S(2)}) collective-permute-start(bf16[352,128]{1,0:T(8,128)(2,1)S(1)} %get-tuple-element.55.refs_0_), channel_id=1, source_target_pairs={{0,4},{1,5},{2,6},{3,7},{4,0},{5,1},{6,2},{7,3},{8,12},{9,13},{10,... | collective-permute-start | bytes 270344 | tf_op jit(solution)/shard_map/ppermute | solution.py:48
  70.4 4.5 %collective-permute-start.20 = (bf16[352,128]{1,0:T(8,128)(2,1)S(1)}, bf16[352,128]{1,0:T(8,128)(2,1)S(1)}, u32[]{:S(2)}, u32[]{:S(2)}) collective-permute-start(bf16[352,128]{1,0:T(8,128)(2,1)S(1)} %get-tuple-element.55.refs_0_), channel_id=1, source_target_pairs={{0,2},{1,3},{2,0},{3,1},{4,6},{5,7},{6,4},{7,5},{8,10},{9,11},{10,... | collective-permute-start | bytes 270344 | tf_op jit(solution)/shard_map/ppermute | solution.py:48
  70.9 4.1 %collective-permute-start.25 = (bf16[576,128]{1,0:T(8,128)(2,1)S(1)}, bf16[576,128]{1,0:T(8,128)(2,1)S(1)}, u32[]{:S(2)}, u32[]{:S(2)}) collective-permute-start(bf16[576,128]{1,0:T(8,128)(2,1)S(1)} %get-tuple-element.56.refs_8_), channel_id=1, source_target_pairs={{0,1},{1,0},{2,3},{3,2},{4,5},{5,4},{6,7},{7,6},{8,9},{9,8},{10,11... | collective-permute-start | bytes 442376 | tf_op jit(solution)/shard_map/ppermute | solution.py:671
  70.9 4.1 %collective-permute-start.21 = (bf16[352,128]{1,0:T(8,128)(2,1)S(1)}, bf16[352,128]{1,0:T(8,128)(2,1)S(1)}, u32[]{:S(2)}, u32[]{:S(2)}) collective-permute-start(bf16[352,128]{1,0:T(8,128)(2,1)S(1)} %get-tuple-element.55.refs_0_), channel_id=1, source_target_pairs={{0,1},{1,0},{2,3},{3,2},{4,5},{5,4},{6,7},{7,6},{8,9},{9,8},{10,11... | collective-permute-start | bytes 270344 | tf_op jit(solution)/shard_map/ppermute | solution.py:670
  72.8 2.2 %collective-permute-start.22 = (bf16[352,128]{1,0:T(8,128)(2,1)S(1)}, bf16[352,128]{1,0:T(8,128)(2,1)S(1)}, u32[]{:S(2)}, u32[]{:S(2)}) collective-permute-start(bf16[352,128]{1,0:T(8,128)(2,1)S(1)} %collective-permute-done.18.refs_1_), channel_id=1, source_target_pairs={{0,1},{1,0},{2,3},{3,2},{4,5},{5,4},{6,7},{7,6},{8,9},{9,8},{10,11... | collective-permute-start | bytes 270344 | tf_op jit(solution)/shard_map/ppermute | solution.py:670
  73.9 1.3 %collective-permute-start.23 = (bf16[352,128]{1,0:T(8,128)(2,1)S(1)}, bf16[352,128]{1,0:T(8,128)(2,1)S(1)}, u32[]{:S(2)}, u32[]{:S(2)}) collective-permute-start(bf16[352,128]{1,0:T(8,128)(2,1)S(1)} %collective-permute-done.19.refs_2_), channel_id=1, source_target_pairs={{0,1},{1,0},{2,3},{3,2},{4,5},{5,4},{6,7},{7,6},{8,9},{9,8},{10,11... | collective-permute-start | bytes 270344 | tf_op jit(solution)/shard_map/ppermute | solution.py:670
  74.9 1.3 %collective-permute-start.24 = (bf16[352,128]{1,0:T(8,128)(2,1)S(1)}, bf16[352,128]{1,0:T(8,128)(2,1)S(1)}, u32[]{:S(2)}, u32[]{:S(2)}) collective-permute-start(bf16[352,128]{1,0:T(8,128)(2,1)S(1)} %collective-permute-done.20.refs_3_), channel_id=1, source_target_pairs={{0,1},{1,0},{2,3},{3,2},{4,5},{5,4},{6,7},{7,6},{8,9},{9,8},{10,11... | collective-permute-start | bytes 270344 | tf_op jit(solution)/shard_map/ppermute | solution.py:670

commit v8 on v7

--- a/solution.py
+++ b/solution.py
@@ -213,8 +213,15 @@
         return [functools.partial(product, group, start) for start in range(0, rows, part)]
 
     sources = (links_ref, own_wide, low_wide, high_wide, win_ref)
+    for call in builders(*sources, GROUPS[0]):
+        call()
+    interleave(products(0), builders(*sources, GROUPS[1]))
+    interleave(products(1), builders(*sources, GROUPS[2]))
+    for call in products(2):
+        call()
+    pre_copy.wait()
+
     place_z = lax.broadcasted_iota(jnp.int32, (BE // 2, BE, channels), 1)
-    targets = []
     for slot in range(slots):
         group = jnp.int32(3 * groups)
         for row in range(3):
@@ -222,51 +229,27 @@
                 group = jnp.where(
                     routes_ref[row, 0, 8 * place] == 8 * slot, row * groups + place, group
                 )
-        targets.append(group)
-
-    def finish(x, slot):
-        start = x * slab + slot * PLANE
-        value = acc_ref[start : start + PLANE, :]
-        pre = pre_ref[slot, x * PLANE : (x + 1) * PLANE, :].astype(F32)
-        value = jnp.where(pre > 0, value, 0.0).reshape(BE // 2, 2, BE, channels)
-        even, odd = value[:, 0], value[:, 1]
-        near = jnp.where(place_z < HALF, even, pltpu.roll(odd, HALF, axis=1))
-        far = jnp.where(place_z < HALF, pltpu.roll(even, HALF, axis=1), odd)
-        side, row = x // HALF, x % HALF * 16
-        for side_y in range(2):
-            for side_z, piece in enumerate((near, far)):
-                block = piece[2 * side_y : 2 * side_y + 2].reshape(16, channels).astype(BF16)
-                start = (4 * side + 2 * side_y + side_z) * PLANE + row
-                octants_ref[targets[slot], start : start + 16, :] = block
-
-    def finishes(planes):
-        return [functools.partial(finish, x, slot) for x in planes for slot in range(slots)]
-
-    for call in builders(*sources, GROUPS[0]):
-        call()
-    pre_copy.wait()
-    interleave(products(0), builders(*sources, GROUPS[1]))
-    interleave(products(1), builders(*sources, GROUPS[2]))
-    last = products(2)
-    last[0]()
-    interleave(last[1:], finishes(range(HALF)))
+
+        def finish(x, carry):
+            value = acc_ref[pl.ds(pl.multiple_of(x * slab + slot * PLANE, PLANE), PLANE), :]
+            pre = pre_ref[slot, pl.ds(pl.multiple_of(x * PLANE, PLANE), PLANE), :].astype(F32)
+            value = jnp.where(pre > 0, value, 0.0).reshape(BE // 2, 2, BE, channels)
+            even, odd = value[:, 0], value[:, 1]
+            near = jnp.where(place_z < HALF, even, pltpu.roll(odd, HALF, axis=1))
+            far = jnp.where(place_z < HALF, pltpu.roll(even, HALF, axis=1), odd)
+            side = x // HALF
+            row = (x - side * HALF) * 16
+            for side_y in range(2):
+                for side_z, piece in enumerate((near, far)):
+                    block = piece[2 * side_y : 2 * side_y + 2].reshape(16, channels).astype(BF16)
+                    start = (4 * side + 2 * side_y + side_z) * PLANE + row
+                    octants_ref[group, pl.ds(pl.multiple_of(start, 16), 16), :] = block
+            return carry
+
+        lax.fori_loop(0, BE, finish, 0)
     outs = []
-
-    def leave(side):
-        rows = pl.ds(side * 4 * PLANE, 4 * PLANE)
-        for row, ref in enumerate((to_lower_ref, stay_ref, to_upper_ref)):
-            outs.append(
-                started(
-                    octants_ref.at[pl.ds(row * groups, groups), rows],
-                    ref.at[:, rows],
-                    out_sems.at[3 * side + row],
-                )
-            )
-
-    leave(0)
-    for call in finishes(range(HALF, BE)):
-        call()
-    leave(1)
+    for row, ref in enumerate((to_lower_ref, stay_ref, to_upper_ref)):
+        outs.append(started(octants_ref.at[pl.ds(row * groups, groups)], ref, out_sems.at[row]))
     for copy in outs:
         copy.wait()
 
@@ -288,7 +271,7 @@
             pltpu.VMEM((rows, channels), F32),
             pltpu.VMEM((3 * groups + 1, voxels, channels), BF16),
             pltpu.VMEM((slots, voxels, channels), BF16),
-            pltpu.SemaphoreType.DMA((6,)),
+            pltpu.SemaphoreType.DMA((3,)),
             pltpu.SemaphoreType.DMA,
         ],
         compiler_params=params(20),
@@ -552,18 +535,19 @@
     return outs[:shards], outs[shards]
 
 
-def last_kernel(factor, shards, *refs):
+def last_kernel(factor, count, *refs):
     *refs, _, planes_ref, slabs_ref = refs
-    total = tree([part[...].astype(F32) for part in refs[:shards]])
+    total = tree([part[...].astype(F32) for part in refs[count:]])
     planes_ref[...] = (total * factor).astype(BF16)
-    total = tree([part[...].astype(F32) for part in refs[shards:]])
+    steps = far_first(count)
+    total = tree([refs[steps.index(step)][...].astype(F32) for step in range(count)])
     slabs_ref[...] = (total * factor).astype(BF16)
 
 
 def last_sum(factor, slabs, planes, after):
-    parts = [*slabs, *planes]
+    parts = [*planes, *slabs]
     return pl.pallas_call(
-        functools.partial(last_kernel, factor, len(slabs)),
+        functools.partial(last_kernel, factor, len(planes)),
         out_shape=[
             jax.ShapeDtypeStruct(slabs[0].shape, BF16), jax.ShapeDtypeStruct(planes[0].shape, BF16)
         ],
@@ -665,7 +649,7 @@
     planes = spread_out(planes, "dom", 2, far_first(count))
     to_slabs, rest = middle_sum(planes, slabs)
     to_slabs = spread_out(to_slabs, "dp", 1, far_first(shards))
-    mine, rest = last_sum(factor, to_slabs, spread_out([rest] * count, "dom", 2), fine_grad)
+    mine, rest = last_sum(factor, to_slabs, spread_out([rest] * count, "dom", 2, far_first(count)), fine_grad)
     near = spread_out([mine] * count, "dom", 2, far_first(count))
     far = [lax.ppermute(value, "dom", swap) for value in near]
     rest_far = lax.ppermute(rest, "dom", swap)

time: 78.1 us -> 77.2 us (0.988)
  Pallas kernels: 23.9 us -> 23.1 us
    pallas_call x1, Pallas kernels: 8.9 us -> 8.05 us  [input_gradient(): pl.pallas_call(input_kernel, out_shape=(out, out, out, windows), in_specs...]
  transfers between devices with their start and end apart: 26 -> 26, of which waited for: 13 -> 12; matrix products, arithmetic and copies ran while one was open for 0% -> 0% of each run, Pallas kernels for 16% -> 17%
where the time goes in v8:
time: 77.2 us; the launch traced here: 77 us
  starting transfers between devices  33.8 us (44%)
  Pallas kernels  23.1 us (30%)
  waiting for transfers between devices  18.2 us (24%)
  local copies, waits for them, and re-layouts  0.98 us (1%)
  between operations  0.94 us (1%)
    ppermute x15, starting transfers between devices, exchange(): return lax.ppermute(value, axis, pairs)  24.4 us
    ppermute x15, waiting for transfers between devices, exchange(): return lax.ppermute(value, axis, pairs)  12.9 us
    pallas_call x1, Pallas kernels, input_gradient(): pl.pallas_call(input_kernel, out_shape=(out, out, out, windows), in_specs...  8.05 us
    pallas_call x1, Pallas kernels, filter_gradient(): pl.pallas_call(functools.partial(filter_kernel, shard_rows), out_shape=(o...  5.64 us
    ppermute x1, starting transfers between devices, body(): from_upper = lax.ppermute(to_lower, 'dom', [(b, a) for a, b in ring])  3.01 us
    pallas_call x1, Pallas kernels, fine_gradient(): pl.pallas_call(functools.partial(fine_kernel, groups), grid=(3 * groups,)...  2.89 us
    pallas_call x1, Pallas kernels, prepare(): pl.pallas_call(prepare_kernel, out_shape=(jax.ShapeDtypeStruct((slots + 1...  2.73 us
    ppermute x1, starting transfers between devices, body(): low = lax.ppermute(own[:, voxels - PLANE:], 'dom', forward)  2.36 us
  transfers between devices with their start and end apart: 26, of which 12 were waited for; matrix products, arithmetic and copies ran while one was open for 0% of the time, Pallas kernels for 17%

profile of v8, /device:TPU:0, one launch (start us, length us, event | category | flops | bytes accessed | tf_op | source)
XLA Modules:
  0.0 77.0 jit_solution(18428022544227861965)
XLA Ops:
  0.7 1.0 %fusion = (bf16[3,64,256]{2,1,0:T(8,128)(2,1)S(1)}, bf16[3,64,256]{2,1,0:T(8,128)(2,1)S(1)}) fusion(bf16[3,512,256]{2,1,0:T(8,128)(2,1)} %bitcast.9), kind=kLoop, calls=%fused_computation | loop fusion | bytes 393216 | tf_op jit(solution)/shard_map/slice | solution.py:632
  1.6 2.4 %collective-permute-start = (bf16[3,64,256]{2,1,0:T(8,128)(2,1)S(1)}, bf16[3,64,256]{2,1,0:T(8,128)(2,1)S(1)}, u32[]{:S(2)}, u32[]{:S(2)}) collective-permute-start(bf16[3,64,256]{2,1,0:T(8,128)(2,1)S(1)} %get-tuple-element.60), channel_id=1, source_target_pairs={{0,1},{1,2},{2,3},{3,4},{4,5},{5,6},{6,7},{8,9},{9,10},{10,11},{11... | collective-permute-start | bytes 294920 | tf_op jit(solution)/shard_map/ppermute | solution.py:631
  4.0 1.3 %collective-permute-start.1 = (bf16[3,64,256]{2,1,0:T(8,128)(2,1)S(1)}, bf16[3,64,256]{2,1,0:T(8,128)(2,1)S(1)}, u32[]{:S(2)}, u32[]{:S(2)}) collective-permute-start(bf16[3,64,256]{2,1,0:T(8,128)(2,1)S(1)} %get-tuple-element.59), channel_id=1, source_target_pairs={{1,0},{2,1},{3,2},{4,3},{5,4},{6,5},{7,6},{9,8},{10,9},{11,10},{12... | collective-permute-start | bytes 294920 | tf_op jit(solution)/shard_map/ppermute | solution.py:632
  5.3 2.7 %prepare.1 = (bf16[4,512,256]{2,1,0:T(8,128)(2,1)S(1)}, bf16[256,1536]{1,0:T(8,128)(2,1)S(1)}, bf16[3,256,2304]{2,1,0:T(8,128)(2,1)S(1)}) custom-call(bf16[1,3,512,256]{3,2,1,0:T(8,128)(2,1)} %own_hbm.1, bf16[1,3,512,256]{3,2,1,0:T(8,128)(2,1)} %pre_hbm.3, bf16[27,256,256]{2,1,0:T(8,128)(2,1)} %weight_hbm.1), custom_call_target="tpu_custom_call" | custom-call | flops 4194304 | bytes 12582912 | tf_op jit(solution)/shard_map/prepare/pallas_call | solution.py:160
  8.0 0.0 collective-permute-done.low_ref
  8.0 1.2 %collective-permute-done.1.high_ref = bf16[3,64,256]{2,1,0:T(8,128)(2,1)S(1)} collective-permute-done((bf16[3,64,256]{2,1,0:T(8,128)(2,1)S(1)}, bf16[3,64,256]{2,1,0:T(8,128)(2,1)S(1)}, u32[]{:S(2)}, u32[]{:S(2)}) %collective-permute-start.1) | collective-permute-done | bytes 98336 | tf_op jit(solution)/shard_map/ppermute | solution.py:632
  9.3 0.0 copy-done.2
  9.3 8.0 %input_gradient.1 = (bf16[1,512,256]{2,1,0:T(8,128)(2,1)S(1)}, bf16[1,512,256]{2,1,0:T(8,128)(2,1)S(1)}, bf16[1,512,256]{2,1,0:T(8,128)(2,1)S(1)}, bf16[1920,2304]{1,0:T(8,128)(2,1)S(1)}) custom-call(s32[3,1,27]{2,1,0:T(1,128)S(1)} %bitcast.6, s32[3,1,8]{2,1,0:T(1,128)S(1)} %bitcast.7, bf16[4,512,256]{2,1,0:T(8,128)(2,1)S(1)} %get-tuple-element.31.own_wide, ...), custom_call_target="tpu_custom_call" | custom-call | flops 5435817984 | bytes 8388608 | tf_op jit(solution)/shard_map/input_gradient/pallas_call | solution.py:263
  17.3 3.0 %collective-permute-start.2 = (bf16[1,512,256]{2,1,0:T(8,128)(2,1)S(1)}, bf16[1,512,256]{2,1,0:T(8,128)(2,1)S(1)}, u32[]{:S(2)}, u32[]{:S(2)}) collective-permute-start(bf16[1,512,256]{2,1,0:T(8,128)(2,1)S(1)} %get-tuple-element.33), channel_id=1, source_target_pairs={{1,0},{2,1},{3,2},{4,3},{5,4},{6,5},{7,6},{0,7},{9,8},{10,9},{11,1... | collective-permute-start | bytes 786440 | tf_op jit(solution)/shard_map/ppermute | solution.py:637
  20.4 0.5 collective-permute-start.3
  20.9 5.6 %filter_gradient.1 = (bf16[4,1728,128]{2,1,0:T(8,128)(2,1)S(1)}, bf16[4,1728,128]{2,1,0:T(8,128)(2,1)S(1)}) custom-call(bf16[1920,2304]{1,0:T(8,128)(2,1)S(1)} %get-tuple-element.36.win_ref, bf16[256,1536]{1,0:T(8,128)(2,1)S(1)} %get-tuple-element.37.act_ref), custom_call_target="tpu_custom_call" | custom-call | flops 5435817984 | bytes 8388608 | tf_op jit(solution)/shard_map/filter_gradient/pallas_call | solution.py:319
  26.5 1.6 %collective-permute-start.4 = (bf16[4,1728,128]{2,1,0:T(8,128)(2,1)S(1)}, bf16[4,1728,128]{2,1,0:T(8,128)(2,1)S(1)}, u32[]{:S(2)}, u32[]{:S(2)}) collective-permute-start(bf16[4,1728,128]{2,1,0:T(8,128)(2,1)S(1)} %get-tuple-element.39), channel_id=1, source_target_pairs={{0,1},{1,0},{2,3},{3,2},{4,5},{5,4},{6,7},{7,6},{8,9},{9,8},{10,11... | collective-permute-start | bytes 5308424 | tf_op jit(solution)/shard_map/ppermute | solution.py:644
  28.1 0.0 collective-permute-done.2.upper_ref
  28.1 1.3 %collective-permute-done.3.lower_ref = bf16[1,512,256]{2,1,0:T(8,128)(2,1)S(1)} collective-permute-done((bf16[1,512,256]{2,1,0:T(8,128)(2,1)S(1)}, bf16[1,512,256]{2,1,0:T(8,128)(2,1)S(1)}, u32[]{:S(2)}, u32[]{:S(2)}) %collective-permute-start.3) | collective-permute-done | bytes 262176 | tf_op jit(solution)/shard_map/ppermute | solution.py:638
  29.4 1.5 %down_gradient.1 = (bf16[4,256,128]{2,1,0:T(8,128)(2,1)S(1)}, bf16[4,256,128]{2,1,0:T(8,128)(2,1)S(1)}) custom-call(bf16[1,512,256]{2,1,0:T(8,128)(2,1)S(1)} %collective-permute-done.2.upper_ref, bf16[1,512,256]{2,1,0:T(8,128)(2,1)S(1)} %get-tuple-element.34.stay_ref, bf16[1,512,256]{2,1,0:T(8,128)(2,1)S(1)} %collective-permute-done.3.lower_ref, ...), custom_call_target="tpu_custom_call" | custom-call | flops 25769803776 | bytes 8388608 | tf_op jit(solution)/shard_map/down_gradient/pallas_call | solution.py:381
  31.0 0.1 collective-permute-start.5
  31.0 1.5 %collective-permute-done.5.down_got_ref = bf16[4,256,128]{2,1,0:T(8,128)(2,1)S(1)} collective-permute-done((bf16[4,256,128]{2,1,0:T(8,128)(2,1)S(1)}, bf16[4,256,128]{2,1,0:T(8,128)(2,1)S(1)}, u32[]{:S(2)}, u32[]{:S(2)}) %collective-permute-start.5) | collective-permute-done | bytes 262176 | tf_op jit(solution)/shard_map/ppermute | solution.py:645
  32.6 0.0 collective-permute-done.4.conv_got_ref
  32.6 0.4 pair_sum.1
  33.0 1.6 %collective-permute-start.6 = (bf16[4,352,128]{2,1,0:T(8,128)(2,1)S(1)}, bf16[4,352,128]{2,1,0:T(8,128)(2,1)S(1)}, u32[]{:S(2)}, u32[]{:S(2)}) collective-permute-start(bf16[4,352,128]{2,1,0:T(8,128)(2,1)S(1)} %get-tuple-element.43), channel_id=1, source_target_pairs={{0,6},{1,7},{2,4},{3,5},{4,2},{5,3},{6,0},{7,1},{8,14},{9,15},{10,... | collective-permute-start | bytes 1081352 | tf_op jit(solution)/shard_map/ppermute | solution.py:48
  34.6 2.5 %collective-permute-start.7 = (bf16[4,352,128]{2,1,0:T(8,128)(2,1)S(1)}, bf16[4,352,128]{2,1,0:T(8,128)(2,1)S(1)}, u32[]{:S(2)}, u32[]{:S(2)}) collective-permute-start(bf16[4,352,128]{2,1,0:T(8,128)(2,1)S(1)} %get-tuple-element.44), channel_id=1, source_target_pairs={{0,4},{1,5},{2,6},{3,7},{4,0},{5,1},{6,2},{7,3},{8,12},{9,13},{10,... | collective-permute-start | bytes 1081352 | tf_op jit(solution)/shard_map/ppermute | solution.py:48
  37.1 0.0 collective-permute-start.8
  37.1 1.6 %collective-permute-start.10 = (bf16[576,128]{1,0:T(8,128)(2,1)S(1)}, bf16[576,128]{1,0:T(8,128)(2,1)S(1)}, u32[]{:S(2)}, u32[]{:S(2)}) collective-permute-start(bf16[576,128]{1,0:T(8,128)(2,1)S(1)} %get-tuple-element.48), channel_id=1, source_target_pairs={{0,8},{8,0},{16,24},{24,16},{1,9},{9,1},{17,25},{25,17},{2,10},{10... | collective-permute-start | bytes 442376 | tf_op jit(solution)/shard_map/ppermute | solution.py:48
  38.7 2.6 %collective-permute-start.11 = (bf16[576,128]{1,0:T(8,128)(2,1)S(1)}, bf16[576,128]{1,0:T(8,128)(2,1)S(1)}, u32[]{:S(2)}, u32[]{:S(2)}) collective-permute-start(bf16[576,128]{1,0:T(8,128)(2,1)S(1)} %get-tuple-element.49), channel_id=1, source_target_pairs={{0,16},{8,24},{16,0},{24,8},{1,17},{9,25},{17,1},{25,9},{2,18},{10... | collective-permute-start | bytes 442376 | tf_op jit(solution)/shard_map/ppermute | solution.py:48
  41.2 4.1 %collective-permute-done.10.refs_6_ = bf16[576,128]{1,0:T(8,128)(2,1)S(1)} collective-permute-done((bf16[576,128]{1,0:T(8,128)(2,1)S(1)}, bf16[576,128]{1,0:T(8,128)(2,1)S(1)}, u32[]{:S(2)}, u32[]{:S(2)}) %collective-permute-start.10) | collective-permute-done | bytes 147488 | tf_op jit(solution)/shard_map/ppermute | solution.py:48
  45.3 2.9 %collective-permute-start.9 = (bf16[576,128]{1,0:T(8,128)(2,1)S(1)}, bf16[576,128]{1,0:T(8,128)(2,1)S(1)}, u32[]{:S(2)}, u32[]{:S(2)}) collective-permute-start(bf16[576,128]{1,0:T(8,128)(2,1)S(1)} %get-tuple-element.47), channel_id=1, source_target_pairs={{0,24},{8,16},{16,8},{24,0},{1,25},{9,17},{17,9},{25,1},{2,26},{10... | collective-permute-start | bytes 442376 | tf_op jit(solution)/shard_map/ppermute | solution.py:48
  48.2 1.8 %collective-permute-done.11.refs_7_ = bf16[576,128]{1,0:T(8,128)(2,1)S(1)} collective-permute-done((bf16[576,128]{1,0:T(8,128)(2,1)S(1)}, bf16[576,128]{1,0:T(8,128)(2,1)S(1)}, u32[]{:S(2)}, u32[]{:S(2)}) %collective-permute-start.11) | collective-permute-done | bytes 147488 | tf_op jit(solution)/shard_map/ppermute | solution.py:48
  50.0 2.4 %collective-permute-done.9.refs_5_ = bf16[576,128]{1,0:T(8,128)(2,1)S(1)} collective-permute-done((bf16[576,128]{1,0:T(8,128)(2,1)S(1)}, bf16[576,128]{1,0:T(8,128)(2,1)S(1)}, u32[]{:S(2)}, u32[]{:S(2)}) %collective-permute-start.9) | collective-permute-done | bytes 147488 | tf_op jit(solution)/shard_map/ppermute | solution.py:48
  52.4 0.0 collective-permute-done.6.refs_1_
  52.4 0.0 collective-permute-done.7.refs_2_
  52.4 0.0 collective-permute-done.8.refs_3_
  52.4 0.2 middle_sum.1
  52.6 3.6 %collective-permute-start.15 = (bf16[352,128]{1,0:T(8,128)(2,1)S(1)}, bf16[352,128]{1,0:T(8,128)(2,1)S(1)}, u32[]{:S(2)}, u32[]{:S(2)}) collective-permute-start(bf16[352,128]{1,0:T(8,128)(2,1)S(1)} %get-tuple-element.52), channel_id=1, source_target_pairs={{0,24},{8,16},{16,8},{24,0},{1,25},{9,17},{17,9},{25,1},{2,26},{10... | collective-permute-start | bytes 270344 | tf_op jit(solution)/shard_map/ppermute | solution.py:48
  56.2 2.6 %collective-permute-start.12 = (bf16[576,128]{1,0:T(8,128)(2,1)S(1)}, bf16[576,128]{1,0:T(8,128)(2,1)S(1)}, u32[]{:S(2)}, u32[]{:S(2)}) collective-permute-start(bf16[576,128]{1,0:T(8,128)(2,1)S(1)} %get-tuple-element.50.refs_0_), channel_id=1, source_target_pairs={{0,6},{1,7},{2,4},{3,5},{4,2},{5,3},{6,0},{7,1},{8,14},{9,15},{10,... | collective-permute-start | bytes 442376 | tf_op jit(solution)/shard_map/ppermute | solution.py:48
  58.9 0.6 collective-permute-start.13
  59.5 0.2 collective-permute-start.14
  59.7 0.5 collective-permute-start.16
  60.2 0.0 collective-permute-done.15.refs_5_
  60.2 2.2 %collective-permute-start.17 = (bf16[352,128]{1,0:T(8,128)(2,1)S(1)}, bf16[352,128]{1,0:T(8,128)(2,1)S(1)}, u32[]{:S(2)}, u32[]{:S(2)}) collective-permute-start(bf16[352,128]{1,0:T(8,128)(2,1)S(1)} %get-tuple-element.54), channel_id=1, source_target_pairs={{0,8},{8,0},{16,24},{24,16},{1,9},{9,1},{17,25},{25,17},{2,10},{10... | collective-permute-start | bytes 270344 | tf_op jit(solution)/shard_map/ppermute | solution.py:48
  62.4 0.0 copy-done
  62.4 2.9 %fine_gradient.1.refs_8_ = bf16[24,512,128]{2,1,0:T(8,128)(2,1)} custom-call(bf16[1,512,256]{2,1,0:T(8,128)(2,1)S(1)} %collective-permute-done.2.upper_ref, bf16[1,512,256]{2,1,0:T(8,128)(2,1)S(1)} %get-tuple-element.34.stay_ref, bf16[1,512,256]{2,1,0:T(8,128)(2,1)S(1)} %collective-permute-done.3.lower_ref, bf16[8,128,256]{2,1,0:T(8,128)(2,1)S(1)} %copy-done), custom_call_target="tpu_custom_call" | custom-call | flops 805306368 | bytes 4194304 | tf_op jit(solution)/shard_map/fine_gradient/pallas_call | solution.py:426
  65.3 0.8 %collective-permute-done.16.refs_6_ = bf16[352,128]{1,0:T(8,128)(2,1)S(1)} collective-permute-done((bf16[352,128]{1,0:T(8,128)(2,1)S(1)}, bf16[352,128]{1,0:T(8,128)(2,1)S(1)}, u32[]{:S(2)}, u32[]{:S(2)}) %collective-permute-start.16) | collective-permute-done | bytes 90144 | tf_op jit(solution)/shard_map/ppermute | solution.py:48
  66.1 0.0 collective-permute-done.17.refs_7_
  66.1 0.0 collective-permute-done.12.refs_1_
  66.1 0.0 collective-permute-done.13.refs_2_
  66.1 0.0 collective-permute-done.14.refs_3_
  66.1 0.1 last_sum.1
  66.3 2.2 %collective-permute-start.18 = (bf16[352,128]{1,0:T(8,128)(2,1)S(1)}, bf16[352,128]{1,0:T(8,128)(2,1)S(1)}, u32[]{:S(2)}, u32[]{:S(2)}) collective-permute-start(bf16[352,128]{1,0:T(8,128)(2,1)S(1)} %get-tuple-element.55.refs_0_), channel_id=1, source_target_pairs={{0,6},{1,7},{2,4},{3,5},{4,2},{5,3},{6,0},{7,1},{8,14},{9,15},{10,... | collective-permute-start | bytes 270344 | tf_op jit(solution)/shard_map/ppermute | solution.py:48
  68.5 1.1 %collective-permute-start.19 = (bf16[352,128]{1,0:T(8,128)(2,1)S(1)}, bf16[352,128]{1,0:T(8,128)(2,1)S(1)}, u32[]{:S(2)}, u32[]{:S(2)}) collective-permute-start(bf16[352,128]{1,0:T(8,128)(2,1)S(1)} %get-tuple-element.55.refs_0_), channel_id=1, source_target_pairs={{0,4},{1,5},{2,6},{3,7},{4,0},{5,1},{6,2},{7,3},{8,12},{9,13},{10,... | collective-permute-start | bytes 270344 | tf_op jit(solution)/shard_map/ppermute | solution.py:48
  69.6 0.3 collective-permute-start.20
  69.8 0.0 collective-permute-start.25
  69.8 0.5 collective-permute-start.21
  70.3 2.2 %collective-permute-done.18.refs_1_ = bf16[352,128]{1,0:T(8,128)(2,1)S(1)} collective-permute-done((bf16[352,128]{1,0:T(8,128)(2,1)S(1)}, bf16[352,128]{1,0:T(8,128)(2,1)S(1)}, u32[]{:S(2)}, u32[]{:S(2)}) %collective-permute-start.18) | collective-permute-done | bytes 90144 | tf_op jit(solution)/shard_map/ppermute | solution.py:48
  72.6 0.0 collective-permute-start.22
  72.6 0.8 %collective-permute-done.19.refs_2_ = bf16[352,128]{1,0:T(8,128)(2,1)S(1)} collective-permute-done((bf16[352,128]{1,0:T(8,128)(2,1)S(1)}, bf16[352,128]{1,0:T(8,128)(2,1)S(1)}, u32[]{:S(2)}, u32[]{:S(2)}) %collective-permute-start.19) | collective-permute-done | bytes 90144 | tf_op jit(solution)/shard_map/ppermute | solution.py:48
  73.3 0.0 collective-permute-start.23
  73.3 0.7 collective-permute-done.20.refs_3_
  74.1 0.0 collective-permute-start.24
  74.1 0.0 collective-permute-done.21.refs_4_
  74.1 0.0 collective-permute-done.25.refs_9_
  74.1 0.0 collective-permute-done.22.refs_5_
  74.1 0.5 collective-permute-done.23.refs_6_
  74.6 0.7 collective-permute-done.24.refs_7_
  75.4 1.5 %gather_up.1 = (f32[1728,256]{1,0:T(8,128)}, f32[256,256]{1,0:T(8,128)}) custom-call(bf16[352,128]{1,0:T(8,128)(2,1)S(1)} %get-tuple-element.55.refs_0_, bf16[352,128]{1,0:T(8,128)(2,1)S(1)} %collective-permute-done.18.refs_1_, bf16[352,128]{1,0:T(8,128)(2,1)S(1)} %collective-permute-done.19.refs_2_, bf16[352,128]{1,0:T(8,128)(2,1)S(1)} %collective-permute-done.20.refs_3_, ...), custom_call_target="tpu_custom_call" | custom-call | flops 2752512 | bytes 2752512 | tf_op jit(solution)/shard_map/gather_up/pallas_call | solution.py:594
  (6 shorter events, 0.0 us)
Async XLA Ops:
  0.6 8.7 %copy-start.2 = (s32[1,3,27]{2,0,1:T(1,128)S(1)}, s32[1,3,27]{2,0,1:T(1,128)}, u32[]{:S(2)}) copy-start(s32[1,3,27]{2,0,1:T(1,128)} %param.12) | copy-start | bytes 976
  0.6 8.7 %copy-start.3 = (s32[1,1,3,8]{3,1,2,0:T(1,128)S(1)}, s32[1,1,3,8]{3,1,2,0:T(1,128)}, u32[]{:S(2)}) copy-start(s32[1,1,3,8]{3,1,2,0:T(1,128)} %param.13) | copy-start | bytes 292
  1.6 6.4 %collective-permute-start = (bf16[3,64,256]{2,1,0:T(8,128)(2,1)S(1)}, bf16[3,64,256]{2,1,0:T(8,128)(2,1)S(1)}, u32[]{:S(2)}, u32[]{:S(2)}) collective-permute-start(bf16[3,64,256]{2,1,0:T(8,128)(2,1)S(1)} %get-tuple-element.60), channel_id=1, source_target_pairs={{0,1},{1,2},{2,3},{3,4},{4,5},{5,6},{6,7},{8,9},{9,10},{10,11},{11... | collective-permute-start | bytes 294920 | tf_op jit(solution)/shard_map/ppermute | solution.py:631
  4.0 5.3 %collective-permute-start.1 = (bf16[3,64,256]{2,1,0:T(8,128)(2,1)S(1)}, bf16[3,64,256]{2,1,0:T(8,128)(2,1)S(1)}, u32[]{:S(2)}, u32[]{:S(2)}) collective-permute-start(bf16[3,64,256]{2,1,0:T(8,128)(2,1)S(1)} %get-tuple-element.59), channel_id=1, source_target_pairs={{1,0},{2,1},{3,2},{4,3},{5,4},{6,5},{7,6},{9,8},{10,9},{11,10},{12... | collective-permute-start | bytes 294920 | tf_op jit(solution)/shard_map/ppermute | solution.py:632
  17.3 10.8 %collective-permute-start.2 = (bf16[1,512,256]{2,1,0:T(8,128)(2,1)S(1)}, bf16[1,512,256]{2,1,0:T(8,128)(2,1)S(1)}, u32[]{:S(2)}, u32[]{:S(2)}) collective-permute-start(bf16[1,512,256]{2,1,0:T(8,128)(2,1)S(1)} %get-tuple-element.33), channel_id=1, source_target_pairs={{1,0},{2,1},{3,2},{4,3},{5,4},{6,5},{7,6},{0,7},{9,8},{10,9},{11,1... | collective-permute-start | bytes 786440 | tf_op jit(solution)/shard_map/ppermute | solution.py:637
  20.4 9.1 %collective-permute-start.3 = (bf16[1,512,256]{2,1,0:T(8,128)(2,1)S(1)}, bf16[1,512,256]{2,1,0:T(8,128)(2,1)S(1)}, u32[]{:S(2)}, u32[]{:S(2)}) collective-permute-start(bf16[1,512,256]{2,1,0:T(8,128)(2,1)S(1)} %get-tuple-element.35), channel_id=1, source_target_pairs={{0,1},{1,2},{2,3},{3,4},{4,5},{5,6},{6,7},{7,0},{8,9},{9,10},{10,1... | collective-permute-start | bytes 786440 | tf_op jit(solution)/shard_map/ppermute | solution.py:638
  20.9 8.5 %copy-start.1 = (bf16[1,24,512,128]{3,2,1,0:T(8,128)(2,1)S(1)}, bf16[1,24,512,128]{3,2,1,0:T(8,128)(2,1)}, u32[]{:S(2)}) copy-start(bf16[1,24,512,128]{3,2,1,0:T(8,128)(2,1)} %param.11) | copy-start | bytes 9437188
  26.5 6.0 %collective-permute-start.4 = (bf16[4,1728,128]{2,1,0:T(8,128)(2,1)S(1)}, bf16[4,1728,128]{2,1,0:T(8,128)(2,1)S(1)}, u32[]{:S(2)}, u32[]{:S(2)}) collective-permute-start(bf16[4,1728,128]{2,1,0:T(8,128)(2,1)S(1)} %get-tuple-element.39), channel_id=1, source_target_pairs={{0,1},{1,0},{2,3},{3,2},{4,5},{5,4},{6,7},{7,6},{8,9},{9,8},{10,11... | collective-permute-start | bytes 5308424 | tf_op jit(solution)/shard_map/ppermute | solution.py:644
  31.0 1.6 %collective-permute-start.5 = (bf16[4,256,128]{2,1,0:T(8,128)(2,1)S(1)}, bf16[4,256,128]{2,1,0:T(8,128)(2,1)S(1)}, u32[]{:S(2)}, u32[]{:S(2)}) collective-permute-start(bf16[4,256,128]{2,1,0:T(8,128)(2,1)S(1)} %get-tuple-element.41), channel_id=1, source_target_pairs={{0,1},{1,0},{2,3},{3,2},{4,5},{5,4},{6,7},{7,6},{8,9},{9,8},{10,11... | collective-permute-start | bytes 786440 | tf_op jit(solution)/shard_map/ppermute | solution.py:645
  32.6 29.8 %copy-start = (bf16[8,128,256]{2,1,0:T(8,128)(2,1)S(1)}, bf16[8,128,256]{2,1,0:T(8,128)(2,1)}, u32[]{:S(2)}) copy-start(bf16[8,128,256]{2,1,0:T(8,128)(2,1)} %weight_ref.1) | copy-start | bytes 1572868
  33.0 19.3 %collective-permute-start.6 = (bf16[4,352,128]{2,1,0:T(8,128)(2,1)S(1)}, bf16[4,352,128]{2,1,0:T(8,128)(2,1)S(1)}, u32[]{:S(2)}, u32[]{:S(2)}) collective-permute-start(bf16[4,352,128]{2,1,0:T(8,128)(2,1)S(1)} %get-tuple-element.43), channel_id=1, source_target_pairs={{0,6},{1,7},{2,4},{3,5},{4,2},{5,3},{6,0},{7,1},{8,14},{9,15},{10,... | collective-permute-start | bytes 1081352 | tf_op jit(solution)/shard_map/ppermute | solution.py:48
  34.6 17.7 %collective-permute-start.7 = (bf16[4,352,128]{2,1,0:T(8,128)(2,1)S(1)}, bf16[4,352,128]{2,1,0:T(8,128)(2,1)S(1)}, u32[]{:S(2)}, u32[]{:S(2)}) collective-permute-start(bf16[4,352,128]{2,1,0:T(8,128)(2,1)S(1)} %get-tuple-element.44), channel_id=1, source_target_pairs={{0,4},{1,5},{2,6},{3,7},{4,0},{5,1},{6,2},{7,3},{8,12},{9,13},{10,... | collective-permute-start | bytes 1081352 | tf_op jit(solution)/shard_map/ppermute | solution.py:48
  37.1 15.3 %collective-permute-start.8 = (bf16[4,352,128]{2,1,0:T(8,128)(2,1)S(1)}, bf16[4,352,128]{2,1,0:T(8,128)(2,1)S(1)}, u32[]{:S(2)}, u32[]{:S(2)}) collective-permute-start(bf16[4,352,128]{2,1,0:T(8,128)(2,1)S(1)} %get-tuple-element.45), channel_id=1, source_target_pairs={{0,2},{1,3},{2,0},{3,1},{4,6},{5,7},{6,4},{7,5},{8,10},{9,11},{10,... | collective-permute-start | bytes 1081352 | tf_op jit(solution)/shard_map/ppermute | solution.py:48
  37.1 8.2 %collective-permute-start.10 = (bf16[576,128]{1,0:T(8,128)(2,1)S(1)}, bf16[576,128]{1,0:T(8,128)(2,1)S(1)}, u32[]{:S(2)}, u32[]{:S(2)}) collective-permute-start(bf16[576,128]{1,0:T(8,128)(2,1)S(1)} %get-tuple-element.48), channel_id=1, source_target_pairs={{0,8},{8,0},{16,24},{24,16},{1,9},{9,1},{17,25},{25,17},{2,10},{10... | collective-permute-start | bytes 442376 | tf_op jit(solution)/shard_map/ppermute | solution.py:48
  38.7 11.3 %collective-permute-start.11 = (bf16[576,128]{1,0:T(8,128)(2,1)S(1)}, bf16[576,128]{1,0:T(8,128)(2,1)S(1)}, u32[]{:S(2)}, u32[]{:S(2)}) collective-permute-start(bf16[576,128]{1,0:T(8,128)(2,1)S(1)} %get-tuple-element.49), channel_id=1, source_target_pairs={{0,16},{8,24},{16,0},{24,8},{1,17},{9,25},{17,1},{25,9},{2,18},{10... | collective-permute-start | bytes 442376 | tf_op jit(solution)/shard_map/ppermute | solution.py:48
  45.3 7.0 %collective-permute-start.9 = (bf16[576,128]{1,0:T(8,128)(2,1)S(1)}, bf16[576,128]{1,0:T(8,128)(2,1)S(1)}, u32[]{:S(2)}, u32[]{:S(2)}) collective-permute-start(bf16[576,128]{1,0:T(8,128)(2,1)S(1)} %get-tuple-element.47), channel_id=1, source_target_pairs={{0,24},{8,16},{16,8},{24,0},{1,25},{9,17},{17,9},{25,1},{2,26},{10... | collective-permute-start | bytes 442376 | tf_op jit(solution)/shard_map/ppermute | solution.py:48
  52.6 7.6 %collective-permute-start.15 = (bf16[352,128]{1,0:T(8,128)(2,1)S(1)}, bf16[352,128]{1,0:T(8,128)(2,1)S(1)}, u32[]{:S(2)}, u32[]{:S(2)}) collective-permute-start(bf16[352,128]{1,0:T(8,128)(2,1)S(1)} %get-tuple-element.52), channel_id=1, source_target_pairs={{0,24},{8,16},{16,8},{24,0},{1,25},{9,17},{17,9},{25,1},{2,26},{10... | collective-permute-start | bytes 270344 | tf_op jit(solution)/shard_map/ppermute | solution.py:48
  56.2 9.9 %collective-permute-start.12 = (bf16[576,128]{1,0:T(8,128)(2,1)S(1)}, bf16[576,128]{1,0:T(8,128)(2,1)S(1)}, u32[]{:S(2)}, u32[]{:S(2)}) collective-permute-start(bf16[576,128]{1,0:T(8,128)(2,1)S(1)} %get-tuple-element.50.refs_0_), channel_id=1, source_target_pairs={{0,6},{1,7},{2,4},{3,5},{4,2},{5,3},{6,0},{7,1},{8,14},{9,15},{10,... | collective-permute-start | bytes 442376 | tf_op jit(solution)/shard_map/ppermute | solution.py:48
  58.9 7.3 %collective-permute-start.13 = (bf16[576,128]{1,0:T(8,128)(2,1)S(1)}, bf16[576,128]{1,0:T(8,128)(2,1)S(1)}, u32[]{:S(2)}, u32[]{:S(2)}) collective-permute-start(bf16[576,128]{1,0:T(8,128)(2,1)S(1)} %get-tuple-element.50.refs_0_), channel_id=1, source_target_pairs={{0,4},{1,5},{2,6},{3,7},{4,0},{5,1},{6,2},{7,3},{8,12},{9,13},{10,... | collective-permute-start | bytes 442376 | tf_op jit(solution)/shard_map/ppermute | solution.py:48
  59.5 6.7 %collective-permute-start.14 = (bf16[576,128]{1,0:T(8,128)(2,1)S(1)}, bf16[576,128]{1,0:T(8,128)(2,1)S(1)}, u32[]{:S(2)}, u32[]{:S(2)}) collective-permute-start(bf16[576,128]{1,0:T(8,128)(2,1)S(1)} %get-tuple-element.50.refs_0_), channel_id=1, source_target_pairs={{0,2},{1,3},{2,0},{3,1},{4,6},{5,7},{6,4},{7,5},{8,10},{9,11},{10,... | collective-permute-start | bytes 442376 | tf_op jit(solution)/shard_map/ppermute | solution.py:48
  59.7 6.4 %collective-permute-start.16 = (bf16[352,128]{1,0:T(8,128)(2,1)S(1)}, bf16[352,128]{1,0:T(8,128)(2,1)S(1)}, u32[]{:S(2)}, u32[]{:S(2)}) collective-permute-start(bf16[352,128]{1,0:T(8,128)(2,1)S(1)} %get-tuple-element.53), channel_id=1, source_target_pairs={{0,16},{8,24},{16,0},{24,8},{1,17},{9,25},{17,1},{25,9},{2,18},{10... | collective-permute-start | bytes 270344 | tf_op jit(solution)/shard_map/ppermute | solution.py:48
  60.2 5.9 %collective-permute-start.17 = (bf16[352,128]{1,0:T(8,128)(2,1)S(1)}, bf16[352,128]{1,0:T(8,128)(2,1)S(1)}, u32[]{:S(2)}, u32[]{:S(2)}) collective-permute-start(bf16[352,128]{1,0:T(8,128)(2,1)S(1)} %get-tuple-element.54), channel_id=1, source_target_pairs={{0,8},{8,0},{16,24},{24,16},{1,9},{9,1},{17,25},{25,17},{2,10},{10... | collective-permute-start | bytes 270344 | tf_op jit(solution)/shard_map/ppermute | solution.py:48
  66.3 6.3 %collective-permute-start.18 = (bf16[352,128]{1,0:T(8,128)(2,1)S(1)}, bf16[352,128]{1,0:T(8,128)(2,1)S(1)}, u32[]{:S(2)}, u32[]{:S(2)}) collective-permute-start(bf16[352,128]{1,0:T(8,128)(2,1)S(1)} %get-tuple-element.55.refs_0_), channel_id=1, source_target_pairs={{0,6},{1,7},{2,4},{3,5},{4,2},{5,3},{6,0},{7,1},{8,14},{9,15},{10,... | collective-permute-start | bytes 270344 | tf_op jit(solution)/shard_map/ppermute | solution.py:48
  68.5 4.9 %collective-permute-start.19 = (bf16[352,128]{1,0:T(8,128)(2,1)S(1)}, bf16[352,128]{1,0:T(8,128)(2,1)S(1)}, u32[]{:S(2)}, u32[]{:S(2)}) collective-permute-start(bf16[352,128]{1,0:T(8,128)(2,1)S(1)} %get-tuple-element.55.refs_0_), channel_id=1, source_target_pairs={{0,4},{1,5},{2,6},{3,7},{4,0},{5,1},{6,2},{7,3},{8,12},{9,13},{10,... | collective-permute-start | bytes 270344 | tf_op jit(solution)/shard_map/ppermute | solution.py:48
  69.6 4.5 %collective-permute-start.20 = (bf16[352,128]{1,0:T(8,128)(2,1)S(1)}, bf16[352,128]{1,0:T(8,128)(2,1)S(1)}, u32[]{:S(2)}, u32[]{:S(2)}) collective-permute-start(bf16[352,128]{1,0:T(8,128)(2,1)S(1)} %get-tuple-element.55.refs_0_), channel_id=1, source_target_pairs={{0,2},{1,3},{2,0},{3,1},{4,6},{5,7},{6,4},{7,5},{8,10},{9,11},{10,... | collective-permute-start | bytes 270344 | tf_op jit(solution)/shard_map/ppermute | solution.py:48
  69.8 4.3 %collective-permute-start.25 = (bf16[576,128]{1,0:T(8,128)(2,1)S(1)}, bf16[576,128]{1,0:T(8,128)(2,1)S(1)}, u32[]{:S(2)}, u32[]{:S(2)}) collective-permute-start(bf16[576,128]{1,0:T(8,128)(2,1)S(1)} %get-tuple-element.56.refs_8_), channel_id=1, source_target_pairs={{0,1},{1,0},{2,3},{3,2},{4,5},{5,4},{6,7},{7,6},{8,9},{9,8},{10,11... | collective-permute-start | bytes 442376 | tf_op jit(solution)/shard_map/ppermute | solution.py:655
  69.8 4.3 %collective-permute-start.21 = (bf16[352,128]{1,0:T(8,128)(2,1)S(1)}, bf16[352,128]{1,0:T(8,128)(2,1)S(1)}, u32[]{:S(2)}, u32[]{:S(2)}) collective-permute-start(bf16[352,128]{1,0:T(8,128)(2,1)S(1)} %get-tuple-element.55.refs_0_), channel_id=1, source_target_pairs={{0,1},{1,0},{2,3},{3,2},{4,5},{5,4},{6,7},{7,6},{8,9},{9,8},{10,11... | collective-permute-start | bytes 270344 | tf_op jit(solution)/shard_map/ppermute | solution.py:654
  72.6 1.5 %collective-permute-start.22 = (bf16[352,128]{1,0:T(8,128)(2,1)S(1)}, bf16[352,128]{1,0:T(8,128)(2,1)S(1)}, u32[]{:S(2)}, u32[]{:S(2)}) collective-permute-start(bf16[352,128]{1,0:T(8,128)(2,1)S(1)} %collective-permute-done.18.refs_1_), channel_id=1, source_target_pairs={{0,1},{1,0},{2,3},{3,2},{4,5},{5,4},{6,7},{7,6},{8,9},{9,8},{10,11... | collective-permute-start | bytes 270344 | tf_op jit(solution)/shard_map/ppermute | solution.py:654
  73.3 1.3 %collective-permute-start.23 = (bf16[352,128]{1,0:T(8,128)(2,1)S(1)}, bf16[352,128]{1,0:T(8,128)(2,1)S(1)}, u32[]{:S(2)}, u32[]{:S(2)}) collective-permute-start(bf16[352,128]{1,0:T(8,128)(2,1)S(1)} %collective-permute-done.19.refs_2_), channel_id=1, source_target_pairs={{0,1},{1,0},{2,3},{3,2},{4,5},{5,4},{6,7},{7,6},{8,9},{9,8},{10,11... | collective-permute-start | bytes 270344 | tf_op jit(solution)/shard_map/ppermute | solution.py:654
  74.1 1.3 %collective-permute-start.24 = (bf16[352,128]{1,0:T(8,128)(2,1)S(1)}, bf16[352,128]{1,0:T(8,128)(2,1)S(1)}, u32[]{:S(2)}, u32[]{:S(2)}) collective-permute-start(bf16[352,128]{1,0:T(8,128)(2,1)S(1)} %collective-permute-done.20.refs_3_), channel_id=1, source_target_pairs={{0,1},{1,0},{2,3},{3,2},{4,5},{5,4},{6,7},{7,6},{8,9},{9,8},{10,11... | collective-permute-start | bytes 270344 | tf_op jit(solution)/shard_map/ppermute | solution.py:654

commit v9 on v7

--- a/solution.py
+++ b/solution.py
@@ -250,23 +250,11 @@
     last = products(2)
     last[0]()
     interleave(last[1:], finishes(range(HALF)))
-    outs = []
-
-    def leave(side):
-        rows = pl.ds(side * 4 * PLANE, 4 * PLANE)
-        for row, ref in enumerate((to_lower_ref, stay_ref, to_upper_ref)):
-            outs.append(
-                started(
-                    octants_ref.at[pl.ds(row * groups, groups), rows],
-                    ref.at[:, rows],
-                    out_sems.at[3 * side + row],
-                )
-            )
-
-    leave(0)
     for call in finishes(range(HALF, BE)):
         call()
-    leave(1)
+    outs = []
+    for row, ref in enumerate((to_lower_ref, stay_ref, to_upper_ref)):
+        outs.append(started(octants_ref.at[pl.ds(row * groups, groups)], ref, out_sems.at[row]))
     for copy in outs:
         copy.wait()
 
@@ -288,7 +276,7 @@
             pltpu.VMEM((rows, channels), F32),
             pltpu.VMEM((3 * groups + 1, voxels, channels), BF16),
             pltpu.VMEM((slots, voxels, channels), BF16),
-            pltpu.SemaphoreType.DMA((6,)),
+            pltpu.SemaphoreType.DMA((3,)),
             pltpu.SemaphoreType.DMA,
         ],
         compiler_params=params(20),
@@ -552,18 +540,19 @@
     return outs[:shards], outs[shards]
 
 
-def last_kernel(factor, shards, *refs):
+def last_kernel(factor, count, *refs):
     *refs, _, planes_ref, slabs_ref = refs
-    total = tree([part[...].astype(F32) for part in refs[:shards]])
+    total = tree([part[...].astype(F32) for part in refs[count:]])
     planes_ref[...] = (total * factor).astype(BF16)
-    total = tree([part[...].astype(F32) for part in refs[shards:]])
+    steps = far_first(count)
+    total = tree([refs[steps.index(step)][...].astype(F32) for step in range(count)])
     slabs_ref[...] = (total * factor).astype(BF16)
 
 
 def last_sum(factor, slabs, planes, after):
-    parts = [*slabs, *planes]
+    parts = [*planes, *slabs]
     return pl.pallas_call(
-        functools.partial(last_kernel, factor, len(slabs)),
+        functools.partial(last_kernel, factor, len(planes)),
         out_shape=[
             jax.ShapeDtypeStruct(slabs[0].shape, BF16), jax.ShapeDtypeStruct(planes[0].shape, BF16)
         ],
@@ -665,7 +654,7 @@
     planes = spread_out(planes, "dom", 2, far_first(count))
     to_slabs, rest = middle_sum(planes, slabs)
     to_slabs = spread_out(to_slabs, "dp", 1, far_first(shards))
-    mine, rest = last_sum(factor, to_slabs, spread_out([rest] * count, "dom", 2), fine_grad)
+    mine, rest = last_sum(factor, to_slabs, spread_out([rest] * count, "dom", 2, far_first(count)), fine_grad)
     near = spread_out([mine] * count, "dom", 2, far_first(count))
     far = [lax.ppermute(value, "dom", swap) for value in near]
     rest_far = lax.ppermute(rest, "dom", swap)

time: 78.1 us -> 76.8 us (0.983)
  Pallas kernels: 23.9 us -> 22.7 us
    pallas_call x1, Pallas kernels: 8.9 us -> 7.64 us  [input_gradient(): pl.pallas_call(input_kernel, out_shape=(out, out, out, windows), in_specs...]
  transfers between devices with their start and end apart: 26 -> 26, of which waited for: 13 -> 12; matrix products, arithmetic and copies ran while one was open for 0% -> 0% of each run, Pallas kernels for 16% -> 17%
where the time goes in v9:
time: 76.8 us; the launch traced here: 76.6 us
  starting transfers between devices  33.8 us (44%)
  Pallas kernels  22.7 us (30%)
  waiting for transfers between devices  18.2 us (24%)
  local copies, waits for them, and re-layouts  0.98 us (1%)
  between operations  0.94 us (1%)
    ppermute x15, starting transfers between devices, exchange(): return lax.ppermute(value, axis, pairs)  24.4 us
    ppermute x15, waiting for transfers between devices, exchange(): return lax.ppermute(value, axis, pairs)  12.8 us
    pallas_call x1, Pallas kernels, input_gradient(): pl.pallas_call(input_kernel, out_shape=(out, out, out, windows), in_specs...  7.64 us
    pallas_call x1, Pallas kernels, filter_gradient(): pl.pallas_call(functools.partial(filter_kernel, shard_rows), out_shape=(o...  5.64 us
    ppermute x1, starting transfers between devices, body(): from_upper = lax.ppermute(to_lower, 'dom', [(b, a) for a, b in ring])  3.03 us
    pallas_call x1, Pallas kernels, fine_gradient(): pl.pallas_call(functools.partial(fine_kernel, groups), grid=(3 * groups,)...  2.89 us
    pallas_call x1, Pallas kernels, prepare(): pl.pallas_call(prepare_kernel, out_shape=(jax.ShapeDtypeStruct((slots + 1...  2.73 us
    ppermute x1, starting transfers between devices, body(): low = lax.ppermute(own[:, voxels - PLANE:], 'dom', forward)  2.36 us
  transfers between devices with their start and end apart: 26, of which 12 were waited for; matrix products, arithmetic and copies ran while one was open for 0% of the time, Pallas kernels for 17%

profile of v9, /device:TPU:0, one launch (start us, length us, event | category | flops | bytes accessed | tf_op | source)
XLA Modules:
  0.0 76.6 jit_solution(1806925838494191777)
XLA Ops:
  0.6 0.0 copy-start.2
  0.6 0.0 copy-start.3
  0.7 1.0 %fusion = (bf16[3,64,256]{2,1,0:T(8,128)(2,1)S(1)}, bf16[3,64,256]{2,1,0:T(8,128)(2,1)S(1)}) fusion(bf16[3,512,256]{2,1,0:T(8,128)(2,1)} %bitcast.9), kind=kLoop, calls=%fused_computation | loop fusion | bytes 393216 | tf_op jit(solution)/shard_map/slice | solution.py:637
  1.6 2.4 %collective-permute-start = (bf16[3,64,256]{2,1,0:T(8,128)(2,1)S(1)}, bf16[3,64,256]{2,1,0:T(8,128)(2,1)S(1)}, u32[]{:S(2)}, u32[]{:S(2)}) collective-permute-start(bf16[3,64,256]{2,1,0:T(8,128)(2,1)S(1)} %get-tuple-element.60), channel_id=1, source_target_pairs={{0,1},{1,2},{2,3},{3,4},{4,5},{5,6},{6,7},{8,9},{9,10},{10,11},{11... | collective-permute-start | bytes 294920 | tf_op jit(solution)/shard_map/ppermute | solution.py:636
  4.0 1.3 %collective-permute-start.1 = (bf16[3,64,256]{2,1,0:T(8,128)(2,1)S(1)}, bf16[3,64,256]{2,1,0:T(8,128)(2,1)S(1)}, u32[]{:S(2)}, u32[]{:S(2)}) collective-permute-start(bf16[3,64,256]{2,1,0:T(8,128)(2,1)S(1)} %get-tuple-element.59), channel_id=1, source_target_pairs={{1,0},{2,1},{3,2},{4,3},{5,4},{6,5},{7,6},{9,8},{10,9},{11,10},{12... | collective-permute-start | bytes 294920 | tf_op jit(solution)/shard_map/ppermute | solution.py:637
  5.3 2.7 %prepare.1 = (bf16[4,512,256]{2,1,0:T(8,128)(2,1)S(1)}, bf16[256,1536]{1,0:T(8,128)(2,1)S(1)}, bf16[3,256,2304]{2,1,0:T(8,128)(2,1)S(1)}) custom-call(bf16[1,3,512,256]{3,2,1,0:T(8,128)(2,1)} %own_hbm.1, bf16[1,3,512,256]{3,2,1,0:T(8,128)(2,1)} %pre_hbm.3, bf16[27,256,256]{2,1,0:T(8,128)(2,1)} %weight_hbm.1), custom_call_target="tpu_custom_call" | custom-call | flops 4194304 | bytes 12582912 | tf_op jit(solution)/shard_map/prepare/pallas_call | solution.py:160
  8.0 0.0 collective-permute-done.low_ref
  8.0 1.2 %collective-permute-done.1.high_ref = bf16[3,64,256]{2,1,0:T(8,128)(2,1)S(1)} collective-permute-done((bf16[3,64,256]{2,1,0:T(8,128)(2,1)S(1)}, bf16[3,64,256]{2,1,0:T(8,128)(2,1)S(1)}, u32[]{:S(2)}, u32[]{:S(2)}) %collective-permute-start.1) | collective-permute-done | bytes 98336 | tf_op jit(solution)/shard_map/ppermute | solution.py:637
  9.3 7.6 %input_gradient.1 = (bf16[1,512,256]{2,1,0:T(8,128)(2,1)S(1)}, bf16[1,512,256]{2,1,0:T(8,128)(2,1)S(1)}, bf16[1,512,256]{2,1,0:T(8,128)(2,1)S(1)}, bf16[1920,2304]{1,0:T(8,128)(2,1)S(1)}) custom-call(s32[3,1,27]{2,1,0:T(1,128)S(1)} %bitcast.6, s32[3,1,8]{2,1,0:T(1,128)S(1)} %bitcast.7, bf16[4,512,256]{2,1,0:T(8,128)(2,1)S(1)} %get-tuple-element.31.own_wide, ...), custom_call_target="tpu_custom_call" | custom-call | flops 5435817984 | bytes 8388608 | tf_op jit(solution)/shard_map/input_gradient/pallas_call | solution.py:268
  16.9 3.0 %collective-permute-start.2 = (bf16[1,512,256]{2,1,0:T(8,128)(2,1)S(1)}, bf16[1,512,256]{2,1,0:T(8,128)(2,1)S(1)}, u32[]{:S(2)}, u32[]{:S(2)}) collective-permute-start(bf16[1,512,256]{2,1,0:T(8,128)(2,1)S(1)} %get-tuple-element.33), channel_id=1, source_target_pairs={{1,0},{2,1},{3,2},{4,3},{5,4},{6,5},{7,6},{0,7},{9,8},{10,9},{11,1... | collective-permute-start | bytes 786440 | tf_op jit(solution)/shard_map/ppermute | solution.py:642
  20.0 0.5 collective-permute-start.3
  20.5 5.6 %filter_gradient.1 = (bf16[4,1728,128]{2,1,0:T(8,128)(2,1)S(1)}, bf16[4,1728,128]{2,1,0:T(8,128)(2,1)S(1)}) custom-call(bf16[1920,2304]{1,0:T(8,128)(2,1)S(1)} %get-tuple-element.36.win_ref, bf16[256,1536]{1,0:T(8,128)(2,1)S(1)} %get-tuple-element.37.act_ref), custom_call_target="tpu_custom_call" | custom-call | flops 5435817984 | bytes 8388608 | tf_op jit(solution)/shard_map/filter_gradient/pallas_call | solution.py:324
  26.1 1.6 %collective-permute-start.4 = (bf16[4,1728,128]{2,1,0:T(8,128)(2,1)S(1)}, bf16[4,1728,128]{2,1,0:T(8,128)(2,1)S(1)}, u32[]{:S(2)}, u32[]{:S(2)}) collective-permute-start(bf16[4,1728,128]{2,1,0:T(8,128)(2,1)S(1)} %get-tuple-element.39), channel_id=1, source_target_pairs={{0,1},{1,0},{2,3},{3,2},{4,5},{5,4},{6,7},{7,6},{8,9},{9,8},{10,11... | collective-permute-start | bytes 5308424 | tf_op jit(solution)/shard_map/ppermute | solution.py:649
  27.7 0.0 collective-permute-done.2.upper_ref
  27.7 1.3 %collective-permute-done.3.lower_ref = bf16[1,512,256]{2,1,0:T(8,128)(2,1)S(1)} collective-permute-done((bf16[1,512,256]{2,1,0:T(8,128)(2,1)S(1)}, bf16[1,512,256]{2,1,0:T(8,128)(2,1)S(1)}, u32[]{:S(2)}, u32[]{:S(2)}) %collective-permute-start.3) | collective-permute-done | bytes 262176 | tf_op jit(solution)/shard_map/ppermute | solution.py:643
  29.0 1.5 %down_gradient.1 = (bf16[4,256,128]{2,1,0:T(8,128)(2,1)S(1)}, bf16[4,256,128]{2,1,0:T(8,128)(2,1)S(1)}) custom-call(bf16[1,512,256]{2,1,0:T(8,128)(2,1)S(1)} %collective-permute-done.2.upper_ref, bf16[1,512,256]{2,1,0:T(8,128)(2,1)S(1)} %get-tuple-element.34.stay_ref, bf16[1,512,256]{2,1,0:T(8,128)(2,1)S(1)} %collective-permute-done.3.lower_ref, ...), custom_call_target="tpu_custom_call" | custom-call | flops 25769803776 | bytes 8388608 | tf_op jit(solution)/shard_map/down_gradient/pallas_call | solution.py:386
  30.6 0.1 collective-permute-start.5
  30.6 1.5 %collective-permute-done.5.down_got_ref = bf16[4,256,128]{2,1,0:T(8,128)(2,1)S(1)} collective-permute-done((bf16[4,256,128]{2,1,0:T(8,128)(2,1)S(1)}, bf16[4,256,128]{2,1,0:T(8,128)(2,1)S(1)}, u32[]{:S(2)}, u32[]{:S(2)}) %collective-permute-start.5) | collective-permute-done | bytes 262176 | tf_op jit(solution)/shard_map/ppermute | solution.py:650
  32.2 0.0 collective-permute-done.4.conv_got_ref
  32.2 0.4 pair_sum.1
  32.6 1.6 %collective-permute-start.6 = (bf16[4,352,128]{2,1,0:T(8,128)(2,1)S(1)}, bf16[4,352,128]{2,1,0:T(8,128)(2,1)S(1)}, u32[]{:S(2)}, u32[]{:S(2)}) collective-permute-start(bf16[4,352,128]{2,1,0:T(8,128)(2,1)S(1)} %get-tuple-element.43), channel_id=1, source_target_pairs={{0,6},{1,7},{2,4},{3,5},{4,2},{5,3},{6,0},{7,1},{8,14},{9,15},{10,... | collective-permute-start | bytes 1081352 | tf_op jit(solution)/shard_map/ppermute | solution.py:48
  34.2 2.4 %collective-permute-start.7 = (bf16[4,352,128]{2,1,0:T(8,128)(2,1)S(1)}, bf16[4,352,128]{2,1,0:T(8,128)(2,1)S(1)}, u32[]{:S(2)}, u32[]{:S(2)}) collective-permute-start(bf16[4,352,128]{2,1,0:T(8,128)(2,1)S(1)} %get-tuple-element.44), channel_id=1, source_target_pairs={{0,4},{1,5},{2,6},{3,7},{4,0},{5,1},{6,2},{7,3},{8,12},{9,13},{10,... | collective-permute-start | bytes 1081352 | tf_op jit(solution)/shard_map/ppermute | solution.py:48
  36.7 0.0 collective-permute-start.8
  36.7 1.6 %collective-permute-start.10 = (bf16[576,128]{1,0:T(8,128)(2,1)S(1)}, bf16[576,128]{1,0:T(8,128)(2,1)S(1)}, u32[]{:S(2)}, u32[]{:S(2)}) collective-permute-start(bf16[576,128]{1,0:T(8,128)(2,1)S(1)} %get-tuple-element.48), channel_id=1, source_target_pairs={{0,8},{8,0},{16,24},{24,16},{1,9},{9,1},{17,25},{25,17},{2,10},{10... | collective-permute-start | bytes 442376 | tf_op jit(solution)/shard_map/ppermute | solution.py:48
  38.2 2.6 %collective-permute-start.11 = (bf16[576,128]{1,0:T(8,128)(2,1)S(1)}, bf16[576,128]{1,0:T(8,128)(2,1)S(1)}, u32[]{:S(2)}, u32[]{:S(2)}) collective-permute-start(bf16[576,128]{1,0:T(8,128)(2,1)S(1)} %get-tuple-element.49), channel_id=1, source_target_pairs={{0,16},{8,24},{16,0},{24,8},{1,17},{9,25},{17,1},{25,9},{2,18},{10... | collective-permute-start | bytes 442376 | tf_op jit(solution)/shard_map/ppermute | solution.py:48
  40.9 4.1 %collective-permute-done.10.refs_6_ = bf16[576,128]{1,0:T(8,128)(2,1)S(1)} collective-permute-done((bf16[576,128]{1,0:T(8,128)(2,1)S(1)}, bf16[576,128]{1,0:T(8,128)(2,1)S(1)}, u32[]{:S(2)}, u32[]{:S(2)}) %collective-permute-start.10) | collective-permute-done | bytes 147488 | tf_op jit(solution)/shard_map/ppermute | solution.py:48
  44.9 2.8 %collective-permute-start.9 = (bf16[576,128]{1,0:T(8,128)(2,1)S(1)}, bf16[576,128]{1,0:T(8,128)(2,1)S(1)}, u32[]{:S(2)}, u32[]{:S(2)}) collective-permute-start(bf16[576,128]{1,0:T(8,128)(2,1)S(1)} %get-tuple-element.47), channel_id=1, source_target_pairs={{0,24},{8,16},{16,8},{24,0},{1,25},{9,17},{17,9},{25,1},{2,26},{10... | collective-permute-start | bytes 442376 | tf_op jit(solution)/shard_map/ppermute | solution.py:48
  47.8 1.8 %collective-permute-done.11.refs_7_ = bf16[576,128]{1,0:T(8,128)(2,1)S(1)} collective-permute-done((bf16[576,128]{1,0:T(8,128)(2,1)S(1)}, bf16[576,128]{1,0:T(8,128)(2,1)S(1)}, u32[]{:S(2)}, u32[]{:S(2)}) %collective-permute-start.11) | collective-permute-done | bytes 147488 | tf_op jit(solution)/shard_map/ppermute | solution.py:48
  49.5 2.4 %collective-permute-done.9.refs_5_ = bf16[576,128]{1,0:T(8,128)(2,1)S(1)} collective-permute-done((bf16[576,128]{1,0:T(8,128)(2,1)S(1)}, bf16[576,128]{1,0:T(8,128)(2,1)S(1)}, u32[]{:S(2)}, u32[]{:S(2)}) %collective-permute-start.9) | collective-permute-done | bytes 147488 | tf_op jit(solution)/shard_map/ppermute | solution.py:48
  52.0 0.0 collective-permute-done.6.refs_1_
  52.0 0.0 collective-permute-done.7.refs_2_
  52.0 0.0 collective-permute-done.8.refs_3_
  52.0 0.2 middle_sum.1
  52.2 3.6 %collective-permute-start.15 = (bf16[352,128]{1,0:T(8,128)(2,1)S(1)}, bf16[352,128]{1,0:T(8,128)(2,1)S(1)}, u32[]{:S(2)}, u32[]{:S(2)}) collective-permute-start(bf16[352,128]{1,0:T(8,128)(2,1)S(1)} %get-tuple-element.52), channel_id=1, source_target_pairs={{0,24},{8,16},{16,8},{24,0},{1,25},{9,17},{17,9},{25,1},{2,26},{10... | collective-permute-start | bytes 270344 | tf_op jit(solution)/shard_map/ppermute | solution.py:48
  55.8 2.6 %collective-permute-start.12 = (bf16[576,128]{1,0:T(8,128)(2,1)S(1)}, bf16[576,128]{1,0:T(8,128)(2,1)S(1)}, u32[]{:S(2)}, u32[]{:S(2)}) collective-permute-start(bf16[576,128]{1,0:T(8,128)(2,1)S(1)} %get-tuple-element.50.refs_0_), channel_id=1, source_target_pairs={{0,6},{1,7},{2,4},{3,5},{4,2},{5,3},{6,0},{7,1},{8,14},{9,15},{10,... | collective-permute-start | bytes 442376 | tf_op jit(solution)/shard_map/ppermute | solution.py:48
  58.5 0.6 collective-permute-start.13
  59.1 0.2 collective-permute-start.14
  59.3 0.5 collective-permute-start.16
  59.8 0.0 collective-permute-done.15.refs_5_
  59.8 2.2 %collective-permute-start.17 = (bf16[352,128]{1,0:T(8,128)(2,1)S(1)}, bf16[352,128]{1,0:T(8,128)(2,1)S(1)}, u32[]{:S(2)}, u32[]{:S(2)}) collective-permute-start(bf16[352,128]{1,0:T(8,128)(2,1)S(1)} %get-tuple-element.54), channel_id=1, source_target_pairs={{0,8},{8,0},{16,24},{24,16},{1,9},{9,1},{17,25},{25,17},{2,10},{10... | collective-permute-start | bytes 270344 | tf_op jit(solution)/shard_map/ppermute | solution.py:48
  62.0 2.9 %fine_gradient.1.refs_8_ = bf16[24,512,128]{2,1,0:T(8,128)(2,1)} custom-call(bf16[1,512,256]{2,1,0:T(8,128)(2,1)S(1)} %collective-permute-done.2.upper_ref, bf16[1,512,256]{2,1,0:T(8,128)(2,1)S(1)} %get-tuple-element.34.stay_ref, bf16[1,512,256]{2,1,0:T(8,128)(2,1)S(1)} %collective-permute-done.3.lower_ref, bf16[8,128,256]{2,1,0:T(8,128)(2,1)S(1)} %copy-done), custom_call_target="tpu_custom_call" | custom-call | flops 805306368 | bytes 4194304 | tf_op jit(solution)/shard_map/fine_gradient/pallas_call | solution.py:431
  64.9 0.8 %collective-permute-done.16.refs_6_ = bf16[352,128]{1,0:T(8,128)(2,1)S(1)} collective-permute-done((bf16[352,128]{1,0:T(8,128)(2,1)S(1)}, bf16[352,128]{1,0:T(8,128)(2,1)S(1)}, u32[]{:S(2)}, u32[]{:S(2)}) %collective-permute-start.16) | collective-permute-done | bytes 90144 | tf_op jit(solution)/shard_map/ppermute | solution.py:48
  65.7 0.0 collective-permute-done.17.refs_7_
  65.7 0.0 collective-permute-done.12.refs_1_
  65.7 0.0 collective-permute-done.13.refs_2_
  65.7 0.0 collective-permute-done.14.refs_3_
  65.7 0.1 last_sum.1
  65.9 2.2 %collective-permute-start.18 = (bf16[352,128]{1,0:T(8,128)(2,1)S(1)}, bf16[352,128]{1,0:T(8,128)(2,1)S(1)}, u32[]{:S(2)}, u32[]{:S(2)}) collective-permute-start(bf16[352,128]{1,0:T(8,128)(2,1)S(1)} %get-tuple-element.55.refs_0_), channel_id=1, source_target_pairs={{0,6},{1,7},{2,4},{3,5},{4,2},{5,3},{6,0},{7,1},{8,14},{9,15},{10,... | collective-permute-start | bytes 270344 | tf_op jit(solution)/shard_map/ppermute | solution.py:48
  68.1 1.1 %collective-permute-start.19 = (bf16[352,128]{1,0:T(8,128)(2,1)S(1)}, bf16[352,128]{1,0:T(8,128)(2,1)S(1)}, u32[]{:S(2)}, u32[]{:S(2)}) collective-permute-start(bf16[352,128]{1,0:T(8,128)(2,1)S(1)} %get-tuple-element.55.refs_0_), channel_id=1, source_target_pairs={{0,4},{1,5},{2,6},{3,7},{4,0},{5,1},{6,2},{7,3},{8,12},{9,13},{10,... | collective-permute-start | bytes 270344 | tf_op jit(solution)/shard_map/ppermute | solution.py:48
  69.2 0.3 collective-permute-start.20
  69.4 0.0 collective-permute-start.25
  69.4 0.5 collective-permute-start.21
  69.9 2.2 %collective-permute-done.18.refs_1_ = bf16[352,128]{1,0:T(8,128)(2,1)S(1)} collective-permute-done((bf16[352,128]{1,0:T(8,128)(2,1)S(1)}, bf16[352,128]{1,0:T(8,128)(2,1)S(1)}, u32[]{:S(2)}, u32[]{:S(2)}) %collective-permute-start.18) | collective-permute-done | bytes 90144 | tf_op jit(solution)/shard_map/ppermute | solution.py:48
  72.2 0.0 collective-permute-start.22
  72.2 0.8 %collective-permute-done.19.refs_2_ = bf16[352,128]{1,0:T(8,128)(2,1)S(1)} collective-permute-done((bf16[352,128]{1,0:T(8,128)(2,1)S(1)}, bf16[352,128]{1,0:T(8,128)(2,1)S(1)}, u32[]{:S(2)}, u32[]{:S(2)}) %collective-permute-start.19) | collective-permute-done | bytes 90144 | tf_op jit(solution)/shard_map/ppermute | solution.py:48
  72.9 0.0 collective-permute-start.23
  73.0 0.7 collective-permute-done.20.refs_3_
  73.7 0.0 collective-permute-start.24
  73.7 0.0 collective-permute-done.21.refs_4_
  73.7 0.0 collective-permute-done.25.refs_9_
  73.7 0.0 collective-permute-done.22.refs_5_
  73.7 0.5 collective-permute-done.23.refs_6_
  74.2 0.7 collective-permute-done.24.refs_7_
  75.0 1.5 %gather_up.1 = (f32[1728,256]{1,0:T(8,128)}, f32[256,256]{1,0:T(8,128)}) custom-call(bf16[352,128]{1,0:T(8,128)(2,1)S(1)} %get-tuple-element.55.refs_0_, bf16[352,128]{1,0:T(8,128)(2,1)S(1)} %collective-permute-done.18.refs_1_, bf16[352,128]{1,0:T(8,128)(2,1)S(1)} %collective-permute-done.19.refs_2_, bf16[352,128]{1,0:T(8,128)(2,1)S(1)} %collective-permute-done.20.refs_3_, ...), custom_call_target="tpu_custom_call" | custom-call | flops 2752512 | bytes 2752512 | tf_op jit(solution)/shard_map/gather_up/pallas_call | solution.py:599
  (6 shorter events, 0.0 us)
Async XLA Ops:
  0.6 8.7 %copy-start.2 = (s32[1,3,27]{2,0,1:T(1,128)S(1)}, s32[1,3,27]{2,0,1:T(1,128)}, u32[]{:S(2)}) copy-start(s32[1,3,27]{2,0,1:T(1,128)} %param.12) | copy-start | bytes 976
  0.6 8.7 %copy-start.3 = (s32[1,1,3,8]{3,1,2,0:T(1,128)S(1)}, s32[1,1,3,8]{3,1,2,0:T(1,128)}, u32[]{:S(2)}) copy-start(s32[1,1,3,8]{3,1,2,0:T(1,128)} %param.13) | copy-start | bytes 292
  1.6 6.4 %collective-permute-start = (bf16[3,64,256]{2,1,0:T(8,128)(2,1)S(1)}, bf16[3,64,256]{2,1,0:T(8,128)(2,1)S(1)}, u32[]{:S(2)}, u32[]{:S(2)}) collective-permute-start(bf16[3,64,256]{2,1,0:T(8,128)(2,1)S(1)} %get-tuple-element.60), channel_id=1, source_target_pairs={{0,1},{1,2},{2,3},{3,4},{4,5},{5,6},{6,7},{8,9},{9,10},{10,11},{11... | collective-permute-start | bytes 294920 | tf_op jit(solution)/shard_map/ppermute | solution.py:636
  4.0 5.3 %collective-permute-start.1 = (bf16[3,64,256]{2,1,0:T(8,128)(2,1)S(1)}, bf16[3,64,256]{2,1,0:T(8,128)(2,1)S(1)}, u32[]{:S(2)}, u32[]{:S(2)}) collective-permute-start(bf16[3,64,256]{2,1,0:T(8,128)(2,1)S(1)} %get-tuple-element.59), channel_id=1, source_target_pairs={{1,0},{2,1},{3,2},{4,3},{5,4},{6,5},{7,6},{9,8},{10,9},{11,10},{12... | collective-permute-start | bytes 294920 | tf_op jit(solution)/shard_map/ppermute | solution.py:637
  16.9 10.8 %collective-permute-start.2 = (bf16[1,512,256]{2,1,0:T(8,128)(2,1)S(1)}, bf16[1,512,256]{2,1,0:T(8,128)(2,1)S(1)}, u32[]{:S(2)}, u32[]{:S(2)}) collective-permute-start(bf16[1,512,256]{2,1,0:T(8,128)(2,1)S(1)} %get-tuple-element.33), channel_id=1, source_target_pairs={{1,0},{2,1},{3,2},{4,3},{5,4},{6,5},{7,6},{0,7},{9,8},{10,9},{11,1... | collective-permute-start | bytes 786440 | tf_op jit(solution)/shard_map/ppermute | solution.py:642
  20.0 9.1 %collective-permute-start.3 = (bf16[1,512,256]{2,1,0:T(8,128)(2,1)S(1)}, bf16[1,512,256]{2,1,0:T(8,128)(2,1)S(1)}, u32[]{:S(2)}, u32[]{:S(2)}) collective-permute-start(bf16[1,512,256]{2,1,0:T(8,128)(2,1)S(1)} %get-tuple-element.35), channel_id=1, source_target_pairs={{0,1},{1,2},{2,3},{3,4},{4,5},{5,6},{6,7},{7,0},{8,9},{9,10},{10,1... | collective-permute-start | bytes 786440 | tf_op jit(solution)/shard_map/ppermute | solution.py:643
  20.5 8.6 %copy-start.1 = (bf16[1,24,512,128]{3,2,1,0:T(8,128)(2,1)S(1)}, bf16[1,24,512,128]{3,2,1,0:T(8,128)(2,1)}, u32[]{:S(2)}) copy-start(bf16[1,24,512,128]{3,2,1,0:T(8,128)(2,1)} %param.11) | copy-start | bytes 9437188
  26.1 6.0 %collective-permute-start.4 = (bf16[4,1728,128]{2,1,0:T(8,128)(2,1)S(1)}, bf16[4,1728,128]{2,1,0:T(8,128)(2,1)S(1)}, u32[]{:S(2)}, u32[]{:S(2)}) collective-permute-start(bf16[4,1728,128]{2,1,0:T(8,128)(2,1)S(1)} %get-tuple-element.39), channel_id=1, source_target_pairs={{0,1},{1,0},{2,3},{3,2},{4,5},{5,4},{6,7},{7,6},{8,9},{9,8},{10,11... | collective-permute-start | bytes 5308424 | tf_op jit(solution)/shard_map/ppermute | solution.py:649
  30.6 1.6 %collective-permute-start.5 = (bf16[4,256,128]{2,1,0:T(8,128)(2,1)S(1)}, bf16[4,256,128]{2,1,0:T(8,128)(2,1)S(1)}, u32[]{:S(2)}, u32[]{:S(2)}) collective-permute-start(bf16[4,256,128]{2,1,0:T(8,128)(2,1)S(1)} %get-tuple-element.41), channel_id=1, source_target_pairs={{0,1},{1,0},{2,3},{3,2},{4,5},{5,4},{6,7},{7,6},{8,9},{9,8},{10,11... | collective-permute-start | bytes 786440 | tf_op jit(solution)/shard_map/ppermute | solution.py:650
  32.2 29.8 %copy-start = (bf16[8,128,256]{2,1,0:T(8,128)(2,1)S(1)}, bf16[8,128,256]{2,1,0:T(8,128)(2,1)}, u32[]{:S(2)}) copy-start(bf16[8,128,256]{2,1,0:T(8,128)(2,1)} %weight_ref.1) | copy-start | bytes 1572868
  32.6 19.3 %collective-permute-start.6 = (bf16[4,352,128]{2,1,0:T(8,128)(2,1)S(1)}, bf16[4,352,128]{2,1,0:T(8,128)(2,1)S(1)}, u32[]{:S(2)}, u32[]{:S(2)}) collective-permute-start(bf16[4,352,128]{2,1,0:T(8,128)(2,1)S(1)} %get-tuple-element.43), channel_id=1, source_target_pairs={{0,6},{1,7},{2,4},{3,5},{4,2},{5,3},{6,0},{7,1},{8,14},{9,15},{10,... | collective-permute-start | bytes 1081352 | tf_op jit(solution)/shard_map/ppermute | solution.py:48
  34.2 17.7 %collective-permute-start.7 = (bf16[4,352,128]{2,1,0:T(8,128)(2,1)S(1)}, bf16[4,352,128]{2,1,0:T(8,128)(2,1)S(1)}, u32[]{:S(2)}, u32[]{:S(2)}) collective-permute-start(bf16[4,352,128]{2,1,0:T(8,128)(2,1)S(1)} %get-tuple-element.44), channel_id=1, source_target_pairs={{0,4},{1,5},{2,6},{3,7},{4,0},{5,1},{6,2},{7,3},{8,12},{9,13},{10,... | collective-permute-start | bytes 1081352 | tf_op jit(solution)/shard_map/ppermute | solution.py:48
  36.7 15.3 %collective-permute-start.8 = (bf16[4,352,128]{2,1,0:T(8,128)(2,1)S(1)}, bf16[4,352,128]{2,1,0:T(8,128)(2,1)S(1)}, u32[]{:S(2)}, u32[]{:S(2)}) collective-permute-start(bf16[4,352,128]{2,1,0:T(8,128)(2,1)S(1)} %get-tuple-element.45), channel_id=1, source_target_pairs={{0,2},{1,3},{2,0},{3,1},{4,6},{5,7},{6,4},{7,5},{8,10},{9,11},{10,... | collective-permute-start | bytes 1081352 | tf_op jit(solution)/shard_map/ppermute | solution.py:48
  36.7 8.2 %collective-permute-start.10 = (bf16[576,128]{1,0:T(8,128)(2,1)S(1)}, bf16[576,128]{1,0:T(8,128)(2,1)S(1)}, u32[]{:S(2)}, u32[]{:S(2)}) collective-permute-start(bf16[576,128]{1,0:T(8,128)(2,1)S(1)} %get-tuple-element.48), channel_id=1, source_target_pairs={{0,8},{8,0},{16,24},{24,16},{1,9},{9,1},{17,25},{25,17},{2,10},{10... | collective-permute-start | bytes 442376 | tf_op jit(solution)/shard_map/ppermute | solution.py:48
  38.2 11.3 %collective-permute-start.11 = (bf16[576,128]{1,0:T(8,128)(2,1)S(1)}, bf16[576,128]{1,0:T(8,128)(2,1)S(1)}, u32[]{:S(2)}, u32[]{:S(2)}) collective-permute-start(bf16[576,128]{1,0:T(8,128)(2,1)S(1)} %get-tuple-element.49), channel_id=1, source_target_pairs={{0,16},{8,24},{16,0},{24,8},{1,17},{9,25},{17,1},{25,9},{2,18},{10... | collective-permute-start | bytes 442376 | tf_op jit(solution)/shard_map/ppermute | solution.py:48
  44.9 7.0 %collective-permute-start.9 = (bf16[576,128]{1,0:T(8,128)(2,1)S(1)}, bf16[576,128]{1,0:T(8,128)(2,1)S(1)}, u32[]{:S(2)}, u32[]{:S(2)}) collective-permute-start(bf16[576,128]{1,0:T(8,128)(2,1)S(1)} %get-tuple-element.47), channel_id=1, source_target_pairs={{0,24},{8,16},{16,8},{24,0},{1,25},{9,17},{17,9},{25,1},{2,26},{10... | collective-permute-start | bytes 442376 | tf_op jit(solution)/shard_map/ppermute | solution.py:48
  52.2 7.6 %collective-permute-start.15 = (bf16[352,128]{1,0:T(8,128)(2,1)S(1)}, bf16[352,128]{1,0:T(8,128)(2,1)S(1)}, u32[]{:S(2)}, u32[]{:S(2)}) collective-permute-start(bf16[352,128]{1,0:T(8,128)(2,1)S(1)} %get-tuple-element.52), channel_id=1, source_target_pairs={{0,24},{8,16},{16,8},{24,0},{1,25},{9,17},{17,9},{25,1},{2,26},{10... | collective-permute-start | bytes 270344 | tf_op jit(solution)/shard_map/ppermute | solution.py:48
  55.8 9.9 %collective-permute-start.12 = (bf16[576,128]{1,0:T(8,128)(2,1)S(1)}, bf16[576,128]{1,0:T(8,128)(2,1)S(1)}, u32[]{:S(2)}, u32[]{:S(2)}) collective-permute-start(bf16[576,128]{1,0:T(8,128)(2,1)S(1)} %get-tuple-element.50.refs_0_), channel_id=1, source_target_pairs={{0,6},{1,7},{2,4},{3,5},{4,2},{5,3},{6,0},{7,1},{8,14},{9,15},{10,... | collective-permute-start | bytes 442376 | tf_op jit(solution)/shard_map/ppermute | solution.py:48
  58.5 7.3 %collective-permute-start.13 = (bf16[576,128]{1,0:T(8,128)(2,1)S(1)}, bf16[576,128]{1,0:T(8,128)(2,1)S(1)}, u32[]{:S(2)}, u32[]{:S(2)}) collective-permute-start(bf16[576,128]{1,0:T(8,128)(2,1)S(1)} %get-tuple-element.50.refs_0_), channel_id=1, source_target_pairs={{0,4},{1,5},{2,6},{3,7},{4,0},{5,1},{6,2},{7,3},{8,12},{9,13},{10,... | collective-permute-start | bytes 442376 | tf_op jit(solution)/shard_map/ppermute | solution.py:48
  59.1 6.7 %collective-permute-start.14 = (bf16[576,128]{1,0:T(8,128)(2,1)S(1)}, bf16[576,128]{1,0:T(8,128)(2,1)S(1)}, u32[]{:S(2)}, u32[]{:S(2)}) collective-permute-start(bf16[576,128]{1,0:T(8,128)(2,1)S(1)} %get-tuple-element.50.refs_0_), channel_id=1, source_target_pairs={{0,2},{1,3},{2,0},{3,1},{4,6},{5,7},{6,4},{7,5},{8,10},{9,11},{10,... | collective-permute-start | bytes 442376 | tf_op jit(solution)/shard_map/ppermute | solution.py:48
  59.3 6.4 %collective-permute-start.16 = (bf16[352,128]{1,0:T(8,128)(2,1)S(1)}, bf16[352,128]{1,0:T(8,128)(2,1)S(1)}, u32[]{:S(2)}, u32[]{:S(2)}) collective-permute-start(bf16[352,128]{1,0:T(8,128)(2,1)S(1)} %get-tuple-element.53), channel_id=1, source_target_pairs={{0,16},{8,24},{16,0},{24,8},{1,17},{9,25},{17,1},{25,9},{2,18},{10... | collective-permute-start | bytes 270344 | tf_op jit(solution)/shard_map/ppermute | solution.py:48
  59.8 5.9 %collective-permute-start.17 = (bf16[352,128]{1,0:T(8,128)(2,1)S(1)}, bf16[352,128]{1,0:T(8,128)(2,1)S(1)}, u32[]{:S(2)}, u32[]{:S(2)}) collective-permute-start(bf16[352,128]{1,0:T(8,128)(2,1)S(1)} %get-tuple-element.54), channel_id=1, source_target_pairs={{0,8},{8,0},{16,24},{24,16},{1,9},{9,1},{17,25},{25,17},{2,10},{10... | collective-permute-start | bytes 270344 | tf_op jit(solution)/shard_map/ppermute | solution.py:48
  65.9 6.3 %collective-permute-start.18 = (bf16[352,128]{1,0:T(8,128)(2,1)S(1)}, bf16[352,128]{1,0:T(8,128)(2,1)S(1)}, u32[]{:S(2)}, u32[]{:S(2)}) collective-permute-start(bf16[352,128]{1,0:T(8,128)(2,1)S(1)} %get-tuple-element.55.refs_0_), channel_id=1, source_target_pairs={{0,6},{1,7},{2,4},{3,5},{4,2},{5,3},{6,0},{7,1},{8,14},{9,15},{10,... | collective-permute-start | bytes 270344 | tf_op jit(solution)/shard_map/ppermute | solution.py:48
  68.1 4.9 %collective-permute-start.19 = (bf16[352,128]{1,0:T(8,128)(2,1)S(1)}, bf16[352,128]{1,0:T(8,128)(2,1)S(1)}, u32[]{:S(2)}, u32[]{:S(2)}) collective-permute-start(bf16[352,128]{1,0:T(8,128)(2,1)S(1)} %get-tuple-element.55.refs_0_), channel_id=1, source_target_pairs={{0,4},{1,5},{2,6},{3,7},{4,0},{5,1},{6,2},{7,3},{8,12},{9,13},{10,... | collective-permute-start | bytes 270344 | tf_op jit(solution)/shard_map/ppermute | solution.py:48
  69.2 4.5 %collective-permute-start.20 = (bf16[352,128]{1,0:T(8,128)(2,1)S(1)}, bf16[352,128]{1,0:T(8,128)(2,1)S(1)}, u32[]{:S(2)}, u32[]{:S(2)}) collective-permute-start(bf16[352,128]{1,0:T(8,128)(2,1)S(1)} %get-tuple-element.55.refs_0_), channel_id=1, source_target_pairs={{0,2},{1,3},{2,0},{3,1},{4,6},{5,7},{6,4},{7,5},{8,10},{9,11},{10,... | collective-permute-start | bytes 270344 | tf_op jit(solution)/shard_map/ppermute | solution.py:48
  69.4 4.3 %collective-permute-start.25 = (bf16[576,128]{1,0:T(8,128)(2,1)S(1)}, bf16[576,128]{1,0:T(8,128)(2,1)S(1)}, u32[]{:S(2)}, u32[]{:S(2)}) collective-permute-start(bf16[576,128]{1,0:T(8,128)(2,1)S(1)} %get-tuple-element.56.refs_8_), channel_id=1, source_target_pairs={{0,1},{1,0},{2,3},{3,2},{4,5},{5,4},{6,7},{7,6},{8,9},{9,8},{10,11... | collective-permute-start | bytes 442376 | tf_op jit(solution)/shard_map/ppermute | solution.py:660
  69.4 4.3 %collective-permute-start.21 = (bf16[352,128]{1,0:T(8,128)(2,1)S(1)}, bf16[352,128]{1,0:T(8,128)(2,1)S(1)}, u32[]{:S(2)}, u32[]{:S(2)}) collective-permute-start(bf16[352,128]{1,0:T(8,128)(2,1)S(1)} %get-tuple-element.55.refs_0_), channel_id=1, source_target_pairs={{0,1},{1,0},{2,3},{3,2},{4,5},{5,4},{6,7},{7,6},{8,9},{9,8},{10,11... | collective-permute-start | bytes 270344 | tf_op jit(solution)/shard_map/ppermute | solution.py:659
  72.2 1.5 %collective-permute-start.22 = (bf16[352,128]{1,0:T(8,128)(2,1)S(1)}, bf16[352,128]{1,0:T(8,128)(2,1)S(1)}, u32[]{:S(2)}, u32[]{:S(2)}) collective-permute-start(bf16[352,128]{1,0:T(8,128)(2,1)S(1)} %collective-permute-done.18.refs_1_), channel_id=1, source_target_pairs={{0,1},{1,0},{2,3},{3,2},{4,5},{5,4},{6,7},{7,6},{8,9},{9,8},{10,11... | collective-permute-start | bytes 270344 | tf_op jit(solution)/shard_map/ppermute | solution.py:659
  72.9 1.3 %collective-permute-start.23 = (bf16[352,128]{1,0:T(8,128)(2,1)S(1)}, bf16[352,128]{1,0:T(8,128)(2,1)S(1)}, u32[]{:S(2)}, u32[]{:S(2)}) collective-permute-start(bf16[352,128]{1,0:T(8,128)(2,1)S(1)} %collective-permute-done.19.refs_2_), channel_id=1, source_target_pairs={{0,1},{1,0},{2,3},{3,2},{4,5},{5,4},{6,7},{7,6},{8,9},{9,8},{10,11... | collective-permute-start | bytes 270344 | tf_op jit(solution)/shard_map/ppermute | solution.py:659
  73.7 1.3 %collective-permute-start.24 = (bf16[352,128]{1,0:T(8,128)(2,1)S(1)}, bf16[352,128]{1,0:T(8,128)(2,1)S(1)}, u32[]{:S(2)}, u32[]{:S(2)}) collective-permute-start(bf16[352,128]{1,0:T(8,128)(2,1)S(1)} %collective-permute-done.20.refs_3_), channel_id=1, source_target_pairs={{0,1},{1,0},{2,3},{3,2},{4,5},{5,4},{6,7},{7,6},{8,9},{9,8},{10,11... | collective-permute-start | bytes 270344 | tf_op jit(solution)/shard_map/ppermute | solution.py:659

commit v10 on v9

--- a/solution.py
+++ b/solution.py
@@ -14,7 +14,7 @@
 F32 = jnp.float32
 BF16 = jnp.bfloat16
 MIB = 1 << 20
-PLANE_FIRST = 0.7
+PLANE_FIRST = 0.74
 
 VMEM = pl.BlockSpec(memory_space=pltpu.VMEM)
 SMEM = pl.BlockSpec(memory_space=pltpu.SMEM)

time: 76.8 us -> 77 us (level)
  waiting for transfers between devices: 18.2 us -> 19.6 us
  starting transfers between devices: 33.8 us -> 32.6 us
    ppermute x15, waiting for transfers between devices: 12.8 us -> 14.3 us  [exchange(): return lax.ppermute(value, axis, pairs)]
    ppermute x15, starting transfers between devices: 24.4 us -> 23.2 us  [exchange(): return lax.ppermute(value, axis, pairs)]
  transfers between devices with their start and end apart: 26 -> 26, of which waited for: 12 -> 14; matrix products, arithmetic and copies ran while one was open for 0% -> 0% of each run, Pallas kernels for 17% -> 17%
where the time goes in v10:
time: 77 us; the launch traced here: 76.8 us
  starting transfers between devices  32.6 us (42%)
  Pallas kernels  22.7 us (29%)
  waiting for transfers between devices  19.6 us (25%)
  local copies, waits for them, and re-layouts  0.98 us (1%)
  between operations  0.93 us (1%)
    ppermute x15, starting transfers between devices, exchange(): return lax.ppermute(value, axis, pairs)  23.2 us
    ppermute x15, waiting for transfers between devices, exchange(): return lax.ppermute(value, axis, pairs)  14.3 us
    pallas_call x1, Pallas kernels, input_gradient(): pl.pallas_call(input_kernel, out_shape=(out, out, out, windows), in_specs...  7.64 us
    pallas_call x1, Pallas kernels, filter_gradient(): pl.pallas_call(functools.partial(filter_kernel, shard_rows), out_shape=(o...  5.64 us
    ppermute x1, starting transfers between devices, body(): from_upper = lax.ppermute(to_lower, 'dom', [(b, a) for a, b in ring])  3.03 us
    pallas_call x1, Pallas kernels, fine_gradient(): pl.pallas_call(functools.partial(fine_kernel, groups), grid=(3 * groups,)...  2.89 us
    pallas_call x1, Pallas kernels, prepare(): pl.pallas_call(prepare_kernel, out_shape=(jax.ShapeDtypeStruct((slots + 1...  2.73 us
    ppermute x1, starting transfers between devices, body(): low = lax.ppermute(own[:, voxels - PLANE:], 'dom', forward)  2.36 us
  transfers between devices with their start and end apart: 26, of which 14 were waited for; matrix products, arithmetic and copies ran while one was open for 0% of the time, Pallas kernels for 17%

profile of v10, /device:TPU:0, one launch (start us, length us, event | category | flops | bytes accessed | tf_op | source)
XLA Modules:
  0.0 76.8 jit_solution(15103135080812109511)
XLA Ops:
  0.6 0.0 copy-start.2
  0.6 0.0 copy-start.3
  0.7 1.0 %fusion = (bf16[3,64,256]{2,1,0:T(8,128)(2,1)S(1)}, bf16[3,64,256]{2,1,0:T(8,128)(2,1)S(1)}) fusion(bf16[3,512,256]{2,1,0:T(8,128)(2,1)} %bitcast.9), kind=kLoop, calls=%fused_computation | loop fusion | bytes 393216 | tf_op jit(solution)/shard_map/slice | solution.py:637
  1.6 2.4 %collective-permute-start = (bf16[3,64,256]{2,1,0:T(8,128)(2,1)S(1)}, bf16[3,64,256]{2,1,0:T(8,128)(2,1)S(1)}, u32[]{:S(2)}, u32[]{:S(2)}) collective-permute-start(bf16[3,64,256]{2,1,0:T(8,128)(2,1)S(1)} %get-tuple-element.60), channel_id=1, source_target_pairs={{0,1},{1,2},{2,3},{3,4},{4,5},{5,6},{6,7},{8,9},{9,10},{10,11},{11... | collective-permute-start | bytes 294920 | tf_op jit(solution)/shard_map/ppermute | solution.py:636
  4.0 1.3 %collective-permute-start.1 = (bf16[3,64,256]{2,1,0:T(8,128)(2,1)S(1)}, bf16[3,64,256]{2,1,0:T(8,128)(2,1)S(1)}, u32[]{:S(2)}, u32[]{:S(2)}) collective-permute-start(bf16[3,64,256]{2,1,0:T(8,128)(2,1)S(1)} %get-tuple-element.59), channel_id=1, source_target_pairs={{1,0},{2,1},{3,2},{4,3},{5,4},{6,5},{7,6},{9,8},{10,9},{11,10},{12... | collective-permute-start | bytes 294920 | tf_op jit(solution)/shard_map/ppermute | solution.py:637
  5.3 2.7 %prepare.1 = (bf16[4,512,256]{2,1,0:T(8,128)(2,1)S(1)}, bf16[256,1536]{1,0:T(8,128)(2,1)S(1)}, bf16[3,256,2304]{2,1,0:T(8,128)(2,1)S(1)}) custom-call(bf16[1,3,512,256]{3,2,1,0:T(8,128)(2,1)} %own_hbm.1, bf16[1,3,512,256]{3,2,1,0:T(8,128)(2,1)} %pre_hbm.3, bf16[27,256,256]{2,1,0:T(8,128)(2,1)} %weight_hbm.1), custom_call_target="tpu_custom_call" | custom-call | flops 4194304 | bytes 12582912 | tf_op jit(solution)/shard_map/prepare/pallas_call | solution.py:160
  8.0 0.0 collective-permute-done.low_ref
  8.0 1.2 %collective-permute-done.1.high_ref = bf16[3,64,256]{2,1,0:T(8,128)(2,1)S(1)} collective-permute-done((bf16[3,64,256]{2,1,0:T(8,128)(2,1)S(1)}, bf16[3,64,256]{2,1,0:T(8,128)(2,1)S(1)}, u32[]{:S(2)}, u32[]{:S(2)}) %collective-permute-start.1) | collective-permute-done | bytes 98336 | tf_op jit(solution)/shard_map/ppermute | solution.py:637
  9.3 7.6 %input_gradient.1 = (bf16[1,512,256]{2,1,0:T(8,128)(2,1)S(1)}, bf16[1,512,256]{2,1,0:T(8,128)(2,1)S(1)}, bf16[1,512,256]{2,1,0:T(8,128)(2,1)S(1)}, bf16[1920,2304]{1,0:T(8,128)(2,1)S(1)}) custom-call(s32[3,1,27]{2,1,0:T(1,128)S(1)} %bitcast.6, s32[3,1,8]{2,1,0:T(1,128)S(1)} %bitcast.7, bf16[4,512,256]{2,1,0:T(8,128)(2,1)S(1)} %get-tuple-element.31.own_wide, ...), custom_call_target="tpu_custom_call" | custom-call | flops 5435817984 | bytes 8388608 | tf_op jit(solution)/shard_map/input_gradient/pallas_call | solution.py:268
  16.9 3.0 %collective-permute-start.2 = (bf16[1,512,256]{2,1,0:T(8,128)(2,1)S(1)}, bf16[1,512,256]{2,1,0:T(8,128)(2,1)S(1)}, u32[]{:S(2)}, u32[]{:S(2)}) collective-permute-start(bf16[1,512,256]{2,1,0:T(8,128)(2,1)S(1)} %get-tuple-element.33), channel_id=1, source_target_pairs={{1,0},{2,1},{3,2},{4,3},{5,4},{6,5},{7,6},{0,7},{9,8},{10,9},{11,1... | collective-permute-start | bytes 786440 | tf_op jit(solution)/shard_map/ppermute | solution.py:642
  20.0 0.5 collective-permute-start.3
  20.5 5.6 %filter_gradient.1 = (bf16[4,1728,128]{2,1,0:T(8,128)(2,1)S(1)}, bf16[4,1728,128]{2,1,0:T(8,128)(2,1)S(1)}) custom-call(bf16[1920,2304]{1,0:T(8,128)(2,1)S(1)} %get-tuple-element.36.win_ref, bf16[256,1536]{1,0:T(8,128)(2,1)S(1)} %get-tuple-element.37.act_ref), custom_call_target="tpu_custom_call" | custom-call | flops 5435817984 | bytes 8388608 | tf_op jit(solution)/shard_map/filter_gradient/pallas_call | solution.py:324
  26.1 1.6 %collective-permute-start.4 = (bf16[4,1728,128]{2,1,0:T(8,128)(2,1)S(1)}, bf16[4,1728,128]{2,1,0:T(8,128)(2,1)S(1)}, u32[]{:S(2)}, u32[]{:S(2)}) collective-permute-start(bf16[4,1728,128]{2,1,0:T(8,128)(2,1)S(1)} %get-tuple-element.39), channel_id=1, source_target_pairs={{0,1},{1,0},{2,3},{3,2},{4,5},{5,4},{6,7},{7,6},{8,9},{9,8},{10,11... | collective-permute-start | bytes 5308424 | tf_op jit(solution)/shard_map/ppermute | solution.py:649
  27.7 0.0 collective-permute-done.2.upper_ref
  27.7 1.3 %collective-permute-done.3.lower_ref = bf16[1,512,256]{2,1,0:T(8,128)(2,1)S(1)} collective-permute-done((bf16[1,512,256]{2,1,0:T(8,128)(2,1)S(1)}, bf16[1,512,256]{2,1,0:T(8,128)(2,1)S(1)}, u32[]{:S(2)}, u32[]{:S(2)}) %collective-permute-start.3) | collective-permute-done | bytes 262176 | tf_op jit(solution)/shard_map/ppermute | solution.py:643
  29.0 1.5 %down_gradient.1 = (bf16[4,256,128]{2,1,0:T(8,128)(2,1)S(1)}, bf16[4,256,128]{2,1,0:T(8,128)(2,1)S(1)}) custom-call(bf16[1,512,256]{2,1,0:T(8,128)(2,1)S(1)} %collective-permute-done.2.upper_ref, bf16[1,512,256]{2,1,0:T(8,128)(2,1)S(1)} %get-tuple-element.34.stay_ref, bf16[1,512,256]{2,1,0:T(8,128)(2,1)S(1)} %collective-permute-done.3.lower_ref, ...), custom_call_target="tpu_custom_call" | custom-call | flops 25769803776 | bytes 8388608 | tf_op jit(solution)/shard_map/down_gradient/pallas_call | solution.py:386
  30.6 0.1 collective-permute-start.5
  30.6 1.5 %collective-permute-done.5.down_got_ref = bf16[4,256,128]{2,1,0:T(8,128)(2,1)S(1)} collective-permute-done((bf16[4,256,128]{2,1,0:T(8,128)(2,1)S(1)}, bf16[4,256,128]{2,1,0:T(8,128)(2,1)S(1)}, u32[]{:S(2)}, u32[]{:S(2)}) %collective-permute-start.5) | collective-permute-done | bytes 262176 | tf_op jit(solution)/shard_map/ppermute | solution.py:650
  32.2 0.0 collective-permute-done.4.conv_got_ref
  32.2 0.4 pair_sum.1
  32.6 1.6 %collective-permute-start.6 = (bf16[4,368,128]{2,1,0:T(8,128)(2,1)S(1)}, bf16[4,368,128]{2,1,0:T(8,128)(2,1)S(1)}, u32[]{:S(2)}, u32[]{:S(2)}) collective-permute-start(bf16[4,368,128]{2,1,0:T(8,128)(2,1)S(1)} %get-tuple-element.43), channel_id=1, source_target_pairs={{0,6},{1,7},{2,4},{3,5},{4,2},{5,3},{6,0},{7,1},{8,14},{9,15},{10,... | collective-permute-start | bytes 1130504 | tf_op jit(solution)/shard_map/ppermute | solution.py:48
  34.2 2.4 %collective-permute-start.7 = (bf16[4,368,128]{2,1,0:T(8,128)(2,1)S(1)}, bf16[4,368,128]{2,1,0:T(8,128)(2,1)S(1)}, u32[]{:S(2)}, u32[]{:S(2)}) collective-permute-start(bf16[4,368,128]{2,1,0:T(8,128)(2,1)S(1)} %get-tuple-element.44), channel_id=1, source_target_pairs={{0,4},{1,5},{2,6},{3,7},{4,0},{5,1},{6,2},{7,3},{8,12},{9,13},{10,... | collective-permute-start | bytes 1130504 | tf_op jit(solution)/shard_map/ppermute | solution.py:48
  36.7 0.0 collective-permute-start.8
  36.7 1.6 %collective-permute-start.10 = (bf16[512,128]{1,0:T(8,128)(2,1)S(1)}, bf16[512,128]{1,0:T(8,128)(2,1)S(1)}, u32[]{:S(2)}, u32[]{:S(2)}) collective-permute-start(bf16[512,128]{1,0:T(8,128)(2,1)S(1)} %get-tuple-element.48), channel_id=1, source_target_pairs={{0,8},{8,0},{16,24},{24,16},{1,9},{9,1},{17,25},{25,17},{2,10},{10... | collective-permute-start | bytes 393224 | tf_op jit(solution)/shard_map/ppermute | solution.py:48
  38.2 2.6 %collective-permute-start.11 = (bf16[512,128]{1,0:T(8,128)(2,1)S(1)}, bf16[512,128]{1,0:T(8,128)(2,1)S(1)}, u32[]{:S(2)}, u32[]{:S(2)}) collective-permute-start(bf16[512,128]{1,0:T(8,128)(2,1)S(1)} %get-tuple-element.49), channel_id=1, source_target_pairs={{0,16},{8,24},{16,0},{24,8},{1,17},{9,25},{17,1},{25,9},{2,18},{10... | collective-permute-start | bytes 393224 | tf_op jit(solution)/shard_map/ppermute | solution.py:48
  40.9 3.0 %collective-permute-done.10.refs_6_ = bf16[512,128]{1,0:T(8,128)(2,1)S(1)} collective-permute-done((bf16[512,128]{1,0:T(8,128)(2,1)S(1)}, bf16[512,128]{1,0:T(8,128)(2,1)S(1)}, u32[]{:S(2)}, u32[]{:S(2)}) %collective-permute-start.10) | collective-permute-done | bytes 131104 | tf_op jit(solution)/shard_map/ppermute | solution.py:48
  43.8 3.2 %collective-permute-start.9 = (bf16[512,128]{1,0:T(8,128)(2,1)S(1)}, bf16[512,128]{1,0:T(8,128)(2,1)S(1)}, u32[]{:S(2)}, u32[]{:S(2)}) collective-permute-start(bf16[512,128]{1,0:T(8,128)(2,1)S(1)} %get-tuple-element.47), channel_id=1, source_target_pairs={{0,24},{8,16},{16,8},{24,0},{1,25},{9,17},{17,9},{25,1},{2,26},{10... | collective-permute-start | bytes 393224 | tf_op jit(solution)/shard_map/ppermute | solution.py:48
  47.1 1.8 %collective-permute-done.11.refs_7_ = bf16[512,128]{1,0:T(8,128)(2,1)S(1)} collective-permute-done((bf16[512,128]{1,0:T(8,128)(2,1)S(1)}, bf16[512,128]{1,0:T(8,128)(2,1)S(1)}, u32[]{:S(2)}, u32[]{:S(2)}) %collective-permute-start.11) | collective-permute-done | bytes 131104 | tf_op jit(solution)/shard_map/ppermute | solution.py:48
  48.8 1.9 %collective-permute-done.9.refs_5_ = bf16[512,128]{1,0:T(8,128)(2,1)S(1)} collective-permute-done((bf16[512,128]{1,0:T(8,128)(2,1)S(1)}, bf16[512,128]{1,0:T(8,128)(2,1)S(1)}, u32[]{:S(2)}, u32[]{:S(2)}) %collective-permute-start.9) | collective-permute-done | bytes 131104 | tf_op jit(solution)/shard_map/ppermute | solution.py:48
  50.7 0.0 collective-permute-done.6.refs_1_
  50.7 1.7 %collective-permute-done.7.refs_2_ = bf16[4,368,128]{2,1,0:T(8,128)(2,1)S(1)} collective-permute-done((bf16[4,368,128]{2,1,0:T(8,128)(2,1)S(1)}, bf16[4,368,128]{2,1,0:T(8,128)(2,1)S(1)}, u32[]{:S(2)}, u32[]{:S(2)}) %collective-permute-start.7) | collective-permute-done | bytes 376864 | tf_op jit(solution)/shard_map/ppermute | solution.py:48
  52.5 0.2 collective-permute-done.8.refs_3_
  52.6 0.3 middle_sum.1
  52.9 3.7 %collective-permute-start.15 = (bf16[368,128]{1,0:T(8,128)(2,1)S(1)}, bf16[368,128]{1,0:T(8,128)(2,1)S(1)}, u32[]{:S(2)}, u32[]{:S(2)}) collective-permute-start(bf16[368,128]{1,0:T(8,128)(2,1)S(1)} %get-tuple-element.52), channel_id=1, source_target_pairs={{0,24},{8,16},{16,8},{24,0},{1,25},{9,17},{17,9},{25,1},{2,26},{10... | collective-permute-start | bytes 282632 | tf_op jit(solution)/shard_map/ppermute | solution.py:48
  56.5 2.6 %collective-permute-start.12 = (bf16[512,128]{1,0:T(8,128)(2,1)S(1)}, bf16[512,128]{1,0:T(8,128)(2,1)S(1)}, u32[]{:S(2)}, u32[]{:S(2)}) collective-permute-start(bf16[512,128]{1,0:T(8,128)(2,1)S(1)} %get-tuple-element.50.refs_0_), channel_id=1, source_target_pairs={{0,6},{1,7},{2,4},{3,5},{4,2},{5,3},{6,0},{7,1},{8,14},{9,15},{10,... | collective-permute-start | bytes 393224 | tf_op jit(solution)/shard_map/ppermute | solution.py:48
  59.2 0.6 collective-permute-start.13
  59.8 0.2 collective-permute-start.14
  60.0 0.0 collective-permute-start.16
  60.0 0.0 collective-permute-done.15.refs_5_
  60.0 1.0 %collective-permute-start.17 = (bf16[368,128]{1,0:T(8,128)(2,1)S(1)}, bf16[368,128]{1,0:T(8,128)(2,1)S(1)}, u32[]{:S(2)}, u32[]{:S(2)}) collective-permute-start(bf16[368,128]{1,0:T(8,128)(2,1)S(1)} %get-tuple-element.54), channel_id=1, source_target_pairs={{0,8},{8,0},{16,24},{24,16},{1,9},{9,1},{17,25},{25,17},{2,10},{10... | collective-permute-start | bytes 282632 | tf_op jit(solution)/shard_map/ppermute | solution.py:48
  61.1 2.9 %fine_gradient.1.refs_8_ = bf16[24,512,128]{2,1,0:T(8,128)(2,1)} custom-call(bf16[1,512,256]{2,1,0:T(8,128)(2,1)S(1)} %collective-permute-done.2.upper_ref, bf16[1,512,256]{2,1,0:T(8,128)(2,1)S(1)} %get-tuple-element.34.stay_ref, bf16[1,512,256]{2,1,0:T(8,128)(2,1)S(1)} %collective-permute-done.3.lower_ref, bf16[8,128,256]{2,1,0:T(8,128)(2,1)S(1)} %copy-done), custom_call_target="tpu_custom_call" | custom-call | flops 805306368 | bytes 4194304 | tf_op jit(solution)/shard_map/fine_gradient/pallas_call | solution.py:431
  63.9 2.0 %collective-permute-done.16.refs_6_ = bf16[368,128]{1,0:T(8,128)(2,1)S(1)} collective-permute-done((bf16[368,128]{1,0:T(8,128)(2,1)S(1)}, bf16[368,128]{1,0:T(8,128)(2,1)S(1)}, u32[]{:S(2)}, u32[]{:S(2)}) %collective-permute-start.16) | collective-permute-done | bytes 94240 | tf_op jit(solution)/shard_map/ppermute | solution.py:48
  66.0 0.0 collective-permute-done.17.refs_7_
  66.0 0.0 collective-permute-done.12.refs_1_
  66.0 0.0 collective-permute-done.13.refs_2_
  66.0 0.0 collective-permute-done.14.refs_3_
  66.0 0.1 last_sum.1
  66.2 2.7 %collective-permute-start.18 = (bf16[368,128]{1,0:T(8,128)(2,1)S(1)}, bf16[368,128]{1,0:T(8,128)(2,1)S(1)}, u32[]{:S(2)}, u32[]{:S(2)}) collective-permute-start(bf16[368,128]{1,0:T(8,128)(2,1)S(1)} %get-tuple-element.55.refs_0_), channel_id=1, source_target_pairs={{0,6},{1,7},{2,4},{3,5},{4,2},{5,3},{6,0},{7,1},{8,14},{9,15},{10,... | collective-permute-start | bytes 282632 | tf_op jit(solution)/shard_map/ppermute | solution.py:48
  68.9 0.5 collective-permute-start.19
  69.3 0.4 collective-permute-start.20
  69.7 0.0 collective-permute-start.25
  69.7 0.5 collective-permute-start.21
  70.2 1.9 %collective-permute-done.18.refs_1_ = bf16[368,128]{1,0:T(8,128)(2,1)S(1)} collective-permute-done((bf16[368,128]{1,0:T(8,128)(2,1)S(1)}, bf16[368,128]{1,0:T(8,128)(2,1)S(1)}, u32[]{:S(2)}, u32[]{:S(2)}) %collective-permute-start.18) | collective-permute-done | bytes 94240 | tf_op jit(solution)/shard_map/ppermute | solution.py:48
  72.2 0.0 collective-permute-start.22
  72.2 1.3 %collective-permute-done.19.refs_2_ = bf16[368,128]{1,0:T(8,128)(2,1)S(1)} collective-permute-done((bf16[368,128]{1,0:T(8,128)(2,1)S(1)}, bf16[368,128]{1,0:T(8,128)(2,1)S(1)}, u32[]{:S(2)}, u32[]{:S(2)}) %collective-permute-start.19) | collective-permute-done | bytes 94240 | tf_op jit(solution)/shard_map/ppermute | solution.py:48
  73.4 0.0 collective-permute-start.23
  73.4 0.5 collective-permute-done.20.refs_3_
  73.9 0.1 collective-permute-start.24
  74.0 0.0 collective-permute-done.21.refs_4_
  74.0 0.0 collective-permute-done.25.refs_9_
  74.0 0.0 collective-permute-done.22.refs_5_
  74.0 0.8 %collective-permute-done.23.refs_6_ = bf16[368,128]{1,0:T(8,128)(2,1)S(1)} collective-permute-done((bf16[368,128]{1,0:T(8,128)(2,1)S(1)}, bf16[368,128]{1,0:T(8,128)(2,1)S(1)}, u32[]{:S(2)}, u32[]{:S(2)}) %collective-permute-start.23) | collective-permute-done | bytes 94240 | tf_op jit(solution)/shard_map/ppermute | solution.py:659
  74.7 0.5 collective-permute-done.24.refs_7_
  75.2 1.4 %gather_up.1 = (f32[1728,256]{1,0:T(8,128)}, f32[256,256]{1,0:T(8,128)}) custom-call(bf16[368,128]{1,0:T(8,128)(2,1)S(1)} %get-tuple-element.55.refs_0_, bf16[368,128]{1,0:T(8,128)(2,1)S(1)} %collective-permute-done.18.refs_1_, bf16[368,128]{1,0:T(8,128)(2,1)S(1)} %collective-permute-done.19.refs_2_, bf16[368,128]{1,0:T(8,128)(2,1)S(1)} %collective-permute-done.20.refs_3_, ...), custom_call_target="tpu_custom_call" | custom-call | flops 2785280 | bytes 2785280 | tf_op jit(solution)/shard_map/gather_up/pallas_call | solution.py:599
  (6 shorter events, 0.0 us)
Async XLA Ops:
  0.6 8.7 %copy-start.2 = (s32[1,3,27]{2,0,1:T(1,128)S(1)}, s32[1,3,27]{2,0,1:T(1,128)}, u32[]{:S(2)}) copy-start(s32[1,3,27]{2,0,1:T(1,128)} %param.12) | copy-start | bytes 976
  0.6 8.7 %copy-start.3 = (s32[1,1,3,8]{3,1,2,0:T(1,128)S(1)}, s32[1,1,3,8]{3,1,2,0:T(1,128)}, u32[]{:S(2)}) copy-start(s32[1,1,3,8]{3,1,2,0:T(1,128)} %param.13) | copy-start | bytes 292
  1.6 6.4 %collective-permute-start = (bf16[3,64,256]{2,1,0:T(8,128)(2,1)S(1)}, bf16[3,64,256]{2,1,0:T(8,128)(2,1)S(1)}, u32[]{:S(2)}, u32[]{:S(2)}) collective-permute-start(bf16[3,64,256]{2,1,0:T(8,128)(2,1)S(1)} %get-tuple-element.60), channel_id=1, source_target_pairs={{0,1},{1,2},{2,3},{3,4},{4,5},{5,6},{6,7},{8,9},{9,10},{10,11},{11... | collective-permute-start | bytes 294920 | tf_op jit(solution)/shard_map/ppermute | solution.py:636
  4.0 5.3 %collective-permute-start.1 = (bf16[3,64,256]{2,1,0:T(8,128)(2,1)S(1)}, bf16[3,64,256]{2,1,0:T(8,128)(2,1)S(1)}, u32[]{:S(2)}, u32[]{:S(2)}) collective-permute-start(bf16[3,64,256]{2,1,0:T(8,128)(2,1)S(1)} %get-tuple-element.59), channel_id=1, source_target_pairs={{1,0},{2,1},{3,2},{4,3},{5,4},{6,5},{7,6},{9,8},{10,9},{11,10},{12... | collective-permute-start | bytes 294920 | tf_op jit(solution)/shard_map/ppermute | solution.py:637
  16.9 10.8 %collective-permute-start.2 = (bf16[1,512,256]{2,1,0:T(8,128)(2,1)S(1)}, bf16[1,512,256]{2,1,0:T(8,128)(2,1)S(1)}, u32[]{:S(2)}, u32[]{:S(2)}) collective-permute-start(bf16[1,512,256]{2,1,0:T(8,128)(2,1)S(1)} %get-tuple-element.33), channel_id=1, source_target_pairs={{1,0},{2,1},{3,2},{4,3},{5,4},{6,5},{7,6},{0,7},{9,8},{10,9},{11,1... | collective-permute-start | bytes 786440 | tf_op jit(solution)/shard_map/ppermute | solution.py:642
  20.0 9.1 %collective-permute-start.3 = (bf16[1,512,256]{2,1,0:T(8,128)(2,1)S(1)}, bf16[1,512,256]{2,1,0:T(8,128)(2,1)S(1)}, u32[]{:S(2)}, u32[]{:S(2)}) collective-permute-start(bf16[1,512,256]{2,1,0:T(8,128)(2,1)S(1)} %get-tuple-element.35), channel_id=1, source_target_pairs={{0,1},{1,2},{2,3},{3,4},{4,5},{5,6},{6,7},{7,0},{8,9},{9,10},{10,1... | collective-permute-start | bytes 786440 | tf_op jit(solution)/shard_map/ppermute | solution.py:643
  20.5 8.6 %copy-start.1 = (bf16[1,24,512,128]{3,2,1,0:T(8,128)(2,1)S(1)}, bf16[1,24,512,128]{3,2,1,0:T(8,128)(2,1)}, u32[]{:S(2)}) copy-start(bf16[1,24,512,128]{3,2,1,0:T(8,128)(2,1)} %param.11) | copy-start | bytes 9437188
  26.1 6.0 %collective-permute-start.4 = (bf16[4,1728,128]{2,1,0:T(8,128)(2,1)S(1)}, bf16[4,1728,128]{2,1,0:T(8,128)(2,1)S(1)}, u32[]{:S(2)}, u32[]{:S(2)}) collective-permute-start(bf16[4,1728,128]{2,1,0:T(8,128)(2,1)S(1)} %get-tuple-element.39), channel_id=1, source_target_pairs={{0,1},{1,0},{2,3},{3,2},{4,5},{5,4},{6,7},{7,6},{8,9},{9,8},{10,11... | collective-permute-start | bytes 5308424 | tf_op jit(solution)/shard_map/ppermute | solution.py:649
  30.6 1.6 %collective-permute-start.5 = (bf16[4,256,128]{2,1,0:T(8,128)(2,1)S(1)}, bf16[4,256,128]{2,1,0:T(8,128)(2,1)S(1)}, u32[]{:S(2)}, u32[]{:S(2)}) collective-permute-start(bf16[4,256,128]{2,1,0:T(8,128)(2,1)S(1)} %get-tuple-element.41), channel_id=1, source_target_pairs={{0,1},{1,0},{2,3},{3,2},{4,5},{5,4},{6,7},{7,6},{8,9},{9,8},{10,11... | collective-permute-start | bytes 786440 | tf_op jit(solution)/shard_map/ppermute | solution.py:650
  32.2 28.9 %copy-start = (bf16[8,128,256]{2,1,0:T(8,128)(2,1)S(1)}, bf16[8,128,256]{2,1,0:T(8,128)(2,1)}, u32[]{:S(2)}) copy-start(bf16[8,128,256]{2,1,0:T(8,128)(2,1)} %weight_ref.1) | copy-start | bytes 1572868
  32.6 18.1 %collective-permute-start.6 = (bf16[4,368,128]{2,1,0:T(8,128)(2,1)S(1)}, bf16[4,368,128]{2,1,0:T(8,128)(2,1)S(1)}, u32[]{:S(2)}, u32[]{:S(2)}) collective-permute-start(bf16[4,368,128]{2,1,0:T(8,128)(2,1)S(1)} %get-tuple-element.43), channel_id=1, source_target_pairs={{0,6},{1,7},{2,4},{3,5},{4,2},{5,3},{6,0},{7,1},{8,14},{9,15},{10,... | collective-permute-start | bytes 1130504 | tf_op jit(solution)/shard_map/ppermute | solution.py:48
  34.2 18.2 %collective-permute-start.7 = (bf16[4,368,128]{2,1,0:T(8,128)(2,1)S(1)}, bf16[4,368,128]{2,1,0:T(8,128)(2,1)S(1)}, u32[]{:S(2)}, u32[]{:S(2)}) collective-permute-start(bf16[4,368,128]{2,1,0:T(8,128)(2,1)S(1)} %get-tuple-element.44), channel_id=1, source_target_pairs={{0,4},{1,5},{2,6},{3,7},{4,0},{5,1},{6,2},{7,3},{8,12},{9,13},{10,... | collective-permute-start | bytes 1130504 | tf_op jit(solution)/shard_map/ppermute | solution.py:48
  36.7 15.9 %collective-permute-start.8 = (bf16[4,368,128]{2,1,0:T(8,128)(2,1)S(1)}, bf16[4,368,128]{2,1,0:T(8,128)(2,1)S(1)}, u32[]{:S(2)}, u32[]{:S(2)}) collective-permute-start(bf16[4,368,128]{2,1,0:T(8,128)(2,1)S(1)} %get-tuple-element.45), channel_id=1, source_target_pairs={{0,2},{1,3},{2,0},{3,1},{4,6},{5,7},{6,4},{7,5},{8,10},{9,11},{10,... | collective-permute-start | bytes 1130504 | tf_op jit(solution)/shard_map/ppermute | solution.py:48
  36.7 7.2 %collective-permute-start.10 = (bf16[512,128]{1,0:T(8,128)(2,1)S(1)}, bf16[512,128]{1,0:T(8,128)(2,1)S(1)}, u32[]{:S(2)}, u32[]{:S(2)}) collective-permute-start(bf16[512,128]{1,0:T(8,128)(2,1)S(1)} %get-tuple-element.48), channel_id=1, source_target_pairs={{0,8},{8,0},{16,24},{24,16},{1,9},{9,1},{17,25},{25,17},{2,10},{10... | collective-permute-start | bytes 393224 | tf_op jit(solution)/shard_map/ppermute | solution.py:48
  38.2 10.6 %collective-permute-start.11 = (bf16[512,128]{1,0:T(8,128)(2,1)S(1)}, bf16[512,128]{1,0:T(8,128)(2,1)S(1)}, u32[]{:S(2)}, u32[]{:S(2)}) collective-permute-start(bf16[512,128]{1,0:T(8,128)(2,1)S(1)} %get-tuple-element.49), channel_id=1, source_target_pairs={{0,16},{8,24},{16,0},{24,8},{1,17},{9,25},{17,1},{25,9},{2,18},{10... | collective-permute-start | bytes 393224 | tf_op jit(solution)/shard_map/ppermute | solution.py:48
  43.8 6.9 %collective-permute-start.9 = (bf16[512,128]{1,0:T(8,128)(2,1)S(1)}, bf16[512,128]{1,0:T(8,128)(2,1)S(1)}, u32[]{:S(2)}, u32[]{:S(2)}) collective-permute-start(bf16[512,128]{1,0:T(8,128)(2,1)S(1)} %get-tuple-element.47), channel_id=1, source_target_pairs={{0,24},{8,16},{16,8},{24,0},{1,25},{9,17},{17,9},{25,1},{2,26},{10... | collective-permute-start | bytes 393224 | tf_op jit(solution)/shard_map/ppermute | solution.py:48
  52.9 7.2 %collective-permute-start.15 = (bf16[368,128]{1,0:T(8,128)(2,1)S(1)}, bf16[368,128]{1,0:T(8,128)(2,1)S(1)}, u32[]{:S(2)}, u32[]{:S(2)}) collective-permute-start(bf16[368,128]{1,0:T(8,128)(2,1)S(1)} %get-tuple-element.52), channel_id=1, source_target_pairs={{0,24},{8,16},{16,8},{24,0},{1,25},{9,17},{17,9},{25,1},{2,26},{10... | collective-permute-start | bytes 282632 | tf_op jit(solution)/shard_map/ppermute | solution.py:48
  56.5 9.5 %collective-permute-start.12 = (bf16[512,128]{1,0:T(8,128)(2,1)S(1)}, bf16[512,128]{1,0:T(8,128)(2,1)S(1)}, u32[]{:S(2)}, u32[]{:S(2)}) collective-permute-start(bf16[512,128]{1,0:T(8,128)(2,1)S(1)} %get-tuple-element.50.refs_0_), channel_id=1, source_target_pairs={{0,6},{1,7},{2,4},{3,5},{4,2},{5,3},{6,0},{7,1},{8,14},{9,15},{10,... | collective-permute-start | bytes 393224 | tf_op jit(solution)/shard_map/ppermute | solution.py:48
  59.2 6.8 %collective-permute-start.13 = (bf16[512,128]{1,0:T(8,128)(2,1)S(1)}, bf16[512,128]{1,0:T(8,128)(2,1)S(1)}, u32[]{:S(2)}, u32[]{:S(2)}) collective-permute-start(bf16[512,128]{1,0:T(8,128)(2,1)S(1)} %get-tuple-element.50.refs_0_), channel_id=1, source_target_pairs={{0,4},{1,5},{2,6},{3,7},{4,0},{5,1},{6,2},{7,3},{8,12},{9,13},{10,... | collective-permute-start | bytes 393224 | tf_op jit(solution)/shard_map/ppermute | solution.py:48
  59.8 6.2 %collective-permute-start.14 = (bf16[512,128]{1,0:T(8,128)(2,1)S(1)}, bf16[512,128]{1,0:T(8,128)(2,1)S(1)}, u32[]{:S(2)}, u32[]{:S(2)}) collective-permute-start(bf16[512,128]{1,0:T(8,128)(2,1)S(1)} %get-tuple-element.50.refs_0_), channel_id=1, source_target_pairs={{0,2},{1,3},{2,0},{3,1},{4,6},{5,7},{6,4},{7,5},{8,10},{9,11},{10,... | collective-permute-start | bytes 393224 | tf_op jit(solution)/shard_map/ppermute | solution.py:48
  60.0 6.0 %collective-permute-start.16 = (bf16[368,128]{1,0:T(8,128)(2,1)S(1)}, bf16[368,128]{1,0:T(8,128)(2,1)S(1)}, u32[]{:S(2)}, u32[]{:S(2)}) collective-permute-start(bf16[368,128]{1,0:T(8,128)(2,1)S(1)} %get-tuple-element.53), channel_id=1, source_target_pairs={{0,16},{8,24},{16,0},{24,8},{1,17},{9,25},{17,1},{25,9},{2,18},{10... | collective-permute-start | bytes 282632 | tf_op jit(solution)/shard_map/ppermute | solution.py:48
  60.0 6.0 %collective-permute-start.17 = (bf16[368,128]{1,0:T(8,128)(2,1)S(1)}, bf16[368,128]{1,0:T(8,128)(2,1)S(1)}, u32[]{:S(2)}, u32[]{:S(2)}) collective-permute-start(bf16[368,128]{1,0:T(8,128)(2,1)S(1)} %get-tuple-element.54), channel_id=1, source_target_pairs={{0,8},{8,0},{16,24},{24,16},{1,9},{9,1},{17,25},{25,17},{2,10},{10... | collective-permute-start | bytes 282632 | tf_op jit(solution)/shard_map/ppermute | solution.py:48
  66.2 6.0 %collective-permute-start.18 = (bf16[368,128]{1,0:T(8,128)(2,1)S(1)}, bf16[368,128]{1,0:T(8,128)(2,1)S(1)}, u32[]{:S(2)}, u32[]{:S(2)}) collective-permute-start(bf16[368,128]{1,0:T(8,128)(2,1)S(1)} %get-tuple-element.55.refs_0_), channel_id=1, source_target_pairs={{0,6},{1,7},{2,4},{3,5},{4,2},{5,3},{6,0},{7,1},{8,14},{9,15},{10,... | collective-permute-start | bytes 282632 | tf_op jit(solution)/shard_map/ppermute | solution.py:48
  68.9 4.6 %collective-permute-start.19 = (bf16[368,128]{1,0:T(8,128)(2,1)S(1)}, bf16[368,128]{1,0:T(8,128)(2,1)S(1)}, u32[]{:S(2)}, u32[]{:S(2)}) collective-permute-start(bf16[368,128]{1,0:T(8,128)(2,1)S(1)} %get-tuple-element.55.refs_0_), channel_id=1, source_target_pairs={{0,4},{1,5},{2,6},{3,7},{4,0},{5,1},{6,2},{7,3},{8,12},{9,13},{10,... | collective-permute-start | bytes 282632 | tf_op jit(solution)/shard_map/ppermute | solution.py:48
  69.3 4.6 %collective-permute-start.20 = (bf16[368,128]{1,0:T(8,128)(2,1)S(1)}, bf16[368,128]{1,0:T(8,128)(2,1)S(1)}, u32[]{:S(2)}, u32[]{:S(2)}) collective-permute-start(bf16[368,128]{1,0:T(8,128)(2,1)S(1)} %get-tuple-element.55.refs_0_), channel_id=1, source_target_pairs={{0,2},{1,3},{2,0},{3,1},{4,6},{5,7},{6,4},{7,5},{8,10},{9,11},{10,... | collective-permute-start | bytes 282632 | tf_op jit(solution)/shard_map/ppermute | solution.py:48
  69.7 4.3 %collective-permute-start.25 = (bf16[512,128]{1,0:T(8,128)(2,1)S(1)}, bf16[512,128]{1,0:T(8,128)(2,1)S(1)}, u32[]{:S(2)}, u32[]{:S(2)}) collective-permute-start(bf16[512,128]{1,0:T(8,128)(2,1)S(1)} %get-tuple-element.56.refs_8_), channel_id=1, source_target_pairs={{0,1},{1,0},{2,3},{3,2},{4,5},{5,4},{6,7},{7,6},{8,9},{9,8},{10,11... | collective-permute-start | bytes 393224 | tf_op jit(solution)/shard_map/ppermute | solution.py:660
  69.7 4.3 %collective-permute-start.21 = (bf16[368,128]{1,0:T(8,128)(2,1)S(1)}, bf16[368,128]{1,0:T(8,128)(2,1)S(1)}, u32[]{:S(2)}, u32[]{:S(2)}) collective-permute-start(bf16[368,128]{1,0:T(8,128)(2,1)S(1)} %get-tuple-element.55.refs_0_), channel_id=1, source_target_pairs={{0,1},{1,0},{2,3},{3,2},{4,5},{5,4},{6,7},{7,6},{8,9},{9,8},{10,11... | collective-permute-start | bytes 282632 | tf_op jit(solution)/shard_map/ppermute | solution.py:659
  72.2 1.8 %collective-permute-start.22 = (bf16[368,128]{1,0:T(8,128)(2,1)S(1)}, bf16[368,128]{1,0:T(8,128)(2,1)S(1)}, u32[]{:S(2)}, u32[]{:S(2)}) collective-permute-start(bf16[368,128]{1,0:T(8,128)(2,1)S(1)} %collective-permute-done.18.refs_1_), channel_id=1, source_target_pairs={{0,1},{1,0},{2,3},{3,2},{4,5},{5,4},{6,7},{7,6},{8,9},{9,8},{10,11... | collective-permute-start | bytes 282632 | tf_op jit(solution)/shard_map/ppermute | solution.py:659
  73.4 1.3 %collective-permute-start.23 = (bf16[368,128]{1,0:T(8,128)(2,1)S(1)}, bf16[368,128]{1,0:T(8,128)(2,1)S(1)}, u32[]{:S(2)}, u32[]{:S(2)}) collective-permute-start(bf16[368,128]{1,0:T(8,128)(2,1)S(1)} %collective-permute-done.19.refs_2_), channel_id=1, source_target_pairs={{0,1},{1,0},{2,3},{3,2},{4,5},{5,4},{6,7},{7,6},{8,9},{9,8},{10,11... | collective-permute-start | bytes 282632 | tf_op jit(solution)/shard_map/ppermute | solution.py:659
  73.9 1.3 %collective-permute-start.24 = (bf16[368,128]{1,0:T(8,128)(2,1)S(1)}, bf16[368,128]{1,0:T(8,128)(2,1)S(1)}, u32[]{:S(2)}, u32[]{:S(2)}) collective-permute-start(bf16[368,128]{1,0:T(8,128)(2,1)S(1)} %collective-permute-done.20.refs_3_), channel_id=1, source_target_pairs={{0,1},{1,0},{2,3},{3,2},{4,5},{5,4},{6,7},{7,6},{8,9},{9,8},{10,11... | collective-permute-start | bytes 282632 | tf_op jit(solution)/shard_map/ppermute | solution.py:659
